TPU v7x, 32 devices: a whole 2x2x4 slice. The times are simulated.
32 devices in a mesh: pu: 4 (over y, core), pv: 8 (over z, x).
Axes of the slice: x: 2, y: 2, z: 4, core: 2. Of those that a mesh axis runs over, the one named last changes fastest.
Arguments:
- density: bfloat16 [24, 48, 128, 768], P('pu', 'pv'), may hold values from -6 to 6
- near_blocks: bfloat16 [24, 48, 6, 128, 128], P('pu', 'pv'), may hold values from -0.21875 to 0.21875
- neighbours: int32 [24, 48, 6], P('pu', 'pv'), may hold values from 0 to 9
- far_right: bfloat16 [24, 48, 128, 128], P('pu', 'pv'), may hold values from -0.09375 to 0.09375
- far_left: float32 [4, 8, 1024, 128], P('pu', 'pv'), may hold values from -0.1875 to 0.1875
- sketch: float32 [256, 128], replicated, may hold values from -0.375 to 0.375
- patch_order: int32 [32], replicated, may hold values from 0 to 31, each once
Outputs:
- corrected: bfloat16 [24, 48, 128, 768], P('pu', 'pv')
- far_field: float32 [1024, 768], P('pu', 'pv')
Inputs may be any that keep to these rules, and one draw needn't show every extreme that they name: `neighbours`: entry e < 9 names the block displaced by e // 3 - 1 patch rows and e % 3 - 1 patch columns (e = 4 is the block itself); 9 marks an empty slot. `patch_order`: A permutation of the patches.
All inputs are finite; a program needn't handle non-finite values.
Results may differ from a plain program's by a relative error of at most 0.0028.
Values may be sent and summed in bfloat16 or wider, within the bound.
No kernel may reach another device: no remote copies, remote signals or barrier semaphores. Data moves between devices by JAX's collectives and lax.ppermute only.
A program may use at most 256 MiB of HBM per device.

v0:
```python
import functools

import jax
import jax.numpy as jnp
from jax import lax
from jax.experimental import pallas as pl
from jax.experimental.pallas import tpu as pltpu
from jax.sharding import PartitionSpec as P

high = lax.Precision.HIGH
empty_slot = 9
vmem_bytes = 48 * 1024 * 1024


def dot_t(a, b, dims, precision=None):
    return lax.dot_general(
        a, b, (dims, ((), ())), precision=precision, preferred_element_type=jnp.float32
    )


def split_dot(a, b, dims):
    return dot_t(a, b, dims, high)


def near_kernel(spans, centre_base, centre_step, n_src, nb_ref, *refs):
    srcs = refs[:n_src]
    near_ref, right_ref = refs[n_src : n_src + 2]
    out_ref, coef_ref, ext_ref, sems = refs[-4:]
    i = pl.program_id(0)
    j = pl.program_id(1)
    rows = ext_ref.shape[0]

    def copies(row):
        found = []
        for index, (source, at, ext_row, ext_col, width) in enumerate(spans):
            if ext_row != row:
                continue
            view = srcs[source]
            for step in at:
                view = view.at[step]
            found.append(
                pltpu.make_async_copy(
                    view, ext_ref.at[ext_row, pl.ds(ext_col, width)], sems.at[index]
                )
            )
        return found

    first = jnp.logical_and(i == 0, j == 0)

    @pl.when(first)
    def _():
        for row in range(rows):
            for copy in copies(row):
                copy.start()
        coef_ref[...] = jnp.zeros_like(coef_ref)
        for row in range(2):
            for copy in copies(row):
                copy.wait()

    for row in range(2, rows):

        @pl.when(jnp.logical_and(j == 0, i == row - 2))
        def _():
            for copy in copies(row):
                copy.wait()

    centre = centre_base + centre_step * j
    total = ext_ref[i + 1, centre].astype(jnp.float32)
    slots = near_ref.shape[2]
    col = centre_base + centre_step * j if centre_step == 1 else j * (nb_ref.shape[1] - 1)
    for slot in range(0, slots, 2):
        weights = []
        values = []
        for part in range(slot, min(slot + 2, slots)):
            link = nb_ref[i, col, part]
            place = jnp.minimum(link, empty_slot - 1)
            weight = near_ref[0, 0, part]
            weights.append(jnp.where(link < empty_slot, weight, jnp.zeros_like(weight)))
            values.append(ext_ref[i + lax.div(place, 3), centre - 1 + lax.rem(place, 3)])
        total = total + jnp.dot(
            jnp.concatenate(weights, axis=1),
            jnp.concatenate(values, axis=0),
            preferred_element_type=jnp.float32,
        )
    corrected = total.astype(jnp.bfloat16)
    out_ref[0, 0] = corrected
    coef_ref[...] += dot_t(right_ref[0, 0], corrected, ((0,), (0,)))


def near_part(sources, spans, ext_cols, centre, column, n_cols, near_blocks, far_right, neighbours, prior):
    gu, gv, slots, size, _ = near_blocks.shape
    rhs = sources[0].shape[-1]
    rank = far_right.shape[-1]
    kernel = functools.partial(near_kernel, spans, centre[0], centre[1], len(sources))
    block = pl.BlockSpec((1, 1, size, rhs), lambda i, j, nb: (i, column(j), 0, 0))
    in_specs = [pl.BlockSpec(memory_space=pl.ANY)] * len(sources) + [
        pl.BlockSpec((1, 1, slots, size, size), lambda i, j, nb: (i, column(j), 0, 0, 0)),
        pl.BlockSpec((1, 1, size, rank), lambda i, j, nb: (i, column(j), 0, 0)),
    ]
    args = list(sources) + [near_blocks, far_right]
    aliases = {}
    if prior is not None:
        in_specs.append(pl.BlockSpec(memory_space=pl.ANY))
        args.append(prior)
        aliases = {len(args): 0}
    return pl.pallas_call(
        kernel,
        grid_spec=pltpu.PrefetchScalarGridSpec(
            num_scalar_prefetch=1,
            grid=(gu, n_cols),
            in_specs=in_specs,
            out_specs=[block, pl.BlockSpec((rank, rhs), lambda i, j, nb: (0, 0))],
            scratch_shapes=[
                pltpu.VMEM((gu + 2, ext_cols, size, rhs), jnp.bfloat16),
                pltpu.SemaphoreType.DMA((len(spans),)),
            ],
        ),
        out_shape=[
            jax.ShapeDtypeStruct((gu, gv, size, rhs), jnp.bfloat16),
            jax.ShapeDtypeStruct((rank, rhs), jnp.float32),
        ],
        input_output_aliases=aliases,
        compiler_params=pltpu.CompilerParams(
            dimension_semantics=("arbitrary", "arbitrary"), vmem_limit_bytes=vmem_bytes
        ),
    )(neighbours, *args)


def near_inner(density, top, bottom, near_blocks, far_right, neighbours):
    gu, gv = density.shape[:2]
    spans = [(1, (0,), 0, 0, gv)]
    spans += [(0, (row,), row + 1, 0, gv) for row in range(gu)]
    spans += [(2, (0,), gu + 1, 0, gv)]
    return near_part(
        (density, top, bottom), spans, gv, (1, 1), lambda j: j + 1, gv - 2, near_blocks, far_right, neighbours, None
    )


def near_outer(density, top, bottom, left, right, corner_top, corner_bottom, near_blocks, far_right, neighbours, prior):
    gu, gv = density.shape[:2]
    spans = []
    for ext_row, source, at in (
        [(0, 1, (0,))] + [(row + 1, 0, (row,)) for row in range(gu)] + [(gu + 1, 2, (0,))]
    ):
        spans.append((source, at + (pl.ds(0, 2),), ext_row, 1, 2))
        spans.append((source, at + (pl.ds(gv - 2, 2),), ext_row, 3, 2))
    for row in range(gu):
        spans.append((3, (row,), row + 1, 0, 1))
        spans.append((4, (row,), row + 1, 5, 1))
    for source, ext_row in ((5, 0), (6, gu + 1)):
        spans.append((source, (pl.ds(0, 1),), ext_row, 0, 1))
        spans.append((source, (pl.ds(1, 1),), ext_row, 5, 1))
    return near_part(
        (density, top, bottom, left, right, corner_top, corner_bottom),
        spans,
        6,
        (1, 3),
        lambda j: j * (gv - 1),
        2,
        near_blocks,
        far_right,
        neighbours,
        prior,
    )


def eliminate(w_k, w_e):
    size = w_k.shape[0]
    step = 32
    tile = 8
    sub = lax.broadcasted_iota(jnp.int32, (tile, size), 0)
    for base in range(0, size, step):
        count = step // tile
        k_rows = [w_k[base + tile * r : base + tile * (r + 1), :] for r in range(count)]
        e_rows = [w_e[base + tile * r : base + tile * (r + 1), :] for r in range(count)]
        for q in range(count):
            at = base + tile * q
            cols = {
                (r, k): jnp.broadcast_to(k_rows[r][:, at + k : at + k + 1], (tile, size))
                for r in range(q, count)
                for k in range(tile)
            }
            pivots = jnp.ones((tile, size), jnp.float32)
            for k in range(tile):
                pivot = jnp.broadcast_to(cols[q, k][k : k + 1, :], (tile, size))
                pivots = jnp.where(sub == k, pivot, pivots)
                inverse = 1.0 / pivot
                k_pivot = jnp.broadcast_to(k_rows[q][k : k + 1, :], (tile, size)) * inverse
                e_pivot = jnp.broadcast_to(e_rows[q][k : k + 1, :], (tile, size)) * inverse
                links = {
                    m: jnp.broadcast_to(cols[q, k][m : m + 1, :], (tile, size)) * inverse
                    for m in range(k + 1, tile)
                }
                for r in range(q, count):
                    factor = cols[r, k]
                    if r == q:
                        factor = jnp.where(sub > k, factor, 0.0)
                    for m in range(k + 1, tile):
                        cols[r, m] = cols[r, m] - factor * links[m]
                    k_rows[r] = k_rows[r] - factor * k_pivot
                    e_rows[r] = e_rows[r] - factor * e_pivot
            root = lax.rsqrt(pivots)
            k_rows[q] = k_rows[q] * root
            e_rows[q] = e_rows[q] * root
        e_now = jnp.concatenate(e_rows, axis=0)
        w_e[base : base + step, :] = e_now
        if base + step < size:
            k_now = jnp.concatenate(k_rows, axis=0)
            k_hi = k_now.astype(jnp.bfloat16)
            k_lo = (k_now - k_hi.astype(jnp.float32)).astype(jnp.bfloat16)
            e_hi = e_now.astype(jnp.bfloat16)
            e_lo = (e_now - e_hi.astype(jnp.float32)).astype(jnp.bfloat16)
            lhs = jnp.concatenate([k_hi, k_hi, k_lo], axis=0)
            k_rhs = jnp.concatenate([k_hi, k_lo, k_hi], axis=0)
            e_rhs = jnp.concatenate([e_hi, e_lo, e_hi], axis=0)
            k_fall = dot_t(lhs, k_rhs, ((0,), (0,)))
            e_fall = dot_t(lhs, e_rhs, ((0,), (0,)))
            w_k[base + step :, :] -= k_fall[base + step :, :]
            w_e[base + step :, :] -= e_fall[base + step :, :]


def merge_kernel(lead_ref, mine_ref, other_ref, sketch_ref, path_ref, left_ref, new_path_ref, w_k, w_e):
    rank = mine_ref.shape[1]
    lead = lead_ref[0] > 0
    first = sketch_ref[:rank, :]
    second = sketch_ref[rank:, :]
    mine = mine_ref[...]
    sketched = split_dot(mine, jnp.where(lead, first, second), ((1,), (0,))) + split_dot(
        other_ref[...], jnp.where(lead, second, first), ((1,), (0,))
    )
    w_k[...] = split_dot(sketched, sketched, ((0,), (0,)))
    rows = lax.broadcasted_iota(jnp.int32, (rank, rank), 0)
    cols = lax.broadcasted_iota(jnp.int32, (rank, rank), 1)
    w_e[...] = jnp.where(rows == cols, 1.0, 0.0)
    eliminate(w_k, w_e)
    inverse = w_e[...]
    left_ref[...] = split_dot(sketched, inverse, ((1,), (1,)))
    own = split_dot(sketched, mine, ((0,), (0,)))
    new_path_ref[...] = split_dot(inverse, split_dot(own, path_ref[...], ((1,), (0,))), ((1,), (0,)))


def merge(lead, mine, other, sketch, path):
    rows, rank = mine.shape
    whole = pl.BlockSpec(memory_space=pltpu.VMEM)
    return pl.pallas_call(
        merge_kernel,
        in_specs=[pl.BlockSpec(memory_space=pltpu.SMEM), whole, whole, whole, whole],
        out_specs=[whole, whole],
        out_shape=[
            jax.ShapeDtypeStruct((rows, rank), jnp.float32),
            jax.ShapeDtypeStruct((rank, rank), jnp.float32),
        ],
        scratch_shapes=[pltpu.VMEM((rank, rank), jnp.float32), pltpu.VMEM((rank, rank), jnp.float32)],
        compiler_params=pltpu.CompilerParams(vmem_limit_bytes=vmem_bytes),
    )(lead, mine, other, sketch, path)


def from_partner(value, axis, distance):
    mask = 2**distance
    pairs = [(source, source ^ mask) for source in range(lax.axis_size(axis))]
    return lax.ppermute(value, axis, pairs)


def mine_leads(group_keys, position, tree_level):
    block_min = group_keys.reshape(-1, 1 << tree_level).min(axis=1)
    mine_key = block_min[position >> tree_level]
    their_key = block_min[position >> tree_level ^ 1]
    return (mine_key < their_key).astype(jnp.int32).reshape(1)


def shifted(value, axis, by):
    count = lax.axis_size(axis)
    return lax.ppermute(value, axis, [(i, i + by) for i in range(count) if 0 <= i + by < count])


def per_device(density, near_blocks, neighbours, far_right, far_left, sketch, patch_order):
    pu_count = lax.axis_size("pu")
    pv_count = lax.axis_size("pv")
    pu_index = lax.axis_index("pu")
    pv_index = lax.axis_index("pv")
    key_grid = patch_order.reshape(pu_count, pv_count)
    row_keys = lax.dynamic_index_in_dim(key_grid, pu_index, 0, keepdims=False)
    column_keys = key_grid.min(axis=1)
    gu, gv, size, rhs = density.shape

    left_now = far_left[0, 0]
    rank = left_now.shape[1]
    path = jnp.eye(rank, dtype=jnp.float32)
    other = from_partner(left_now, "pv", 0)

    left = shifted(density[:, gv - 1 :], "pv", 1)
    right = shifted(density[:, :1], "pv", -1)
    top = shifted(density[gu - 1 :], "pu", 1)
    bottom = shifted(density[:1], "pu", -1)

    corrected, inner_coef = near_inner(density, top, bottom, near_blocks, far_right, neighbours)

    corner_top = shifted(jnp.concatenate([left[gu - 1], right[gu - 1]], axis=0), "pu", 1)
    corner_bottom = shifted(jnp.concatenate([left[0], right[0]], axis=0), "pu", -1)

    pv_levels = pv_count.bit_length() - 1
    pu_levels = pu_count.bit_length() - 1
    for level in range(pv_levels + pu_levels):
        if level < pv_levels:
            lead = mine_leads(row_keys, pv_index, level)
            if level:
                other = from_partner(left_now, "pv", level)
        else:
            lead = mine_leads(column_keys, pu_index, level - pv_levels)
            other = from_partner(left_now, "pu", level - pv_levels)
        left_now, path = merge(lead, left_now, other, sketch, path)

    corrected, outer_coef = near_outer(
        density, top, bottom, left, right, corner_top, corner_bottom, near_blocks, far_right, neighbours, corrected
    )
    coef = inner_coef + outer_coef
    share = lax.dot_general(coef, path, (((0,), (1,)), ((), ())), precision=high)
    chunks = lax.all_to_all(share.reshape(pv_count, rhs // pv_count, rank), "pv", 0, 0)
    root_coef = chunks.sum(axis=0)
    for level in range(pu_levels):
        root_coef = root_coef + from_partner(root_coef, "pu", level)
    obs_rows = left_now.shape[0] // pu_count
    left_rows = lax.dynamic_slice_in_dim(left_now, pu_index * obs_rows, obs_rows, 0)
    far_field = lax.dot_general(left_rows, root_coef, (((1,), (1,)), ((), ())), precision=high)
    return (corrected, far_field)


def solution(mesh):
    in_specs = (
        P("pu", "pv", None, None),
        P("pu", "pv", None, None, None),
        P("pu", "pv", None),
        P("pu", "pv", None, None),
        P("pu", "pv", None, None),
        P(),
        P(),
    )
    out_specs = (P("pu", "pv", None, None), P("pu", "pv"))
    return jax.shard_map(
        per_device, mesh=mesh, in_specs=in_specs, out_specs=out_specs, check_vma=False
    )
```

profile of v0, /device:TPU:0, one launch (start us, length us, event | category | flops | bytes accessed | tf_op | source)
XLA Modules:
  0.0 202.1 jit_solution(716003585227768600)
XLA Ops:
  0.7 3.0 %collective-permute-start.6 = (f32[1024,128]{1,0:T(8,128)}, f32[1024,128]{1,0:T(8,128)S(1)}, u32[]{:S(2)}, u32[]{:S(2)}) collective-permute-start(f32[1024,128]{1,0:T(8,128)} %bitcast.14), channel_id=1, source_target_pairs={{0,1},{1,0},{2,3},{3,2},{4,5},{5,4},{6,7},{7,6},{8,9},{9,8},{10,11... | collective-permute-start | bytes 1572872 | tf_op jit(solution)/shard_map/ppermute | solution.py:261
  3.7 3.2 %fusion.9 = (bf16[6,1,128,768]{3,2,1,0:T(8,128)(2,1)}, bf16[6,1,128,768]{3,2,1,0:T(8,128)(2,1)}) fusion(bf16[6,6,128,768]{3,2,1,0:T(8,128)(2,1)} %refs_0_.3), kind=kLoop, calls=%fused_computation.17 | loop fusion | bytes 4718592 | tf_op jit(solution)/shard_map/slice | solution.py:292
  6.9 1.3 collective-permute-start.3
  10.2 30.3 %collective-permute-done.6.other_ref = f32[1024,128]{1,0:T(8,128)S(1)} collective-permute-done((f32[1024,128]{1,0:T(8,128)}, f32[1024,128]{1,0:T(8,128)S(1)}, u32[]{:S(2)}, u32[]{:S(2)}) %collective-permute-start.6) | collective-permute-done | bytes 524320 | tf_op jit(solution)/shard_map/ppermute | solution.py:261
  40.4 6.0 %shard_map.88 = (f32[1024,128]{1,0:T(8,128)S(1)}, f32[128,128]{1,0:T(8,128)S(1)}) custom-call(s32[1]{0:T(128)} %bitcast.4.lead_ref, f32[1024,128]{1,0:T(8,128)S(1)} %bitcast.15, f32[1024,128]{1,0:T(8,128)S(1)} %collective-permute-done.6.other_ref, f32[256,128]{1,0:T(8,128)S(1)} %copy-done.1, f32[128,128]{1,0:T(8,128)S(1)} %fusion.4.path_ref), custom_call_target="tpu_custom_call" | custom-call | tf_op jit(solution)/shard_map/pallas_call | solution.py:245
  46.4 1.6 collective-permute-start.7
  48.1 5.3 %collective-permute-start.2 = (bf16[6,1,128,768]{3,2,1,0:T(8,128)(2,1)}, bf16[6,1,128,768]{3,2,1,0:T(8,128)(2,1)}, u32[]{:S(2)}, u32[]{:S(2)}) collective-permute-start(bf16[6,1,128,768]{3,2,1,0:T(8,128)(2,1)} %get-tuple-element.31), channel_id=1, source_target_pairs={{0,1},{1,2},{2,3},{3,4},{4,5},{5,6},{6,7},{8,9},{9,10},{10,11},{11... | collective-permute-start | bytes 3538952 | tf_op jit(solution)/shard_map/ppermute | solution.py:273
  55.5 3.8 %collective-permute-done.7.other_ref = f32[1024,128]{1,0:T(8,128)S(1)} collective-permute-done((f32[1024,128]{1,0:T(8,128)S(1)}, f32[1024,128]{1,0:T(8,128)S(1)}, u32[]{:S(2)}, u32[]{:S(2)}) %collective-permute-start.7) | collective-permute-done | bytes 524320 | tf_op jit(solution)/shard_map/ppermute | solution.py:261
  59.3 6.0 %shard_map.89 = (f32[1024,128]{1,0:T(8,128)S(1)}, f32[128,128]{1,0:T(8,128)S(1)}) custom-call(s32[1]{0:T(128)S(6)} %convert_element_type.24.lead_ref, f32[1024,128]{1,0:T(8,128)S(1)} %get-tuple-element.18.mine_ref, f32[1024,128]{1,0:T(8,128)S(1)} %collective-permute-done.7.other_ref, f32[256,128]{1,0:T(8,128)S(1)} %copy-done.1, ...), custom_call_target="tpu_custom_call" | custom-call | tf_op jit(solution)/shard_map/pallas_call | solution.py:245
  65.3 2.6 %collective-permute-start.8 = (f32[1024,128]{1,0:T(8,128)S(1)}, f32[1024,128]{1,0:T(8,128)S(1)}, u32[]{:S(2)}, u32[]{:S(2)}) collective-permute-start(f32[1024,128]{1,0:T(8,128)S(1)} %get-tuple-element.20.mine_ref), channel_id=1, source_target_pairs={{0,4},{1,5},{2,6},{3,7},{4,0},{5,1},{6,2},{7,3},{8,12},{9,13},{10,... | collective-permute-start | bytes 1572872 | tf_op jit(solution)/shard_map/ppermute | solution.py:261
  68.0 3.2 %fusion.10 = (bf16[1,6,128,768]{3,2,1,0:T(8,128)(2,1)}, bf16[1,6,128,768]{3,2,1,0:T(8,128)(2,1)}) fusion(bf16[6,6,128,768]{3,2,1,0:T(8,128)(2,1)} %refs_0_.3), kind=kLoop, calls=%fused_computation.18 | loop fusion | bytes 4718592 | tf_op jit(solution)/shard_map/slice | solution.py:294
  71.1 1.4 collective-permute-start
  72.5 1.5 collective-permute-start.1
  76.0 13.5 %collective-permute-done.8.other_ref = f32[1024,128]{1,0:T(8,128)S(1)} collective-permute-done((f32[1024,128]{1,0:T(8,128)S(1)}, f32[1024,128]{1,0:T(8,128)S(1)}, u32[]{:S(2)}, u32[]{:S(2)}) %collective-permute-start.8) | collective-permute-done | bytes 524320 | tf_op jit(solution)/shard_map/ppermute | solution.py:261
  90.3 1.0 copy-done.8
  92.1 6.0 %shard_map.90 = (f32[1024,128]{1,0:T(8,128)S(1)}, f32[128,128]{1,0:T(8,128)S(1)}) custom-call(s32[1]{0:T(128)S(6)} %convert_element_type.23.lead_ref, f32[1024,128]{1,0:T(8,128)S(1)} %get-tuple-element.20.mine_ref, f32[1024,128]{1,0:T(8,128)S(1)} %copy-done.8, f32[256,128]{1,0:T(8,128)S(1)} %copy-done.1, f32[128,128]{1,0:T(8,128)S(1)} %copy-done.15), custom_call_target="tpu_custom_call" | custom-call | tf_op jit(solution)/shard_map/pallas_call | solution.py:245
  100.8 1.0 slice_bitcast_fusion
  101.8 1.0 slice_bitcast_fusion.1
  103.7 0.9 copy-done.2
  104.6 1.0 copy-done.6
  105.7 1.0 copy-done.10
  106.7 6.4 %shard_map.91 = (f32[1024,128]{1,0:T(8,128)}, f32[128,128]{1,0:T(8,128)S(1)}) custom-call(s32[1]{0:T(128)S(6)} %convert_element_type.22.lead_ref, f32[1024,128]{1,0:T(8,128)S(1)} %copy-done.6, f32[1024,128]{1,0:T(8,128)S(1)} %copy-done.10, f32[256,128]{1,0:T(8,128)S(1)} %copy-done.2, f32[128,128]{1,0:T(8,128)S(1)} %copy-done.17), custom_call_target="tpu_custom_call" | custom-call | tf_op jit(solution)/shard_map/pallas_call | solution.py:245
  113.7 1.5 collective-permute-start.10
  116.0 2.9 %collective-permute-start.4 = (bf16[2,128,768]{2,1,0:T(8,128)(2,1)}, bf16[2,128,768]{2,1,0:T(8,128)(2,1)}, u32[]{:S(2)}, u32[]{:S(2)}) collective-permute-start(bf16[2,128,768]{2,1,0:T(8,128)(2,1)} %pad_maximum_fusion), channel_id=1, source_target_pairs={{0,8},{8,16},{16,24},{1,9},{9,17},{17,25},{2,10},{10,18},{18,26},{... | collective-permute-start | bytes 1179656 | tf_op jit(solution)/shard_map/ppermute | solution.py:273
  119.7 1.5 collective-permute-start.5
  124.2 22.7 %shard_map.86 = (bf16[6,6,128,768]{3,2,1,0:T(8,128)(2,1)}, f32[128,768]{1,0:T(8,128)S(1)}) custom-call(s32[6,6,6]{2,1,0:T(8,128)S(1)} %copy-done.11, bf16[6,6,128,768]{3,2,1,0:T(8,128)(2,1)} %refs_0_.3, bf16[1,6,128,768]{3,2,1,0:T(8,128)(2,1)S(1)} %collective-permute-done.refs_1_, bf16[1,6,128,768]{3,2,1,0:T(8,128)(2,1)S(1)} %collective-permute-done.1.refs_2_, ...), custom_call_target="tpu_custom_call" | custom-call | tf_op jit(solution)/shard_map/pallas_call | solution.py:106
  146.9 14.1 %shard_map.87 = (bf16[6,6,128,768]{3,2,1,0:T(8,128)(2,1)}, f32[128,768]{1,0:T(8,128)S(1)}) custom-call(s32[6,6,6]{2,1,0:T(8,128)S(1)} %copy-done.11, bf16[6,6,128,768]{3,2,1,0:T(8,128)(2,1)} %refs_0_.3, bf16[1,6,128,768]{3,2,1,0:T(8,128)(2,1)S(1)} %collective-permute-done.refs_1_, ...), custom_call_target="tpu_custom_call", output_to_operand_aliasing={{0}: (10, {})} | custom-call | tf_op jit(solution)/shard_map/pallas_call | solution.py:106
  161.1 7.2 %shard_map.92 = (f32[1024,128]{1,0:T(8,128)S(1)}, f32[128,128]{1,0:T(8,128)S(1)}) custom-call(s32[1]{0:T(128)S(6)} %convert_element_type.21.lead_ref, f32[1024,128]{1,0:T(8,128)} %get-tuple-element.24.mine_ref, f32[1024,128]{1,0:T(8,128)} %collective-permute-done.10.other_ref, f32[256,128]{1,0:T(8,128)S(1)} %copy-done.3, f32[128,128]{1,0:T(8,128)S(1)} %copy-done.13), custom_call_target="tpu_custom_call" | custom-call | tf_op jit(solution)/shard_map/pallas_call | solution.py:245
  168.8 27.0 %all_to_all.5 = f32[8,96,128]{2,1,0:T(8,128)S(1)} all-to-all(f32[8,96,128]{2,1,0:T(8,128)S(1)} %bitcast.16), channel_id=1, replica_groups=mesh['pu'=4,'pv'=8] {'pv'}, dimensions={0} | all-to-all | bytes 786432 | tf_op jit(solution)/shard_map/all_to_all | solution.py:318
  195.9 1.2 collective-permute-done.11
  197.9 3.4 %collective-permute-done.12 = f32[96,128]{1,0:T(8,128)S(1)} collective-permute-done((f32[96,128]{1,0:T(8,128)S(1)}, f32[96,128]{1,0:T(8,128)S(1)}, u32[]{:S(2)}, u32[]{:S(2)}) %collective-permute-start.12) | collective-permute-done | bytes 49184 | tf_op jit(solution)/shard_map/ppermute | solution.py:261
  201.2 0.9 fusion.2
  (65 shorter events, 11.4 us)
Async XLA Ops:
  0.6 7.5 %copy-start.18 = (s32[32]{0:T(128)S(1)}, s32[32]{0:T(128)}, u32[]{:S(2)}) copy-start(s32[32]{0:T(128)} %param.13) | copy-start | bytes 388
  0.6 39.8 %copy-start.1 = (f32[256,128]{1,0:T(8,128)S(1)}, f32[256,128]{1,0:T(8,128)}, u32[]{:S(2)}) copy-start(f32[256,128]{1,0:T(8,128)} %sketch_ref.9) | copy-start | bytes 393220
  0.7 39.8 %copy-start.4 = (f32[1,1,1024,128]{3,2,1,0:T(8,128)S(1)}, f32[1,1,1024,128]{3,2,1,0:T(8,128)}, u32[]{:S(2)}) copy-start(f32[1,1,1024,128]{3,2,1,0:T(8,128)} %param.11) | copy-start | bytes 1572868
  0.7 39.8 %collective-permute-start.6 = (f32[1024,128]{1,0:T(8,128)}, f32[1024,128]{1,0:T(8,128)S(1)}, u32[]{:S(2)}, u32[]{:S(2)}) collective-permute-start(f32[1024,128]{1,0:T(8,128)} %bitcast.14), channel_id=1, source_target_pairs={{0,1},{1,0},{2,3},{3,2},{4,5},{5,4},{6,7},{7,6},{8,9},{9,8},{10,11... | collective-permute-start | bytes 1572872 | tf_op jit(solution)/shard_map/ppermute | solution.py:261
  6.9 93.9 %collective-permute-start.3 = (bf16[6,1,128,768]{3,2,1,0:T(8,128)(2,1)}, bf16[6,1,128,768]{3,2,1,0:T(8,128)(2,1)}, u32[]{:S(2)}, u32[]{:S(2)}) collective-permute-start(bf16[6,1,128,768]{3,2,1,0:T(8,128)(2,1)} %get-tuple-element.30), channel_id=1, source_target_pairs={{1,0},{2,1},{3,2},{4,3},{5,4},{6,5},{7,6},{9,8},{10,9},{11,10},{12... | collective-permute-start | bytes 3538952 | tf_op jit(solution)/shard_map/ppermute | solution.py:273
  46.4 12.9 %collective-permute-start.7 = (f32[1024,128]{1,0:T(8,128)S(1)}, f32[1024,128]{1,0:T(8,128)S(1)}, u32[]{:S(2)}, u32[]{:S(2)}) collective-permute-start(f32[1024,128]{1,0:T(8,128)S(1)} %get-tuple-element.18.mine_ref), channel_id=1, source_target_pairs={{0,2},{1,3},{2,0},{3,1},{4,6},{5,7},{6,4},{7,5},{8,10},{9,11},{10,... | collective-permute-start | bytes 1572872 | tf_op jit(solution)/shard_map/ppermute | solution.py:261
  48.1 53.8 %collective-permute-start.2 = (bf16[6,1,128,768]{3,2,1,0:T(8,128)(2,1)}, bf16[6,1,128,768]{3,2,1,0:T(8,128)(2,1)}, u32[]{:S(2)}, u32[]{:S(2)}) collective-permute-start(bf16[6,1,128,768]{3,2,1,0:T(8,128)(2,1)} %get-tuple-element.31), channel_id=1, source_target_pairs={{0,1},{1,2},{2,3},{3,4},{4,5},{5,6},{6,7},{8,9},{9,10},{10,11},{11... | collective-permute-start | bytes 3538952 | tf_op jit(solution)/shard_map/ppermute | solution.py:273
  65.3 5.8 %copy-start.14 = (f32[128,128]{1,0:T(8,128)}, f32[128,128]{1,0:T(8,128)S(1)}, u32[]{:S(2)}) copy-start(f32[128,128]{1,0:T(8,128)S(1)} %get-tuple-element.21.path_ref) | copy-start | bytes 196612
  65.3 24.1 %collective-permute-start.8 = (f32[1024,128]{1,0:T(8,128)S(1)}, f32[1024,128]{1,0:T(8,128)S(1)}, u32[]{:S(2)}, u32[]{:S(2)}) collective-permute-start(f32[1024,128]{1,0:T(8,128)S(1)} %get-tuple-element.20.mine_ref), channel_id=1, source_target_pairs={{0,4},{1,5},{2,6},{3,7},{4,0},{5,1},{6,2},{7,3},{8,12},{9,13},{10,... | collective-permute-start | bytes 1572872 | tf_op jit(solution)/shard_map/ppermute | solution.py:261
  71.1 52.3 %collective-permute-start = (bf16[1,6,128,768]{3,2,1,0:T(8,128)(2,1)}, bf16[1,6,128,768]{3,2,1,0:T(8,128)(2,1)S(1)}, u32[]{:S(2)}, u32[]{:S(2)}) collective-permute-start(bf16[1,6,128,768]{3,2,1,0:T(8,128)(2,1)} %get-tuple-element.33), channel_id=1, source_target_pairs={{0,8},{8,16},{16,24},{1,9},{9,17},{17,25},{2,10},{10,18},{18,26},{... | collective-permute-start | bytes 3538952 | tf_op jit(solution)/shard_map/ppermute | solution.py:273
  72.5 50.9 %collective-permute-start.1 = (bf16[1,6,128,768]{3,2,1,0:T(8,128)(2,1)}, bf16[1,6,128,768]{3,2,1,0:T(8,128)(2,1)S(1)}, u32[]{:S(2)}, u32[]{:S(2)}) collective-permute-start(bf16[1,6,128,768]{3,2,1,0:T(8,128)(2,1)} %get-tuple-element.32), channel_id=1, source_target_pairs={{8,0},{16,8},{24,16},{9,1},{17,9},{25,17},{10,2},{18,10},{26,18},{... | collective-permute-start | bytes 3538952 | tf_op jit(solution)/shard_map/ppermute | solution.py:273
  89.4 0.8 copy-start.7
  90.3 1.0 copy-start.8
  91.3 0.8 copy-start.15
  98.1 0.6 copy-start.16
  98.8 4.1 %copy-start.5 = (f32[1024,128]{1,0:T(8,128)}, f32[1024,128]{1,0:T(8,128)S(1)}, u32[]{:S(2)}) copy-start(f32[1024,128]{1,0:T(8,128)S(1)} %get-tuple-element.22.mine_ref) | copy-start | bytes 1572868
  98.8 4.1 %collective-permute-start.9 = (f32[1024,128]{1,0:T(8,128)S(1)}, f32[1024,128]{1,0:T(8,128)S(1)}, u32[]{:S(2)}, u32[]{:S(2)}) collective-permute-start(f32[1024,128]{1,0:T(8,128)S(1)} %get-tuple-element.22.mine_ref), channel_id=1, source_target_pairs={{0,8},{8,0},{16,24},{24,16},{1,9},{9,1},{17,25},{25,17},{2,10},{10... | collective-permute-start | bytes 1572872 | tf_op jit(solution)/shard_map/ppermute | solution.py:261
  98.9 4.8 %copy-start.17 = (f32[128,128]{1,0:T(8,128)S(1)}, f32[128,128]{1,0:T(8,128)}, u32[]{:S(2)}) copy-start(f32[128,128]{1,0:T(8,128)} %copy-done.16) | copy-start | bytes 196612
  102.9 0.8 copy-start.9
  103.7 0.9 copy-start.2
  104.6 1.0 copy-start.6
  105.7 1.0 copy-start.10
  106.7 16.7 %copy-start = (bf16[6,6,128,128]{3,2,1,0:T(8,128)(2,1)S(1)}, bf16[6,6,128,128]{3,2,1,0:T(8,128)(2,1)}, u32[]{:S(2)}) copy-start(bf16[6,6,128,128]{3,2,1,0:T(8,128)(2,1)} %refs_8_.1) | copy-start | bytes 3538948
  113.1 0.6 copy-start.12
  113.7 47.4 %collective-permute-start.10 = (f32[1024,128]{1,0:T(8,128)}, f32[1024,128]{1,0:T(8,128)}, u32[]{:S(2)}, u32[]{:S(2)}) collective-permute-start(f32[1024,128]{1,0:T(8,128)} %get-tuple-element.24.mine_ref), channel_id=1, source_target_pairs={{0,16},{8,24},{16,0},{24,8},{1,17},{9,25},{17,1},{25,9},{2,18},{10... | collective-permute-start | bytes 1572872 | tf_op jit(solution)/shard_map/ppermute | solution.py:261
  116.0 30.9 %collective-permute-start.4 = (bf16[2,128,768]{2,1,0:T(8,128)(2,1)}, bf16[2,128,768]{2,1,0:T(8,128)(2,1)}, u32[]{:S(2)}, u32[]{:S(2)}) collective-permute-start(bf16[2,128,768]{2,1,0:T(8,128)(2,1)} %pad_maximum_fusion), channel_id=1, source_target_pairs={{0,8},{8,16},{16,24},{1,9},{9,17},{17,25},{2,10},{10,18},{18,26},{... | collective-permute-start | bytes 1179656 | tf_op jit(solution)/shard_map/ppermute | solution.py:273
  119.7 27.2 %collective-permute-start.5 = (bf16[2,128,768]{2,1,0:T(8,128)(2,1)}, bf16[2,128,768]{2,1,0:T(8,128)(2,1)}, u32[]{:S(2)}, u32[]{:S(2)}) collective-permute-start(bf16[2,128,768]{2,1,0:T(8,128)(2,1)} %pad_maximum_fusion.1), channel_id=1, source_target_pairs={{8,0},{16,8},{24,16},{9,1},{17,9},{25,17},{10,2},{18,10},{26,18},{... | collective-permute-start | bytes 1179656 | tf_op jit(solution)/shard_map/ppermute | solution.py:273
  123.5 0.7 copy-start.11
  146.9 14.2 %copy-start.3 = (f32[256,128]{1,0:T(8,128)S(1)}, f32[256,128]{1,0:T(8,128)}, u32[]{:S(2)}) copy-start(f32[256,128]{1,0:T(8,128)} %sketch_ref.9) | copy-start | bytes 393220
  146.9 14.2 %copy-start.13 = (f32[128,128]{1,0:T(8,128)S(1)}, f32[128,128]{1,0:T(8,128)}, u32[]{:S(2)}) copy-start(f32[128,128]{1,0:T(8,128)} %copy-done.12) | copy-start | bytes 196612
  195.8 1.3 collective-permute-start.11
  197.1 4.2 %collective-permute-start.12 = (f32[96,128]{1,0:T(8,128)S(1)}, f32[96,128]{1,0:T(8,128)S(1)}, u32[]{:S(2)}, u32[]{:S(2)}) collective-permute-start(f32[96,128]{1,0:T(8,128)S(1)} %add.63), channel_id=1, source_target_pairs={{0,16},{8,24},{16,0},{24,8},{1,17},{9,25},{17,1},{25,9},{2,18},{10... | collective-permute-start | bytes 147464 | tf_op jit(solution)/shard_map/ppermute | solution.py:261
where the time goes:
time: 204 us; the launch traced here: 202 us
  Pallas kernels  68.3 us (33%)
  waiting for transfers between devices  52.1 us (26%)
  blocking collectives  27 us (13%)
  starting transfers between devices  23.5 us (12%)
  local copies, waits for them, and re-layouts  20.4 us (10%)
  between operations  7.31 us (4%)
  other arithmetic  2.12 us (1%)
    ppermute x7, waiting for transfers between devices, from_partner(): return lax.ppermute(value, axis, pairs)  52.1 us
    pallas_call x2, Pallas kernels, near_part(): pl.pallas_call(kernel, grid_spec=pltpu.PrefetchScalarGridSpec(num_scalar_...  36.8 us
    pallas_call x5, Pallas kernels, merge(): pl.pallas_call(merge_kernel, in_specs=[pl.BlockSpec(memory_space=pltpu.SM...  31.5 us
    all_to_all x1, blocking collectives, per_device(): lax.all_to_all(share.reshape(pv_count, rhs // pv_count, rank), 'pv', 0, 0)  27 us
    ppermute x6, starting transfers between devices, shifted(): lax.ppermute(value, axis, [(i, i + by) for i in range(count) if 0 <= i +...  13.8 us
    ppermute x7, starting transfers between devices, from_partner(): return lax.ppermute(value, axis, pairs)  9.69 us
    unnamed x38, local copies, waits for them, and re-layouts  8.5 us
  transfers between devices with their start and end apart: 13, of which 5 were waited for; matrix products, arithmetic and copies ran while one was open for 7% of the time, Pallas kernels for 30%

commit v1 on v0

v1 whole, which is shorter than its diff:
```python
import functools

import jax
import jax.numpy as jnp
from jax import lax
from jax.experimental import pallas as pl
from jax.experimental.pallas import tpu as pltpu
from jax.sharding import PartitionSpec as P

high = lax.Precision.HIGH
empty_slot = 9
near_vmem = 32 * 1024 * 1024
merge_vmem = 12 * 1024 * 1024


def dot_t(a, b, dims, precision=None):
    return lax.dot_general(
        a, b, (dims, ((), ())), precision=precision, preferred_element_type=jnp.float32
    )


def split_dot(a, b, dims):
    return dot_t(a, b, dims, high)


def near_kernel(plan, n_src, nb_ref, *refs):
    spans, wanted, block_rows, block_cols, centre_rows, centre_cols = plan
    count = len(block_cols)
    srcs = refs[:n_src]
    near_refs = refs[n_src : n_src + count]
    right_refs = refs[n_src + count : n_src + 2 * count]
    out_ref, coef_ref, ext_ref, stage_ref, sems, out_sems = refs[-6:]
    step = pl.program_id(0)
    steps = len(block_rows)

    def copies(row):
        found = []
        for index, (source, at, ext_row, ext_col, width) in enumerate(spans):
            if ext_row == row:
                view = srcs[source]
                for part in at:
                    view = view.at[part]
                target = ext_ref.at[ext_row, pl.ds(ext_col, width)]
                found.append(pltpu.make_async_copy(view, target, sems.at[index]))
        return found

    def send(place, at_step, part):
        row = block_rows[0] + at_step * (block_rows[1] - block_rows[0])
        return pltpu.make_async_copy(
            stage_ref.at[place, part], out_ref.at[row, block_cols[part]], out_sems.at[place, part]
        )

    @pl.when(step == 0)
    def _():
        for row in range(ext_ref.shape[0]):
            for copy in copies(row):
                copy.start()
        coef_ref[...] = jnp.zeros_like(coef_ref)

    for at_step, rows in enumerate(wanted):

        @pl.when(step == at_step)
        def _():
            for row in rows:
                for copy in copies(row):
                    copy.wait()

    place = lax.rem(step, 2)

    @pl.when(step >= 2)
    def _():
        for part in range(count):
            send(place, step - 2, part).wait()

    row = block_rows[0] + step * (block_rows[1] - block_rows[0])
    centre = centre_rows[0] + step * (centre_rows[1] - centre_rows[0])
    coef = coef_ref[...]
    for part in range(count):
        near_ref = near_refs[part]
        middle = centre_cols[part]
        weights = []
        values = []
        for slot in range(near_ref.shape[2]):
            link = nb_ref[row, block_cols[part], slot]
            there = jnp.minimum(link, empty_slot - 1)
            weight = near_ref[0, 0, slot]
            weights.append(jnp.where(link < empty_slot, weight, jnp.zeros_like(weight)))
            values.append(ext_ref[centre - 1 + lax.div(there, 3), middle - 1 + lax.rem(there, 3)])
        total = jnp.dot(
            jnp.concatenate(weights, axis=1),
            jnp.concatenate(values, axis=0),
            preferred_element_type=jnp.float32,
        )
        corrected = (ext_ref[centre, middle].astype(jnp.float32) + total).astype(jnp.bfloat16)
        stage_ref[place, part] = corrected
        send(place, step, part).start()
        coef = coef + dot_t(right_refs[part][0, 0], corrected, ((0,), (0,)))
    coef_ref[...] = coef

    @pl.when(step == steps - 1)
    def _():
        for at_step in range(max(steps - 2, 0), steps):
            for part in range(count):
                send(at_step % 2, at_step, part).wait()


def near_part(sources, plan, near_blocks, far_right, neighbours, prior):
    spans, _, block_rows, block_cols, _, _ = plan
    gu, gv, slots, size, _ = near_blocks.shape
    rhs = sources[0].shape[-1]
    rank = far_right.shape[-1]
    ext_rows = 1 + max(span[2] for span in spans)
    ext_cols = max(span[3] + span[4] for span in spans)
    at, by = block_rows[0], block_rows[1] - block_rows[0]
    in_specs = [pl.BlockSpec(memory_space=pl.ANY)] * len(sources)
    in_specs += [
        pl.BlockSpec((1, 1, slots, size, size), lambda i, nb, col=col: (at + i * by, col, 0, 0, 0))
        for col in block_cols
    ]
    in_specs += [
        pl.BlockSpec((1, 1, size, rank), lambda i, nb, col=col: (at + i * by, col, 0, 0))
        for col in block_cols
    ]
    args = list(sources) + [near_blocks] * len(block_cols) + [far_right] * len(block_cols)
    aliases = {}
    if prior is not None:
        in_specs.append(pl.BlockSpec(memory_space=pl.ANY))
        args.append(prior)
        aliases = {len(args): 0}
    return pl.pallas_call(
        functools.partial(near_kernel, plan, len(sources)),
        grid_spec=pltpu.PrefetchScalarGridSpec(
            num_scalar_prefetch=1,
            grid=(len(block_rows),),
            in_specs=in_specs,
            out_specs=[
                pl.BlockSpec(memory_space=pl.ANY),
                pl.BlockSpec((rank, rhs), lambda i, nb: (0, 0)),
            ],
            scratch_shapes=[
                pltpu.VMEM((ext_rows, ext_cols, size, rhs), jnp.bfloat16),
                pltpu.VMEM((2, len(block_cols), size, rhs), jnp.bfloat16),
                pltpu.SemaphoreType.DMA((len(spans),)),
                pltpu.SemaphoreType.DMA((2, len(block_cols))),
            ],
        ),
        out_shape=[
            jax.ShapeDtypeStruct((gu, gv, size, rhs), jnp.bfloat16),
            jax.ShapeDtypeStruct((rank, rhs), jnp.float32),
        ],
        input_output_aliases=aliases,
        compiler_params=pltpu.CompilerParams(
            dimension_semantics=("arbitrary",), vmem_limit_bytes=near_vmem
        ),
    )(neighbours, *args)


def near_middle(density, near_blocks, far_right, neighbours, prior):
    gu, gv = density.shape[:2]
    spans = [(0, (row,), row, 0, gv) for row in range(gu)]
    rows = list(range(1, gu - 1))
    wanted = [(0, 1, 2)] + [(row + 1,) for row in rows[1:]]
    cols = list(range(1, gv - 1))
    plan = (spans, wanted, rows, cols, rows, cols)
    return near_part((density,), plan, near_blocks, far_right, neighbours, prior)


def near_rows(density, top, bottom, near_blocks, far_right, neighbours, prior):
    gu, gv = density.shape[:2]
    spans = [(1, (), 0, 0, gv)]
    spans += [(0, (row,), at, 0, gv) for at, row in ((1, 0), (2, 1), (3, gu - 2), (4, gu - 1))]
    spans += [(2, (), 5, 0, gv)]
    cols = list(range(1, gv - 1))
    plan = (spans, [(0, 1, 2), (3, 4, 5)], [0, gu - 1], cols, [1, 4], cols)
    return near_part((density, top, bottom), plan, near_blocks, far_right, neighbours, prior)


def near_cols(density, top, bottom, ends, mids, corner_top, corner_bottom, near_blocks, far_right, neighbours, prior):
    gu, gv = density.shape[:2]
    spans = []
    for ext_row, source, at in (
        [(0, 1, ())] + [(row + 1, 0, (row,)) for row in range(gu)] + [(gu + 1, 2, ())]
    ):
        spans.append((source, at + (pl.ds(0, 2),), ext_row, 1, 2))
        spans.append((source, at + (pl.ds(gv - 2, 2),), ext_row, 3, 2))
    for side in range(2):
        col = 5 * side
        for row in range(gu):
            if row in (0, gu - 1):
                spans.append((3 + side, (pl.ds(0 if row == 0 else 1, 1),), row + 1, col, 1))
            else:
                spans.append((5 + side, (pl.ds(row - 1, 1),), row + 1, col, 1))
        spans.append((7, (pl.ds(side, 1),), 0, col, 1))
        spans.append((8, (pl.ds(side, 1),), gu + 1, col, 1))
    rows = list(range(gu))
    wanted = [(0, 1, 2)] + [(row + 2,) for row in rows[1:]]
    plan = (spans, wanted, rows, [0, gv - 1], [row + 1 for row in rows], [1, 4])
    sources = (density, top, bottom, *ends, *mids, corner_top, corner_bottom)
    return near_part(sources, plan, near_blocks, far_right, neighbours, prior)


def edges_kernel(density, *refs):
    *outs, sems = refs
    gu, gv = density.shape[:2]
    copies = []
    for side, col in ((0, gv - 1), (1, 0)):
        copies.append((density.at[0, pl.ds(col, 1)], outs[side].at[pl.ds(0, 1)]))
        copies.append((density.at[gu - 1, pl.ds(col, 1)], outs[side].at[pl.ds(1, 1)]))
        copies.append((density.at[pl.ds(1, gu - 2), col], outs[2 + side]))
    copies.append((density.at[gu - 1], outs[4]))
    copies.append((density.at[0], outs[5]))
    copies = [
        pltpu.make_async_copy(source, target, sems.at[index])
        for index, (source, target) in enumerate(copies)
    ]
    for copy in copies:
        copy.start()
    for copy in copies:
        copy.wait()


def patch_edges(density):
    gu, gv, size, rhs = density.shape
    counts = (2, 2, gu - 2, gu - 2, gv, gv)
    return pl.pallas_call(
        edges_kernel,
        in_specs=[pl.BlockSpec(memory_space=pl.ANY)],
        out_specs=[pl.BlockSpec(memory_space=pl.ANY)] * len(counts),
        out_shape=[jax.ShapeDtypeStruct((count, size, rhs), density.dtype) for count in counts],
        scratch_shapes=[pltpu.SemaphoreType.DMA((8,))],
    )(density)


def eliminate(w_k, w_e):
    size = w_k.shape[0]
    step = 32
    tile = 8
    sub = lax.broadcasted_iota(jnp.int32, (tile, size), 0)
    for base in range(0, size, step):
        count = step // tile
        k_rows = [w_k[base + tile * r : base + tile * (r + 1), :] for r in range(count)]
        e_rows = [w_e[base + tile * r : base + tile * (r + 1), :] for r in range(count)]
        for q in range(count):
            at = base + tile * q
            cols = {
                (r, k): jnp.broadcast_to(k_rows[r][:, at + k : at + k + 1], (tile, size))
                for r in range(q, count)
                for k in range(tile)
            }
            pivots = jnp.ones((tile, size), jnp.float32)
            for k in range(tile):
                pivot = jnp.broadcast_to(cols[q, k][k : k + 1, :], (tile, size))
                pivots = jnp.where(sub == k, pivot, pivots)
                inverse = 1.0 / pivot
                k_pivot = jnp.broadcast_to(k_rows[q][k : k + 1, :], (tile, size)) * inverse
                e_pivot = jnp.broadcast_to(e_rows[q][k : k + 1, :], (tile, size)) * inverse
                links = {
                    m: jnp.broadcast_to(cols[q, k][m : m + 1, :], (tile, size)) * inverse
                    for m in range(k + 1, tile)
                }
                for r in range(q, count):
                    factor = cols[r, k]
                    if r == q:
                        factor = jnp.where(sub > k, factor, 0.0)
                    for m in range(k + 1, tile):
                        cols[r, m] = cols[r, m] - factor * links[m]
                    k_rows[r] = k_rows[r] - factor * k_pivot
                    e_rows[r] = e_rows[r] - factor * e_pivot
            root = lax.rsqrt(pivots)
            k_rows[q] = k_rows[q] * root
            e_rows[q] = e_rows[q] * root
        e_now = jnp.concatenate(e_rows, axis=0)
        w_e[base : base + step, :] = e_now
        if base + step < size:
            k_now = jnp.concatenate(k_rows, axis=0)
            k_hi = k_now.astype(jnp.bfloat16)
            k_lo = (k_now - k_hi.astype(jnp.float32)).astype(jnp.bfloat16)
            e_hi = e_now.astype(jnp.bfloat16)
            e_lo = (e_now - e_hi.astype(jnp.float32)).astype(jnp.bfloat16)
            lhs = jnp.concatenate([k_hi, k_hi, k_lo], axis=0)
            k_rhs = jnp.concatenate([k_hi, k_lo, k_hi], axis=0)
            e_rhs = jnp.concatenate([e_hi, e_lo, e_hi], axis=0)
            k_fall = dot_t(lhs, k_rhs, ((0,), (0,)))
            e_fall = dot_t(lhs, e_rhs, ((0,), (0,)))
            w_k[base + step :, :] -= k_fall[base + step :, :]
            w_e[base + step :, :] -= e_fall[base + step :, :]


code_rows = 16


def encode(value, out_ref):
    rows = value.shape[0]
    top = jnp.max(jnp.abs(value), axis=0, keepdims=True)
    power = jnp.clip(jnp.floor(jnp.log2(32000.0 / jnp.maximum(top, 1e-30))), -60.0, 60.0)
    scaled = jnp.floor(value * jnp.exp2(power) + 0.5)
    out_ref[:rows, :] = scaled.astype(jnp.int32).astype(jnp.int16)
    powers = jnp.broadcast_to(power, (code_rows, value.shape[1]))
    out_ref[rows:, :] = powers.astype(jnp.int32).astype(jnp.int16)


def decode(ref):
    rows = ref.shape[0] - code_rows
    power = ref[rows:, :].astype(jnp.int32).astype(jnp.float32)[:1]
    return ref[:rows, :].astype(jnp.int32).astype(jnp.float32) * jnp.exp2(-power)


def encode_kernel(value_ref, out_ref):
    encode(value_ref[...], out_ref)


def encoded(value):
    rows, cols = value.shape
    return pl.pallas_call(
        encode_kernel,
        out_shape=jax.ShapeDtypeStruct((rows + code_rows, cols), jnp.int16),
        compiler_params=pltpu.CompilerParams(vmem_limit_bytes=merge_vmem),
    )(value)


def merge_kernel(has_path, last, info_ref, mine_ref, other_ref, sketch_ref, *refs):
    if has_path:
        path_ref, *refs = refs
    left_ref, new_path_ref, w_k, w_e, y_ref = refs
    rank = mine_ref.shape[1]
    lead = info_ref[0] > 0
    first = sketch_ref[:rank, :]
    second = sketch_ref[rank:, :]
    mine = decode(mine_ref)
    sketched = split_dot(mine, jnp.where(lead, first, second), ((1,), (0,))) + split_dot(
        decode(other_ref), jnp.where(lead, second, first), ((1,), (0,))
    )
    w_k[...] = split_dot(sketched, sketched, ((0,), (0,)))
    rows = lax.broadcasted_iota(jnp.int32, (rank, rank), 0)
    cols = lax.broadcasted_iota(jnp.int32, (rank, rank), 1)
    w_e[...] = jnp.where(rows == cols, 1.0, 0.0)
    eliminate(w_k, w_e)
    inverse = w_e[...]
    if last:
        y_ref[...] = sketched
        count = left_ref.shape[0]
        part = y_ref[pl.ds(pl.multiple_of(info_ref[1] * count, 8), count), :]
        left_ref[...] = split_dot(part, inverse, ((1,), (1,)))
    else:
        encode(split_dot(sketched, inverse, ((1,), (1,))), left_ref)
    own = split_dot(sketched, mine, ((0,), (0,)))
    if has_path:
        own = split_dot(own, path_ref[...], ((1,), (0,)))
    new_path_ref[...] = split_dot(inverse, own, ((1,), (0,)))


def merge(info, mine, other, sketch, path, last_rows):
    rows, rank = mine.shape
    whole = pl.BlockSpec(memory_space=pltpu.VMEM)
    paths = () if path is None else (path,)
    if last_rows:
        left = jax.ShapeDtypeStruct((last_rows, rank), jnp.float32)
    else:
        left = jax.ShapeDtypeStruct(mine.shape, jnp.int16)
    return pl.pallas_call(
        functools.partial(merge_kernel, bool(paths), bool(last_rows)),
        in_specs=[pl.BlockSpec(memory_space=pltpu.SMEM), whole, whole, whole] + [whole] * len(paths),
        out_specs=[whole, whole],
        out_shape=[left, jax.ShapeDtypeStruct((rank, rank), jnp.float32)],
        scratch_shapes=[
            pltpu.VMEM((rank, rank), jnp.float32),
            pltpu.VMEM((rank, rank), jnp.float32),
            pltpu.VMEM((rows - code_rows, rank), jnp.float32),
        ],
        compiler_params=pltpu.CompilerParams(vmem_limit_bytes=merge_vmem),
    )(info, mine, other, sketch, *paths)


def from_partner(value, axis, distance):
    mask = 2**distance
    pairs = [(source, source ^ mask) for source in range(lax.axis_size(axis))]
    return lax.ppermute(value, axis, pairs)


def mine_leads(group_keys, position, tree_level):
    block_min = group_keys.reshape(-1, 1 << tree_level).min(axis=1)
    mine_key = block_min[position >> tree_level]
    their_key = block_min[position >> tree_level ^ 1]
    return (mine_key < their_key).astype(jnp.int32).reshape(1)


def shifted(value, axis, by):
    count = lax.axis_size(axis)
    return lax.ppermute(value, axis, [(i, i + by) for i in range(count) if 0 <= i + by < count])


def tied(*values):
    return lax.optimization_barrier(values)


def per_device(density, near_blocks, neighbours, far_right, far_left, sketch, patch_order):
    pu_count = lax.axis_size("pu")
    pv_count = lax.axis_size("pv")
    pu_index = lax.axis_index("pu")
    pv_index = lax.axis_index("pv")
    key_grid = patch_order.reshape(pu_count, pv_count)
    row_keys = lax.dynamic_index_in_dim(key_grid, pu_index, 0, keepdims=False)
    column_keys = key_grid.min(axis=1)
    gu, gv, size, rhs = density.shape
    pv_levels = pv_count.bit_length() - 1
    pu_levels = pu_count.bit_length() - 1
    levels = pv_levels + pu_levels
    place = pu_index.astype(jnp.int32).reshape(1)

    def info(level):
        if level < pv_levels:
            lead = mine_leads(row_keys, pv_index, level)
        else:
            lead = mine_leads(column_keys, pu_index, level - pv_levels)
        return jnp.concatenate([lead, place])

    def partner(value, level):
        if level < pv_levels:
            return from_partner(value, "pv", level)
        return from_partner(value, "pu", level - pv_levels)

    rows = far_left.shape[2]
    left = encoded(far_left[0, 0])
    other = partner(left, 0)
    density, left = tied(density, left)
    *columns, last_row, first_row = patch_edges(density)
    top = shifted(last_row, "pu", 1)
    bottom = shifted(first_row, "pu", -1)
    columns, other = tied(columns, other)
    ends = [shifted(columns[0], "pv", 1), shifted(columns[1], "pv", -1)]
    mids = [shifted(columns[2], "pv", 1), shifted(columns[3], "pv", -1)]
    corner_top = shifted(jnp.concatenate([ends[0][1:], ends[1][1:]], axis=0), "pu", 1)
    corner_bottom = shifted(jnp.concatenate([ends[0][:1], ends[1][:1]], axis=0), "pu", -1)

    coefs = []
    corrected = None
    pv_path = pu_path = None
    for level in range(levels):
        if level:
            other = partner(left, level)
            if level in (1, 2, levels - 1):
                links, left = tied(neighbours, left)
                if level == 1:
                    corrected, coef = near_rows(density, top, bottom, near_blocks, far_right, links, corrected)
                elif level == 2:
                    corrected, coef = near_middle(density, near_blocks, far_right, links, corrected)
                else:
                    corrected, coef = near_cols(
                        density,
                        top,
                        bottom,
                        ends,
                        mids,
                        corner_top,
                        corner_bottom,
                        near_blocks,
                        far_right,
                        links,
                        corrected,
                    )
                other, coef = tied(other, coef)
                coefs.append(coef)
        path = pv_path if level < pv_levels else pu_path
        last_rows = rows // pu_count if level == levels - 1 else 0
        left, path = merge(info(level), left, other, sketch, path, last_rows)
        if level < pv_levels:
            pv_path = path
        else:
            pu_path = path

    coef = functools.reduce(lambda a, b: a + b, coefs)
    share = lax.dot_general(coef, pv_path, (((0,), (1,)), ((), ())), precision=high)
    share = share.reshape(pv_count, rhs // pv_count, -1)
    for level in range(pv_levels):
        bit = (pv_index >> level) & 1
        pairs = share.reshape(share.shape[0] // 2, 2, *share.shape[1:])
        keep = lax.dynamic_index_in_dim(pairs, bit, 1, keepdims=False)
        give = lax.dynamic_index_in_dim(pairs, 1 - bit, 1, keepdims=False)
        share = keep + from_partner(give, "pv", level)
    root_coef = lax.dot_general(share[0], pu_path, (((1,), (1,)), ((), ())), precision=high)
    for level in range(pu_levels):
        root_coef = root_coef + from_partner(root_coef, "pu", level)
    far_field = lax.dot_general(left, root_coef, (((1,), (1,)), ((), ())), precision=high)
    return (corrected, far_field)


def solution(mesh):
    in_specs = (
        P("pu", "pv", None, None),
        P("pu", "pv", None, None, None),
        P("pu", "pv", None),
        P("pu", "pv", None, None),
        P("pu", "pv", None, None),
        P(),
        P(),
    )
    out_specs = (P("pu", "pv", None, None), P("pu", "pv"))
    return jax.shard_map(
        per_device, mesh=mesh, in_specs=in_specs, out_specs=out_specs, check_vma=False
    )
```

time: 204 us -> 303 us (1.49)
  Pallas kernels: 68.3 us -> 206 us
  waiting for transfers between devices: 52.1 us -> 20 us
  blocking collectives: 27 us -> 0 us
  starting transfers between devices: 23.5 us -> 36.2 us
  local copies, waits for them, and re-layouts: 20.4 us -> 28.6 us
    pallas_call x7 -> x10, Pallas kernels: 68.3 us -> 206 us  [the longest x1 144 us: patch_edges(): pl.pallas_call(edges_kernel, in_specs=[pl.BlockSpec(memory_space=pl.ANY)]...]
    ppermute x7 -> x10, waiting for transfers between devices: 52.1 us -> 20 us  [from_partner(): return lax.ppermute(value, axis, pairs)]
    all_to_all x1 -> x0, blocking collectives: 27 us -> none  [per_device(): lax.all_to_all(share.reshape(pv_count, rhs // pv_count, rank), 'pv', 0, 0)]
    unnamed x38 -> x56, local copies, waits for them, and re-layouts: 8.5 us -> 22.7 us
    ppermute x6 -> x8, starting transfers between devices: 13.8 us -> 21.6 us  [shifted(): lax.ppermute(value, axis, [(i, i + by) for i in range(count) if 0 <= i +...]
    ppermute x7 -> x10, starting transfers between devices: 9.69 us -> 14.5 us  [from_partner(): return lax.ppermute(value, axis, pairs)]
    slice x2, local copies, waits for them, and re-layouts: 6.36 us -> 2.1 us  [the longest x1 1.05 us: per_device(): ends[1][:1]]
  transfers between devices with their start and end apart: 13 -> 18, of which waited for: 5 -> 6; matrix products, arithmetic and copies ran while one was open for 7% -> 3% of each run, Pallas kernels for 30% -> 20%
where the time goes in v1:
time: 303 us; the launch traced here: 302 us
  Pallas kernels  206 us (68%)
  starting transfers between devices  36.2 us (12%)
  local copies, waits for them, and re-layouts  28.6 us (9%)
  waiting for transfers between devices  20 us (7%)
  between operations  7.72 us (3%)
    pallas_call x1, Pallas kernels, patch_edges(): pl.pallas_call(edges_kernel, in_specs=[pl.BlockSpec(memory_space=pl.ANY)]...  144 us
    pallas_call x5, Pallas kernels, merge(): pl.pallas_call(functools.partial(merge_kernel, bool(paths), bool(last_row...  35.5 us
    pallas_call x3, Pallas kernels, near_part(): pl.pallas_call(functools.partial(near_kernel, plan, len(sources)), grid_s...  25.9 us
    unnamed x56, local copies, waits for them, and re-layouts  22.7 us
    ppermute x8, starting transfers between devices, shifted(): lax.ppermute(value, axis, [(i, i + by) for i in range(count) if 0 <= i +...  21.6 us
    ppermute x10, waiting for transfers between devices, from_partner(): return lax.ppermute(value, axis, pairs)  20 us
    ppermute x10, starting transfers between devices, from_partner(): return lax.ppermute(value, axis, pairs)  14.5 us
  transfers between devices with their start and end apart: 18, of which 6 were waited for; matrix products, arithmetic and copies ran while one was open for 3% of the time, Pallas kernels for 20%

profile of v1, /device:TPU:0, one launch (start us, length us, event | category | flops | bytes accessed | tf_op | source)
XLA Modules:
  0.0 302.1 jit_solution(16520791623725238040)
XLA Ops:
  0.7 1.1 copy-done.12
  2.0 144.1 %shard_map.87 = (bf16[2,128,768]{2,1,0:T(8,128)(2,1)}, bf16[2,128,768]{2,1,0:T(8,128)(2,1)}, bf16[4,128,768]{2,1,0:T(8,128)(2,1)}, bf16[4,128,768]{2,1,0:T(8,128...) custom-call(bf16[6,6,128,768]{3,2,1,0:T(8,128)(2,1)} %refs_0_.2), custom_call_target="tpu_custom_call" | custom-call | tf_op jit(solution)/shard_map/pallas_call | solution.py:225
  146.1 2.4 collective-permute-start.2
  148.6 1.3 collective-permute-start.3
  149.9 2.4 collective-permute-start
  152.3 5.7 %collective-permute-done.other_ref = s16[1040,128]{1,0:T(8,128)(2,1)S(1)} collective-permute-done((s16[1040,128]{1,0:T(8,128)(2,1)}, s16[1040,128]{1,0:T(8,128)(2,1)S(1)}, u32[]{:S(2)}, u32[]{:S(2)}) %collective-permute-start) | collective-permute-done | bytes 266272 | tf_op jit(solution)/shard_map/ppermute | solution.py:377
  158.6 5.0 %collective-permute-start.6 = (bf16[2,128,768]{2,1,0:T(8,128)(2,1)}, bf16[2,128,768]{2,1,0:T(8,128)(2,1)}, u32[]{:S(2)}, u32[]{:S(2)}) collective-permute-start(bf16[2,128,768]{2,1,0:T(8,128)(2,1)} %get-tuple-element.68), channel_id=1, source_target_pairs={{0,1},{1,2},{2,3},{3,4},{4,5},{5,6},{6,7},{8,9},{9,10},{10,11},{11... | collective-permute-start | bytes 1179656 | tf_op jit(solution)/shard_map/ppermute | solution.py:389
  168.6 7.0 %shard_map.88 = (s16[1040,128]{1,0:T(8,128)(2,1)}, f32[128,128]{1,0:T(8,128)S(1)}) custom-call(s32[2]{0:T(128)S(1)} %pad_add_fusion.3.info_ref, s16[1040,128]{1,0:T(8,128)(2,1)S(1)} %copy-done.11, s16[1040,128]{1,0:T(8,128)(2,1)S(1)} %copy-done.18, f32[256,128]{1,0:T(8,128)S(1)} %copy-done.6), custom_call_target="tpu_custom_call" | custom-call | tf_op jit(solution)/shard_map/pallas_call | solution.py:360
  177.1 1.3 collective-permute-start.7
  182.9 5.4 %collective-permute-start.8 = (bf16[4,128,768]{2,1,0:T(8,128)(2,1)}, bf16[4,128,768]{2,1,0:T(8,128)(2,1)}, u32[]{:S(2)}, u32[]{:S(2)}) collective-permute-start(bf16[4,128,768]{2,1,0:T(8,128)(2,1)} %get-tuple-element.70), channel_id=1, source_target_pairs={{0,1},{1,2},{2,3},{3,4},{4,5},{5,6},{6,7},{8,9},{9,10},{10,11},{11... | collective-permute-start | bytes 2359304 | tf_op jit(solution)/shard_map/ppermute | solution.py:389
  188.3 1.5 collective-permute-start.9
  189.8 3.0 %copy-done = bf16[6,6,6,128,128]{4,3,2,1,0:T(8,128)(2,1)S(1)} copy-done((bf16[6,6,6,128,128]{4,3,2,1,0:T(8,128)(2,1)S(1)}, bf16[6,6,6,128,128]{4,3,2,1,0:T(8,128)(2,1)}, u32[]{:S(2)}) %copy-start) | copy-done | bytes 7077912
  192.9 3.0 copy-done.4
  196.6 6.1 %shard_map.89 = (bf16[6,6,128,768]{3,2,1,0:T(8,128)(2,1)}, f32[128,768]{1,0:T(8,128)S(1)}) custom-call(s32[6,6,6]{2,1,0:T(8,128)S(1)} %copy-done.19, bf16[6,6,128,768]{3,2,1,0:T(8,128)(2,1)S(1)} %copy-done.4, bf16[6,128,768]{2,1,0:T(8,128)(2,1)S(1)} %collective-permute-done.2.refs_1_, bf16[6,128,768]{2,1,0:T(8,128)(2,1)S(1)} %collective-permute-done.3.refs_2_, ...), custom_call_target="tpu_custom_call" | custom-call | tf_op jit(solution)/shard_map/pallas_call | solution.py:130
  202.8 7.3 %shard_map.90 = (s16[1040,128]{1,0:T(8,128)(2,1)S(1)}, f32[128,128]{1,0:T(8,128)S(1)}) custom-call(s32[2]{0:T(128)S(1)} %get-tuple-element.103.info_ref, s16[1040,128]{1,0:T(8,128)(2,1)} %get-tuple-element.51.mine_ref, s16[1040,128]{1,0:T(8,128)(2,1)} %collective-permute-done.1.other_ref, f32[256,128]{1,0:T(8,128)S(1)} %copy-done.7, f32[128,128]{1,0:T(8,128)S(1)} %copy-done.26), custom_call_target="tpu_custom_call" | custom-call | tf_op jit(solution)/shard_map/pallas_call | solution.py:360
  210.1 3.6 %collective-permute-start.4 = (s16[1040,128]{1,0:T(8,128)(2,1)S(1)}, s16[1040,128]{1,0:T(8,128)(2,1)S(1)}, u32[]{:S(2)}, u32[]{:S(2)}) collective-permute-start(s16[1040,128]{1,0:T(8,128)(2,1)S(1)} %get-tuple-element.59.mine_ref), channel_id=1, source_target_pairs={{0,4},{1,5},{2,6},{3,7},{4,0},{5,1},{6,2},{7,3},{8,12},{9,13},{10,... | collective-permute-start | bytes 798728 | tf_op jit(solution)/shard_map/ppermute | solution.py:377
  215.8 9.1 %shard_map.91 = (bf16[6,6,128,768]{3,2,1,0:T(8,128)(2,1)}, f32[128,768]{1,0:T(8,128)S(1)}) custom-call(s32[6,6,6]{2,1,0:T(8,128)S(1)} %copy-done.19, bf16[6,6,128,768]{3,2,1,0:T(8,128)(2,1)S(1)} %copy-done.4, bf16[6,6,6,128,128]{4,3,2,1,0:T(8,128)(2,1)S(1)} %copy-done.1, ...), custom_call_target="tpu_custom_call", output_to_operand_aliasing={{0}: (10, {})} | custom-call | tf_op jit(solution)/shard_map/pallas_call | solution.py:130
  225.8 7.0 %shard_map.92 = (s16[1040,128]{1,0:T(8,128)(2,1)}, f32[128,128]{1,0:T(8,128)S(1)}) custom-call(s32[2]{0:T(128)S(1)} %get-tuple-element.102.info_ref, s16[1040,128]{1,0:T(8,128)(2,1)S(1)} %get-tuple-element.59.mine_ref, s16[1040,128]{1,0:T(8,128)(2,1)S(1)} %collective-permute-done.4.other_ref, f32[256,128]{1,0:T(8,128)S(1)} %copy-done.7, ...), custom_call_target="tpu_custom_call" | custom-call | tf_op jit(solution)/shard_map/pallas_call | solution.py:360
  234.2 3.2 %collective-permute-start.10 = (bf16[2,128,768]{2,1,0:T(8,128)(2,1)}, bf16[2,128,768]{2,1,0:T(8,128)(2,1)}, u32[]{:S(2)}, u32[]{:S(2)}) collective-permute-start(bf16[2,128,768]{2,1,0:T(8,128)(2,1)} %pad_maximum_fusion), channel_id=1, source_target_pairs={{0,8},{8,16},{16,24},{1,9},{9,17},{17,25},{2,10},{10,18},{18,26},{... | collective-permute-start | bytes 1179656 | tf_op jit(solution)/shard_map/ppermute | solution.py:389
  238.2 1.5 collective-permute-start.11
  245.1 7.5 %shard_map.93 = (s16[1040,128]{1,0:T(8,128)(2,1)}, f32[128,128]{1,0:T(8,128)S(1)}) custom-call(s32[2]{0:T(128)S(1)} %get-tuple-element.100.info_ref, s16[1040,128]{1,0:T(8,128)(2,1)} %get-tuple-element.65.mine_ref, s16[1040,128]{1,0:T(8,128)(2,1)} %collective-permute-done.5.other_ref, f32[256,128]{1,0:T(8,128)S(1)} %copy-done.8), custom_call_target="tpu_custom_call" | custom-call | tf_op jit(solution)/shard_map/pallas_call | solution.py:360
  253.2 3.5 %collective-permute-start.12 = (s16[1040,128]{1,0:T(8,128)(2,1)}, s16[1040,128]{1,0:T(8,128)(2,1)}, u32[]{:S(2)}, u32[]{:S(2)}) collective-permute-start(s16[1040,128]{1,0:T(8,128)(2,1)} %get-tuple-element.74.mine_ref), channel_id=1, source_target_pairs={{0,16},{8,24},{16,0},{24,8},{1,17},{9,25},{17,1},{25,9},{2,18},{10... | collective-permute-start | bytes 798728 | tf_op jit(solution)/shard_map/ppermute | solution.py:377
  256.7 3.0 %copy-done.2 = bf16[6,6,6,128,128]{4,3,2,1,0:T(8,128)(2,1)S(1)} copy-done((bf16[6,6,6,128,128]{4,3,2,1,0:T(8,128)(2,1)S(1)}, bf16[6,6,6,128,128]{4,3,2,1,0:T(8,128)(2,1)}, u32[]{:S(2)}) %copy-start.2) | copy-done | bytes 7077912
  259.7 3.0 copy-done.5
  263.5 10.6 %shard_map.94 = (bf16[6,6,128,768]{3,2,1,0:T(8,128)(2,1)}, f32[128,768]{1,0:T(8,128)S(1)}) custom-call(s32[6,6,6]{2,1,0:T(8,128)S(1)} %copy-done.20, bf16[6,6,128,768]{3,2,1,0:T(8,128)(2,1)S(1)} %copy-done.5, bf16[6,128,768]{2,1,0:T(8,128)(2,1)S(1)} %collective-permute-done.2.refs_1_, ...), custom_call_target="tpu_custom_call", output_to_operand_aliasing={{0}: (14, {})} | custom-call | tf_op jit(solution)/shard_map/pallas_call | solution.py:130
  275.6 5.5 %collective-permute-done.13 = f32[4,96,128]{2,1,0:T(8,128)S(1)} collective-permute-done((f32[4,96,128]{2,1,0:T(8,128)S(1)}, f32[4,96,128]{2,1,0:T(8,128)S(1)}, u32[]{:S(2)}, u32[]{:S(2)}) %collective-permute-start.13) | collective-permute-done | bytes 196640 | tf_op jit(solution)/shard_map/ppermute | solution.py:377
  281.1 1.2 collective-permute-start.14
  282.3 3.5 %collective-permute-done.14 = f32[2,96,128]{2,1,0:T(8,128)S(1)} collective-permute-done((f32[2,96,128]{2,1,0:T(8,128)S(1)}, f32[2,96,128]{2,1,0:T(8,128)S(1)}, u32[]{:S(2)}, u32[]{:S(2)}) %collective-permute-start.14) | collective-permute-done | bytes 98336 | tf_op jit(solution)/shard_map/ppermute | solution.py:377
  285.9 1.1 collective-permute-start.15
  288.7 6.9 %shard_map.95 = (f32[256,128]{1,0:T(8,128)S(1)}, f32[128,128]{1,0:T(8,128)S(1)}) custom-call(s32[2]{0:T(128)S(1)} %get-tuple-element.101.info_ref, s16[1040,128]{1,0:T(8,128)(2,1)} %get-tuple-element.74.mine_ref, s16[1040,128]{1,0:T(8,128)(2,1)} %collective-permute-done.12.other_ref, f32[256,128]{1,0:T(8,128)S(1)} %copy-done.9, f32[128,128]{1,0:T(8,128)S(1)} %copy-done.24), custom_call_target="tpu_custom_call" | custom-call | tf_op jit(solution)/shard_map/pallas_call | solution.py:360
  295.9 1.2 collective-permute-done.16
  298.0 3.2 %collective-permute-done.17 = f32[96,128]{1,0:T(8,128)S(1)} collective-permute-done((f32[96,128]{1,0:T(8,128)S(1)}, f32[96,128]{1,0:T(8,128)S(1)}, u32[]{:S(2)}, u32[]{:S(2)}) %collective-permute-start.17) | collective-permute-done | bytes 49184 | tf_op jit(solution)/shard_map/ppermute | solution.py:377
  (100 shorter events, 23.2 us)
Async XLA Ops:
  0.6 189.2 %copy-start.3 = (bf16[6,6,128,128]{3,2,1,0:T(8,128)(2,1)S(1)}, bf16[6,6,128,128]{3,2,1,0:T(8,128)(2,1)}, u32[]{:S(2)}) copy-start(bf16[6,6,128,128]{3,2,1,0:T(8,128)(2,1)} %refs_12_.1) | copy-start | bytes 3538948
  1.8 161.9 %copy-start.27 = (s32[32]{0:T(128)S(1)}, s32[32]{0:T(128)}, u32[]{:S(2)}) copy-start(s32[32]{0:T(128)} %param.13) | copy-start | bytes 388
  2.0 144.1 %copy-start.10 = (s16[1040,128]{1,0:T(8,128)(2,1)}, s16[1040,128]{1,0:T(8,128)(2,1)S(1)}, u32[]{:S(2)}) copy-start(s16[1040,128]{1,0:T(8,128)(2,1)S(1)} %shard_map.86.mine_ref) | copy-start | bytes 798724
  146.1 36.8 %collective-permute-start.2 = (bf16[6,128,768]{2,1,0:T(8,128)(2,1)}, bf16[6,128,768]{2,1,0:T(8,128)(2,1)S(1)}, u32[]{:S(2)}, u32[]{:S(2)}) collective-permute-start(bf16[6,128,768]{2,1,0:T(8,128)(2,1)} %get-tuple-element.53), channel_id=1, source_target_pairs={{0,8},{8,16},{16,24},{1,9},{9,17},{17,25},{2,10},{10,18},{18,26},{... | collective-permute-start | bytes 3538952 | tf_op jit(solution)/shard_map/ppermute | solution.py:389
  148.6 39.8 %collective-permute-start.3 = (bf16[6,128,768]{2,1,0:T(8,128)(2,1)}, bf16[6,128,768]{2,1,0:T(8,128)(2,1)S(1)}, u32[]{:S(2)}, u32[]{:S(2)}) collective-permute-start(bf16[6,128,768]{2,1,0:T(8,128)(2,1)} %get-tuple-element.54), channel_id=1, source_target_pairs={{8,0},{16,8},{24,16},{9,1},{17,9},{25,17},{10,2},{18,10},{26,18},{... | collective-permute-start | bytes 3538952 | tf_op jit(solution)/shard_map/ppermute | solution.py:389
  149.9 8.1 %collective-permute-start = (s16[1040,128]{1,0:T(8,128)(2,1)}, s16[1040,128]{1,0:T(8,128)(2,1)S(1)}, u32[]{:S(2)}, u32[]{:S(2)}) collective-permute-start(s16[1040,128]{1,0:T(8,128)(2,1)} %copy-done.10), channel_id=1, source_target_pairs={{0,1},{1,0},{2,3},{3,2},{4,5},{5,4},{6,7},{7,6},{8,9},{9,8},{10,11... | collective-permute-start | bytes 798728 | tf_op jit(solution)/shard_map/ppermute | solution.py:377
  158.6 55.1 %collective-permute-start.6 = (bf16[2,128,768]{2,1,0:T(8,128)(2,1)}, bf16[2,128,768]{2,1,0:T(8,128)(2,1)}, u32[]{:S(2)}, u32[]{:S(2)}) collective-permute-start(bf16[2,128,768]{2,1,0:T(8,128)(2,1)} %get-tuple-element.68), channel_id=1, source_target_pairs={{0,1},{1,2},{2,3},{3,4},{4,5},{5,6},{6,7},{8,9},{9,10},{10,11},{11... | collective-permute-start | bytes 1179656 | tf_op jit(solution)/shard_map/ppermute | solution.py:389
  176.2 26.5 %collective-permute-start.1 = (s16[1040,128]{1,0:T(8,128)(2,1)}, s16[1040,128]{1,0:T(8,128)(2,1)}, u32[]{:S(2)}, u32[]{:S(2)}) collective-permute-start(s16[1040,128]{1,0:T(8,128)(2,1)} %get-tuple-element.51.mine_ref), channel_id=1, source_target_pairs={{0,2},{1,3},{2,0},{3,1},{4,6},{5,7},{6,4},{7,5},{8,10},{9,11},{10,... | collective-permute-start | bytes 798728 | tf_op jit(solution)/shard_map/ppermute | solution.py:377
  177.1 37.6 %collective-permute-start.7 = (bf16[2,128,768]{2,1,0:T(8,128)(2,1)}, bf16[2,128,768]{2,1,0:T(8,128)(2,1)}, u32[]{:S(2)}, u32[]{:S(2)}) collective-permute-start(bf16[2,128,768]{2,1,0:T(8,128)(2,1)} %get-tuple-element.69), channel_id=1, source_target_pairs={{1,0},{2,1},{3,2},{4,3},{5,4},{6,5},{7,6},{9,8},{10,9},{11,10},{12... | collective-permute-start | bytes 1179656 | tf_op jit(solution)/shard_map/ppermute | solution.py:389
  182.9 73.8 %collective-permute-start.8 = (bf16[4,128,768]{2,1,0:T(8,128)(2,1)}, bf16[4,128,768]{2,1,0:T(8,128)(2,1)}, u32[]{:S(2)}, u32[]{:S(2)}) collective-permute-start(bf16[4,128,768]{2,1,0:T(8,128)(2,1)} %get-tuple-element.70), channel_id=1, source_target_pairs={{0,1},{1,2},{2,3},{3,4},{4,5},{5,6},{6,7},{8,9},{9,10},{10,11},{11... | collective-permute-start | bytes 2359304 | tf_op jit(solution)/shard_map/ppermute | solution.py:389
  188.3 68.4 %collective-permute-start.9 = (bf16[4,128,768]{2,1,0:T(8,128)(2,1)}, bf16[4,128,768]{2,1,0:T(8,128)(2,1)}, u32[]{:S(2)}, u32[]{:S(2)}) collective-permute-start(bf16[4,128,768]{2,1,0:T(8,128)(2,1)} %get-tuple-element.71), channel_id=1, source_target_pairs={{1,0},{2,1},{3,2},{4,3},{5,4},{6,5},{7,6},{9,8},{10,9},{11,10},{12... | collective-permute-start | bytes 2359304 | tf_op jit(solution)/shard_map/ppermute | solution.py:389
  189.8 3.0 %copy-start = (bf16[6,6,6,128,128]{4,3,2,1,0:T(8,128)(2,1)S(1)}, bf16[6,6,6,128,128]{4,3,2,1,0:T(8,128)(2,1)}, u32[]{:S(2)}) copy-start(bf16[6,6,6,128,128]{4,3,2,1,0:T(8,128)(2,1)} %refs_10_.3) | copy-start | bytes 21233668
  192.9 3.0 copy-start.4
  196.6 6.2 %copy-start.7 = (f32[256,128]{1,0:T(8,128)S(1)}, f32[256,128]{1,0:T(8,128)}, u32[]{:S(2)}) copy-start(f32[256,128]{1,0:T(8,128)} %sketch_ref.9) | copy-start | bytes 393220
  196.6 6.2 %copy-start.26 = (f32[128,128]{1,0:T(8,128)S(1)}, f32[128,128]{1,0:T(8,128)}, u32[]{:S(2)}) copy-start(f32[128,128]{1,0:T(8,128)} %copy-done.25) | copy-start | bytes 196612
  196.6 19.2 %copy-start.1 = (bf16[6,6,6,128,128]{4,3,2,1,0:T(8,128)(2,1)S(1)}, bf16[6,6,6,128,128]{4,3,2,1,0:T(8,128)(2,1)}, u32[]{:S(2)}) copy-start(bf16[6,6,6,128,128]{4,3,2,1,0:T(8,128)(2,1)} %refs_10_.3) | copy-start | bytes 21233668
  202.8 22.2 %copy-start.13 = (f32[128,768]{1,0:T(8,128)}, f32[128,768]{1,0:T(8,128)S(1)}, u32[]{:S(2)}) copy-start(f32[128,768]{1,0:T(8,128)S(1)} %get-tuple-element.79) | copy-start | bytes 1179652
  210.1 15.8 %collective-permute-start.4 = (s16[1040,128]{1,0:T(8,128)(2,1)S(1)}, s16[1040,128]{1,0:T(8,128)(2,1)S(1)}, u32[]{:S(2)}, u32[]{:S(2)}) collective-permute-start(s16[1040,128]{1,0:T(8,128)(2,1)S(1)} %get-tuple-element.59.mine_ref), channel_id=1, source_target_pairs={{0,4},{1,5},{2,6},{3,7},{4,0},{5,1},{6,2},{7,3},{8,12},{9,13},{10,... | collective-permute-start | bytes 798728 | tf_op jit(solution)/shard_map/ppermute | solution.py:377
  224.9 7.9 %copy-start.15 = (f32[128,768]{1,0:T(8,128)}, f32[128,768]{1,0:T(8,128)S(1)}, u32[]{:S(2)}) copy-start(f32[128,768]{1,0:T(8,128)S(1)} %get-tuple-element.80) | copy-start | bytes 1179652
  233.4 10.8 %collective-permute-start.5 = (s16[1040,128]{1,0:T(8,128)(2,1)}, s16[1040,128]{1,0:T(8,128)(2,1)}, u32[]{:S(2)}, u32[]{:S(2)}) collective-permute-start(s16[1040,128]{1,0:T(8,128)(2,1)} %get-tuple-element.65.mine_ref), channel_id=1, source_target_pairs={{0,8},{8,0},{16,24},{24,16},{1,9},{9,1},{17,25},{25,17},{2,10},{10... | collective-permute-start | bytes 798728 | tf_op jit(solution)/shard_map/ppermute | solution.py:377
  234.2 22.5 %collective-permute-start.10 = (bf16[2,128,768]{2,1,0:T(8,128)(2,1)}, bf16[2,128,768]{2,1,0:T(8,128)(2,1)}, u32[]{:S(2)}, u32[]{:S(2)}) collective-permute-start(bf16[2,128,768]{2,1,0:T(8,128)(2,1)} %pad_maximum_fusion), channel_id=1, source_target_pairs={{0,8},{8,16},{16,24},{1,9},{9,17},{17,25},{2,10},{10,18},{18,26},{... | collective-permute-start | bytes 1179656 | tf_op jit(solution)/shard_map/ppermute | solution.py:389
  238.2 18.5 %collective-permute-start.11 = (bf16[2,128,768]{2,1,0:T(8,128)(2,1)}, bf16[2,128,768]{2,1,0:T(8,128)(2,1)}, u32[]{:S(2)}, u32[]{:S(2)}) collective-permute-start(bf16[2,128,768]{2,1,0:T(8,128)(2,1)} %pad_maximum_fusion.1), channel_id=1, source_target_pairs={{8,0},{16,8},{24,16},{9,1},{17,9},{25,17},{10,2},{18,10},{26,18},{... | collective-permute-start | bytes 1179656 | tf_op jit(solution)/shard_map/ppermute | solution.py:389
  253.2 20.9 %collective-permute-start.12 = (s16[1040,128]{1,0:T(8,128)(2,1)}, s16[1040,128]{1,0:T(8,128)(2,1)}, u32[]{:S(2)}, u32[]{:S(2)}) collective-permute-start(s16[1040,128]{1,0:T(8,128)(2,1)} %get-tuple-element.74.mine_ref), channel_id=1, source_target_pairs={{0,16},{8,24},{16,0},{24,8},{1,17},{9,25},{17,1},{25,9},{2,18},{10... | collective-permute-start | bytes 798728 | tf_op jit(solution)/shard_map/ppermute | solution.py:377
  256.7 3.0 %copy-start.2 = (bf16[6,6,6,128,128]{4,3,2,1,0:T(8,128)(2,1)S(1)}, bf16[6,6,6,128,128]{4,3,2,1,0:T(8,128)(2,1)}, u32[]{:S(2)}) copy-start(bf16[6,6,6,128,128]{4,3,2,1,0:T(8,128)(2,1)} %refs_10_.3) | copy-start | bytes 21233668
  263.5 10.7 %copy-start.14 = (f32[128,768]{1,0:T(8,128)S(1)}, f32[128,768]{1,0:T(8,128)}, u32[]{:S(2)}) copy-start(f32[128,768]{1,0:T(8,128)} %copy-done.13) | copy-start | bytes 1179652
  263.5 10.7 %copy-start.16 = (f32[128,768]{1,0:T(8,128)S(1)}, f32[128,768]{1,0:T(8,128)}, u32[]{:S(2)}) copy-start(f32[128,768]{1,0:T(8,128)} %copy-done.15) | copy-start | bytes 1179652
  263.5 10.7 %copy-start.22 = (f32[128,128]{1,0:T(8,128)S(1)}, f32[128,128]{1,0:T(8,128)}, u32[]{:S(2)}) copy-start(f32[128,128]{1,0:T(8,128)} %copy-done.21) | copy-start | bytes 196612
  274.7 6.4 %collective-permute-start.13 = (f32[4,96,128]{2,1,0:T(8,128)S(1)}, f32[4,96,128]{2,1,0:T(8,128)S(1)}, u32[]{:S(2)}, u32[]{:S(2)}) collective-permute-start(f32[4,96,128]{2,1,0:T(8,128)S(1)} %dynamic-slice_bitcast_fusion), channel_id=1, source_target_pairs={{0,1},{1,0},{2,3},{3,2},{4,5},{5,4},{6,7},{7,6},{8,9},{9,8},{10,11... | collective-permute-start | bytes 589832 | tf_op jit(solution)/shard_map/ppermute | solution.py:377
  281.1 4.7 %collective-permute-start.14 = (f32[2,96,128]{2,1,0:T(8,128)S(1)}, f32[2,96,128]{2,1,0:T(8,128)S(1)}, u32[]{:S(2)}, u32[]{:S(2)}) collective-permute-start(f32[2,96,128]{2,1,0:T(8,128)S(1)} %dynamic-slice_bitcast_fusion.1), channel_id=1, source_target_pairs={{0,2},{1,3},{2,0},{3,1},{4,6},{5,7},{6,4},{7,5},{8,10},{9,11},{10,... | collective-permute-start | bytes 294920 | tf_op jit(solution)/shard_map/ppermute | solution.py:377
  285.9 9.7 %collective-permute-start.15 = (f32[1,96,128]{2,1,0:T(8,128)S(1)}, f32[1,96,128]{2,1,0:T(8,128)S(1)}, u32[]{:S(2)}, u32[]{:S(2)}) collective-permute-start(f32[1,96,128]{2,1,0:T(8,128)S(1)} %constant_dynamic-slice_fusion), channel_id=1, source_target_pairs={{0,4},{1,5},{2,6},{3,7},{4,0},{5,1},{6,2},{7,3},{8,12},{9,13},{10,... | collective-permute-start | bytes 147464 | tf_op jit(solution)/shard_map/ppermute | solution.py:377
  295.8 1.3 collective-permute-start.16
  297.1 4.2 %collective-permute-start.17 = (f32[96,128]{1,0:T(8,128)S(1)}, f32[96,128]{1,0:T(8,128)S(1)}, u32[]{:S(2)}, u32[]{:S(2)}) collective-permute-start(f32[96,128]{1,0:T(8,128)S(1)} %add.105), channel_id=1, source_target_pairs={{0,16},{8,24},{16,0},{24,8},{1,17},{9,25},{17,1},{25,9},{2,18},{10... | collective-permute-start | bytes 147464 | tf_op jit(solution)/shard_map/ppermute | solution.py:377
  (14 other events, 13.7 us)

commit v2 on v1

v2 whole, which is shorter than its diff:
```python
import functools

import jax
import jax.numpy as jnp
from jax import lax
from jax.experimental import pallas as pl
from jax.experimental.pallas import tpu as pltpu
from jax.sharding import PartitionSpec as P

high = lax.Precision.HIGH
empty_slot = 9
near_vmem = 26 * 1024 * 1024
merge_vmem = 12 * 1024 * 1024


def dot_t(a, b, dims, precision=None):
    return lax.dot_general(
        a, b, (dims, ((), ())), precision=precision, preferred_element_type=jnp.float32
    )


def split_dot(a, b, dims):
    return dot_t(a, b, dims, high)


def near_kernel(plan, nb_ref, *refs):
    spans, wanted, block_rows, block_cols, centre_rows, centre_cols = plan
    near_hbm, right_hbm, *srcs = refs[:-8]
    out_ref, coef_ref, ext_ref, near_ref, right_ref, stage_ref, sems, out_sems = refs[-8:]
    count = len(block_cols)
    steps = len(block_rows)
    step = pl.program_id(0)
    together = block_cols == list(range(block_cols[0], block_cols[0] + count))
    groups = [(block_cols[0], 0, count)] if together else [(c, k, 1) for k, c in enumerate(block_cols)]

    def fetch(at_step):
        found = []
        for index, (source, at, ext_row, ext_col, width) in enumerate(spans):
            if ext_row in wanted[at_step]:
                view = srcs[source]
                for part in at:
                    view = view.at[part]
                target = ext_ref.at[ext_row, pl.ds(ext_col, width)]
                found.append(pltpu.make_async_copy(view, target, sems.at[index]))
        base = len(spans) + 2 * at_step * len(groups)
        for index, (col, slot, width) in enumerate(groups):
            row = block_rows[at_step]
            for offset, source, target in ((0, near_hbm, near_ref), (1, right_hbm, right_ref)):
                found.append(
                    pltpu.make_async_copy(
                        source.at[row, pl.ds(col, width)],
                        target.at[at_step, pl.ds(slot, width)],
                        sems.at[base + 2 * index + offset],
                    )
                )
        return found

    def send(place, at_step, part):
        row = block_rows[0] + at_step * (block_rows[1] - block_rows[0])
        return pltpu.make_async_copy(
            stage_ref.at[place, part], out_ref.at[row, block_cols[part]], out_sems.at[place, part]
        )

    @pl.when(step == 0)
    def _():
        for at_step in range(steps):
            for copy in fetch(at_step):
                copy.start()

    for at_step in range(steps):

        @pl.when(step == at_step)
        def _():
            for copy in fetch(at_step):
                copy.wait()

    place = lax.rem(step, 2)

    @pl.when(step >= 2)
    def _():
        for part in range(count):
            send(place, step - 2, part).wait()

    row = block_rows[0] + step * (block_rows[1] - block_rows[0])
    centre = centre_rows[0] + step * (centre_rows[1] - centre_rows[0])
    rhs = ext_ref.shape[-1]
    tile = 256 if rhs % 256 == 0 else rhs
    for part in range(count):
        middle = centre_cols[part]
        weights = []
        places = []
        for slot in range(near_ref.shape[2]):
            link = nb_ref[row, block_cols[part], slot]
            there = jnp.minimum(link, empty_slot - 1)
            weight = near_ref[step, part, slot]
            weights.append(jnp.where(link < empty_slot, weight, jnp.zeros_like(weight)))
            places.append((centre - 1 + lax.div(there, 3), middle - 1 + lax.rem(there, 3)))
        weights = jnp.concatenate(weights, axis=1)
        for at in range(0, rhs, tile):
            values = [ext_ref[i, j, :, at : at + tile] for i, j in places]
            total = jnp.dot(weights, jnp.concatenate(values, axis=0), preferred_element_type=jnp.float32)
            own = ext_ref[centre, middle, :, at : at + tile].astype(jnp.float32)
            stage_ref[place, part, :, at : at + tile] = (own + total).astype(jnp.bfloat16)
        send(place, step, part).start()
    rights = jnp.concatenate([right_ref[step, part] for part in range(count)], axis=0)
    blocks = jnp.concatenate([stage_ref[place, part] for part in range(count)], axis=0)
    coef = dot_t(rights, blocks, ((0,), (0,)))

    @pl.when(step == 0)
    def _():
        coef_ref[...] = coef

    @pl.when(step > 0)
    def _():
        coef_ref[...] += coef

    @pl.when(step == steps - 1)
    def _():
        for at_step in range(max(steps - 2, 0), steps):
            for part in range(count):
                send(at_step % 2, at_step, part).wait()


def in_hbm(value):
    return pltpu.with_memory_space_constraint(value, pltpu.HBM)


def near_part(sources, plan, near_blocks, far_right, neighbours, prior):
    spans, _, block_rows, block_cols, _, _ = plan
    gu, gv, slots, size, _ = near_blocks.shape
    rhs = sources[0].shape[-1]
    rank = far_right.shape[-1]
    ext_rows = 1 + max(span[2] for span in spans)
    ext_cols = max(span[3] + span[4] for span in spans)
    steps, count = len(block_rows), len(block_cols)
    args = [near_blocks, far_right, *sources]
    args = [in_hbm(value) if value.ndim > 3 else value for value in args]
    aliases = {}
    if prior is not None:
        args.append(prior)
        aliases = {len(args): 0}
    held = pl.BlockSpec(memory_space=pltpu.HBM)
    return pl.pallas_call(
        functools.partial(near_kernel, plan),
        grid_spec=pltpu.PrefetchScalarGridSpec(
            num_scalar_prefetch=1,
            grid=(steps,),
            in_specs=[held, held]
            + [held if source.ndim == 4 else pl.BlockSpec(memory_space=pl.ANY) for source in sources]
            + [held] * len(aliases),
            out_specs=[held, pl.BlockSpec((rank, rhs), lambda i, nb: (0, 0))],
            scratch_shapes=[
                pltpu.VMEM((ext_rows, ext_cols, size, rhs), jnp.bfloat16),
                pltpu.VMEM((steps, count, slots, size, size), jnp.bfloat16),
                pltpu.VMEM((steps, count, size, rank), jnp.bfloat16),
                pltpu.VMEM((2, count, size, rhs), jnp.bfloat16),
                pltpu.SemaphoreType.DMA((len(spans) + 2 * steps * count,)),
                pltpu.SemaphoreType.DMA((2, count)),
            ],
        ),
        out_shape=[
            jax.ShapeDtypeStruct((gu, gv, size, rhs), jnp.bfloat16),
            jax.ShapeDtypeStruct((rank, rhs), jnp.float32),
        ],
        input_output_aliases=aliases,
        cost_estimate=pl.CostEstimate(flops=7000000000, bytes_accessed=10000000, transcendentals=0),
        compiler_params=pltpu.CompilerParams(
            dimension_semantics=("arbitrary",), vmem_limit_bytes=near_vmem
        ),
    )(neighbours, *args)


def near_middle(density, near_blocks, far_right, neighbours, prior):
    gu, gv = density.shape[:2]
    spans = [(0, (row,), row, 0, gv) for row in range(gu)]
    rows = list(range(1, gu - 1))
    wanted = [(0, 1, 2)] + [(row + 1,) for row in rows[1:]]
    cols = list(range(1, gv - 1))
    plan = (spans, wanted, rows, cols, rows, cols)
    return near_part((density,), plan, near_blocks, far_right, neighbours, prior)


def near_rows(density, top, bottom, near_blocks, far_right, neighbours, prior):
    gu, gv = density.shape[:2]
    spans = [(1, (), 0, 0, gv)]
    spans += [(0, (row,), at, 0, gv) for at, row in ((1, 0), (2, 1), (3, gu - 2), (4, gu - 1))]
    spans += [(2, (), 5, 0, gv)]
    cols = list(range(1, gv - 1))
    plan = (spans, [(0, 1, 2), (3, 4, 5)], [0, gu - 1], cols, [1, 4], cols)
    return near_part((density, top, bottom), plan, near_blocks, far_right, neighbours, prior)


def near_cols(density, top, bottom, ends, mids, corner_top, corner_bottom, near_blocks, far_right, neighbours, prior):
    gu, gv = density.shape[:2]
    spans = []
    for ext_row, source, at in (
        [(0, 1, ())] + [(row + 1, 0, (row,)) for row in range(gu)] + [(gu + 1, 2, ())]
    ):
        spans.append((source, at + (pl.ds(0, 2),), ext_row, 1, 2))
        spans.append((source, at + (pl.ds(gv - 2, 2),), ext_row, 3, 2))
    for side in range(2):
        col = 5 * side
        for row in range(gu):
            if row in (0, gu - 1):
                spans.append((3 + side, (pl.ds(0 if row == 0 else 1, 1),), row + 1, col, 1))
            else:
                spans.append((5 + side, (pl.ds(row - 1, 1),), row + 1, col, 1))
        spans.append((7, (pl.ds(side, 1),), 0, col, 1))
        spans.append((8, (pl.ds(side, 1),), gu + 1, col, 1))
    rows = list(range(gu))
    wanted = [(0, 1, 2)] + [(row + 2,) for row in rows[1:]]
    plan = (spans, wanted, rows, [0, gv - 1], [row + 1 for row in rows], [1, 4])
    sources = (density, top, bottom, *ends, *mids, corner_top, corner_bottom)
    return near_part(sources, plan, near_blocks, far_right, neighbours, prior)


def run_copies(pairs, sems):
    copies = [
        pltpu.make_async_copy(source, target, sems.at[index])
        for index, (source, target) in enumerate(pairs)
    ]
    for copy in copies:
        copy.start()
    for copy in copies:
        copy.wait()


def edges_kernel(density, *refs):
    *outs, sems = refs
    gu, gv = density.shape[:2]
    pairs = []
    for side, col in ((0, gv - 1), (1, 0)):
        pairs.append((density.at[0, pl.ds(col, 1)], outs[side].at[pl.ds(0, 1)]))
        pairs.append((density.at[gu - 1, pl.ds(col, 1)], outs[side].at[pl.ds(1, 1)]))
        pairs.append((density.at[pl.ds(1, gu - 2), col], outs[2 + side]))
    pairs.append((density.at[gu - 1], outs[4]))
    pairs.append((density.at[0], outs[5]))
    run_copies(pairs, sems)


def patch_edges(density):
    gu, gv, size, rhs = density.shape
    counts = (2, 2, gu - 2, gu - 2, gv, gv)
    return pl.pallas_call(
        edges_kernel,
        in_specs=[pl.BlockSpec(memory_space=pltpu.HBM)],
        out_specs=[pl.BlockSpec(memory_space=pltpu.VMEM)] * len(counts),
        out_shape=[jax.ShapeDtypeStruct((count, size, rhs), density.dtype) for count in counts],
        scratch_shapes=[pltpu.SemaphoreType.DMA((8,))],
        cost_estimate=pl.CostEstimate(flops=7000000000, bytes_accessed=10000000, transcendentals=0),
        compiler_params=pltpu.CompilerParams(vmem_limit_bytes=merge_vmem),
    )(in_hbm(density))


def corners_kernel(first, last, top, bottom):
    for side, ends in enumerate((first, last)):
        top[side] = ends[1]
        bottom[side] = ends[0]


def patch_corners(ends):
    whole = pl.BlockSpec(memory_space=pltpu.VMEM)
    return pl.pallas_call(
        corners_kernel,
        in_specs=[whole, whole],
        out_specs=[whole, whole],
        out_shape=[jax.ShapeDtypeStruct(ends[0].shape, ends[0].dtype)] * 2,
        cost_estimate=pl.CostEstimate(flops=7000000000, bytes_accessed=10000000, transcendentals=0),
        compiler_params=pltpu.CompilerParams(vmem_limit_bytes=merge_vmem),
    )(*ends)


def reciprocal(value):
    guess = pl.reciprocal(value, approx=True)
    return guess * (2.0 - value * guess)


def eliminate(w_k, w_e):
    size = w_k.shape[0]
    step = 32
    tile = 8
    sub = lax.broadcasted_iota(jnp.int32, (tile, size), 0)

    def spread(value, row):
        return jnp.broadcast_to(value[row : row + 1, :], (tile, size))

    for base in range(0, size, step):
        count = step // tile
        k_rows = [w_k[base + tile * r : base + tile * (r + 1), :] for r in range(count)]
        e_rows = [w_e[base + tile * r : base + tile * (r + 1), :] for r in range(count)]
        for q in range(count):
            at = base + tile * q
            cols = {
                (r, k): jnp.broadcast_to(k_rows[r][:, at + k : at + k + 1], (tile, size))
                for r in range(q, count)
                for k in range(tile)
            }
            k_done = k_rows[q]
            e_done = e_rows[q]
            for k in range(0, tile, 2):
                a = spread(cols[q, k], k)
                b = spread(cols[q, k], k + 1)
                c = spread(cols[q, k + 1], k + 1)
                det = a * c - b * b
                inverse = reciprocal(det)

                def solved(one, two):
                    return (c * one - b * two) * inverse, (a * two - b * one) * inverse

                k_one, k_two = spread(k_rows[q], k), spread(k_rows[q], k + 1)
                e_one, e_two = spread(e_rows[q], k), spread(e_rows[q], k + 1)
                k_solved = solved(k_one, k_two)
                e_solved = solved(e_one, e_two)
                links = {
                    m: solved(spread(cols[q, k], m), spread(cols[q, k + 1], m)) for m in range(k + 2, tile)
                }
                root = lax.rsqrt(a)
                second = lax.rsqrt(det) * a * root
                slope = b * root * root
                k_done = jnp.where(sub == k, k_one * root, k_done)
                e_done = jnp.where(sub == k, e_one * root, e_done)
                k_done = jnp.where(sub == k + 1, (k_two - slope * k_one) * second, k_done)
                e_done = jnp.where(sub == k + 1, (e_two - slope * e_one) * second, e_done)
                for r in range(q, count):
                    one, two = cols[r, k], cols[r, k + 1]
                    if r == q:
                        if k + 2 == tile:
                            continue
                        one = jnp.where(sub > k + 1, one, 0.0)
                        two = jnp.where(sub > k + 1, two, 0.0)
                    for m in range(k + 2, tile):
                        cols[r, m] = cols[r, m] - (one * links[m][0] + two * links[m][1])
                    k_rows[r] = k_rows[r] - (one * k_solved[0] + two * k_solved[1])
                    e_rows[r] = e_rows[r] - (one * e_solved[0] + two * e_solved[1])
            k_rows[q] = k_done
            e_rows[q] = e_done
        e_now = jnp.concatenate(e_rows, axis=0)
        w_e[base : base + step, :] = e_now
        if base + step < size:
            k_now = jnp.concatenate(k_rows, axis=0)
            k_hi = k_now.astype(jnp.bfloat16)
            k_lo = (k_now - k_hi.astype(jnp.float32)).astype(jnp.bfloat16)
            e_hi = e_now.astype(jnp.bfloat16)
            e_lo = (e_now - e_hi.astype(jnp.float32)).astype(jnp.bfloat16)
            lhs = jnp.concatenate([k_hi, k_hi, k_lo], axis=0)
            k_rhs = jnp.concatenate([k_hi, k_lo, k_hi], axis=0)
            e_rhs = jnp.concatenate([e_hi, e_lo, e_hi], axis=0)
            k_fall = dot_t(lhs, k_rhs, ((0,), (0,)))
            e_fall = dot_t(lhs, e_rhs, ((0,), (0,)))
            w_k[base + step :, :] -= k_fall[base + step :, :]
            w_e[base + step :, :] -= e_fall[base + step :, :]


code_rows = 16


def encode(value, out_ref):
    rows = value.shape[0]
    top = jnp.max(jnp.abs(value), axis=0, keepdims=True)
    power = jnp.clip(jnp.floor(jnp.log2(32000.0 / jnp.maximum(top, 1e-30))), -60.0, 60.0)
    scaled = jnp.floor(value * jnp.exp2(power) + 0.5)
    out_ref[:rows, :] = scaled.astype(jnp.int32).astype(jnp.int16)
    powers = jnp.broadcast_to(power, (code_rows, value.shape[1]))
    out_ref[rows:, :] = powers.astype(jnp.int32).astype(jnp.int16)


def decode(ref):
    rows = ref.shape[0] - code_rows
    power = ref[rows:, :].astype(jnp.int32).astype(jnp.float32)[:1]
    return ref[:rows, :].astype(jnp.int32).astype(jnp.float32) * jnp.exp2(-power)


def first_kernel(counts, order_ref, value_ref, code_ref, info_ref):
    pu_count, pv_count = counts
    pu_index = lax.axis_index("pu")
    pv_index = lax.axis_index("pv")

    def least(values):
        return functools.reduce(jnp.minimum, values)

    at = 0
    width = 1
    while width < pv_count:
        start = lax.div(pv_index, width) * width
        other = start + width - 2 * width * lax.rem(lax.div(pv_index, width), 2)
        mine = least([order_ref[pu_index * pv_count + start + k] for k in range(width)])
        theirs = least([order_ref[pu_index * pv_count + other + k] for k in range(width)])
        info_ref[at] = (mine < theirs).astype(jnp.int32)
        at += 1
        width *= 2
    width = 1
    while width < pu_count:
        start = lax.div(pu_index, width) * width
        other = start + width - 2 * width * lax.rem(lax.div(pu_index, width), 2)
        mine = least([order_ref[start * pv_count + k] for k in range(width * pv_count)])
        theirs = least([order_ref[other * pv_count + k] for k in range(width * pv_count)])
        info_ref[at] = (mine < theirs).astype(jnp.int32)
        at += 1
        width *= 2
    info_ref[at] = pu_index
    encode(value_ref[0, 0], code_ref)


def first_step(value, order, counts, levels):
    rows, cols = value.shape[2:]
    return pl.pallas_call(
        functools.partial(first_kernel, counts),
        in_specs=[pl.BlockSpec(memory_space=pltpu.SMEM), pl.BlockSpec(memory_space=pltpu.VMEM)],
        out_specs=[pl.BlockSpec(memory_space=pltpu.VMEM), pl.BlockSpec(memory_space=pltpu.SMEM)],
        out_shape=[
            jax.ShapeDtypeStruct((rows + code_rows, cols), jnp.int16),
            jax.ShapeDtypeStruct((levels + 1,), jnp.int32),
        ],
        cost_estimate=pl.CostEstimate(flops=7000000000, bytes_accessed=10000000, transcendentals=0),
        compiler_params=pltpu.CompilerParams(vmem_limit_bytes=merge_vmem),
    )(order, value)


def merge_kernel(level, has_path, last, info_ref, mine_ref, other_ref, sketch_ref, *refs):
    if has_path:
        path_ref, *refs = refs
    left_ref, new_path_ref, w_k, w_e, y_ref = refs
    rank = mine_ref.shape[1]
    lead = info_ref[level] > 0
    mine = decode(mine_ref)
    other = decode(other_ref)
    stacked = jnp.concatenate([jnp.where(lead, mine, other), jnp.where(lead, other, mine)], axis=1)
    sketched = split_dot(stacked, sketch_ref[...], ((1,), (0,)))
    w_k[...] = split_dot(sketched, sketched, ((0,), (0,)))
    rows = lax.broadcasted_iota(jnp.int32, (rank, rank), 0)
    cols = lax.broadcasted_iota(jnp.int32, (rank, rank), 1)
    w_e[...] = jnp.where(rows == cols, 1.0, 0.0)
    eliminate(w_k, w_e)
    inverse = w_e[...]
    if last:
        y_ref[...] = sketched
        count = left_ref.shape[0]
        part = y_ref[pl.ds(pl.multiple_of(info_ref[info_ref.shape[0] - 1] * count, 8), count), :]
        left_ref[...] = split_dot(part, inverse, ((1,), (1,)))
    else:
        encode(split_dot(sketched, inverse, ((1,), (1,))), left_ref)
    own = split_dot(sketched, mine, ((0,), (0,)))
    if has_path:
        own = split_dot(own, path_ref[...], ((1,), (0,)))
    new_path_ref[...] = split_dot(inverse, own, ((1,), (0,)))


def merge(level, info, mine, other, sketch, path, last_rows):
    rows, rank = mine.shape
    whole = pl.BlockSpec(memory_space=pltpu.VMEM)
    paths = () if path is None else (path,)
    if last_rows:
        left = jax.ShapeDtypeStruct((last_rows, rank), jnp.float32)
    else:
        left = jax.ShapeDtypeStruct(mine.shape, jnp.int16)
    return pl.pallas_call(
        functools.partial(merge_kernel, level, bool(paths), bool(last_rows)),
        in_specs=[pl.BlockSpec(memory_space=pltpu.SMEM), whole, whole, whole] + [whole] * len(paths),
        out_specs=[whole, whole],
        out_shape=[left, jax.ShapeDtypeStruct((rank, rank), jnp.float32)],
        scratch_shapes=[
            pltpu.VMEM((rank, rank), jnp.float32),
            pltpu.VMEM((rank, rank), jnp.float32),
            pltpu.VMEM((rows - code_rows, rank), jnp.float32),
        ],
        cost_estimate=pl.CostEstimate(flops=7000000000, bytes_accessed=10000000, transcendentals=0),
        compiler_params=pltpu.CompilerParams(vmem_limit_bytes=merge_vmem),
    )(info, mine, other, sketch, *paths)


def from_partner(value, axis, distance):
    mask = 2**distance
    pairs = [(source, source ^ mask) for source in range(lax.axis_size(axis))]
    return lax.ppermute(value, axis, pairs)


def shifted(value, axis, by):
    count = lax.axis_size(axis)
    return lax.ppermute(value, axis, [(i, i + by) for i in range(count) if 0 <= i + by < count])


def tied(*values):
    return lax.optimization_barrier(values)


def per_device(density, near_blocks, neighbours, far_right, far_left, sketch, patch_order):
    pu_count = lax.axis_size("pu")
    pv_count = lax.axis_size("pv")
    pv_index = lax.axis_index("pv")
    rhs = density.shape[3]
    pv_levels = pv_count.bit_length() - 1
    pu_levels = pu_count.bit_length() - 1
    levels = pv_levels + pu_levels

    def partner(value, level):
        if level < pv_levels:
            return from_partner(value, "pv", level)
        return from_partner(value, "pu", level - pv_levels)

    rows = far_left.shape[2]
    left, info = first_step(far_left, patch_order, (pu_count, pv_count), levels)
    other = partner(left, 0)
    density, left = tied(density, left)
    *columns, last_row, first_row = patch_edges(density)
    top = shifted(last_row, "pu", 1)
    bottom = shifted(first_row, "pu", -1)
    columns, other = tied(columns, other)
    ends = [shifted(columns[0], "pv", 1), shifted(columns[1], "pv", -1)]

    coefs = []
    corrected = None
    pv_path = pu_path = None
    for level in range(levels):
        if level:
            other = partner(left, level)
            links, left = tied(neighbours, left)
            if level == 1:
                columns, left = tied(columns, left)
                mids = [shifted(columns[2], "pv", 1), shifted(columns[3], "pv", -1)]
                corrected, coef = near_middle(density, near_blocks, far_right, links, corrected)
            elif level == 2:
                corner_top, corner_bottom = patch_corners(ends)
                corner_top = shifted(corner_top, "pu", 1)
                corner_bottom = shifted(corner_bottom, "pu", -1)
                corrected, coef = near_rows(density, top, bottom, near_blocks, far_right, links, corrected)
            elif level == levels - 1:
                corrected, coef = near_cols(
                    density,
                    top,
                    bottom,
                    ends,
                    mids,
                    corner_top,
                    corner_bottom,
                    near_blocks,
                    far_right,
                    links,
                    corrected,
                )
            else:
                coef = None
            if coef is not None:
                other, coef = tied(other, coef)
                coefs.append(coef)
        path = pv_path if level < pv_levels else pu_path
        last_rows = rows // pu_count if level == levels - 1 else 0
        left, path = merge(level, info, left, other, sketch, path, last_rows)
        if level < pv_levels:
            pv_path = path
        else:
            pu_path = path

    coef = functools.reduce(lambda a, b: a + b, coefs)
    share = lax.dot_general(coef, pv_path, (((0,), (1,)), ((), ())), precision=high)
    share = share.reshape(pv_count, rhs // pv_count, -1)
    for level in range(pv_levels):
        bit = (pv_index >> level) & 1
        pairs = share.reshape(share.shape[0] // 2, 2, *share.shape[1:])
        keep = lax.dynamic_index_in_dim(pairs, bit, 1, keepdims=False)
        give = lax.dynamic_index_in_dim(pairs, 1 - bit, 1, keepdims=False)
        share = keep + from_partner(give, "pv", level)
    root_coef = lax.dot_general(share[0], pu_path, (((1,), (1,)), ((), ())), precision=high)
    for level in range(pu_levels):
        root_coef = root_coef + from_partner(root_coef, "pu", level)
    far_field = lax.dot_general(left, root_coef, (((1,), (1,)), ((), ())), precision=high)
    return (corrected, far_field)


def solution(mesh):
    in_specs = (
        P("pu", "pv", None, None),
        P("pu", "pv", None, None, None),
        P("pu", "pv", None),
        P("pu", "pv", None, None),
        P("pu", "pv", None, None),
        P(),
        P(),
    )
    out_specs = (P("pu", "pv", None, None), P("pu", "pv"))
    return jax.shard_map(
        per_device, mesh=mesh, in_specs=in_specs, out_specs=out_specs, check_vma=False
    )
```

time: 303 us -> 143 us (0.47)
  Pallas kernels: 206 us -> 63.1 us
  local copies, waits for them, and re-layouts: 28.6 us -> 5.95 us
  waiting for transfers between devices: 20 us -> 38.2 us
  between operations: 7.72 us -> 1.05 us
  starting transfers between devices: 36.2 us -> 32.3 us
    pallas_call x10 -> x11, Pallas kernels: 206 us -> 63.1 us  [the longest x5 32.1 us: merge(): pl.pallas_call(functools.partial(merge_kernel, level, bool(paths), bool(l...]
    ppermute x10, waiting for transfers between devices: 20 us -> 38.2 us  [from_partner(): return lax.ppermute(value, axis, pairs)]
    unnamed x56 -> x28, local copies, waits for them, and re-layouts: 22.7 us -> 5.89 us
    ppermute x8, starting transfers between devices: 21.6 us -> 16 us  [shifted(): lax.ppermute(value, axis, [(i, i + by) for i in range(count) if 0 <= i +...]
    dynamic_slice x6 -> x0, local copies, waits for them, and re-layouts: 3.39 us -> none  [the longest x5 3.36 us: mine_leads(): their_key = block_min[position >> tree_level ^ 1]]
  transfers between devices with their start and end apart: 18 -> 18, of which waited for: 6 -> 5; matrix products, arithmetic and copies ran while one was open for 3% -> 0% of each run, Pallas kernels for 20% -> 43%
where the time goes in v2:
time: 143 us; the launch traced here: 142 us
  Pallas kernels  63.1 us (44%)
  waiting for transfers between devices  38.2 us (27%)
  starting transfers between devices  32.3 us (23%)
  local copies, waits for them, and re-layouts  5.95 us (4%)
  matrix products  1.56 us (1%)
    ppermute x10, waiting for transfers between devices, from_partner(): return lax.ppermute(value, axis, pairs)  38.2 us
    pallas_call x5, Pallas kernels, merge(): pl.pallas_call(functools.partial(merge_kernel, level, bool(paths), bool(l...  32.1 us
    pallas_call x3, Pallas kernels, near_part(): pl.pallas_call(functools.partial(near_kernel, plan), grid_spec=pltpu.Pref...  25.9 us
    ppermute x10, starting transfers between devices, from_partner(): return lax.ppermute(value, axis, pairs)  16.2 us
    ppermute x8, starting transfers between devices, shifted(): lax.ppermute(value, axis, [(i, i + by) for i in range(count) if 0 <= i +...  16 us
    unnamed x28, local copies, waits for them, and re-layouts  5.89 us
    pallas_call x1, Pallas kernels, patch_edges(): pl.pallas_call(edges_kernel, in_specs=[pl.BlockSpec(memory_space=pltpu.HB...  3.54 us
  transfers between devices with their start and end apart: 18, of which 5 were waited for; matrix products, arithmetic and copies ran while one was open for 0% of the time, Pallas kernels for 43%

profile of v2, /device:TPU:0, one launch (start us, length us, event | category | flops | bytes accessed | tf_op | source)
XLA Modules:
  0.0 142.2 jit_solution(6036654036838340476)
XLA Ops:
  0.6 1.0 copy-done.5
  2.3 1.5 %shard_map.86 = (s16[1040,128]{1,0:T(8,128)(2,1)}, s32[6]{0:T(128)S(1)}) custom-call(s32[32]{0:T(128)S(1)} %copy-done.13, f32[1,1,1024,128]{3,2,1,0:T(8,128)S(1)} %copy-done.5), custom_call_target="tpu_custom_call" | custom-call | flops 7000000000 | bytes 10000000 | tf_op jit(solution)/shard_map/pallas_call | solution.py:406
  3.8 3.0 %collective-permute-start = (s16[1040,128]{1,0:T(8,128)(2,1)}, s16[1040,128]{1,0:T(8,128)(2,1)}, u32[]{:S(2)}, u32[]{:S(2)}) collective-permute-start(s16[1040,128]{1,0:T(8,128)(2,1)} %get-tuple-element.62.mine_ref), channel_id=1, source_target_pairs={{0,1},{1,0},{2,3},{3,2},{4,5},{5,4},{6,7},{7,6},{8,9},{9,8},{10,11... | collective-permute-start | bytes 798728 | tf_op jit(solution)/shard_map/ppermute | solution.py:474
  6.8 3.5 %shard_map.87 = (bf16[2,128,768]{2,1,0:T(8,128)(2,1)S(1)}, bf16[2,128,768]{2,1,0:T(8,128)(2,1)S(1)}, bf16[4,128,768]{2,1,0:T(8,128)(2,1)S(1)}, bf16[4,128,768]{2...) custom-call(bf16[6,6,128,768]{3,2,1,0:T(8,128)(2,1)} %refs_2_.2), custom_call_target="tpu_custom_call" | custom-call | flops 7000000000 | bytes 10000000 | tf_op jit(solution)/shard_map/pallas_call | solution.py:244
  10.4 0.9 copy-done.1
  11.2 0.9 copy-done.3
  13.6 1.5 %collective-permute-start.3 = (bf16[6,128,768]{2,1,0:T(8,128)(2,1)}, bf16[6,128,768]{2,1,0:T(8,128)(2,1)S(1)}, u32[]{:S(2)}, u32[]{:S(2)}) collective-permute-start(bf16[6,128,768]{2,1,0:T(8,128)(2,1)} %get-tuple-element.74), channel_id=1, source_target_pairs={{0,8},{8,16},{16,24},{1,9},{9,17},{17,25},{2,10},{10,18},{18,26},{... | collective-permute-start | bytes 3538952 | tf_op jit(solution)/shard_map/ppermute | solution.py:479
  15.2 1.3 collective-permute-start.4
  16.5 0.9 copy-done.10
  17.4 6.8 %shard_map.88 = (s16[1040,128]{1,0:T(8,128)(2,1)S(1)}, f32[128,128]{1,0:T(8,128)S(1)}) custom-call(s32[6]{0:T(128)S(1)} %get-tuple-element.51.info_ref, s16[1040,128]{1,0:T(8,128)(2,1)} %get-tuple-element.62.mine_ref, s16[1040,128]{1,0:T(8,128)(2,1)} %collective-permute-done.other_ref, f32[256,128]{1,0:T(8,128)S(1)} %copy-done.10), custom_call_target="tpu_custom_call" | custom-call | flops 7000000000 | bytes 10000000 | tf_op jit(solution)/shard_map/pallas_call | solution.py:456
  24.2 1.6 %collective-permute-start.1 = (s16[1040,128]{1,0:T(8,128)(2,1)S(1)}, s16[1040,128]{1,0:T(8,128)(2,1)S(1)}, u32[]{:S(2)}, u32[]{:S(2)}) collective-permute-start(s16[1040,128]{1,0:T(8,128)(2,1)S(1)} %get-tuple-element.66.mine_ref), channel_id=1, source_target_pairs={{0,2},{1,3},{2,0},{3,1},{4,6},{5,7},{6,4},{7,5},{8,10},{9,11},{10,... | collective-permute-start | bytes 798728 | tf_op jit(solution)/shard_map/ppermute | solution.py:474
  25.9 2.5 %collective-permute-start.6 = (bf16[2,128,768]{2,1,0:T(8,128)(2,1)S(1)}, bf16[2,128,768]{2,1,0:T(8,128)(2,1)S(1)}, u32[]{:S(2)}, u32[]{:S(2)}) collective-permute-start(bf16[2,128,768]{2,1,0:T(8,128)(2,1)S(1)} %copy-done.9), channel_id=1, source_target_pairs={{0,1},{1,2},{2,3},{3,4},{4,5},{5,6},{6,7},{8,9},{9,10},{10,11},{11... | collective-permute-start | bytes 1179656 | tf_op jit(solution)/shard_map/ppermute | solution.py:479
  28.3 1.3 collective-permute-start.7
  29.6 8.3 %shard_map.89 = (bf16[6,6,128,768]{3,2,1,0:T(8,128)(2,1)}, f32[128,768]{1,0:T(8,128)S(1)}) custom-call(s32[6,6,6]{2,1,0:T(8,128)S(1)} %copy-done, bf16[6,6,6,128,128]{4,3,2,1,0:T(8,128)(2,1)} %refs_0_.5, bf16[6,6,128,128]{3,2,1,0:T(8,128)(2,1)} %refs_1_.5, bf16[6,6,128,768]{3,2,1,0:T(8,128)(2,1)} %refs_2_.2), custom_call_target="tpu_custom_call" | custom-call | flops 7000000000 | bytes 10000000 | tf_op jit(solution)/shard_map/pallas_call | solution.py:143
  38.0 4.6 %collective-permute-start.8 = (bf16[4,128,768]{2,1,0:T(8,128)(2,1)S(1)}, bf16[4,128,768]{2,1,0:T(8,128)(2,1)S(1)}, u32[]{:S(2)}, u32[]{:S(2)}) collective-permute-start(bf16[4,128,768]{2,1,0:T(8,128)(2,1)S(1)} %copy-done.4), channel_id=1, source_target_pairs={{0,1},{1,2},{2,3},{3,4},{4,5},{5,6},{6,7},{8,9},{9,10},{10,11},{11... | collective-permute-start | bytes 2359304 | tf_op jit(solution)/shard_map/ppermute | solution.py:479
  42.6 6.5 %shard_map.90 = (s16[1040,128]{1,0:T(8,128)(2,1)S(1)}, f32[128,128]{1,0:T(8,128)S(1)}) custom-call(s32[6]{0:T(128)S(1)} %get-tuple-element.51.info_ref, s16[1040,128]{1,0:T(8,128)(2,1)S(1)} %get-tuple-element.66.mine_ref, s16[1040,128]{1,0:T(8,128)(2,1)S(1)} %collective-permute-done.1.other_ref, f32[256,128]{1,0:T(8,128)S(1)} %copy-done.11, ...), custom_call_target="tpu_custom_call" | custom-call | flops 7000000000 | bytes 10000000 | tf_op jit(solution)/shard_map/pallas_call | solution.py:456
  49.1 1.5 %collective-permute-start.9 = (bf16[4,128,768]{2,1,0:T(8,128)(2,1)S(1)}, bf16[4,128,768]{2,1,0:T(8,128)(2,1)S(1)}, u32[]{:S(2)}, u32[]{:S(2)}) collective-permute-start(bf16[4,128,768]{2,1,0:T(8,128)(2,1)S(1)} %copy-done.2), channel_id=1, source_target_pairs={{1,0},{2,1},{3,2},{4,3},{5,4},{6,5},{7,6},{9,8},{10,9},{11,10},{12... | collective-permute-start | bytes 2359304 | tf_op jit(solution)/shard_map/ppermute | solution.py:479
  50.6 6.5 %collective-permute-start.2 = (s16[1040,128]{1,0:T(8,128)(2,1)S(1)}, s16[1040,128]{1,0:T(8,128)(2,1)S(1)}, u32[]{:S(2)}, u32[]{:S(2)}) collective-permute-start(s16[1040,128]{1,0:T(8,128)(2,1)S(1)} %get-tuple-element.72.mine_ref), channel_id=1, source_target_pairs={{0,4},{1,5},{2,6},{3,7},{4,0},{5,1},{6,2},{7,3},{8,12},{9,13},{10,... | collective-permute-start | bytes 798728 | tf_op jit(solution)/shard_map/ppermute | solution.py:474
  57.1 5.9 %shard_map.91 = (bf16[6,6,128,768]{3,2,1,0:T(8,128)(2,1)}, f32[128,768]{1,0:T(8,128)S(1)}) custom-call(s32[6,6,6]{2,1,0:T(8,128)S(1)} %copy-done, bf16[6,6,6,128,128]{4,3,2,1,0:T(8,128)(2,1)} %refs_0_.5, bf16[6,6,128,128]{3,2,1,0:T(8,128)(2,1)} %refs_1_.5, bf16[6,6,128,768]{3,2,1,0:T(8,128)(2,1)} %refs_2_.2, ...), custom_call_target="tpu_custom_call", output_to_operand_aliasing={{0}: (6, {})} | custom-call | flops 7000000000 | bytes 10000000 | tf_op jit(solution)/shard_map/pallas_call | solution.py:143
  63.0 23.2 %collective-permute-done.2.other_ref = s16[1040,128]{1,0:T(8,128)(2,1)S(1)} collective-permute-done((s16[1040,128]{1,0:T(8,128)(2,1)S(1)}, s16[1040,128]{1,0:T(8,128)(2,1)S(1)}, u32[]{:S(2)}, u32[]{:S(2)}) %collective-permute-start.2) | collective-permute-done | bytes 266272 | tf_op jit(solution)/shard_map/ppermute | solution.py:474
  86.2 6.5 %shard_map.92 = (s16[1040,128]{1,0:T(8,128)(2,1)S(1)}, f32[128,128]{1,0:T(8,128)S(1)}) custom-call(s32[6]{0:T(128)S(1)} %get-tuple-element.51.info_ref, s16[1040,128]{1,0:T(8,128)(2,1)S(1)} %get-tuple-element.72.mine_ref, s16[1040,128]{1,0:T(8,128)(2,1)S(1)} %collective-permute-done.2.other_ref, f32[256,128]{1,0:T(8,128)S(1)} %copy-done.11, ...), custom_call_target="tpu_custom_call" | custom-call | flops 7000000000 | bytes 10000000 | tf_op jit(solution)/shard_map/pallas_call | solution.py:456
  93.1 2.1 %collective-permute-start.10 = (bf16[2,128,768]{2,1,0:T(8,128)(2,1)S(1)}, bf16[2,128,768]{2,1,0:T(8,128)(2,1)S(1)}, u32[]{:S(2)}, u32[]{:S(2)}) collective-permute-start(bf16[2,128,768]{2,1,0:T(8,128)(2,1)S(1)} %get-tuple-element.86), channel_id=1, source_target_pairs={{0,8},{8,16},{16,24},{1,9},{9,17},{17,25},{2,10},{10,18},{18,26},{... | collective-permute-start | bytes 1179656 | tf_op jit(solution)/shard_map/ppermute | solution.py:479
  95.2 1.3 collective-permute-start.11
  96.5 6.2 %shard_map.93 = (s16[1040,128]{1,0:T(8,128)(2,1)S(1)}, f32[128,128]{1,0:T(8,128)S(1)}) custom-call(s32[6]{0:T(128)S(1)} %get-tuple-element.51.info_ref, s16[1040,128]{1,0:T(8,128)(2,1)S(1)} %get-tuple-element.81.mine_ref, s16[1040,128]{1,0:T(8,128)(2,1)S(1)} %collective-permute-done.5.other_ref, f32[256,128]{1,0:T(8,128)S(1)} %copy-done.11), custom_call_target="tpu_custom_call" | custom-call | flops 7000000000 | bytes 10000000 | tf_op jit(solution)/shard_map/pallas_call | solution.py:456
  102.8 3.4 %collective-permute-start.12 = (s16[1040,128]{1,0:T(8,128)(2,1)S(1)}, s16[1040,128]{1,0:T(8,128)(2,1)S(1)}, u32[]{:S(2)}, u32[]{:S(2)}) collective-permute-start(s16[1040,128]{1,0:T(8,128)(2,1)S(1)} %get-tuple-element.90.mine_ref), channel_id=1, source_target_pairs={{0,16},{8,24},{16,0},{24,8},{1,17},{9,25},{17,1},{25,9},{2,18},{10... | collective-permute-start | bytes 798728 | tf_op jit(solution)/shard_map/ppermute | solution.py:474
  106.2 11.8 %shard_map.95 = (bf16[6,6,128,768]{3,2,1,0:T(8,128)(2,1)}, f32[128,768]{1,0:T(8,128)S(1)}) custom-call(s32[6,6,6]{2,1,0:T(8,128)S(1)} %copy-done, bf16[6,6,6,128,128]{4,3,2,1,0:T(8,128)(2,1)} %refs_0_.5, bf16[6,6,128,128]{3,2,1,0:T(8,128)(2,1)} %refs_1_.5, bf16[6,6,128,768]{3,2,1,0:T(8,128)(2,1)} %refs_2_.2, ...), custom_call_target="tpu_custom_call", output_to_operand_aliasing={{0}: (12, {})} | custom-call | flops 7000000000 | bytes 10000000 | tf_op jit(solution)/shard_map/pallas_call | solution.py:143
  118.6 6.0 %collective-permute-done.13 = f32[4,96,128]{2,1,0:T(8,128)S(1)} collective-permute-done((f32[4,96,128]{2,1,0:T(8,128)S(1)}, f32[4,96,128]{2,1,0:T(8,128)S(1)}, u32[]{:S(2)}, u32[]{:S(2)}) %collective-permute-start.13) | collective-permute-done | bytes 196640 | tf_op jit(solution)/shard_map/ppermute | solution.py:474
  124.8 4.6 %collective-permute-done.14 = f32[2,96,128]{2,1,0:T(8,128)S(1)} collective-permute-done((f32[2,96,128]{2,1,0:T(8,128)S(1)}, f32[2,96,128]{2,1,0:T(8,128)S(1)}, u32[]{:S(2)}, u32[]{:S(2)}) %collective-permute-start.14) | collective-permute-done | bytes 98336 | tf_op jit(solution)/shard_map/ppermute | solution.py:474
  129.5 6.1 %shard_map.96 = (f32[256,128]{1,0:T(8,128)S(1)}, f32[128,128]{1,0:T(8,128)S(1)}) custom-call(s32[6]{0:T(128)S(1)} %get-tuple-element.51.info_ref, s16[1040,128]{1,0:T(8,128)(2,1)S(1)} %get-tuple-element.90.mine_ref, s16[1040,128]{1,0:T(8,128)(2,1)S(1)} %collective-permute-done.12.other_ref, f32[256,128]{1,0:T(8,128)S(1)} %copy-done.12, ...), custom_call_target="tpu_custom_call" | custom-call | flops 7000000000 | bytes 10000000 | tf_op jit(solution)/shard_map/pallas_call | solution.py:456
  136.0 1.2 collective-permute-done.16
  137.2 1.0 collective-permute-start.17
  138.2 3.2 %collective-permute-done.17 = f32[96,128]{1,0:T(8,128)S(1)} collective-permute-done((f32[96,128]{1,0:T(8,128)S(1)}, f32[96,128]{1,0:T(8,128)S(1)}, u32[]{:S(2)}, u32[]{:S(2)}) %collective-permute-start.17) | collective-permute-done | bytes 49184 | tf_op jit(solution)/shard_map/ppermute | solution.py:474
  (52 shorter events, 4.6 us)
Async XLA Ops:
  0.6 1.0 copy-start.5
  1.7 0.7 copy-start.13
  3.8 12.7 %collective-permute-start = (s16[1040,128]{1,0:T(8,128)(2,1)}, s16[1040,128]{1,0:T(8,128)(2,1)}, u32[]{:S(2)}, u32[]{:S(2)}) collective-permute-start(s16[1040,128]{1,0:T(8,128)(2,1)} %get-tuple-element.62.mine_ref), channel_id=1, source_target_pairs={{0,1},{1,0},{2,3},{3,2},{4,5},{5,4},{6,7},{7,6},{8,9},{9,8},{10,11... | collective-permute-start | bytes 798728 | tf_op jit(solution)/shard_map/ppermute | solution.py:474
  10.4 0.9 copy-start.1
  11.2 0.9 copy-start.3
  12.1 0.8 copy-start.6
  12.9 0.7 copy-start.8
  13.6 35.4 %collective-permute-start.3 = (bf16[6,128,768]{2,1,0:T(8,128)(2,1)}, bf16[6,128,768]{2,1,0:T(8,128)(2,1)S(1)}, u32[]{:S(2)}, u32[]{:S(2)}) collective-permute-start(bf16[6,128,768]{2,1,0:T(8,128)(2,1)} %get-tuple-element.74), channel_id=1, source_target_pairs={{0,8},{8,16},{16,24},{1,9},{9,17},{17,25},{2,10},{10,18},{18,26},{... | collective-permute-start | bytes 3538952 | tf_op jit(solution)/shard_map/ppermute | solution.py:479
  15.2 35.4 %collective-permute-start.4 = (bf16[6,128,768]{2,1,0:T(8,128)(2,1)S(1)}, bf16[6,128,768]{2,1,0:T(8,128)(2,1)S(1)}, u32[]{:S(2)}, u32[]{:S(2)}) collective-permute-start(bf16[6,128,768]{2,1,0:T(8,128)(2,1)S(1)} %get-tuple-element.75), channel_id=1, source_target_pairs={{8,0},{16,8},{24,16},{9,1},{17,9},{25,17},{10,2},{18,10},{26,18},{... | collective-permute-start | bytes 3538952 | tf_op jit(solution)/shard_map/ppermute | solution.py:479
  16.5 0.9 copy-start.10
  17.4 8.5 %copy-start.9 = (bf16[2,128,768]{2,1,0:T(8,128)(2,1)S(1)}, bf16[2,128,768]{2,1,0:T(8,128)(2,1)}, u32[]{:S(2)}) copy-start(bf16[2,128,768]{2,1,0:T(8,128)(2,1)} %copy-done.8) | copy-start | bytes 1179652
  17.4 10.9 %copy-start.7 = (bf16[2,128,768]{2,1,0:T(8,128)(2,1)S(1)}, bf16[2,128,768]{2,1,0:T(8,128)(2,1)}, u32[]{:S(2)}) copy-start(bf16[2,128,768]{2,1,0:T(8,128)(2,1)} %copy-done.6) | copy-start | bytes 1179652
  17.4 12.2 %copy-start = (s32[6,6,6]{2,1,0:T(8,128)S(1)}, s32[6,6,6]{2,1,0:T(8,128)}, u32[]{:S(2)}) copy-start(s32[6,6,6]{2,1,0:T(8,128)} %nb_ref.2) | copy-start | bytes 2596
  24.2 13.8 %copy-start.4 = (bf16[4,128,768]{2,1,0:T(8,128)(2,1)S(1)}, bf16[4,128,768]{2,1,0:T(8,128)(2,1)}, u32[]{:S(2)}) copy-start(bf16[4,128,768]{2,1,0:T(8,128)(2,1)} %copy-done.3) | copy-start | bytes 2359300
  24.2 18.4 %copy-start.11 = (f32[256,128]{1,0:T(8,128)S(1)}, f32[256,128]{1,0:T(8,128)}, u32[]{:S(2)}) copy-start(f32[256,128]{1,0:T(8,128)} %sketch_ref.9) | copy-start | bytes 393220
  24.2 13.7 %collective-permute-start.1 = (s16[1040,128]{1,0:T(8,128)(2,1)S(1)}, s16[1040,128]{1,0:T(8,128)(2,1)S(1)}, u32[]{:S(2)}, u32[]{:S(2)}) collective-permute-start(s16[1040,128]{1,0:T(8,128)(2,1)S(1)} %get-tuple-element.66.mine_ref), channel_id=1, source_target_pairs={{0,2},{1,3},{2,0},{3,1},{4,6},{5,7},{6,4},{7,5},{8,10},{9,11},{10,... | collective-permute-start | bytes 798728 | tf_op jit(solution)/shard_map/ppermute | solution.py:474
  25.9 67.2 %collective-permute-start.6 = (bf16[2,128,768]{2,1,0:T(8,128)(2,1)S(1)}, bf16[2,128,768]{2,1,0:T(8,128)(2,1)S(1)}, u32[]{:S(2)}, u32[]{:S(2)}) collective-permute-start(bf16[2,128,768]{2,1,0:T(8,128)(2,1)S(1)} %copy-done.9), channel_id=1, source_target_pairs={{0,1},{1,2},{2,3},{3,4},{4,5},{5,6},{6,7},{8,9},{9,10},{10,11},{11... | collective-permute-start | bytes 1179656 | tf_op jit(solution)/shard_map/ppermute | solution.py:479
  28.3 64.7 %collective-permute-start.7 = (bf16[2,128,768]{2,1,0:T(8,128)(2,1)S(1)}, bf16[2,128,768]{2,1,0:T(8,128)(2,1)S(1)}, u32[]{:S(2)}, u32[]{:S(2)}) collective-permute-start(bf16[2,128,768]{2,1,0:T(8,128)(2,1)S(1)} %copy-done.7), channel_id=1, source_target_pairs={{1,0},{2,1},{3,2},{4,3},{5,4},{6,5},{7,6},{9,8},{10,9},{11,10},{12... | collective-permute-start | bytes 1179656 | tf_op jit(solution)/shard_map/ppermute | solution.py:479
  38.0 68.2 %collective-permute-start.8 = (bf16[4,128,768]{2,1,0:T(8,128)(2,1)S(1)}, bf16[4,128,768]{2,1,0:T(8,128)(2,1)S(1)}, u32[]{:S(2)}, u32[]{:S(2)}) collective-permute-start(bf16[4,128,768]{2,1,0:T(8,128)(2,1)S(1)} %copy-done.4), channel_id=1, source_target_pairs={{0,1},{1,2},{2,3},{3,4},{4,5},{5,6},{6,7},{8,9},{9,10},{10,11},{11... | collective-permute-start | bytes 2359304 | tf_op jit(solution)/shard_map/ppermute | solution.py:479
  42.6 6.5 %copy-start.2 = (bf16[4,128,768]{2,1,0:T(8,128)(2,1)S(1)}, bf16[4,128,768]{2,1,0:T(8,128)(2,1)}, u32[]{:S(2)}) copy-start(bf16[4,128,768]{2,1,0:T(8,128)(2,1)} %copy-done.1) | copy-start | bytes 2359300
  49.1 57.1 %collective-permute-start.9 = (bf16[4,128,768]{2,1,0:T(8,128)(2,1)S(1)}, bf16[4,128,768]{2,1,0:T(8,128)(2,1)S(1)}, u32[]{:S(2)}, u32[]{:S(2)}) collective-permute-start(bf16[4,128,768]{2,1,0:T(8,128)(2,1)S(1)} %copy-done.2), channel_id=1, source_target_pairs={{1,0},{2,1},{3,2},{4,3},{5,4},{6,5},{7,6},{9,8},{10,9},{11,10},{12... | collective-permute-start | bytes 2359304 | tf_op jit(solution)/shard_map/ppermute | solution.py:479
  50.6 35.6 %collective-permute-start.2 = (s16[1040,128]{1,0:T(8,128)(2,1)S(1)}, s16[1040,128]{1,0:T(8,128)(2,1)S(1)}, u32[]{:S(2)}, u32[]{:S(2)}) collective-permute-start(s16[1040,128]{1,0:T(8,128)(2,1)S(1)} %get-tuple-element.72.mine_ref), channel_id=1, source_target_pairs={{0,4},{1,5},{2,6},{3,7},{4,0},{5,1},{6,2},{7,3},{8,12},{9,13},{10,... | collective-permute-start | bytes 798728 | tf_op jit(solution)/shard_map/ppermute | solution.py:474
  92.7 3.9 %collective-permute-start.5 = (s16[1040,128]{1,0:T(8,128)(2,1)S(1)}, s16[1040,128]{1,0:T(8,128)(2,1)S(1)}, u32[]{:S(2)}, u32[]{:S(2)}) collective-permute-start(s16[1040,128]{1,0:T(8,128)(2,1)S(1)} %get-tuple-element.81.mine_ref), channel_id=1, source_target_pairs={{0,8},{8,0},{16,24},{24,16},{1,9},{9,1},{17,25},{25,17},{2,10},{10... | collective-permute-start | bytes 798728 | tf_op jit(solution)/shard_map/ppermute | solution.py:474
  93.1 13.1 %collective-permute-start.10 = (bf16[2,128,768]{2,1,0:T(8,128)(2,1)S(1)}, bf16[2,128,768]{2,1,0:T(8,128)(2,1)S(1)}, u32[]{:S(2)}, u32[]{:S(2)}) collective-permute-start(bf16[2,128,768]{2,1,0:T(8,128)(2,1)S(1)} %get-tuple-element.86), channel_id=1, source_target_pairs={{0,8},{8,16},{16,24},{1,9},{9,17},{17,25},{2,10},{10,18},{18,26},{... | collective-permute-start | bytes 1179656 | tf_op jit(solution)/shard_map/ppermute | solution.py:479
  95.2 11.0 %collective-permute-start.11 = (bf16[2,128,768]{2,1,0:T(8,128)(2,1)S(1)}, bf16[2,128,768]{2,1,0:T(8,128)(2,1)S(1)}, u32[]{:S(2)}, u32[]{:S(2)}) collective-permute-start(bf16[2,128,768]{2,1,0:T(8,128)(2,1)S(1)} %get-tuple-element.87), channel_id=1, source_target_pairs={{8,0},{16,8},{24,16},{9,1},{17,9},{25,17},{10,2},{18,10},{26,18},{... | collective-permute-start | bytes 1179656 | tf_op jit(solution)/shard_map/ppermute | solution.py:479
  102.8 15.2 %collective-permute-start.12 = (s16[1040,128]{1,0:T(8,128)(2,1)S(1)}, s16[1040,128]{1,0:T(8,128)(2,1)S(1)}, u32[]{:S(2)}, u32[]{:S(2)}) collective-permute-start(s16[1040,128]{1,0:T(8,128)(2,1)S(1)} %get-tuple-element.90.mine_ref), channel_id=1, source_target_pairs={{0,16},{8,24},{16,0},{24,8},{1,17},{9,25},{17,1},{25,9},{2,18},{10... | collective-permute-start | bytes 798728 | tf_op jit(solution)/shard_map/ppermute | solution.py:474
  106.2 23.3 %copy-start.12 = (f32[256,128]{1,0:T(8,128)S(1)}, f32[256,128]{1,0:T(8,128)}, u32[]{:S(2)}) copy-start(f32[256,128]{1,0:T(8,128)} %sketch_ref.9) | copy-start | bytes 393220
  118.5 6.1 %collective-permute-start.13 = (f32[4,96,128]{2,1,0:T(8,128)S(1)}, f32[4,96,128]{2,1,0:T(8,128)S(1)}, u32[]{:S(2)}, u32[]{:S(2)}) collective-permute-start(f32[4,96,128]{2,1,0:T(8,128)S(1)} %dynamic-slice_bitcast_fusion), channel_id=1, source_target_pairs={{0,1},{1,0},{2,3},{3,2},{4,5},{5,4},{6,7},{7,6},{8,9},{9,8},{10,11... | collective-permute-start | bytes 589832 | tf_op jit(solution)/shard_map/ppermute | solution.py:474
  124.7 4.7 %collective-permute-start.14 = (f32[2,96,128]{2,1,0:T(8,128)S(1)}, f32[2,96,128]{2,1,0:T(8,128)S(1)}, u32[]{:S(2)}, u32[]{:S(2)}) collective-permute-start(f32[2,96,128]{2,1,0:T(8,128)S(1)} %dynamic-slice_bitcast_fusion.1), channel_id=1, source_target_pairs={{0,2},{1,3},{2,0},{3,1},{4,6},{5,7},{6,4},{7,5},{8,10},{9,11},{10,... | collective-permute-start | bytes 294920 | tf_op jit(solution)/shard_map/ppermute | solution.py:474
  129.4 6.2 %collective-permute-start.15 = (f32[1,96,128]{2,1,0:T(8,128)S(1)}, f32[1,96,128]{2,1,0:T(8,128)S(1)}, u32[]{:S(2)}, u32[]{:S(2)}) collective-permute-start(f32[1,96,128]{2,1,0:T(8,128)S(1)} %constant_dynamic-slice_fusion), channel_id=1, source_target_pairs={{0,4},{1,5},{2,6},{3,7},{4,0},{5,1},{6,2},{7,3},{8,12},{9,13},{10,... | collective-permute-start | bytes 147464 | tf_op jit(solution)/shard_map/ppermute | solution.py:474
  135.9 1.3 collective-permute-start.16
  137.2 4.2 %collective-permute-start.17 = (f32[96,128]{1,0:T(8,128)S(1)}, f32[96,128]{1,0:T(8,128)S(1)}, u32[]{:S(2)}, u32[]{:S(2)}) collective-permute-start(f32[96,128]{1,0:T(8,128)S(1)} %add.56), channel_id=1, source_target_pairs={{0,16},{8,24},{16,0},{24,8},{1,17},{9,25},{17,1},{25,9},{2,18},{10... | collective-permute-start | bytes 147464 | tf_op jit(solution)/shard_map/ppermute | solution.py:474

commit v3 on v2

--- a/solution.py
+++ b/solution.py
@@ -23,42 +23,41 @@
     return dot_t(a, b, dims, high)
 
 
-def near_kernel(plan, nb_ref, *refs):
-    spans, wanted, block_rows, block_cols, centre_rows, centre_cols = plan
-    near_hbm, right_hbm, *srcs = refs[:-8]
+def in_hbm(value):
+    return pltpu.with_memory_space_constraint(value, pltpu.HBM)
+
+
+def cost(microseconds):
+    return pl.CostEstimate(flops=int(microseconds * 1.1e9), bytes_accessed=0, transcendentals=0)
+
+
+def near_kernel(plan, n_src, nb_ref, near_hbm, right_hbm, *refs):
+    spans, block_rows, centre_rows, count, first_col, centre_col = plan
+    srcs = refs[:n_src]
     out_ref, coef_ref, ext_ref, near_ref, right_ref, stage_ref, sems, out_sems = refs[-8:]
-    count = len(block_cols)
     steps = len(block_rows)
     step = pl.program_id(0)
-    together = block_cols == list(range(block_cols[0], block_cols[0] + count))
-    groups = [(block_cols[0], 0, count)] if together else [(c, k, 1) for k, c in enumerate(block_cols)]
+    col = first_col()
 
     def fetch(at_step):
         found = []
-        for index, (source, at, ext_row, ext_col, width) in enumerate(spans):
-            if ext_row in wanted[at_step]:
-                view = srcs[source]
-                for part in at:
-                    view = view.at[part]
-                target = ext_ref.at[ext_row, pl.ds(ext_col, width)]
-                found.append(pltpu.make_async_copy(view, target, sems.at[index]))
-        base = len(spans) + 2 * at_step * len(groups)
-        for index, (col, slot, width) in enumerate(groups):
-            row = block_rows[at_step]
-            for offset, source, target in ((0, near_hbm, near_ref), (1, right_hbm, right_ref)):
-                found.append(
-                    pltpu.make_async_copy(
-                        source.at[row, pl.ds(col, width)],
-                        target.at[at_step, pl.ds(slot, width)],
-                        sems.at[base + 2 * index + offset],
-                    )
+        for index, (needed, views) in enumerate(spans):
+            if needed == at_step:
+                source, target = views(srcs, ext_ref)
+                found.append(pltpu.make_async_copy(source, target, sems.at[index]))
+        base = len(spans) + 2 * at_step
+        for offset, source, target in ((0, near_hbm, near_ref), (1, right_hbm, right_ref)):
+            found.append(
+                pltpu.make_async_copy(
+                    source.at[block_rows[at_step], pl.ds(col, count)], target.at[at_step], sems.at[base + offset]
                 )
+            )
         return found
 
     def send(place, at_step, part):
         row = block_rows[0] + at_step * (block_rows[1] - block_rows[0])
         return pltpu.make_async_copy(
-            stage_ref.at[place, part], out_ref.at[row, block_cols[part]], out_sems.at[place, part]
+            stage_ref.at[place, part], out_ref.at[row, col + part], out_sems.at[place, part]
         )
 
     @pl.when(step == 0)
@@ -86,11 +85,11 @@
     rhs = ext_ref.shape[-1]
     tile = 256 if rhs % 256 == 0 else rhs
     for part in range(count):
-        middle = centre_cols[part]
+        middle = centre_col + part
         weights = []
         places = []
         for slot in range(near_ref.shape[2]):
-            link = nb_ref[row, block_cols[part], slot]
+            link = nb_ref[row, col + part, slot]
             there = jnp.minimum(link, empty_slot - 1)
             weight = near_ref[step, part, slot]
             weights.append(jnp.where(link < empty_slot, weight, jnp.zeros_like(weight)))
@@ -121,18 +120,12 @@
                 send(at_step % 2, at_step, part).wait()
 
 
-def in_hbm(value):
-    return pltpu.with_memory_space_constraint(value, pltpu.HBM)
-
-
-def near_part(sources, plan, near_blocks, far_right, neighbours, prior):
-    spans, _, block_rows, block_cols, _, _ = plan
+def near_part(sources, plan, ext_shape, near_blocks, far_right, neighbours, prior, time):
+    spans, block_rows, _, count, _, _ = plan
     gu, gv, slots, size, _ = near_blocks.shape
     rhs = sources[0].shape[-1]
     rank = far_right.shape[-1]
-    ext_rows = 1 + max(span[2] for span in spans)
-    ext_cols = max(span[3] + span[4] for span in spans)
-    steps, count = len(block_rows), len(block_cols)
+    steps = len(block_rows)
     args = [near_blocks, far_right, *sources]
     args = [in_hbm(value) if value.ndim > 3 else value for value in args]
     aliases = {}
@@ -141,7 +134,7 @@
         aliases = {len(args): 0}
     held = pl.BlockSpec(memory_space=pltpu.HBM)
     return pl.pallas_call(
-        functools.partial(near_kernel, plan),
+        functools.partial(near_kernel, plan, len(sources)),
         grid_spec=pltpu.PrefetchScalarGridSpec(
             num_scalar_prefetch=1,
             grid=(steps,),
@@ -150,11 +143,11 @@
             + [held] * len(aliases),
             out_specs=[held, pl.BlockSpec((rank, rhs), lambda i, nb: (0, 0))],
             scratch_shapes=[
-                pltpu.VMEM((ext_rows, ext_cols, size, rhs), jnp.bfloat16),
+                pltpu.VMEM((*ext_shape, size, rhs), jnp.bfloat16),
                 pltpu.VMEM((steps, count, slots, size, size), jnp.bfloat16),
                 pltpu.VMEM((steps, count, size, rank), jnp.bfloat16),
                 pltpu.VMEM((2, count, size, rhs), jnp.bfloat16),
-                pltpu.SemaphoreType.DMA((len(spans) + 2 * steps * count,)),
+                pltpu.SemaphoreType.DMA((len(spans) + 2 * steps,)),
                 pltpu.SemaphoreType.DMA((2, count)),
             ],
         ),
@@ -163,111 +156,104 @@
             jax.ShapeDtypeStruct((rank, rhs), jnp.float32),
         ],
         input_output_aliases=aliases,
-        cost_estimate=pl.CostEstimate(flops=7000000000, bytes_accessed=10000000, transcendentals=0),
+        cost_estimate=cost(time),
         compiler_params=pltpu.CompilerParams(
             dimension_semantics=("arbitrary",), vmem_limit_bytes=near_vmem
         ),
     )(neighbours, *args)
 
 
+def odd(axis):
+    return lax.rem(lax.axis_index(axis), 2)
+
+
+def row_span(row, ext_row):
+    return lambda srcs, ext: (srcs[0].at[row], ext.at[ext_row])
+
+
 def near_middle(density, near_blocks, far_right, neighbours, prior):
     gu, gv = density.shape[:2]
-    spans = [(0, (row,), row, 0, gv) for row in range(gu)]
+    spans = [(max(row - 2, 0), row_span(row, row)) for row in range(gu)]
     rows = list(range(1, gu - 1))
-    wanted = [(0, 1, 2)] + [(row + 1,) for row in rows[1:]]
-    cols = list(range(1, gv - 1))
-    plan = (spans, wanted, rows, cols, rows, cols)
-    return near_part((density,), plan, near_blocks, far_right, neighbours, prior)
-
-
-def near_rows(density, top, bottom, near_blocks, far_right, neighbours, prior):
+    plan = (spans, rows, rows, gv - 2, lambda: 1, 1)
+    return near_part((density,), plan, (gu, gv), near_blocks, far_right, neighbours, prior, 8)
+
+
+def near_rows(density, pu_near, pu_far, near_blocks, far_right, neighbours, prior):
     gu, gv = density.shape[:2]
-    spans = [(1, (), 0, 0, gv)]
-    spans += [(0, (row,), at, 0, gv) for at, row in ((1, 0), (2, 1), (3, gu - 2), (4, gu - 1))]
-    spans += [(2, (), 5, 0, gv)]
-    cols = list(range(1, gv - 1))
-    plan = (spans, [(0, 1, 2), (3, 4, 5)], [0, gu - 1], cols, [1, 4], cols)
-    return near_part((density, top, bottom), plan, near_blocks, far_right, neighbours, prior)
-
-
-def near_cols(density, top, bottom, ends, mids, corner_top, corner_bottom, near_blocks, far_right, neighbours, prior):
+    spans = [(at, row_span(row, ext_row)) for at, row, ext_row in ((0, 0, 1), (0, 1, 2), (1, gu - 2, 3), (1, gu - 1, 4))]
+    spans.append((0, lambda srcs, ext: (srcs[1], ext.at[5 * (1 - odd("pu"))])))
+    spans.append((0, lambda srcs, ext: (srcs[2], ext.at[5 * odd("pu")])))
+    plan = (spans, [0, gu - 1], [1, 4], gv - 2, lambda: 1, 1)
+    return near_part((density, pu_near, pu_far), plan, (6, gv), near_blocks, far_right, neighbours, prior, 1.5)
+
+
+def near_column(far, density, pu_near, pu_far, corner_near, corner_far, halo, near_blocks, far_right, neighbours, prior):
     gu, gv = density.shape[:2]
+
+    def left_side():
+        return 1 - odd("pv") if far else odd("pv")
+
     spans = []
-    for ext_row, source, at in (
-        [(0, 1, ())] + [(row + 1, 0, (row,)) for row in range(gu)] + [(gu + 1, 2, ())]
-    ):
-        spans.append((source, at + (pl.ds(0, 2),), ext_row, 1, 2))
-        spans.append((source, at + (pl.ds(gv - 2, 2),), ext_row, 3, 2))
-    for side in range(2):
-        col = 5 * side
-        for row in range(gu):
-            if row in (0, gu - 1):
-                spans.append((3 + side, (pl.ds(0 if row == 0 else 1, 1),), row + 1, col, 1))
-            else:
-                spans.append((5 + side, (pl.ds(row - 1, 1),), row + 1, col, 1))
-        spans.append((7, (pl.ds(side, 1),), 0, col, 1))
-        spans.append((8, (pl.ds(side, 1),), gu + 1, col, 1))
+
+    def start_col():
+        return (gv - 2) * (1 - left_side())
+
+    def inner(source, at, ext_row):
+        def views(srcs, ext):
+            view = srcs[source]
+            if at is not None:
+                view = view.at[at]
+            return view.at[pl.ds(start_col(), 2)], ext.at[ext_row(), pl.ds(left_side(), 2)]
+
+        return views
+
+    def outer(source, at, ext_row):
+        return lambda srcs, ext: (srcs[source].at[at], ext.at[ext_row(), 2 * (1 - left_side())])
+
+    def near_row():
+        return (gu + 1) * (1 - odd("pu"))
+
+    def far_row():
+        return (gu + 1) * odd("pu")
+
+    for row in range(gu):
+        at = max(row - 1, 0)
+        spans.append((at, inner(0, row, lambda row=row: row + 1)))
+        if len(halo) == 1:
+            spans.append((at, outer(5, row, lambda row=row: row + 1)))
+        elif row in (0, gu - 1):
+            spans.append((at, outer(5, min(row, 1), lambda row=row: row + 1)))
+        else:
+            spans.append((at, outer(6, row - 1, lambda row=row: row + 1)))
+    spans.append((0, inner(1, None, near_row)))
+    spans.append((0, inner(2, None, far_row)))
+    spans.append((0, outer(3, int(far), near_row)))
+    spans.append((0, outer(4, int(far), far_row)))
     rows = list(range(gu))
-    wanted = [(0, 1, 2)] + [(row + 2,) for row in rows[1:]]
-    plan = (spans, wanted, rows, [0, gv - 1], [row + 1 for row in rows], [1, 4])
-    sources = (density, top, bottom, *ends, *mids, corner_top, corner_bottom)
-    return near_part(sources, plan, near_blocks, far_right, neighbours, prior)
-
-
-def run_copies(pairs, sems):
-    copies = [
-        pltpu.make_async_copy(source, target, sems.at[index])
-        for index, (source, target) in enumerate(pairs)
-    ]
-    for copy in copies:
-        copy.start()
-    for copy in copies:
-        copy.wait()
-
-
-def edges_kernel(density, *refs):
-    *outs, sems = refs
-    gu, gv = density.shape[:2]
-    pairs = []
-    for side, col in ((0, gv - 1), (1, 0)):
-        pairs.append((density.at[0, pl.ds(col, 1)], outs[side].at[pl.ds(0, 1)]))
-        pairs.append((density.at[gu - 1, pl.ds(col, 1)], outs[side].at[pl.ds(1, 1)]))
-        pairs.append((density.at[pl.ds(1, gu - 2), col], outs[2 + side]))
-    pairs.append((density.at[gu - 1], outs[4]))
-    pairs.append((density.at[0], outs[5]))
-    run_copies(pairs, sems)
-
-
-def patch_edges(density):
-    gu, gv, size, rhs = density.shape
-    counts = (2, 2, gu - 2, gu - 2, gv, gv)
-    return pl.pallas_call(
-        edges_kernel,
-        in_specs=[pl.BlockSpec(memory_space=pltpu.HBM)],
-        out_specs=[pl.BlockSpec(memory_space=pltpu.VMEM)] * len(counts),
-        out_shape=[jax.ShapeDtypeStruct((count, size, rhs), density.dtype) for count in counts],
-        scratch_shapes=[pltpu.SemaphoreType.DMA((8,))],
-        cost_estimate=pl.CostEstimate(flops=7000000000, bytes_accessed=10000000, transcendentals=0),
-        compiler_params=pltpu.CompilerParams(vmem_limit_bytes=merge_vmem),
-    )(in_hbm(density))
-
-
-def corners_kernel(first, last, top, bottom):
-    for side, ends in enumerate((first, last)):
-        top[side] = ends[1]
-        bottom[side] = ends[0]
-
-
-def patch_corners(ends):
+    plan = (spans, rows, [row + 1 for row in rows], 1, lambda: (gv - 1) * (1 - left_side()), 1)
+    sources = (density, pu_near, pu_far, corner_near, corner_far, *halo)
+    return near_part(sources, plan, (gu + 2, 3), near_blocks, far_right, neighbours, prior, 1.5)
+
+
+def corners_kernel(beside, ends, to_near, to_far):
+    low = odd("pu")
+    rows = beside.shape[0]
+    for target, last in ((to_near, 1 - low), (to_far, low)):
+        target[0] = beside[(rows - 1) * last]
+        target[1] = ends[last]
+
+
+def patch_corners(beside, ends):
     whole = pl.BlockSpec(memory_space=pltpu.VMEM)
     return pl.pallas_call(
         corners_kernel,
         in_specs=[whole, whole],
         out_specs=[whole, whole],
-        out_shape=[jax.ShapeDtypeStruct(ends[0].shape, ends[0].dtype)] * 2,
-        cost_estimate=pl.CostEstimate(flops=7000000000, bytes_accessed=10000000, transcendentals=0),
+        out_shape=[jax.ShapeDtypeStruct(ends.shape, ends.dtype)] * 2,
+        cost_estimate=cost(0.7),
         compiler_params=pltpu.CompilerParams(vmem_limit_bytes=merge_vmem),
-    )(*ends)
+    )(beside, ends)
 
 
 def reciprocal(value):
@@ -370,10 +356,25 @@
     return ref[:rows, :].astype(jnp.int32).astype(jnp.float32) * jnp.exp2(-power)
 
 
-def first_kernel(counts, order_ref, value_ref, code_ref, info_ref):
+def first_kernel(counts, order_ref, value_ref, density, code_ref, info_ref, *refs):
+    beside, ends, mids, pu_near, pu_far, sems = refs
     pu_count, pv_count = counts
     pu_index = lax.axis_index("pu")
     pv_index = lax.axis_index("pv")
+    gu, gv = density.shape[:2]
+    near_col = (gv - 1) * (1 - odd("pv"))
+    far_col = (gv - 1) * odd("pv")
+    pairs = [(density.at[row, near_col], beside.at[row]) for row in range(gu)]
+    pairs += [(density.at[(gu - 1) * row, far_col], ends.at[row]) for row in range(2)]
+    pairs += [(density.at[row + 1, far_col], mids.at[row]) for row in range(gu - 2)]
+    pairs.append((density.at[(gu - 1) * (1 - odd("pu"))], pu_near))
+    pairs.append((density.at[(gu - 1) * odd("pu")], pu_far))
+    copies = [
+        pltpu.make_async_copy(source, target, sems.at[index])
+        for index, (source, target) in enumerate(pairs)
+    ]
+    for copy in copies:
+        copy.start()
 
     def least(values):
         return functools.reduce(jnp.minimum, values)
@@ -399,21 +400,29 @@
         width *= 2
     info_ref[at] = pu_index
     encode(value_ref[0, 0], code_ref)
-
-
-def first_step(value, order, counts, levels):
+    for copy in copies:
+        copy.wait()
+
+
+def first_step(value, density, order, counts, levels):
     rows, cols = value.shape[2:]
+    gu, gv, size, rhs = density.shape
+    blocks = (gu, 2, gu - 2, gv, gv)
+    whole = pl.BlockSpec(memory_space=pltpu.VMEM)
+    scalars = pl.BlockSpec(memory_space=pltpu.SMEM)
     return pl.pallas_call(
         functools.partial(first_kernel, counts),
-        in_specs=[pl.BlockSpec(memory_space=pltpu.SMEM), pl.BlockSpec(memory_space=pltpu.VMEM)],
-        out_specs=[pl.BlockSpec(memory_space=pltpu.VMEM), pl.BlockSpec(memory_space=pltpu.SMEM)],
+        in_specs=[scalars, whole, pl.BlockSpec(memory_space=pltpu.HBM)],
+        out_specs=[whole, scalars] + [whole] * len(blocks),
         out_shape=[
             jax.ShapeDtypeStruct((rows + code_rows, cols), jnp.int16),
             jax.ShapeDtypeStruct((levels + 1,), jnp.int32),
-        ],
-        cost_estimate=pl.CostEstimate(flops=7000000000, bytes_accessed=10000000, transcendentals=0),
+        ]
+        + [jax.ShapeDtypeStruct((count, size, rhs), density.dtype) for count in blocks],
+        scratch_shapes=[pltpu.SemaphoreType.DMA((2 * gu + 2,))],
+        cost_estimate=cost(3),
         compiler_params=pltpu.CompilerParams(vmem_limit_bytes=merge_vmem),
-    )(order, value)
+    )(order, value, in_hbm(density))
 
 
 def merge_kernel(level, has_path, last, info_ref, mine_ref, other_ref, sketch_ref, *refs):
@@ -463,7 +472,7 @@
             pltpu.VMEM((rank, rank), jnp.float32),
             pltpu.VMEM((rows - code_rows, rank), jnp.float32),
         ],
-        cost_estimate=pl.CostEstimate(flops=7000000000, bytes_accessed=10000000, transcendentals=0),
+        cost_estimate=cost(4 if level < 2 else 2),
         compiler_params=pltpu.CompilerParams(vmem_limit_bytes=merge_vmem),
     )(info, mine, other, sketch, *paths)
 
@@ -474,9 +483,12 @@
     return lax.ppermute(value, axis, pairs)
 
 
-def shifted(value, axis, by):
+def swapped(value, axis, far):
     count = lax.axis_size(axis)
-    return lax.ppermute(value, axis, [(i, i + by) for i in range(count) if 0 <= i + by < count])
+    pairs = []
+    for low in range(int(far), count - 1, 2):
+        pairs += [(low, low + 1), (low + 1, low)]
+    return lax.ppermute(value, axis, pairs)
 
 
 def tied(*values):
@@ -498,50 +510,39 @@
         return from_partner(value, "pu", level - pv_levels)
 
     rows = far_left.shape[2]
-    left, info = first_step(far_left, patch_order, (pu_count, pv_count), levels)
+    left, info, beside, ends, mids, pu_near, pu_far = first_step(
+        far_left, density, patch_order, (pu_count, pv_count), levels
+    )
     other = partner(left, 0)
-    density, left = tied(density, left)
-    *columns, last_row, first_row = patch_edges(density)
-    top = shifted(last_row, "pu", 1)
-    bottom = shifted(first_row, "pu", -1)
-    columns, other = tied(columns, other)
-    ends = [shifted(columns[0], "pv", 1), shifted(columns[1], "pv", -1)]
+    beside = swapped(beside, "pv", False)
+    pu_near = swapped(pu_near, "pu", False)
+    pu_far = swapped(pu_far, "pu", True)
 
     coefs = []
     corrected = None
     pv_path = pu_path = None
     for level in range(levels):
+        coef = None
         if level:
             other = partner(left, level)
+        if level in (1, 2, levels - 1):
             links, left = tied(neighbours, left)
-            if level == 1:
-                columns, left = tied(columns, left)
-                mids = [shifted(columns[2], "pv", 1), shifted(columns[3], "pv", -1)]
-                corrected, coef = near_middle(density, near_blocks, far_right, links, corrected)
-            elif level == 2:
-                corner_top, corner_bottom = patch_corners(ends)
-                corner_top = shifted(corner_top, "pu", 1)
-                corner_bottom = shifted(corner_bottom, "pu", -1)
-                corrected, coef = near_rows(density, top, bottom, near_blocks, far_right, links, corrected)
-            elif level == levels - 1:
-                corrected, coef = near_cols(
-                    density,
-                    top,
-                    bottom,
-                    ends,
-                    mids,
-                    corner_top,
-                    corner_bottom,
-                    near_blocks,
-                    far_right,
-                    links,
-                    corrected,
-                )
-            else:
-                coef = None
-            if coef is not None:
-                other, coef = tied(other, coef)
-                coefs.append(coef)
+        if level == 1:
+            corrected, coef = near_middle(density, near_blocks, far_right, links, corrected)
+        elif level == 2:
+            ends, mids, left = tied(ends, mids, left)
+            ends = swapped(ends, "pv", True)
+            mids = swapped(mids, "pv", True)
+            corrected, coef = near_rows(density, pu_near, pu_far, near_blocks, far_right, links, corrected)
+        elif level == levels - 1:
+            corner_near, corner_far = patch_corners(beside, ends)
+            corner_near = swapped(corner_near, "pu", False)
+            corner_far = swapped(corner_far, "pu", True)
+            halo = (density, pu_near, pu_far, corner_near, corner_far)
+            corrected, coef = near_column(False, *halo, (beside,), near_blocks, far_right, links, corrected)
+        if coef is not None:
+            other, coef = tied(other, coef)
+            coefs.append(coef)
         path = pv_path if level < pv_levels else pu_path
         last_rows = rows // pu_count if level == levels - 1 else 0
         left, path = merge(level, info, left, other, sketch, path, last_rows)
@@ -549,6 +550,9 @@
             pv_path = path
         else:
             pu_path = path
+
+    corrected, coef = near_column(True, *halo, (ends, mids), near_blocks, far_right, neighbours, corrected)
+    coefs.append(coef)
 
     coef = functools.reduce(lambda a, b: a + b, coefs)
     share = lax.dot_general(coef, pv_path, (((0,), (1,)), ((), ())), precision=high)

time: 143 us -> 118 us (0.83)
  waiting for transfers between devices: 38.2 us -> 21.7 us
  starting transfers between devices: 32.3 us -> 23.5 us
  Pallas kernels: 63.1 us -> 66.5 us
  local copies, waits for them, and re-layouts: 5.95 us -> 3.91 us
    ppermute x10, waiting for transfers between devices: 38.2 us -> 21.7 us  [from_partner(): return lax.ppermute(value, axis, pairs)]
    ppermute x8 -> x7, starting transfers between devices: 16 us -> 4.3 us  [swapped(): return lax.ppermute(value, axis, pairs)]
    ppermute x10, starting transfers between devices: 16.2 us -> 19.2 us  [from_partner(): return lax.ppermute(value, axis, pairs)]
    pallas_call x5, Pallas kernels: 30.9 us -> 33.1 us  [the longest x4 29 us: near_part(): pl.pallas_call(functools.partial(near_kernel, plan, len(sources)), grid_s...]
    unnamed x28 -> x42, local copies, waits for them, and re-layouts: 5.89 us -> 3.85 us
  transfers between devices with their start and end apart: 18 -> 17, of which waited for: 5 -> 6; matrix products, arithmetic and copies ran while one was open for 0% -> 0% of each run, Pallas kernels for 43% -> 53%
where the time goes in v3:
time: 118 us
  Pallas kernels  66.5 us (56%)
  starting transfers between devices  23.5 us (20%)
  waiting for transfers between devices  21.7 us (18%)
  local copies, waits for them, and re-layouts  3.91 us (3%)
  matrix products  1.59 us (1%)
    pallas_call x5, Pallas kernels, merge(): pl.pallas_call(functools.partial(merge_kernel, level, bool(paths), bool(l...  32.3 us
    pallas_call x4, Pallas kernels, near_part(): pl.pallas_call(functools.partial(near_kernel, plan, len(sources)), grid_s...  29 us
    ppermute x10, waiting for transfers between devices, from_partner(): return lax.ppermute(value, axis, pairs)  21.7 us
    ppermute x10, starting transfers between devices, from_partner(): return lax.ppermute(value, axis, pairs)  19.2 us
    ppermute x7, starting transfers between devices, swapped(): return lax.ppermute(value, axis, pairs)  4.3 us
    pallas_call x1, Pallas kernels, first_step(): pl.pallas_call(functools.partial(first_kernel, counts), in_specs=[scalars...  4.11 us
    unnamed x42, local copies, waits for them, and re-layouts  3.85 us
  transfers between devices with their start and end apart: 17, of which 6 were waited for; matrix products, arithmetic and copies ran while one was open for 0% of the time, Pallas kernels for 53%

profile of v3, /device:TPU:0, one launch (start us, length us, event | category | flops | bytes accessed | tf_op | source)
XLA Modules:
  0.0 118.2 jit_solution(3608662211142885214)
XLA Ops:
  0.6 1.0 copy-done.10
  2.3 4.1 %shard_map.86 = (s16[1040,128]{1,0:T(8,128)(2,1)S(1)}, s32[6]{0:T(128)S(1)}, bf16[6,128,768]{2,1,0:T(8,128)(2,1)S(1)}, bf16[2,128,768]{2,1,0:T(8,128)(2,1)S(1)},...) custom-call(s32[32]{0:T(128)S(1)} %copy-done.18, ...), custom_call_target="tpu_custom_call" | custom-call | flops 3300000000 | tf_op jit(solution)/shard_map/pallas_call | solution.py:413
  6.5 3.0 %collective-permute-start.3 = (s16[1040,128]{1,0:T(8,128)(2,1)S(1)}, s16[1040,128]{1,0:T(8,128)(2,1)S(1)}, u32[]{:S(2)}, u32[]{:S(2)}) collective-permute-start(s16[1040,128]{1,0:T(8,128)(2,1)S(1)} %get-tuple-element.50.mine_ref), channel_id=1, source_target_pairs={{0,1},{1,0},{2,3},{3,2},{4,5},{5,4},{6,7},{7,6},{8,9},{9,8},{10,11... | collective-permute-start | bytes 798728 | tf_op jit(solution)/shard_map/ppermute | solution.py:483
  9.5 0.7 collective-permute-start.1
  10.4 5.9 %collective-permute-done.3.other_ref = s16[1040,128]{1,0:T(8,128)(2,1)S(1)} collective-permute-done((s16[1040,128]{1,0:T(8,128)(2,1)S(1)}, s16[1040,128]{1,0:T(8,128)(2,1)S(1)}, u32[]{:S(2)}, u32[]{:S(2)}) %collective-permute-start.3) | collective-permute-done | bytes 266272 | tf_op jit(solution)/shard_map/ppermute | solution.py:483
  16.3 6.2 %shard_map.87 = (s16[1040,128]{1,0:T(8,128)(2,1)S(1)}, f32[128,128]{1,0:T(8,128)S(1)}) custom-call(s32[6]{0:T(128)S(1)} %get-tuple-element.49.info_ref, s16[1040,128]{1,0:T(8,128)(2,1)S(1)} %get-tuple-element.50.mine_ref, s16[1040,128]{1,0:T(8,128)(2,1)S(1)} %collective-permute-done.3.other_ref, f32[256,128]{1,0:T(8,128)S(1)} %copy-done.15), custom_call_target="tpu_custom_call" | custom-call | flops 4400000000 | tf_op jit(solution)/shard_map/pallas_call | solution.py:465
  22.5 1.9 %collective-permute-start.4 = (s16[1040,128]{1,0:T(8,128)(2,1)S(1)}, s16[1040,128]{1,0:T(8,128)(2,1)S(1)}, u32[]{:S(2)}, u32[]{:S(2)}) collective-permute-start(s16[1040,128]{1,0:T(8,128)(2,1)S(1)} %get-tuple-element.52.mine_ref), channel_id=1, source_target_pairs={{0,2},{1,3},{2,0},{3,1},{4,6},{5,7},{6,4},{7,5},{8,10},{9,11},{10,... | collective-permute-start | bytes 798728 | tf_op jit(solution)/shard_map/ppermute | solution.py:483
  24.3 8.1 %shard_map.88 = (bf16[6,6,128,768]{3,2,1,0:T(8,128)(2,1)}, f32[128,768]{1,0:T(8,128)S(1)}) custom-call(s32[6,6,6]{2,1,0:T(8,128)S(1)} %copy-done.6, bf16[6,6,6,128,128]{4,3,2,1,0:T(8,128)(2,1)} %near_hbm.7, bf16[6,6,128,128]{3,2,1,0:T(8,128)(2,1)} %right_hbm.7, bf16[6,6,128,768]{3,2,1,0:T(8,128)(2,1)} %refs_0_.7), custom_call_target="tpu_custom_call" | custom-call | flops 8800000000 | tf_op jit(solution)/shard_map/pallas_call | solution.py:136
  32.4 6.5 %shard_map.89 = (s16[1040,128]{1,0:T(8,128)(2,1)S(1)}, f32[128,128]{1,0:T(8,128)S(1)}) custom-call(s32[6]{0:T(128)S(1)} %get-tuple-element.49.info_ref, s16[1040,128]{1,0:T(8,128)(2,1)S(1)} %get-tuple-element.52.mine_ref, s16[1040,128]{1,0:T(8,128)(2,1)S(1)} %collective-permute-done.4.other_ref, f32[256,128]{1,0:T(8,128)S(1)} %copy-done.15, ...), custom_call_target="tpu_custom_call" | custom-call | flops 4400000000 | tf_op jit(solution)/shard_map/pallas_call | solution.py:465
  38.9 2.6 %collective-permute-start.9 = (s16[1040,128]{1,0:T(8,128)(2,1)S(1)}, s16[1040,128]{1,0:T(8,128)(2,1)S(1)}, u32[]{:S(2)}, u32[]{:S(2)}) collective-permute-start(s16[1040,128]{1,0:T(8,128)(2,1)S(1)} %get-tuple-element.63.mine_ref), channel_id=1, source_target_pairs={{0,4},{1,5},{2,6},{3,7},{4,0},{5,1},{6,2},{7,3},{8,12},{9,13},{10,... | collective-permute-start | bytes 798728 | tf_op jit(solution)/shard_map/ppermute | solution.py:483
  41.6 0.7 collective-permute-start.5
  42.3 1.6 %collective-permute-start.8 = (bf16[4,128,768]{2,1,0:T(8,128)(2,1)}, bf16[4,128,768]{2,1,0:T(8,128)(2,1)}, u32[]{:S(2)}, u32[]{:S(2)}) collective-permute-start(bf16[4,128,768]{2,1,0:T(8,128)(2,1)} %get-tuple-element.62), channel_id=1, source_target_pairs={{1,2},{2,1},{3,4},{4,3},{5,6},{6,5},{9,10},{10,9},{11,12},{12,11},... | collective-permute-start | bytes 2359304 | tf_op jit(solution)/shard_map/ppermute | solution.py:491
  43.8 5.6 %shard_map.91 = (bf16[6,6,128,768]{3,2,1,0:T(8,128)(2,1)}, f32[128,768]{1,0:T(8,128)S(1)}) custom-call(s32[6,6,6]{2,1,0:T(8,128)S(1)} %copy-done.6, bf16[6,6,6,128,128]{4,3,2,1,0:T(8,128)(2,1)} %near_hbm.7, bf16[6,6,128,128]{3,2,1,0:T(8,128)(2,1)} %right_hbm.7, bf16[6,6,128,768]{3,2,1,0:T(8,128)(2,1)} %refs_0_.7, ...), custom_call_target="tpu_custom_call", output_to_operand_aliasing={{0}: (6, {})} | custom-call | flops 1650000000 | tf_op jit(solution)/shard_map/pallas_call | solution.py:136
  49.4 2.8 %collective-permute-done.9.other_ref = s16[1040,128]{1,0:T(8,128)(2,1)S(1)} collective-permute-done((s16[1040,128]{1,0:T(8,128)(2,1)S(1)}, s16[1040,128]{1,0:T(8,128)(2,1)S(1)}, u32[]{:S(2)}, u32[]{:S(2)}) %collective-permute-start.9) | collective-permute-done | bytes 266272 | tf_op jit(solution)/shard_map/ppermute | solution.py:483
  52.3 6.8 %shard_map.92 = (s16[1040,128]{1,0:T(8,128)(2,1)}, f32[128,128]{1,0:T(8,128)S(1)}) custom-call(s32[6]{0:T(128)S(1)} %get-tuple-element.49.info_ref, s16[1040,128]{1,0:T(8,128)(2,1)S(1)} %get-tuple-element.63.mine_ref, s16[1040,128]{1,0:T(8,128)(2,1)S(1)} %collective-permute-done.9.other_ref, f32[256,128]{1,0:T(8,128)S(1)} %copy-done.15, ...), custom_call_target="tpu_custom_call" | custom-call | flops 2200000000 | tf_op jit(solution)/shard_map/pallas_call | solution.py:465
  59.1 1.0 shard_map.90
  61.0 0.7 collective-permute-start.7
  61.7 1.0 copy-done.16
  62.7 6.7 %shard_map.93 = (s16[1040,128]{1,0:T(8,128)(2,1)S(1)}, f32[128,128]{1,0:T(8,128)S(1)}) custom-call(s32[6]{0:T(128)S(1)} %get-tuple-element.49.info_ref, s16[1040,128]{1,0:T(8,128)(2,1)} %get-tuple-element.69.mine_ref, s16[1040,128]{1,0:T(8,128)(2,1)} %collective-permute-done.10.other_ref, f32[256,128]{1,0:T(8,128)S(1)} %copy-done.16), custom_call_target="tpu_custom_call" | custom-call | flops 2200000000 | tf_op jit(solution)/shard_map/pallas_call | solution.py:465
  70.1 3.3 %collective-permute-start.11 = (s16[1040,128]{1,0:T(8,128)(2,1)S(1)}, s16[1040,128]{1,0:T(8,128)(2,1)S(1)}, u32[]{:S(2)}, u32[]{:S(2)}) collective-permute-start(s16[1040,128]{1,0:T(8,128)(2,1)S(1)} %get-tuple-element.75.mine_ref), channel_id=1, source_target_pairs={{0,16},{8,24},{16,0},{24,8},{1,17},{9,25},{17,1},{25,9},{2,18},{10... | collective-permute-start | bytes 798728 | tf_op jit(solution)/shard_map/ppermute | solution.py:483
  73.5 7.8 %shard_map.94 = (bf16[6,6,128,768]{3,2,1,0:T(8,128)(2,1)}, f32[128,768]{1,0:T(8,128)S(1)}) custom-call(s32[6,6,6]{2,1,0:T(8,128)S(1)} %copy-done.7, bf16[6,6,6,128,128]{4,3,2,1,0:T(8,128)(2,1)} %near_hbm.7, bf16[6,6,128,128]{3,2,1,0:T(8,128)(2,1)} %right_hbm.7, bf16[6,6,128,768]{3,2,1,0:T(8,128)(2,1)} %refs_0_.7, ...), custom_call_target="tpu_custom_call", output_to_operand_aliasing={{0}: (9, {})} | custom-call | flops 1650000000 | tf_op jit(solution)/shard_map/pallas_call | solution.py:136
  81.4 7.5 %shard_map.95 = (bf16[6,6,128,768]{3,2,1,0:T(8,128)(2,1)}, f32[128,768]{1,0:T(8,128)S(1)}) custom-call(s32[6,6,6]{2,1,0:T(8,128)S(1)} %copy-done.7, bf16[6,6,6,128,128]{4,3,2,1,0:T(8,128)(2,1)} %near_hbm.7, bf16[6,6,128,128]{3,2,1,0:T(8,128)(2,1)} %right_hbm.7, bf16[6,6,128,768]{3,2,1,0:T(8,128)(2,1)} %refs_0_.7, ...), custom_call_target="tpu_custom_call", output_to_operand_aliasing={{0}: (10, {})} | custom-call | flops 1650000000 | tf_op jit(solution)/shard_map/pallas_call | solution.py:136
  89.6 3.7 %collective-permute-start.12 = (f32[4,96,128]{2,1,0:T(8,128)S(1)}, f32[4,96,128]{2,1,0:T(8,128)S(1)}, u32[]{:S(2)}, u32[]{:S(2)}) collective-permute-start(f32[4,96,128]{2,1,0:T(8,128)S(1)} %dynamic-slice_bitcast_fusion), channel_id=1, source_target_pairs={{0,1},{1,0},{2,3},{3,2},{4,5},{5,4},{6,7},{7,6},{8,9},{9,8},{10,11... | collective-permute-start | bytes 589832 | tf_op jit(solution)/shard_map/ppermute | solution.py:483
  93.2 5.1 %collective-permute-done.12 = f32[4,96,128]{2,1,0:T(8,128)S(1)} collective-permute-done((f32[4,96,128]{2,1,0:T(8,128)S(1)}, f32[4,96,128]{2,1,0:T(8,128)S(1)}, u32[]{:S(2)}, u32[]{:S(2)}) %collective-permute-start.12) | collective-permute-done | bytes 196640 | tf_op jit(solution)/shard_map/ppermute | solution.py:483
  98.4 0.8 collective-permute-start.13
  99.1 3.9 %collective-permute-done.13 = f32[2,96,128]{2,1,0:T(8,128)S(1)} collective-permute-done((f32[2,96,128]{2,1,0:T(8,128)S(1)}, f32[2,96,128]{2,1,0:T(8,128)S(1)}, u32[]{:S(2)}, u32[]{:S(2)}) %collective-permute-start.13) | collective-permute-done | bytes 98336 | tf_op jit(solution)/shard_map/ppermute | solution.py:483
  103.1 2.4 %collective-permute-start.14 = (f32[1,96,128]{2,1,0:T(8,128)S(1)}, f32[1,96,128]{2,1,0:T(8,128)S(1)}, u32[]{:S(2)}, u32[]{:S(2)}) collective-permute-start(f32[1,96,128]{2,1,0:T(8,128)S(1)} %constant_dynamic-slice_fusion), channel_id=1, source_target_pairs={{0,4},{1,5},{2,6},{3,7},{4,0},{5,1},{6,2},{7,3},{8,12},{9,13},{10,... | collective-permute-start | bytes 147464 | tf_op jit(solution)/shard_map/ppermute | solution.py:483
  105.5 6.1 %shard_map.96 = (f32[256,128]{1,0:T(8,128)S(1)}, f32[128,128]{1,0:T(8,128)S(1)}) custom-call(s32[6]{0:T(128)S(1)} %get-tuple-element.49.info_ref, s16[1040,128]{1,0:T(8,128)(2,1)S(1)} %copy-done.12, s16[1040,128]{1,0:T(8,128)(2,1)S(1)} %copy-done.14, f32[256,128]{1,0:T(8,128)S(1)} %copy-done.17, f32[128,128]{1,0:T(8,128)S(1)} %copy-done.20), custom_call_target="tpu_custom_call" | custom-call | flops 2200000000 | tf_op jit(solution)/shard_map/pallas_call | solution.py:465
  111.9 1.2 %collective-permute-done.15 = f32[96,128]{1,0:T(8,128)S(1)} collective-permute-done((f32[96,128]{1,0:T(8,128)S(1)}, f32[96,128]{1,0:T(8,128)S(1)}, u32[]{:S(2)}, u32[]{:S(2)}) %collective-permute-start.15) | collective-permute-done | bytes 49184 | tf_op jit(solution)/shard_map/ppermute | solution.py:483
  113.2 1.5 %collective-permute-start.16 = (f32[96,128]{1,0:T(8,128)S(1)}, f32[96,128]{1,0:T(8,128)S(1)}, u32[]{:S(2)}, u32[]{:S(2)}) collective-permute-start(f32[96,128]{1,0:T(8,128)S(1)} %add.60), channel_id=1, source_target_pairs={{0,16},{8,24},{16,0},{24,8},{1,17},{9,25},{17,1},{25,9},{2,18},{10... | collective-permute-start | bytes 147464 | tf_op jit(solution)/shard_map/ppermute | solution.py:483
  114.6 2.7 %collective-permute-done.16 = f32[96,128]{1,0:T(8,128)S(1)} collective-permute-done((f32[96,128]{1,0:T(8,128)S(1)}, f32[96,128]{1,0:T(8,128)S(1)}, u32[]{:S(2)}, u32[]{:S(2)}) %collective-permute-start.16) | collective-permute-done | bytes 49184 | tf_op jit(solution)/shard_map/ppermute | solution.py:483
  117.3 0.9 fusion.6
  (64 shorter events, 3.4 us)
Async XLA Ops:
  2.3 13.9 %copy-start.15 = (f32[256,128]{1,0:T(8,128)S(1)}, f32[256,128]{1,0:T(8,128)}, u32[]{:S(2)}) copy-start(f32[256,128]{1,0:T(8,128)} %sketch_ref.9) | copy-start | bytes 393220
  6.5 9.8 %collective-permute-start.3 = (s16[1040,128]{1,0:T(8,128)(2,1)S(1)}, s16[1040,128]{1,0:T(8,128)(2,1)S(1)}, u32[]{:S(2)}, u32[]{:S(2)}) collective-permute-start(s16[1040,128]{1,0:T(8,128)(2,1)S(1)} %get-tuple-element.50.mine_ref), channel_id=1, source_target_pairs={{0,1},{1,0},{2,3},{3,2},{4,5},{5,4},{6,7},{7,6},{8,9},{9,8},{10,11... | collective-permute-start | bytes 798728 | tf_op jit(solution)/shard_map/ppermute | solution.py:483
  9.5 32.8 %collective-permute-start = (bf16[6,128,768]{2,1,0:T(8,128)(2,1)S(1)}, bf16[6,128,768]{2,1,0:T(8,128)(2,1)S(1)}, u32[]{:S(2)}, u32[]{:S(2)}) collective-permute-start(bf16[6,128,768]{2,1,0:T(8,128)(2,1)S(1)} %get-tuple-element.44), channel_id=1, source_target_pairs={{0,8},{8,0},{16,24},{24,16},{1,9},{9,1},{17,25},{25,17},{2,10},{10... | collective-permute-start | bytes 3538952 | tf_op jit(solution)/shard_map/ppermute | solution.py:491
  9.5 34.4 %collective-permute-start.1 = (bf16[6,128,768]{2,1,0:T(8,128)(2,1)S(1)}, bf16[6,128,768]{2,1,0:T(8,128)(2,1)S(1)}, u32[]{:S(2)}, u32[]{:S(2)}) collective-permute-start(bf16[6,128,768]{2,1,0:T(8,128)(2,1)S(1)} %get-tuple-element.45), channel_id=1, source_target_pairs={{8,16},{16,8},{9,17},{17,9},{10,18},{18,10},{11,19},{19,11},{12,20... | collective-permute-start | bytes 3538952 | tf_op jit(solution)/shard_map/ppermute | solution.py:491
  10.2 48.9 %collective-permute-start.2 = (bf16[6,128,768]{2,1,0:T(8,128)(2,1)S(1)}, bf16[6,128,768]{2,1,0:T(8,128)(2,1)S(1)}, u32[]{:S(2)}, u32[]{:S(2)}) collective-permute-start(bf16[6,128,768]{2,1,0:T(8,128)(2,1)S(1)} %get-tuple-element.46), channel_id=1, source_target_pairs={{0,1},{1,0},{2,3},{3,2},{4,5},{5,4},{6,7},{7,6},{8,9},{9,8},{10,11... | collective-permute-start | bytes 3538952 | tf_op jit(solution)/shard_map/ppermute | solution.py:491
  16.3 8.1 %copy-start.6 = (s32[6,6,6]{2,1,0:T(8,128)S(1)}, s32[6,6,6]{2,1,0:T(8,128)}, u32[]{:S(2)}) copy-start(s32[6,6,6]{2,1,0:T(8,128)} %nb_ref.4) | copy-start | bytes 2596
  22.5 9.9 %collective-permute-start.4 = (s16[1040,128]{1,0:T(8,128)(2,1)S(1)}, s16[1040,128]{1,0:T(8,128)(2,1)S(1)}, u32[]{:S(2)}, u32[]{:S(2)}) collective-permute-start(s16[1040,128]{1,0:T(8,128)(2,1)S(1)} %get-tuple-element.52.mine_ref), channel_id=1, source_target_pairs={{0,2},{1,3},{2,0},{3,1},{4,6},{5,7},{6,4},{7,5},{8,10},{9,11},{10,... | collective-permute-start | bytes 798728 | tf_op jit(solution)/shard_map/ppermute | solution.py:483
  38.9 13.4 %collective-permute-start.9 = (s16[1040,128]{1,0:T(8,128)(2,1)S(1)}, s16[1040,128]{1,0:T(8,128)(2,1)S(1)}, u32[]{:S(2)}, u32[]{:S(2)}) collective-permute-start(s16[1040,128]{1,0:T(8,128)(2,1)S(1)} %get-tuple-element.63.mine_ref), channel_id=1, source_target_pairs={{0,4},{1,5},{2,6},{3,7},{4,0},{5,1},{6,2},{7,3},{8,12},{9,13},{10,... | collective-permute-start | bytes 798728 | tf_op jit(solution)/shard_map/ppermute | solution.py:483
  41.6 17.5 %collective-permute-start.5 = (bf16[2,128,768]{2,1,0:T(8,128)(2,1)S(1)}, bf16[2,128,768]{2,1,0:T(8,128)(2,1)S(1)}, u32[]{:S(2)}, u32[]{:S(2)}) collective-permute-start(bf16[2,128,768]{2,1,0:T(8,128)(2,1)S(1)} %get-tuple-element.59), channel_id=1, source_target_pairs={{1,2},{2,1},{3,4},{4,3},{5,6},{6,5},{9,10},{10,9},{11,12},{12,11},... | collective-permute-start | bytes 1179656 | tf_op jit(solution)/shard_map/ppermute | solution.py:491
  42.3 39.1 %collective-permute-start.8 = (bf16[4,128,768]{2,1,0:T(8,128)(2,1)}, bf16[4,128,768]{2,1,0:T(8,128)(2,1)}, u32[]{:S(2)}, u32[]{:S(2)}) collective-permute-start(bf16[4,128,768]{2,1,0:T(8,128)(2,1)} %get-tuple-element.62), channel_id=1, source_target_pairs={{1,2},{2,1},{3,4},{4,3},{5,6},{6,5},{9,10},{10,9},{11,12},{12,11},... | collective-permute-start | bytes 2359304 | tf_op jit(solution)/shard_map/ppermute | solution.py:491
  49.4 9.6 %copy-start.2 = (f32[128,768]{1,0:T(8,128)}, f32[128,768]{1,0:T(8,128)S(1)}, u32[]{:S(2)}) copy-start(f32[128,768]{1,0:T(8,128)S(1)} %get-tuple-element.81) | copy-start | bytes 1179652
  59.0 1.1 copy-start.8
  59.0 2.7 %collective-permute-start.10 = (s16[1040,128]{1,0:T(8,128)(2,1)}, s16[1040,128]{1,0:T(8,128)(2,1)}, u32[]{:S(2)}, u32[]{:S(2)}) collective-permute-start(s16[1040,128]{1,0:T(8,128)(2,1)} %get-tuple-element.69.mine_ref), channel_id=1, source_target_pairs={{0,8},{8,0},{16,24},{24,16},{1,9},{9,1},{17,25},{25,17},{2,10},{10... | collective-permute-start | bytes 798728 | tf_op jit(solution)/shard_map/ppermute | solution.py:483
  59.1 1.4 %copy-start = (bf16[6,128,768]{2,1,0:T(8,128)(2,1)}, bf16[6,128,768]{2,1,0:T(8,128)(2,1)S(1)}, u32[]{:S(2)}) copy-start(bf16[6,128,768]{2,1,0:T(8,128)(2,1)S(1)} %collective-permute-done.2.beside.refs_5_) | copy-start | bytes 3538948
  60.5 12.9 %collective-permute-start.6 = (bf16[2,128,768]{2,1,0:T(8,128)(2,1)}, bf16[2,128,768]{2,1,0:T(8,128)(2,1)S(1)}, u32[]{:S(2)}, u32[]{:S(2)}) collective-permute-start(bf16[2,128,768]{2,1,0:T(8,128)(2,1)} %get-tuple-element.60), channel_id=1, source_target_pairs={{0,8},{8,0},{16,24},{24,16},{1,9},{9,1},{17,25},{25,17},{2,10},{10... | collective-permute-start | bytes 1179656 | tf_op jit(solution)/shard_map/ppermute | solution.py:491
  61.0 12.4 %collective-permute-start.7 = (bf16[2,128,768]{2,1,0:T(8,128)(2,1)}, bf16[2,128,768]{2,1,0:T(8,128)(2,1)S(1)}, u32[]{:S(2)}, u32[]{:S(2)}) collective-permute-start(bf16[2,128,768]{2,1,0:T(8,128)(2,1)} %get-tuple-element.61), channel_id=1, source_target_pairs={{8,16},{16,8},{9,17},{17,9},{10,18},{18,10},{11,19},{19,11},{12,20... | collective-permute-start | bytes 1179656 | tf_op jit(solution)/shard_map/ppermute | solution.py:491
  61.7 11.7 %copy-start.1 = (bf16[6,128,768]{2,1,0:T(8,128)(2,1)S(1)}, bf16[6,128,768]{2,1,0:T(8,128)(2,1)}, u32[]{:S(2)}) copy-start(bf16[6,128,768]{2,1,0:T(8,128)(2,1)} %copy-done) | copy-start | bytes 3538948
  61.7 11.7 %copy-start.7 = (s32[6,6,6]{2,1,0:T(8,128)S(1)}, s32[6,6,6]{2,1,0:T(8,128)}, u32[]{:S(2)}) copy-start(s32[6,6,6]{2,1,0:T(8,128)} %nb_ref.4) | copy-start | bytes 2596
  70.1 11.2 %copy-start.11 = (s16[1040,128]{1,0:T(8,128)(2,1)}, s16[1040,128]{1,0:T(8,128)(2,1)S(1)}, u32[]{:S(2)}) copy-start(s16[1040,128]{1,0:T(8,128)(2,1)S(1)} %get-tuple-element.75.mine_ref) | copy-start | bytes 798724
  70.1 18.8 %collective-permute-start.11 = (s16[1040,128]{1,0:T(8,128)(2,1)S(1)}, s16[1040,128]{1,0:T(8,128)(2,1)S(1)}, u32[]{:S(2)}, u32[]{:S(2)}) collective-permute-start(s16[1040,128]{1,0:T(8,128)(2,1)S(1)} %get-tuple-element.75.mine_ref), channel_id=1, source_target_pairs={{0,16},{8,24},{16,0},{24,8},{1,17},{9,25},{17,1},{25,9},{2,18},{10... | collective-permute-start | bytes 798728 | tf_op jit(solution)/shard_map/ppermute | solution.py:483
  73.5 7.9 %copy-start.5 = (bf16[2,128,768]{2,1,0:T(8,128)(2,1)S(1)}, bf16[2,128,768]{2,1,0:T(8,128)(2,1)}, u32[]{:S(2)}) copy-start(bf16[2,128,768]{2,1,0:T(8,128)(2,1)} %copy-done.4) | copy-start | bytes 1179652
  81.3 7.5 %copy-start.3 = (f32[128,768]{1,0:T(8,128)S(1)}, f32[128,768]{1,0:T(8,128)}, u32[]{:S(2)}) copy-start(f32[128,768]{1,0:T(8,128)} %copy-done.2) | copy-start | bytes 1179652
  81.4 7.5 %copy-start.9 = (f32[128,128]{1,0:T(8,128)S(1)}, f32[128,128]{1,0:T(8,128)}, u32[]{:S(2)}) copy-start(f32[128,128]{1,0:T(8,128)} %copy-done.8) | copy-start | bytes 196612
  89.4 16.0 %copy-start.12 = (s16[1040,128]{1,0:T(8,128)(2,1)S(1)}, s16[1040,128]{1,0:T(8,128)(2,1)}, u32[]{:S(2)}) copy-start(s16[1040,128]{1,0:T(8,128)(2,1)} %copy-done.11) | copy-start | bytes 798724
  89.4 16.0 %copy-start.17 = (f32[256,128]{1,0:T(8,128)S(1)}, f32[256,128]{1,0:T(8,128)}, u32[]{:S(2)}) copy-start(f32[256,128]{1,0:T(8,128)} %sketch_ref.9) | copy-start | bytes 393220
  89.4 16.0 %copy-start.20 = (f32[128,128]{1,0:T(8,128)S(1)}, f32[128,128]{1,0:T(8,128)}, u32[]{:S(2)}) copy-start(f32[128,128]{1,0:T(8,128)} %copy-done.19) | copy-start | bytes 196612
  89.6 8.8 %collective-permute-start.12 = (f32[4,96,128]{2,1,0:T(8,128)S(1)}, f32[4,96,128]{2,1,0:T(8,128)S(1)}, u32[]{:S(2)}, u32[]{:S(2)}) collective-permute-start(f32[4,96,128]{2,1,0:T(8,128)S(1)} %dynamic-slice_bitcast_fusion), channel_id=1, source_target_pairs={{0,1},{1,0},{2,3},{3,2},{4,5},{5,4},{6,7},{7,6},{8,9},{9,8},{10,11... | collective-permute-start | bytes 589832 | tf_op jit(solution)/shard_map/ppermute | solution.py:483
  93.2 12.2 %copy-start.14 = (s16[1040,128]{1,0:T(8,128)(2,1)S(1)}, s16[1040,128]{1,0:T(8,128)(2,1)}, u32[]{:S(2)}) copy-start(s16[1040,128]{1,0:T(8,128)(2,1)} %copy-done.13) | copy-start | bytes 798724
  98.4 4.7 %collective-permute-start.13 = (f32[2,96,128]{2,1,0:T(8,128)S(1)}, f32[2,96,128]{2,1,0:T(8,128)S(1)}, u32[]{:S(2)}, u32[]{:S(2)}) collective-permute-start(f32[2,96,128]{2,1,0:T(8,128)S(1)} %dynamic-slice_bitcast_fusion.1), channel_id=1, source_target_pairs={{0,2},{1,3},{2,0},{3,1},{4,6},{5,7},{6,4},{7,5},{8,10},{9,11},{10,... | collective-permute-start | bytes 294920 | tf_op jit(solution)/shard_map/ppermute | solution.py:483
  103.1 8.5 %collective-permute-start.14 = (f32[1,96,128]{2,1,0:T(8,128)S(1)}, f32[1,96,128]{2,1,0:T(8,128)S(1)}, u32[]{:S(2)}, u32[]{:S(2)}) collective-permute-start(f32[1,96,128]{2,1,0:T(8,128)S(1)} %constant_dynamic-slice_fusion), channel_id=1, source_target_pairs={{0,4},{1,5},{2,6},{3,7},{4,0},{5,1},{6,2},{7,3},{8,12},{9,13},{10,... | collective-permute-start | bytes 147464 | tf_op jit(solution)/shard_map/ppermute | solution.py:483
  111.9 1.3 %collective-permute-start.15 = (f32[96,128]{1,0:T(8,128)S(1)}, f32[96,128]{1,0:T(8,128)S(1)}, u32[]{:S(2)}, u32[]{:S(2)}) collective-permute-start(f32[96,128]{1,0:T(8,128)S(1)} %fusion.4), channel_id=1, source_target_pairs={{0,8},{8,0},{16,24},{24,16},{1,9},{9,1},{17,25},{25,17},{2,10},{10... | collective-permute-start | bytes 147464 | tf_op jit(solution)/shard_map/ppermute | solution.py:483
  113.2 4.2 %collective-permute-start.16 = (f32[96,128]{1,0:T(8,128)S(1)}, f32[96,128]{1,0:T(8,128)S(1)}, u32[]{:S(2)}, u32[]{:S(2)}) collective-permute-start(f32[96,128]{1,0:T(8,128)S(1)} %add.60), channel_id=1, source_target_pairs={{0,16},{8,24},{16,0},{24,8},{1,17},{9,25},{17,1},{25,9},{2,18},{10... | collective-permute-start | bytes 147464 | tf_op jit(solution)/shard_map/ppermute | solution.py:483
  (6 other events, 5.1 us)

commit v4 on v3

--- a/solution.py
+++ b/solution.py
@@ -32,12 +32,11 @@
 
 
 def near_kernel(plan, n_src, nb_ref, near_hbm, right_hbm, *refs):
-    spans, block_rows, centre_rows, count, first_col, centre_col = plan
+    steps, spans, parts = plan
     srcs = refs[:n_src]
     out_ref, coef_ref, ext_ref, near_ref, right_ref, stage_ref, sems, out_sems = refs[-8:]
-    steps = len(block_rows)
     step = pl.program_id(0)
-    col = first_col()
+    count = len(parts)
 
     def fetch(at_step):
         found = []
@@ -45,19 +44,20 @@
             if needed == at_step:
                 source, target = views(srcs, ext_ref)
                 found.append(pltpu.make_async_copy(source, target, sems.at[index]))
-        base = len(spans) + 2 * at_step
-        for offset, source, target in ((0, near_hbm, near_ref), (1, right_hbm, right_ref)):
-            found.append(
-                pltpu.make_async_copy(
-                    source.at[block_rows[at_step], pl.ds(col, count)], target.at[at_step], sems.at[base + offset]
+        for part, (row, by, col, *_) in enumerate(parts):
+            at = len(spans) + 2 * (at_step * count + part)
+            for offset, source, target in ((0, near_hbm, near_ref), (1, right_hbm, right_ref)):
+                found.append(
+                    pltpu.make_async_copy(
+                        source.at[row + by * at_step, col()], target.at[at_step, part], sems.at[at + offset]
+                    )
                 )
-            )
         return found
 
     def send(place, at_step, part):
-        row = block_rows[0] + at_step * (block_rows[1] - block_rows[0])
+        row, by, col = parts[part][:3]
         return pltpu.make_async_copy(
-            stage_ref.at[place, part], out_ref.at[row, col + part], out_sems.at[place, part]
+            stage_ref.at[place, part], out_ref.at[row + by * at_step, col()], out_sems.at[place, part]
         )
 
     @pl.when(step == 0)
@@ -80,16 +80,14 @@
         for part in range(count):
             send(place, step - 2, part).wait()
 
-    row = block_rows[0] + step * (block_rows[1] - block_rows[0])
-    centre = centre_rows[0] + step * (centre_rows[1] - centre_rows[0])
     rhs = ext_ref.shape[-1]
     tile = 256 if rhs % 256 == 0 else rhs
-    for part in range(count):
-        middle = centre_col + part
+    for part, (row, by, col, ext_row, ext_by, middle) in enumerate(parts):
+        centre = ext_row + ext_by * step
         weights = []
         places = []
         for slot in range(near_ref.shape[2]):
-            link = nb_ref[row, col + part, slot]
+            link = nb_ref[row + by * step, col(), slot]
             there = jnp.minimum(link, empty_slot - 1)
             weight = near_ref[step, part, slot]
             weights.append(jnp.where(link < empty_slot, weight, jnp.zeros_like(weight)))
@@ -121,11 +119,11 @@
 
 
 def near_part(sources, plan, ext_shape, near_blocks, far_right, neighbours, prior, time):
-    spans, block_rows, _, count, _, _ = plan
+    steps, spans, parts = plan
+    count = len(parts)
     gu, gv, slots, size, _ = near_blocks.shape
     rhs = sources[0].shape[-1]
     rank = far_right.shape[-1]
-    steps = len(block_rows)
     args = [near_blocks, far_right, *sources]
     args = [in_hbm(value) if value.ndim > 3 else value for value in args]
     aliases = {}
@@ -147,7 +145,7 @@
                 pltpu.VMEM((steps, count, slots, size, size), jnp.bfloat16),
                 pltpu.VMEM((steps, count, size, rank), jnp.bfloat16),
                 pltpu.VMEM((2, count, size, rhs), jnp.bfloat16),
-                pltpu.SemaphoreType.DMA((len(spans) + 2 * steps,)),
+                pltpu.SemaphoreType.DMA((len(spans) + 2 * steps * count,)),
                 pltpu.SemaphoreType.DMA((2, count)),
             ],
         ),
@@ -174,8 +172,8 @@
 def near_middle(density, near_blocks, far_right, neighbours, prior):
     gu, gv = density.shape[:2]
     spans = [(max(row - 2, 0), row_span(row, row)) for row in range(gu)]
-    rows = list(range(1, gu - 1))
-    plan = (spans, rows, rows, gv - 2, lambda: 1, 1)
+    parts = [(1, 1, lambda col=col: col, 1, 1, col) for col in range(1, gv - 1)]
+    plan = (gu - 2, spans, parts)
     return near_part((density,), plan, (gu, gv), near_blocks, far_right, neighbours, prior, 8)
 
 
@@ -184,32 +182,16 @@
     spans = [(at, row_span(row, ext_row)) for at, row, ext_row in ((0, 0, 1), (0, 1, 2), (1, gu - 2, 3), (1, gu - 1, 4))]
     spans.append((0, lambda srcs, ext: (srcs[1], ext.at[5 * (1 - odd("pu"))])))
     spans.append((0, lambda srcs, ext: (srcs[2], ext.at[5 * odd("pu")])))
-    plan = (spans, [0, gu - 1], [1, 4], gv - 2, lambda: 1, 1)
+    parts = [(0, gu - 1, lambda col=col: col, 1, 3, col) for col in range(1, gv - 1)]
+    plan = (2, spans, parts)
     return near_part((density, pu_near, pu_far), plan, (6, gv), near_blocks, far_right, neighbours, prior, 1.5)
 
 
-def near_column(far, density, pu_near, pu_far, corner_near, corner_far, halo, near_blocks, far_right, neighbours, prior):
+def near_columns(density, pu_near, pu_far, corner_near, corner_far, beside, ends, mids, near_blocks, far_right, neighbours, prior):
     gu, gv = density.shape[:2]
-
-    def left_side():
-        return 1 - odd("pv") if far else odd("pv")
-
+    per_step = 2
     spans = []
-
-    def start_col():
-        return (gv - 2) * (1 - left_side())
-
-    def inner(source, at, ext_row):
-        def views(srcs, ext):
-            view = srcs[source]
-            if at is not None:
-                view = view.at[at]
-            return view.at[pl.ds(start_col(), 2)], ext.at[ext_row(), pl.ds(left_side(), 2)]
-
-        return views
-
-    def outer(source, at, ext_row):
-        return lambda srcs, ext: (srcs[source].at[at], ext.at[ext_row(), 2 * (1 - left_side())])
+    parts = []
 
     def near_row():
         return (gu + 1) * (1 - odd("pu"))
@@ -217,23 +199,43 @@
     def far_row():
         return (gu + 1) * odd("pu")
 
-    for row in range(gu):
-        at = max(row - 1, 0)
-        spans.append((at, inner(0, row, lambda row=row: row + 1)))
-        if len(halo) == 1:
-            spans.append((at, outer(5, row, lambda row=row: row + 1)))
-        elif row in (0, gu - 1):
-            spans.append((at, outer(5, min(row, 1), lambda row=row: row + 1)))
-        else:
-            spans.append((at, outer(6, row - 1, lambda row=row: row + 1)))
-    spans.append((0, inner(1, None, near_row)))
-    spans.append((0, inner(2, None, far_row)))
-    spans.append((0, outer(3, int(far), near_row)))
-    spans.append((0, outer(4, int(far), far_row)))
-    rows = list(range(gu))
-    plan = (spans, rows, [row + 1 for row in rows], 1, lambda: (gv - 1) * (1 - left_side()), 1)
-    sources = (density, pu_near, pu_far, corner_near, corner_far, *halo)
-    return near_part(sources, plan, (gu + 2, 3), near_blocks, far_right, neighbours, prior, 1.5)
+    for far in (0, 1):
+
+        def left_side(far=far):
+            return 1 - odd("pv") if far else odd("pv")
+
+        def inner(source, at, ext_row, far=far, left_side=left_side):
+            def views(srcs, ext):
+                view = srcs[source]
+                if at is not None:
+                    view = view.at[at]
+                from_cols = pl.ds((gv - 2) * (1 - left_side()), 2)
+                return view.at[from_cols], ext.at[ext_row(), pl.ds(3 * far + left_side(), 2)]
+
+            return views
+
+        def outer(source, at, ext_row, far=far, left_side=left_side):
+            return lambda srcs, ext: (srcs[source].at[at], ext.at[ext_row(), 3 * far + 2 * (1 - left_side())])
+
+        for row in range(gu):
+            at = max((row - 1) // per_step, 0)
+            here = lambda row=row: row + 1
+            spans.append((at, inner(0, row, here)))
+            if not far:
+                spans.append((at, outer(5, row, here)))
+            elif row in (0, gu - 1):
+                spans.append((at, outer(6, min(row, 1), here)))
+            else:
+                spans.append((at, outer(7, row - 1, here)))
+        spans.append((0, inner(1, None, near_row)))
+        spans.append((0, inner(2, None, far_row)))
+        spans.append((0, outer(3, far, near_row)))
+        spans.append((0, outer(4, far, far_row)))
+        col = lambda left_side=left_side: (gv - 1) * (1 - left_side())
+        parts += [(row, per_step, col, row + 1, per_step, 3 * far + 1) for row in range(per_step)]
+    plan = (gu // per_step, spans, parts)
+    sources = (density, pu_near, pu_far, corner_near, corner_far, beside, ends, mids)
+    return near_part(sources, plan, (gu + 2, 6), near_blocks, far_right, neighbours, prior, 1.5)
 
 
 def corners_kernel(beside, ends, to_near, to_far):
@@ -337,144 +339,137 @@
             w_e[base + step :, :] -= e_fall[base + step :, :]
 
 
-code_rows = 16
-
-
-def encode(value, out_ref):
-    rows = value.shape[0]
-    top = jnp.max(jnp.abs(value), axis=0, keepdims=True)
+tail_lanes = 128
+
+
+def encode(value, key, out_ref):
+    cols = value.shape[1]
+    top = jnp.max(jnp.abs(value), axis=1, keepdims=True)
     power = jnp.clip(jnp.floor(jnp.log2(32000.0 / jnp.maximum(top, 1e-30))), -60.0, 60.0)
     scaled = jnp.floor(value * jnp.exp2(power) + 0.5)
-    out_ref[:rows, :] = scaled.astype(jnp.int32).astype(jnp.int16)
-    powers = jnp.broadcast_to(power, (code_rows, value.shape[1]))
-    out_ref[rows:, :] = powers.astype(jnp.int32).astype(jnp.int16)
+    out_ref[:, :cols] = scaled.astype(jnp.int32).astype(jnp.int16)
+    lanes = lax.broadcasted_iota(jnp.int32, (value.shape[0], tail_lanes), 1)
+    out_ref[:, cols:] = jnp.where(lanes < tail_lanes // 2, power, key).astype(jnp.int32).astype(jnp.int16)
 
 
 def decode(ref):
-    rows = ref.shape[0] - code_rows
-    power = ref[rows:, :].astype(jnp.int32).astype(jnp.float32)[:1]
-    return ref[:rows, :].astype(jnp.int32).astype(jnp.float32) * jnp.exp2(-power)
-
-
-def first_kernel(counts, order_ref, value_ref, density, code_ref, info_ref, *refs):
-    beside, ends, mids, pu_near, pu_far, sems = refs
-    pu_count, pv_count = counts
-    pu_index = lax.axis_index("pu")
-    pv_index = lax.axis_index("pv")
+    cols = ref.shape[1] - tail_lanes
+    tail = ref[:, cols:].astype(jnp.int32).astype(jnp.float32)
+    value = ref[:, :cols].astype(jnp.int32).astype(jnp.float32) * jnp.exp2(-tail[:, :1])
+    return value, tail[:, tail_lanes - 1 :]
+
+
+def first_kernel(counts, order_hbm, value_hbm, sketch_hbm, density, code_ref, sketch_ref, *refs):
+    beside, ends, mids, pu_near, pu_far, order, value, sketch, sems = refs
     gu, gv = density.shape[:2]
     near_col = (gv - 1) * (1 - odd("pv"))
     far_col = (gv - 1) * odd("pv")
-    pairs = [(density.at[row, near_col], beside.at[row]) for row in range(gu)]
+    pairs = [(value_hbm.at[0, 0], value), (order_hbm, order), (sketch_hbm, sketch)]
+    inputs = len(pairs)
+    pairs += [(density.at[row, near_col], beside.at[row]) for row in range(gu)]
+    pairs.append((density.at[(gu - 1) * (1 - odd("pu"))], pu_near))
+    pairs.append((density.at[(gu - 1) * odd("pu")], pu_far))
     pairs += [(density.at[(gu - 1) * row, far_col], ends.at[row]) for row in range(2)]
     pairs += [(density.at[row + 1, far_col], mids.at[row]) for row in range(gu - 2)]
-    pairs.append((density.at[(gu - 1) * (1 - odd("pu"))], pu_near))
-    pairs.append((density.at[(gu - 1) * odd("pu")], pu_far))
     copies = [
         pltpu.make_async_copy(source, target, sems.at[index])
         for index, (source, target) in enumerate(pairs)
     ]
     for copy in copies:
         copy.start()
-
-    def least(values):
-        return functools.reduce(jnp.minimum, values)
-
-    at = 0
-    width = 1
-    while width < pv_count:
-        start = lax.div(pv_index, width) * width
-        other = start + width - 2 * width * lax.rem(lax.div(pv_index, width), 2)
-        mine = least([order_ref[pu_index * pv_count + start + k] for k in range(width)])
-        theirs = least([order_ref[pu_index * pv_count + other + k] for k in range(width)])
-        info_ref[at] = (mine < theirs).astype(jnp.int32)
-        at += 1
-        width *= 2
-    width = 1
-    while width < pu_count:
-        start = lax.div(pu_index, width) * width
-        other = start + width - 2 * width * lax.rem(lax.div(pu_index, width), 2)
-        mine = least([order_ref[start * pv_count + k] for k in range(width * pv_count)])
-        theirs = least([order_ref[other * pv_count + k] for k in range(width * pv_count)])
-        info_ref[at] = (mine < theirs).astype(jnp.int32)
-        at += 1
-        width *= 2
-    info_ref[at] = pu_index
-    encode(value_ref[0, 0], code_ref)
-    for copy in copies:
+    for copy in copies[:inputs]:
         copy.wait()
-
-
-def first_step(value, density, order, counts, levels):
+    key = order[lax.axis_index("pu") * counts[1] + lax.axis_index("pv")]
+    encode(jnp.transpose(value[...]), key.astype(jnp.float32), code_ref)
+    sketch_ref[...] = jnp.transpose(sketch[...])
+    for copy in copies[inputs:]:
+        copy.wait()
+
+
+def first_step(value, sketch, density, order, counts):
     rows, cols = value.shape[2:]
     gu, gv, size, rhs = density.shape
     blocks = (gu, 2, gu - 2, gv, gv)
     whole = pl.BlockSpec(memory_space=pltpu.VMEM)
-    scalars = pl.BlockSpec(memory_space=pltpu.SMEM)
+    held = pl.BlockSpec(memory_space=pltpu.HBM)
+    args = [in_hbm(array) for array in (order, value, sketch, density)]
     return pl.pallas_call(
         functools.partial(first_kernel, counts),
-        in_specs=[scalars, whole, pl.BlockSpec(memory_space=pltpu.HBM)],
-        out_specs=[whole, scalars] + [whole] * len(blocks),
+        in_specs=[held] * len(args),
+        out_specs=[whole] * (2 + len(blocks)),
         out_shape=[
-            jax.ShapeDtypeStruct((rows + code_rows, cols), jnp.int16),
-            jax.ShapeDtypeStruct((levels + 1,), jnp.int32),
+            jax.ShapeDtypeStruct((cols, rows + tail_lanes), jnp.int16),
+            jax.ShapeDtypeStruct(sketch.shape[::-1], jnp.float32),
         ]
         + [jax.ShapeDtypeStruct((count, size, rhs), density.dtype) for count in blocks],
-        scratch_shapes=[pltpu.SemaphoreType.DMA((2 * gu + 2,))],
+        scratch_shapes=[
+            pltpu.SMEM(order.shape, jnp.int32),
+            pltpu.VMEM((rows, cols), jnp.float32),
+            pltpu.VMEM(sketch.shape, jnp.float32),
+            pltpu.SemaphoreType.DMA((2 * gu + 5,)),
+        ],
         cost_estimate=cost(3),
         compiler_params=pltpu.CompilerParams(vmem_limit_bytes=merge_vmem),
-    )(order, value, in_hbm(density))
-
-
-def merge_kernel(level, has_path, last, info_ref, mine_ref, other_ref, sketch_ref, *refs):
+    )(*args)
+
+
+natural = ((1,), (0,))
+
+
+def merge_kernel(has_path, last, mine_ref, other_ref, sketch_ref, *refs):
     if has_path:
         path_ref, *refs = refs
-    left_ref, new_path_ref, w_k, w_e, y_ref = refs
-    rank = mine_ref.shape[1]
-    lead = info_ref[level] > 0
-    mine = decode(mine_ref)
-    other = decode(other_ref)
-    stacked = jnp.concatenate([jnp.where(lead, mine, other), jnp.where(lead, other, mine)], axis=1)
-    sketched = split_dot(stacked, sketch_ref[...], ((1,), (0,)))
-    w_k[...] = split_dot(sketched, sketched, ((0,), (0,)))
+    left_ref, new_path_ref, w_k, w_e, z_ref = refs
+    rank = mine_ref.shape[0]
+    mine, my_key = decode(mine_ref)
+    other, other_key = decode(other_ref)
+    lead = my_key < other_key
+    z_ref[:rank, :] = jnp.where(lead, mine, other)
+    z_ref[rank:, :] = jnp.where(lead, other, mine)
+    stacked = z_ref[...]
+    sketch = sketch_ref[...]
+    gram = split_dot(stacked, stacked, ((1,), (1,)))
+    reduced = split_dot(sketch, gram, natural)
+    w_k[...] = split_dot(reduced, sketch, ((1,), (1,)))
     rows = lax.broadcasted_iota(jnp.int32, (rank, rank), 0)
     cols = lax.broadcasted_iota(jnp.int32, (rank, rank), 1)
     w_e[...] = jnp.where(rows == cols, 1.0, 0.0)
+    own = jnp.where(lead, reduced[:, :rank], reduced[:, rank:])
+    if has_path:
+        own = split_dot(own, path_ref[...], natural)
     eliminate(w_k, w_e)
     inverse = w_e[...]
+    mixed = split_dot(inverse, sketch, natural)
     if last:
-        y_ref[...] = sketched
-        count = left_ref.shape[0]
-        part = y_ref[pl.ds(pl.multiple_of(info_ref[info_ref.shape[0] - 1] * count, 8), count), :]
-        left_ref[...] = split_dot(part, inverse, ((1,), (1,)))
+        count = left_ref.shape[1]
+        part = z_ref[:, pl.ds(pl.multiple_of(lax.axis_index("pu") * count, 128), count)]
+        left_ref[...] = split_dot(mixed, part, natural)
     else:
-        encode(split_dot(sketched, inverse, ((1,), (1,))), left_ref)
-    own = split_dot(sketched, mine, ((0,), (0,)))
-    if has_path:
-        own = split_dot(own, path_ref[...], ((1,), (0,)))
-    new_path_ref[...] = split_dot(inverse, own, ((1,), (0,)))
-
-
-def merge(level, info, mine, other, sketch, path, last_rows):
-    rows, rank = mine.shape
+        encode(split_dot(mixed, z_ref[...], natural), jnp.minimum(my_key, other_key), left_ref)
+    new_path_ref[...] = split_dot(inverse, own, natural)
+
+
+def merge(level, mine, other, sketch, path, last_rows):
+    rank, cols = mine.shape
     whole = pl.BlockSpec(memory_space=pltpu.VMEM)
     paths = () if path is None else (path,)
     if last_rows:
-        left = jax.ShapeDtypeStruct((last_rows, rank), jnp.float32)
+        left = jax.ShapeDtypeStruct((rank, last_rows), jnp.float32)
     else:
         left = jax.ShapeDtypeStruct(mine.shape, jnp.int16)
     return pl.pallas_call(
-        functools.partial(merge_kernel, level, bool(paths), bool(last_rows)),
-        in_specs=[pl.BlockSpec(memory_space=pltpu.SMEM), whole, whole, whole] + [whole] * len(paths),
+        functools.partial(merge_kernel, bool(paths), bool(last_rows)),
+        in_specs=[whole, whole, whole] + [whole] * len(paths),
         out_specs=[whole, whole],
         out_shape=[left, jax.ShapeDtypeStruct((rank, rank), jnp.float32)],
         scratch_shapes=[
             pltpu.VMEM((rank, rank), jnp.float32),
             pltpu.VMEM((rank, rank), jnp.float32),
-            pltpu.VMEM((rows - code_rows, rank), jnp.float32),
+            pltpu.VMEM((2 * rank, cols - tail_lanes), jnp.float32),
         ],
         cost_estimate=cost(4 if level < 2 else 2),
         compiler_params=pltpu.CompilerParams(vmem_limit_bytes=merge_vmem),
-    )(info, mine, other, sketch, *paths)
+    )(mine, other, sketch, *paths)
 
 
 def from_partner(value, axis, distance):
@@ -509,9 +504,16 @@
             return from_partner(value, "pv", level)
         return from_partner(value, "pu", level - pv_levels)
 
+    def scattered(share, level):
+        bit = (pv_index >> level) & 1
+        pairs = share.reshape(share.shape[0] // 2, 2, *share.shape[1:])
+        keep = lax.dynamic_index_in_dim(pairs, bit, 1, keepdims=False)
+        give = lax.dynamic_index_in_dim(pairs, 1 - bit, 1, keepdims=False)
+        return keep + from_partner(give, "pv", level)
+
     rows = far_left.shape[2]
-    left, info, beside, ends, mids, pu_near, pu_far = first_step(
-        far_left, density, patch_order, (pu_count, pv_count), levels
+    left, sketch, beside, ends, mids, pu_near, pu_far = first_step(
+        far_left, sketch, density, patch_order, (pu_count, pv_count)
     )
     other = partner(left, 0)
     beside = swapped(beside, "pv", False)
@@ -519,13 +521,14 @@
     pu_far = swapped(pu_far, "pu", True)
 
     coefs = []
-    corrected = None
+    corrected = share = None
     pv_path = pu_path = None
     for level in range(levels):
+        last = level == levels - 1
         coef = None
         if level:
             other = partner(left, level)
-        if level in (1, 2, levels - 1):
+        if level in (1, 2) or last:
             links, left = tied(neighbours, left)
         if level == 1:
             corrected, coef = near_middle(density, near_blocks, far_right, links, corrected)
@@ -534,39 +537,48 @@
             ends = swapped(ends, "pv", True)
             mids = swapped(mids, "pv", True)
             corrected, coef = near_rows(density, pu_near, pu_far, near_blocks, far_right, links, corrected)
-        elif level == levels - 1:
+        elif last:
             corner_near, corner_far = patch_corners(beside, ends)
             corner_near = swapped(corner_near, "pu", False)
             corner_far = swapped(corner_far, "pu", True)
-            halo = (density, pu_near, pu_far, corner_near, corner_far)
-            corrected, coef = near_column(False, *halo, (beside,), near_blocks, far_right, links, corrected)
+            corrected, coef = near_columns(
+                density,
+                pu_near,
+                pu_far,
+                corner_near,
+                corner_far,
+                beside,
+                ends,
+                mids,
+                near_blocks,
+                far_right,
+                links,
+                corrected,
+            )
         if coef is not None:
             other, coef = tied(other, coef)
             coefs.append(coef)
+        if last:
+            coef = functools.reduce(lambda a, b: a + b, coefs)
+            share = lax.dot_general(coef, pv_path, (((0,), (1,)), ((), ())), precision=high)
+            share = share.reshape(pv_count, rhs // pv_count, -1)
+            share, other = tied(share, other)
+            share = scattered(share, 0)
         path = pv_path if level < pv_levels else pu_path
-        last_rows = rows // pu_count if level == levels - 1 else 0
-        left, path = merge(level, info, left, other, sketch, path, last_rows)
+        last_rows = rows // pu_count if last else 0
+        left, path = merge(level, left, other, sketch, path, last_rows)
         if level < pv_levels:
             pv_path = path
         else:
             pu_path = path
 
-    corrected, coef = near_column(True, *halo, (ends, mids), near_blocks, far_right, neighbours, corrected)
-    coefs.append(coef)
-
-    coef = functools.reduce(lambda a, b: a + b, coefs)
-    share = lax.dot_general(coef, pv_path, (((0,), (1,)), ((), ())), precision=high)
-    share = share.reshape(pv_count, rhs // pv_count, -1)
-    for level in range(pv_levels):
-        bit = (pv_index >> level) & 1
-        pairs = share.reshape(share.shape[0] // 2, 2, *share.shape[1:])
-        keep = lax.dynamic_index_in_dim(pairs, bit, 1, keepdims=False)
-        give = lax.dynamic_index_in_dim(pairs, 1 - bit, 1, keepdims=False)
-        share = keep + from_partner(give, "pv", level)
+    share, left = tied(share, left)
+    for level in range(1, pv_levels):
+        share = scattered(share, level)
     root_coef = lax.dot_general(share[0], pu_path, (((1,), (1,)), ((), ())), precision=high)
     for level in range(pu_levels):
         root_coef = root_coef + from_partner(root_coef, "pu", level)
-    far_field = lax.dot_general(left, root_coef, (((1,), (1,)), ((), ())), precision=high)
+    far_field = lax.dot_general(left, root_coef, (((0,), (1,)), ((), ())), precision=high)
     return (corrected, far_field)
 
 

time: 118 us -> 111 us (0.941)
  Pallas kernels: 66.5 us -> 57.8 us
  starting transfers between devices: 23.5 us -> 28.4 us
  waiting for transfers between devices: 21.7 us -> 19.2 us
  local copies, waits for them, and re-layouts: 3.91 us -> 2.45 us
    pallas_call x4 -> x3, Pallas kernels: 29 us -> 22.6 us  [near_part(): pl.pallas_call(functools.partial(near_kernel, plan, len(sources)), grid_s...]
    ppermute x10, starting transfers between devices: 19.2 us -> 23.3 us  [from_partner(): return lax.ppermute(value, axis, pairs)]
    ppermute x10, waiting for transfers between devices: 21.7 us -> 19.2 us  [from_partner(): return lax.ppermute(value, axis, pairs)]
    pallas_call x6, Pallas kernels: 36.4 us -> 34.1 us  [the longest x5 30.6 us: merge(): pl.pallas_call(functools.partial(merge_kernel, bool(paths), bool(last_row...]
    unnamed x42 -> x28, local copies, waits for them, and re-layouts: 3.85 us -> 2.4 us
  transfers between devices with their start and end apart: 17 -> 17, of which waited for: 6 -> 6; matrix products, arithmetic and copies ran while one was open for 0% -> 0% of each run, Pallas kernels for 53% -> 49%
where the time goes in v4:
time: 111 us; the launch traced here: 110 us
  Pallas kernels  57.8 us (52%)
  starting transfers between devices  28.4 us (26%)
  waiting for transfers between devices  19.2 us (17%)
  local copies, waits for them, and re-layouts  2.45 us (2%)
  matrix products  1.54 us (1%)
    pallas_call x5, Pallas kernels, merge(): pl.pallas_call(functools.partial(merge_kernel, bool(paths), bool(last_row...  30.6 us
    ppermute x10, starting transfers between devices, from_partner(): return lax.ppermute(value, axis, pairs)  23.3 us
    pallas_call x3, Pallas kernels, near_part(): pl.pallas_call(functools.partial(near_kernel, plan, len(sources)), grid_s...  22.6 us
    ppermute x10, waiting for transfers between devices, from_partner(): return lax.ppermute(value, axis, pairs)  19.2 us
    ppermute x7, starting transfers between devices, swapped(): return lax.ppermute(value, axis, pairs)  5.04 us
    pallas_call x1, Pallas kernels, first_step(): pl.pallas_call(functools.partial(first_kernel, counts), in_specs=[held] *...  3.53 us
    unnamed x28, local copies, waits for them, and re-layouts  2.4 us
  transfers between devices with their start and end apart: 17, of which 6 were waited for; matrix products, arithmetic and copies ran while one was open for 0% of the time, Pallas kernels for 49%

profile of v4, /device:TPU:0, one launch (start us, length us, event | category | flops | bytes accessed | tf_op | source)
XLA Modules:
  0.0 110.4 jit_solution(17071607286798294142)
XLA Ops:
  0.6 3.5 %shard_map.86 = (s16[128,1152]{1,0:T(8,128)(2,1)S(1)}, f32[128,256]{1,0:T(8,128)S(1)}, bf16[6,128,768]{2,1,0:T(8,128)(2,1)S(1)}, bf16[2,128,768]{2,1,0:T(8,128)(...) custom-call(s32[32]{0:T(128)} %order_hbm.1, ...), custom_call_target="tpu_custom_call" | custom-call | flops 3300000000 | tf_op jit(solution)/shard_map/pallas_call | solution.py:396
  4.2 3.0 %collective-permute-start = (s16[128,1152]{1,0:T(8,128)(2,1)S(1)}, s16[128,1152]{1,0:T(8,128)(2,1)S(1)}, u32[]{:S(2)}, u32[]{:S(2)}) collective-permute-start(s16[128,1152]{1,0:T(8,128)(2,1)S(1)} %get-tuple-element.48.mine_ref), channel_id=1, source_target_pairs={{0,1},{1,0},{2,3},{3,2},{4,5},{5,4},{6,7},{7,6},{8,9},{9,8},{10,11... | collective-permute-start | bytes 884744 | tf_op jit(solution)/shard_map/ppermute | solution.py:478
  7.2 0.7 collective-permute-start.4
  8.1 6.8 %collective-permute-done.other_ref = s16[128,1152]{1,0:T(8,128)(2,1)S(1)} collective-permute-done((s16[128,1152]{1,0:T(8,128)(2,1)S(1)}, s16[128,1152]{1,0:T(8,128)(2,1)S(1)}, u32[]{:S(2)}, u32[]{:S(2)}) %collective-permute-start) | collective-permute-done | bytes 294944 | tf_op jit(solution)/shard_map/ppermute | solution.py:478
  14.9 5.8 %shard_map.87 = (s16[128,1152]{1,0:T(8,128)(2,1)S(1)}, f32[128,128]{1,0:T(8,128)S(1)}) custom-call(s16[128,1152]{1,0:T(8,128)(2,1)S(1)} %get-tuple-element.48.mine_ref, s16[128,1152]{1,0:T(8,128)(2,1)S(1)} %collective-permute-done.other_ref, f32[128,256]{1,0:T(8,128)S(1)} %get-tuple-element.49.sketch_ref), custom_call_target="tpu_custom_call" | custom-call | flops 4400000000 | tf_op jit(solution)/shard_map/pallas_call | solution.py:460
  20.8 2.1 %collective-permute-start.1 = (s16[128,1152]{1,0:T(8,128)(2,1)S(1)}, s16[128,1152]{1,0:T(8,128)(2,1)S(1)}, u32[]{:S(2)}, u32[]{:S(2)}) collective-permute-start(s16[128,1152]{1,0:T(8,128)(2,1)S(1)} %get-tuple-element.51.mine_ref), channel_id=1, source_target_pairs={{0,2},{1,3},{2,0},{3,1},{4,6},{5,7},{6,4},{7,5},{8,10},{9,11},{10,... | collective-permute-start | bytes 884744 | tf_op jit(solution)/shard_map/ppermute | solution.py:478
  22.9 8.3 %shard_map.88 = (bf16[6,6,128,768]{3,2,1,0:T(8,128)(2,1)}, f32[128,768]{1,0:T(8,128)S(1)}) custom-call(s32[6,6,6]{2,1,0:T(8,128)S(1)} %copy-done.6, bf16[6,6,6,128,128]{4,3,2,1,0:T(8,128)(2,1)} %near_hbm.5, bf16[6,6,128,128]{3,2,1,0:T(8,128)(2,1)} %right_hbm.5, bf16[6,6,128,768]{3,2,1,0:T(8,128)(2,1)} %refs_0_.5), custom_call_target="tpu_custom_call" | custom-call | flops 8800000000 | tf_op jit(solution)/shard_map/pallas_call | solution.py:134
  31.2 5.9 %shard_map.89 = (s16[128,1152]{1,0:T(8,128)(2,1)S(1)}, f32[128,128]{1,0:T(8,128)S(1)}) custom-call(s16[128,1152]{1,0:T(8,128)(2,1)S(1)} %get-tuple-element.51.mine_ref, s16[128,1152]{1,0:T(8,128)(2,1)S(1)} %collective-permute-done.1.other_ref, f32[128,256]{1,0:T(8,128)S(1)} %get-tuple-element.49.sketch_ref, f32[128,128]{1,0:T(8,128)S(1)} %get-tuple-element.55.refs_0_), custom_call_target="tpu_custom_call" | custom-call | flops 4400000000 | tf_op jit(solution)/shard_map/pallas_call | solution.py:460
  37.1 2.6 %collective-permute-start.2 = (s16[128,1152]{1,0:T(8,128)(2,1)S(1)}, s16[128,1152]{1,0:T(8,128)(2,1)S(1)}, u32[]{:S(2)}, u32[]{:S(2)}) collective-permute-start(s16[128,1152]{1,0:T(8,128)(2,1)S(1)} %get-tuple-element.58.mine_ref), channel_id=1, source_target_pairs={{0,4},{1,5},{2,6},{3,7},{4,0},{5,1},{6,2},{7,3},{8,12},{9,13},{10,... | collective-permute-start | bytes 884744 | tf_op jit(solution)/shard_map/ppermute | solution.py:478
  39.8 0.7 collective-permute-start.7
  40.5 1.6 %collective-permute-start.10 = (bf16[4,128,768]{2,1,0:T(8,128)(2,1)}, bf16[4,128,768]{2,1,0:T(8,128)(2,1)}, u32[]{:S(2)}, u32[]{:S(2)}) collective-permute-start(bf16[4,128,768]{2,1,0:T(8,128)(2,1)} %get-tuple-element.73), channel_id=1, source_target_pairs={{1,2},{2,1},{3,4},{4,3},{5,6},{6,5},{9,10},{10,9},{11,12},{12,11},... | collective-permute-start | bytes 2359304 | tf_op jit(solution)/shard_map/ppermute | solution.py:486
  42.0 5.7 %shard_map.90 = (bf16[6,6,128,768]{3,2,1,0:T(8,128)(2,1)}, f32[128,768]{1,0:T(8,128)S(1)}) custom-call(s32[6,6,6]{2,1,0:T(8,128)S(1)} %copy-done.6, bf16[6,6,6,128,128]{4,3,2,1,0:T(8,128)(2,1)} %near_hbm.5, bf16[6,6,128,128]{3,2,1,0:T(8,128)(2,1)} %right_hbm.5, bf16[6,6,128,768]{3,2,1,0:T(8,128)(2,1)} %refs_0_.5, ...), custom_call_target="tpu_custom_call", output_to_operand_aliasing={{0}: (6, {})} | custom-call | flops 1650000000 | tf_op jit(solution)/shard_map/pallas_call | solution.py:134
  47.8 3.3 %collective-permute-done.2.other_ref = s16[128,1152]{1,0:T(8,128)(2,1)S(1)} collective-permute-done((s16[128,1152]{1,0:T(8,128)(2,1)S(1)}, s16[128,1152]{1,0:T(8,128)(2,1)S(1)}, u32[]{:S(2)}, u32[]{:S(2)}) %collective-permute-start.2) | collective-permute-done | bytes 294944 | tf_op jit(solution)/shard_map/ppermute | solution.py:478
  51.1 5.9 %shard_map.91 = (s16[128,1152]{1,0:T(8,128)(2,1)S(1)}, f32[128,128]{1,0:T(8,128)S(1)}) custom-call(s16[128,1152]{1,0:T(8,128)(2,1)S(1)} %get-tuple-element.58.mine_ref, s16[128,1152]{1,0:T(8,128)(2,1)S(1)} %collective-permute-done.2.other_ref, f32[128,256]{1,0:T(8,128)S(1)} %get-tuple-element.49.sketch_ref, f32[128,128]{1,0:T(8,128)S(1)} %get-tuple-element.65.refs_0_), custom_call_target="tpu_custom_call" | custom-call | flops 2200000000 | tf_op jit(solution)/shard_map/pallas_call | solution.py:460
  57.1 1.0 shard_map.93
  58.6 1.4 %collective-permute-start.9 = (bf16[2,128,768]{2,1,0:T(8,128)(2,1)}, bf16[2,128,768]{2,1,0:T(8,128)(2,1)}, u32[]{:S(2)}, u32[]{:S(2)}) collective-permute-start(bf16[2,128,768]{2,1,0:T(8,128)(2,1)} %get-tuple-element.72), channel_id=1, source_target_pairs={{8,16},{16,8},{9,17},{17,9},{10,18},{18,10},{11,19},{19,11},{12,20... | collective-permute-start | bytes 1179656 | tf_op jit(solution)/shard_map/ppermute | solution.py:486
  60.1 6.6 %shard_map.92 = (s16[128,1152]{1,0:T(8,128)(2,1)}, f32[128,128]{1,0:T(8,128)S(1)}) custom-call(s16[128,1152]{1,0:T(8,128)(2,1)S(1)} %get-tuple-element.66.mine_ref, s16[128,1152]{1,0:T(8,128)(2,1)S(1)} %collective-permute-done.5.other_ref, f32[128,256]{1,0:T(8,128)S(1)} %get-tuple-element.49.sketch_ref), custom_call_target="tpu_custom_call" | custom-call | flops 2200000000 | tf_op jit(solution)/shard_map/pallas_call | solution.py:460
  66.6 0.6 copy-done.12
  67.3 2.2 %collective-permute-start.11 = (s16[128,1152]{1,0:T(8,128)(2,1)}, s16[128,1152]{1,0:T(8,128)(2,1)}, u32[]{:S(2)}, u32[]{:S(2)}) collective-permute-start(s16[128,1152]{1,0:T(8,128)(2,1)} %get-tuple-element.83.mine_ref), channel_id=1, source_target_pairs={{0,16},{8,24},{16,0},{24,8},{1,17},{9,25},{17,1},{25,9},{2,18},{10... | collective-permute-start | bytes 884744 | tf_op jit(solution)/shard_map/ppermute | solution.py:478
  69.4 1.0 copy-done.5
  70.4 0.7 copy-done.7
  71.2 8.6 %shard_map.94 = (bf16[6,6,128,768]{3,2,1,0:T(8,128)(2,1)}, f32[128,768]{1,0:T(8,128)S(1)}) custom-call(s32[6,6,6]{2,1,0:T(8,128)S(1)} %copy-done.7, bf16[6,6,6,128,128]{4,3,2,1,0:T(8,128)(2,1)} %near_hbm.5, bf16[6,6,128,128]{3,2,1,0:T(8,128)(2,1)} %right_hbm.5, bf16[6,6,128,768]{3,2,1,0:T(8,128)(2,1)} %refs_0_.5, ...), custom_call_target="tpu_custom_call", output_to_operand_aliasing={{0}: (11, {})} | custom-call | flops 1650000000 | tf_op jit(solution)/shard_map/pallas_call | solution.py:134
  80.4 6.3 %collective-permute-start.12 = (f32[4,96,128]{2,1,0:T(8,128)S(1)}, f32[4,96,128]{2,1,0:T(8,128)S(1)}, u32[]{:S(2)}, u32[]{:S(2)}) collective-permute-start(f32[4,96,128]{2,1,0:T(8,128)S(1)} %dynamic-slice_bitcast_fusion), channel_id=1, source_target_pairs={{0,1},{1,0},{2,3},{3,2},{4,5},{5,4},{6,7},{7,6},{8,9},{9,8},{10,11... | collective-permute-start | bytes 589832 | tf_op jit(solution)/shard_map/ppermute | solution.py:478
  86.6 6.5 %shard_map.95 = (f32[128,256]{1,0:T(8,128)S(1)}, f32[128,128]{1,0:T(8,128)S(1)}) custom-call(s16[128,1152]{1,0:T(8,128)(2,1)} %get-tuple-element.83.mine_ref, s16[128,1152]{1,0:T(8,128)(2,1)} %collective-permute-done.11.other_ref, f32[128,256]{1,0:T(8,128)S(1)} %copy-done.11, f32[128,128]{1,0:T(8,128)S(1)} %copy-done.13), custom_call_target="tpu_custom_call" | custom-call | flops 2200000000 | tf_op jit(solution)/shard_map/pallas_call | solution.py:460
  93.2 2.9 %collective-permute-start.13 = (f32[2,96,128]{2,1,0:T(8,128)S(1)}, f32[2,96,128]{2,1,0:T(8,128)S(1)}, u32[]{:S(2)}, u32[]{:S(2)}) collective-permute-start(f32[2,96,128]{2,1,0:T(8,128)S(1)} %dynamic-slice_bitcast_fusion.1), channel_id=1, source_target_pairs={{0,2},{1,3},{2,0},{3,1},{4,6},{5,7},{6,4},{7,5},{8,10},{9,11},{10,... | collective-permute-start | bytes 294920 | tf_op jit(solution)/shard_map/ppermute | solution.py:478
  96.1 2.7 %collective-permute-done.13 = f32[2,96,128]{2,1,0:T(8,128)S(1)} collective-permute-done((f32[2,96,128]{2,1,0:T(8,128)S(1)}, f32[2,96,128]{2,1,0:T(8,128)S(1)}, u32[]{:S(2)}, u32[]{:S(2)}) %collective-permute-start.13) | collective-permute-done | bytes 98336 | tf_op jit(solution)/shard_map/ppermute | solution.py:478
  98.8 2.7 %collective-permute-start.14 = (f32[1,96,128]{2,1,0:T(8,128)S(1)}, f32[1,96,128]{2,1,0:T(8,128)S(1)}, u32[]{:S(2)}, u32[]{:S(2)}) collective-permute-start(f32[1,96,128]{2,1,0:T(8,128)S(1)} %constant_dynamic-slice_fusion), channel_id=1, source_target_pairs={{0,4},{1,5},{2,6},{3,7},{4,0},{5,1},{6,2},{7,3},{8,12},{9,13},{10,... | collective-permute-start | bytes 147464 | tf_op jit(solution)/shard_map/ppermute | solution.py:478
  101.5 2.4 %collective-permute-done.14 = f32[1,96,128]{2,1,0:T(8,128)S(1)} collective-permute-done((f32[1,96,128]{2,1,0:T(8,128)S(1)}, f32[1,96,128]{2,1,0:T(8,128)S(1)}, u32[]{:S(2)}, u32[]{:S(2)}) %collective-permute-start.14) | collective-permute-done | bytes 49184 | tf_op jit(solution)/shard_map/ppermute | solution.py:478
  104.2 1.2 %collective-permute-done.15 = f32[96,128]{1,0:T(8,128)S(1)} collective-permute-done((f32[96,128]{1,0:T(8,128)S(1)}, f32[96,128]{1,0:T(8,128)S(1)}, u32[]{:S(2)}, u32[]{:S(2)}) %collective-permute-start.15) | collective-permute-done | bytes 49184 | tf_op jit(solution)/shard_map/ppermute | solution.py:478
  105.4 1.4 %collective-permute-start.16 = (f32[96,128]{1,0:T(8,128)S(1)}, f32[96,128]{1,0:T(8,128)S(1)}, u32[]{:S(2)}, u32[]{:S(2)}) collective-permute-start(f32[96,128]{1,0:T(8,128)S(1)} %add.56), channel_id=1, source_target_pairs={{0,16},{8,24},{16,0},{24,8},{1,17},{9,25},{17,1},{25,9},{2,18},{10... | collective-permute-start | bytes 147464 | tf_op jit(solution)/shard_map/ppermute | solution.py:478
  106.8 2.8 %collective-permute-done.16 = f32[96,128]{1,0:T(8,128)S(1)} collective-permute-done((f32[96,128]{1,0:T(8,128)S(1)}, f32[96,128]{1,0:T(8,128)S(1)}, u32[]{:S(2)}, u32[]{:S(2)}) %collective-permute-start.16) | collective-permute-done | bytes 49184 | tf_op jit(solution)/shard_map/ppermute | solution.py:478
  109.5 0.8 fusion.5
  (49 shorter events, 1.7 us)
Async XLA Ops:
  4.2 55.9 %copy-start.10 = (f32[128,256]{1,0:T(8,128)}, f32[128,256]{1,0:T(8,128)S(1)}, u32[]{:S(2)}) copy-start(f32[128,256]{1,0:T(8,128)S(1)} %get-tuple-element.49.sketch_ref) | copy-start | bytes 393220
  4.2 10.8 %collective-permute-start = (s16[128,1152]{1,0:T(8,128)(2,1)S(1)}, s16[128,1152]{1,0:T(8,128)(2,1)S(1)}, u32[]{:S(2)}, u32[]{:S(2)}) collective-permute-start(s16[128,1152]{1,0:T(8,128)(2,1)S(1)} %get-tuple-element.48.mine_ref), channel_id=1, source_target_pairs={{0,1},{1,0},{2,3},{3,2},{4,5},{5,4},{6,7},{7,6},{8,9},{9,8},{10,11... | collective-permute-start | bytes 884744 | tf_op jit(solution)/shard_map/ppermute | solution.py:478
  7.2 33.3 %collective-permute-start.3 = (bf16[6,128,768]{2,1,0:T(8,128)(2,1)S(1)}, bf16[6,128,768]{2,1,0:T(8,128)(2,1)S(1)}, u32[]{:S(2)}, u32[]{:S(2)}) collective-permute-start(bf16[6,128,768]{2,1,0:T(8,128)(2,1)S(1)} %get-tuple-element.60), channel_id=1, source_target_pairs={{0,8},{8,0},{16,24},{24,16},{1,9},{9,1},{17,25},{25,17},{2,10},{10... | collective-permute-start | bytes 3538952 | tf_op jit(solution)/shard_map/ppermute | solution.py:486
  7.2 34.8 %collective-permute-start.4 = (bf16[6,128,768]{2,1,0:T(8,128)(2,1)S(1)}, bf16[6,128,768]{2,1,0:T(8,128)(2,1)S(1)}, u32[]{:S(2)}, u32[]{:S(2)}) collective-permute-start(bf16[6,128,768]{2,1,0:T(8,128)(2,1)S(1)} %get-tuple-element.61), channel_id=1, source_target_pairs={{8,16},{16,8},{9,17},{17,9},{10,18},{18,10},{11,19},{19,11},{12,20... | collective-permute-start | bytes 3538952 | tf_op jit(solution)/shard_map/ppermute | solution.py:486
  7.9 49.2 %collective-permute-start.6 = (bf16[6,128,768]{2,1,0:T(8,128)(2,1)S(1)}, bf16[6,128,768]{2,1,0:T(8,128)(2,1)S(1)}, u32[]{:S(2)}, u32[]{:S(2)}) collective-permute-start(bf16[6,128,768]{2,1,0:T(8,128)(2,1)S(1)} %get-tuple-element.69), channel_id=1, source_target_pairs={{0,1},{1,0},{2,3},{3,2},{4,5},{5,4},{6,7},{7,6},{8,9},{9,8},{10,11... | collective-permute-start | bytes 3538952 | tf_op jit(solution)/shard_map/ppermute | solution.py:486
  14.9 8.0 %copy-start.6 = (s32[6,6,6]{2,1,0:T(8,128)S(1)}, s32[6,6,6]{2,1,0:T(8,128)}, u32[]{:S(2)}) copy-start(s32[6,6,6]{2,1,0:T(8,128)} %nb_ref.2) | copy-start | bytes 2596
  20.8 10.5 %collective-permute-start.1 = (s16[128,1152]{1,0:T(8,128)(2,1)S(1)}, s16[128,1152]{1,0:T(8,128)(2,1)S(1)}, u32[]{:S(2)}, u32[]{:S(2)}) collective-permute-start(s16[128,1152]{1,0:T(8,128)(2,1)S(1)} %get-tuple-element.51.mine_ref), channel_id=1, source_target_pairs={{0,2},{1,3},{2,0},{3,1},{4,6},{5,7},{6,4},{7,5},{8,10},{9,11},{10,... | collective-permute-start | bytes 884744 | tf_op jit(solution)/shard_map/ppermute | solution.py:478
  31.2 5.9 %copy-start = (f32[128,768]{1,0:T(8,128)}, f32[128,768]{1,0:T(8,128)S(1)}, u32[]{:S(2)}) copy-start(f32[128,768]{1,0:T(8,128)S(1)} %get-tuple-element.76) | copy-start | bytes 1179652
  37.1 14.0 %collective-permute-start.2 = (s16[128,1152]{1,0:T(8,128)(2,1)S(1)}, s16[128,1152]{1,0:T(8,128)(2,1)S(1)}, u32[]{:S(2)}, u32[]{:S(2)}) collective-permute-start(s16[128,1152]{1,0:T(8,128)(2,1)S(1)} %get-tuple-element.58.mine_ref), channel_id=1, source_target_pairs={{0,4},{1,5},{2,6},{3,7},{4,0},{5,1},{6,2},{7,3},{8,12},{9,13},{10,... | collective-permute-start | bytes 884744 | tf_op jit(solution)/shard_map/ppermute | solution.py:478
  39.8 17.3 %collective-permute-start.7 = (bf16[2,128,768]{2,1,0:T(8,128)(2,1)S(1)}, bf16[2,128,768]{2,1,0:T(8,128)(2,1)S(1)}, u32[]{:S(2)}, u32[]{:S(2)}) collective-permute-start(bf16[2,128,768]{2,1,0:T(8,128)(2,1)S(1)} %get-tuple-element.70), channel_id=1, source_target_pairs={{1,2},{2,1},{3,4},{4,3},{5,6},{6,5},{9,10},{10,9},{11,12},{12,11},... | collective-permute-start | bytes 1179656 | tf_op jit(solution)/shard_map/ppermute | solution.py:486
  40.5 28.9 %collective-permute-start.10 = (bf16[4,128,768]{2,1,0:T(8,128)(2,1)}, bf16[4,128,768]{2,1,0:T(8,128)(2,1)}, u32[]{:S(2)}, u32[]{:S(2)}) collective-permute-start(bf16[4,128,768]{2,1,0:T(8,128)(2,1)} %get-tuple-element.73), channel_id=1, source_target_pairs={{1,2},{2,1},{3,4},{4,3},{5,6},{6,5},{9,10},{10,9},{11,12},{12,11},... | collective-permute-start | bytes 2359304 | tf_op jit(solution)/shard_map/ppermute | solution.py:486
  47.8 9.2 %copy-start.2 = (f32[128,768]{1,0:T(8,128)}, f32[128,768]{1,0:T(8,128)S(1)}, u32[]{:S(2)}) copy-start(f32[128,768]{1,0:T(8,128)S(1)} %get-tuple-element.77) | copy-start | bytes 1179652
  57.0 1.1 %copy-start.8 = (f32[128,128]{1,0:T(8,128)}, f32[128,128]{1,0:T(8,128)S(1)}, u32[]{:S(2)}) copy-start(f32[128,128]{1,0:T(8,128)S(1)} %get-tuple-element.80) | copy-start | bytes 196612
  57.0 3.1 %collective-permute-start.5 = (s16[128,1152]{1,0:T(8,128)(2,1)S(1)}, s16[128,1152]{1,0:T(8,128)(2,1)S(1)}, u32[]{:S(2)}, u32[]{:S(2)}) collective-permute-start(s16[128,1152]{1,0:T(8,128)(2,1)S(1)} %get-tuple-element.66.mine_ref), channel_id=1, source_target_pairs={{0,8},{8,0},{16,24},{24,16},{1,9},{9,1},{17,25},{25,17},{2,10},{10... | collective-permute-start | bytes 884744 | tf_op jit(solution)/shard_map/ppermute | solution.py:478
  57.1 1.1 copy-start.4
  58.2 11.3 %collective-permute-start.8 = (bf16[2,128,768]{2,1,0:T(8,128)(2,1)}, bf16[2,128,768]{2,1,0:T(8,128)(2,1)}, u32[]{:S(2)}, u32[]{:S(2)}) collective-permute-start(bf16[2,128,768]{2,1,0:T(8,128)(2,1)} %get-tuple-element.71), channel_id=1, source_target_pairs={{0,8},{8,0},{16,24},{24,16},{1,9},{9,1},{17,25},{25,17},{2,10},{10... | collective-permute-start | bytes 1179656 | tf_op jit(solution)/shard_map/ppermute | solution.py:486
  58.6 10.8 %collective-permute-start.9 = (bf16[2,128,768]{2,1,0:T(8,128)(2,1)}, bf16[2,128,768]{2,1,0:T(8,128)(2,1)}, u32[]{:S(2)}, u32[]{:S(2)}) collective-permute-start(bf16[2,128,768]{2,1,0:T(8,128)(2,1)} %get-tuple-element.72), channel_id=1, source_target_pairs={{8,16},{16,8},{9,17},{17,9},{10,18},{18,10},{11,19},{19,11},{12,20... | collective-permute-start | bytes 1179656 | tf_op jit(solution)/shard_map/ppermute | solution.py:486
  66.6 0.6 copy-start.12
  67.3 12.5 %collective-permute-start.11 = (s16[128,1152]{1,0:T(8,128)(2,1)}, s16[128,1152]{1,0:T(8,128)(2,1)}, u32[]{:S(2)}, u32[]{:S(2)}) collective-permute-start(s16[128,1152]{1,0:T(8,128)(2,1)} %get-tuple-element.83.mine_ref), channel_id=1, source_target_pairs={{0,16},{8,24},{16,0},{24,8},{1,17},{9,25},{17,1},{25,9},{2,18},{10... | collective-permute-start | bytes 884744 | tf_op jit(solution)/shard_map/ppermute | solution.py:478
  69.4 1.0 copy-start.5
  70.4 0.7 copy-start.7
  71.2 8.6 %copy-start.1 = (f32[128,768]{1,0:T(8,128)S(1)}, f32[128,768]{1,0:T(8,128)}, u32[]{:S(2)}) copy-start(f32[128,768]{1,0:T(8,128)} %copy-done) | copy-start | bytes 1179652
  71.2 8.7 %copy-start.3 = (f32[128,768]{1,0:T(8,128)S(1)}, f32[128,768]{1,0:T(8,128)}, u32[]{:S(2)}) copy-start(f32[128,768]{1,0:T(8,128)} %copy-done.2) | copy-start | bytes 1179652
  71.2 8.7 %copy-start.9 = (f32[128,128]{1,0:T(8,128)S(1)}, f32[128,128]{1,0:T(8,128)}, u32[]{:S(2)}) copy-start(f32[128,128]{1,0:T(8,128)} %copy-done.8) | copy-start | bytes 196612
  79.8 6.9 %copy-start.11 = (f32[128,256]{1,0:T(8,128)S(1)}, f32[128,256]{1,0:T(8,128)}, u32[]{:S(2)}) copy-start(f32[128,256]{1,0:T(8,128)} %copy-done.10) | copy-start | bytes 393220
  79.8 6.9 %copy-start.13 = (f32[128,128]{1,0:T(8,128)S(1)}, f32[128,128]{1,0:T(8,128)}, u32[]{:S(2)}) copy-start(f32[128,128]{1,0:T(8,128)} %copy-done.12) | copy-start | bytes 196612
  80.4 12.8 %collective-permute-start.12 = (f32[4,96,128]{2,1,0:T(8,128)S(1)}, f32[4,96,128]{2,1,0:T(8,128)S(1)}, u32[]{:S(2)}, u32[]{:S(2)}) collective-permute-start(f32[4,96,128]{2,1,0:T(8,128)S(1)} %dynamic-slice_bitcast_fusion), channel_id=1, source_target_pairs={{0,1},{1,0},{2,3},{3,2},{4,5},{5,4},{6,7},{7,6},{8,9},{9,8},{10,11... | collective-permute-start | bytes 589832 | tf_op jit(solution)/shard_map/ppermute | solution.py:478
  93.2 5.6 %collective-permute-start.13 = (f32[2,96,128]{2,1,0:T(8,128)S(1)}, f32[2,96,128]{2,1,0:T(8,128)S(1)}, u32[]{:S(2)}, u32[]{:S(2)}) collective-permute-start(f32[2,96,128]{2,1,0:T(8,128)S(1)} %dynamic-slice_bitcast_fusion.1), channel_id=1, source_target_pairs={{0,2},{1,3},{2,0},{3,1},{4,6},{5,7},{6,4},{7,5},{8,10},{9,11},{10,... | collective-permute-start | bytes 294920 | tf_op jit(solution)/shard_map/ppermute | solution.py:478
  98.8 5.1 %collective-permute-start.14 = (f32[1,96,128]{2,1,0:T(8,128)S(1)}, f32[1,96,128]{2,1,0:T(8,128)S(1)}, u32[]{:S(2)}, u32[]{:S(2)}) collective-permute-start(f32[1,96,128]{2,1,0:T(8,128)S(1)} %constant_dynamic-slice_fusion), channel_id=1, source_target_pairs={{0,4},{1,5},{2,6},{3,7},{4,0},{5,1},{6,2},{7,3},{8,12},{9,13},{10,... | collective-permute-start | bytes 147464 | tf_op jit(solution)/shard_map/ppermute | solution.py:478
  104.1 1.3 %collective-permute-start.15 = (f32[96,128]{1,0:T(8,128)S(1)}, f32[96,128]{1,0:T(8,128)S(1)}, u32[]{:S(2)}, u32[]{:S(2)}) collective-permute-start(f32[96,128]{1,0:T(8,128)S(1)} %fusion.3), channel_id=1, source_target_pairs={{0,8},{8,0},{16,24},{24,16},{1,9},{9,1},{17,25},{25,17},{2,10},{10... | collective-permute-start | bytes 147464 | tf_op jit(solution)/shard_map/ppermute | solution.py:478
  105.4 4.2 %collective-permute-start.16 = (f32[96,128]{1,0:T(8,128)S(1)}, f32[96,128]{1,0:T(8,128)S(1)}, u32[]{:S(2)}, u32[]{:S(2)}) collective-permute-start(f32[96,128]{1,0:T(8,128)S(1)} %add.56), channel_id=1, source_target_pairs={{0,16},{8,24},{16,0},{24,8},{1,17},{9,25},{17,1},{25,9},{2,18},{10... | collective-permute-start | bytes 147464 | tf_op jit(solution)/shard_map/ppermute | solution.py:478

commit v5 on v4

--- a/solution.py
+++ b/solution.py
@@ -9,7 +9,7 @@
 
 high = lax.Precision.HIGH
 empty_slot = 9
-near_vmem = 26 * 1024 * 1024
+near_vmem = 18 * 1024 * 1024
 merge_vmem = 12 * 1024 * 1024
 
 
@@ -174,7 +174,7 @@
     spans = [(max(row - 2, 0), row_span(row, row)) for row in range(gu)]
     parts = [(1, 1, lambda col=col: col, 1, 1, col) for col in range(1, gv - 1)]
     plan = (gu - 2, spans, parts)
-    return near_part((density,), plan, (gu, gv), near_blocks, far_right, neighbours, prior, 8)
+    return near_part((density,), plan, (gu, gv), near_blocks, far_right, neighbours, prior, 1.5)
 
 
 def near_rows(density, pu_near, pu_far, near_blocks, far_right, neighbours, prior):
@@ -467,7 +467,7 @@
             pltpu.VMEM((rank, rank), jnp.float32),
             pltpu.VMEM((2 * rank, cols - tail_lanes), jnp.float32),
         ],
-        cost_estimate=cost(4 if level < 2 else 2),
+        cost_estimate=cost((9, 1.5)[level] if level < 2 else 2),
         compiler_params=pltpu.CompilerParams(vmem_limit_bytes=merge_vmem),
     )(mine, other, sketch, *paths)
 
@@ -524,20 +524,20 @@
     corrected = share = None
     pv_path = pu_path = None
     for level in range(levels):
-        last = level == levels - 1
         coef = None
         if level:
             other = partner(left, level)
-        if level in (1, 2) or last:
+        if level in (1, 2, pv_levels):
             links, left = tied(neighbours, left)
         if level == 1:
-            corrected, coef = near_middle(density, near_blocks, far_right, links, corrected)
-        elif level == 2:
             ends, mids, left = tied(ends, mids, left)
             ends = swapped(ends, "pv", True)
             mids = swapped(mids, "pv", True)
             corrected, coef = near_rows(density, pu_near, pu_far, near_blocks, far_right, links, corrected)
-        elif last:
+        elif level == 2:
+            corrected, coef = near_middle(density, near_blocks, far_right, links, corrected)
+        elif level == pv_levels:
+            beside, ends, coefs[-1] = tied(beside, ends, coefs[-1])
             corner_near, corner_far = patch_corners(beside, ends)
             corner_near = swapped(corner_near, "pu", False)
             corner_far = swapped(corner_far, "pu", True)
@@ -558,14 +558,15 @@
         if coef is not None:
             other, coef = tied(other, coef)
             coefs.append(coef)
-        if last:
+        if level == pv_levels:
             coef = functools.reduce(lambda a, b: a + b, coefs)
             share = lax.dot_general(coef, pv_path, (((0,), (1,)), ((), ())), precision=high)
             share = share.reshape(pv_count, rhs // pv_count, -1)
+        if pv_levels <= level < 2 * pv_levels:
             share, other = tied(share, other)
-            share = scattered(share, 0)
+            share = scattered(share, level - pv_levels)
         path = pv_path if level < pv_levels else pu_path
-        last_rows = rows // pu_count if last else 0
+        last_rows = rows // pu_count if level == levels - 1 else 0
         left, path = merge(level, left, other, sketch, path, last_rows)
         if level < pv_levels:
             pv_path = path
@@ -573,7 +574,7 @@
             pu_path = path
 
     share, left = tied(share, left)
-    for level in range(1, pv_levels):
+    for level in range(pu_levels, pv_levels):
         share = scattered(share, level)
     root_coef = lax.dot_general(share[0], pu_path, (((1,), (1,)), ((), ())), precision=high)
     for level in range(pu_levels):

time: 111 us -> 124 us (1.12)
  waiting for transfers between devices: 19.2 us -> 34.8 us
  starting transfers between devices: 28.4 us -> 26.7 us
    ppermute x10, waiting for transfers between devices: 19.2 us -> 34.7 us  [from_partner(): return lax.ppermute(value, axis, pairs)]
  transfers between devices with their start and end apart: 17 -> 17, of which waited for: 6 -> 7; matrix products, arithmetic and copies ran while one was open for 0% -> 0% of each run, Pallas kernels for 49% -> 44%
where the time goes in v5:
time: 124 us
  Pallas kernels  57.7 us (47%)
  waiting for transfers between devices  34.8 us (28%)
  starting transfers between devices  26.7 us (22%)
  local copies, waits for them, and re-layouts  2.43 us (2%)
  matrix products  1.54 us (1%)
    ppermute x10, waiting for transfers between devices, from_partner(): return lax.ppermute(value, axis, pairs)  34.7 us
    pallas_call x5, Pallas kernels, merge(): pl.pallas_call(functools.partial(merge_kernel, bool(paths), bool(last_row...  30.6 us
    pallas_call x3, Pallas kernels, near_part(): pl.pallas_call(functools.partial(near_kernel, plan, len(sources)), grid_s...  22.6 us
    ppermute x10, starting transfers between devices, from_partner(): return lax.ppermute(value, axis, pairs)  22.2 us
    ppermute x7, starting transfers between devices, swapped(): return lax.ppermute(value, axis, pairs)  4.57 us
    pallas_call x1, Pallas kernels, first_step(): pl.pallas_call(functools.partial(first_kernel, counts), in_specs=[held] *...  3.55 us
  transfers between devices with their start and end apart: 17, of which 7 were waited for; matrix products, arithmetic and copies ran while one was open for 0% of the time, Pallas kernels for 44%

profile of v5, /device:TPU:0, one launch (start us, length us, event | category | flops | bytes accessed | tf_op | source)
XLA Modules:
  0.0 124.1 jit_solution(11888960717054355211)
XLA Ops:
  0.6 3.5 %shard_map.86 = (s16[128,1152]{1,0:T(8,128)(2,1)S(1)}, f32[128,256]{1,0:T(8,128)S(1)}, bf16[6,128,768]{2,1,0:T(8,128)(2,1)S(1)}, bf16[2,128,768]{2,1,0:T(8,128)(...) custom-call(s32[32]{0:T(128)} %order_hbm.1, ...), custom_call_target="tpu_custom_call" | custom-call | flops 3300000000 | tf_op jit(solution)/shard_map/pallas_call | solution.py:396
  4.2 3.0 %collective-permute-start = (s16[128,1152]{1,0:T(8,128)(2,1)S(1)}, s16[128,1152]{1,0:T(8,128)(2,1)S(1)}, u32[]{:S(2)}, u32[]{:S(2)}) collective-permute-start(s16[128,1152]{1,0:T(8,128)(2,1)S(1)} %get-tuple-element.53.mine_ref), channel_id=1, source_target_pairs={{0,1},{1,0},{2,3},{3,2},{4,5},{5,4},{6,7},{7,6},{8,9},{9,8},{10,11... | collective-permute-start | bytes 884744 | tf_op jit(solution)/shard_map/ppermute | solution.py:478
  7.2 0.7 collective-permute-start.3
  8.1 6.8 %collective-permute-done.other_ref = s16[128,1152]{1,0:T(8,128)(2,1)S(1)} collective-permute-done((s16[128,1152]{1,0:T(8,128)(2,1)S(1)}, s16[128,1152]{1,0:T(8,128)(2,1)S(1)}, u32[]{:S(2)}, u32[]{:S(2)}) %collective-permute-start) | collective-permute-done | bytes 294944 | tf_op jit(solution)/shard_map/ppermute | solution.py:478
  15.0 5.8 %shard_map.87 = (s16[128,1152]{1,0:T(8,128)(2,1)S(1)}, f32[128,128]{1,0:T(8,128)S(1)}) custom-call(s16[128,1152]{1,0:T(8,128)(2,1)S(1)} %get-tuple-element.53.mine_ref, s16[128,1152]{1,0:T(8,128)(2,1)S(1)} %collective-permute-done.other_ref, f32[128,256]{1,0:T(8,128)S(1)} %get-tuple-element.54.sketch_ref), custom_call_target="tpu_custom_call" | custom-call | flops 9900000256 | tf_op jit(solution)/shard_map/pallas_call | solution.py:460
  20.8 2.1 %collective-permute-start.1 = (s16[128,1152]{1,0:T(8,128)(2,1)S(1)}, s16[128,1152]{1,0:T(8,128)(2,1)S(1)}, u32[]{:S(2)}, u32[]{:S(2)}) collective-permute-start(s16[128,1152]{1,0:T(8,128)(2,1)S(1)} %get-tuple-element.57.mine_ref), channel_id=1, source_target_pairs={{0,2},{1,3},{2,0},{3,1},{4,6},{5,7},{6,4},{7,5},{8,10},{9,11},{10,... | collective-permute-start | bytes 884744 | tf_op jit(solution)/shard_map/ppermute | solution.py:478
  22.9 0.7 collective-permute-start.6
  23.6 1.6 %collective-permute-start.9 = (bf16[4,128,768]{2,1,0:T(8,128)(2,1)}, bf16[4,128,768]{2,1,0:T(8,128)(2,1)}, u32[]{:S(2)}, u32[]{:S(2)}) collective-permute-start(bf16[4,128,768]{2,1,0:T(8,128)(2,1)} %get-tuple-element.80), channel_id=1, source_target_pairs={{1,2},{2,1},{3,4},{4,3},{5,6},{6,5},{9,10},{10,9},{11,12},{12,11},... | collective-permute-start | bytes 2359304 | tf_op jit(solution)/shard_map/ppermute | solution.py:486
  25.2 5.7 %shard_map.88 = (bf16[6,6,128,768]{3,2,1,0:T(8,128)(2,1)}, f32[128,768]{1,0:T(8,128)S(1)}) custom-call(s32[6,6,6]{2,1,0:T(8,128)S(1)} %copy-done.6, bf16[6,6,6,128,128]{4,3,2,1,0:T(8,128)(2,1)} %near_hbm.5, bf16[6,6,128,128]{3,2,1,0:T(8,128)(2,1)} %right_hbm.5, bf16[6,6,128,768]{3,2,1,0:T(8,128)(2,1)} %refs_0_.5, ...), custom_call_target="tpu_custom_call" | custom-call | flops 1650000000 | tf_op jit(solution)/shard_map/pallas_call | solution.py:134
  30.9 5.9 %shard_map.89 = (s16[128,1152]{1,0:T(8,128)(2,1)S(1)}, f32[128,128]{1,0:T(8,128)S(1)}) custom-call(s16[128,1152]{1,0:T(8,128)(2,1)S(1)} %get-tuple-element.57.mine_ref, s16[128,1152]{1,0:T(8,128)(2,1)S(1)} %collective-permute-done.1.other_ref, f32[128,256]{1,0:T(8,128)S(1)} %get-tuple-element.54.sketch_ref, f32[128,128]{1,0:T(8,128)S(1)} %get-tuple-element.63.refs_0_), custom_call_target="tpu_custom_call" | custom-call | flops 1650000000 | tf_op jit(solution)/shard_map/pallas_call | solution.py:460
  36.8 7.2 %collective-permute-start.4 = (s16[128,1152]{1,0:T(8,128)(2,1)S(1)}, s16[128,1152]{1,0:T(8,128)(2,1)S(1)}, u32[]{:S(2)}, u32[]{:S(2)}) collective-permute-start(s16[128,1152]{1,0:T(8,128)(2,1)S(1)} %get-tuple-element.65.mine_ref), channel_id=1, source_target_pairs={{0,4},{1,5},{2,6},{3,7},{4,0},{5,1},{6,2},{7,3},{8,12},{9,13},{10,... | collective-permute-start | bytes 884744 | tf_op jit(solution)/shard_map/ppermute | solution.py:478
  44.0 8.3 %shard_map.90 = (bf16[6,6,128,768]{3,2,1,0:T(8,128)(2,1)}, f32[128,768]{1,0:T(8,128)S(1)}) custom-call(s32[6,6,6]{2,1,0:T(8,128)S(1)} %copy-done.6, bf16[6,6,6,128,128]{4,3,2,1,0:T(8,128)(2,1)} %near_hbm.5, bf16[6,6,128,128]{3,2,1,0:T(8,128)(2,1)} %right_hbm.5, bf16[6,6,128,768]{3,2,1,0:T(8,128)(2,1)} %refs_0_.5, ...), custom_call_target="tpu_custom_call", output_to_operand_aliasing={{0}: (4, {})} | custom-call | flops 1650000000 | tf_op jit(solution)/shard_map/pallas_call | solution.py:134
  52.3 11.6 %collective-permute-done.4.other_ref = s16[128,1152]{1,0:T(8,128)(2,1)S(1)} collective-permute-done((s16[128,1152]{1,0:T(8,128)(2,1)S(1)}, s16[128,1152]{1,0:T(8,128)(2,1)S(1)}, u32[]{:S(2)}, u32[]{:S(2)}) %collective-permute-start.4) | collective-permute-done | bytes 294944 | tf_op jit(solution)/shard_map/ppermute | solution.py:478
  64.0 0.9 shard_map.92
  65.0 1.4 %collective-permute-start.8 = (bf16[2,128,768]{2,1,0:T(8,128)(2,1)}, bf16[2,128,768]{2,1,0:T(8,128)(2,1)}, u32[]{:S(2)}, u32[]{:S(2)}) collective-permute-start(bf16[2,128,768]{2,1,0:T(8,128)(2,1)} %get-tuple-element.79), channel_id=1, source_target_pairs={{8,16},{16,8},{9,17},{17,9},{10,18},{18,10},{11,19},{19,11},{12,20... | collective-permute-start | bytes 1179656 | tf_op jit(solution)/shard_map/ppermute | solution.py:486
  66.4 6.6 %shard_map.91 = (s16[128,1152]{1,0:T(8,128)(2,1)}, f32[128,128]{1,0:T(8,128)S(1)}) custom-call(s16[128,1152]{1,0:T(8,128)(2,1)S(1)} %get-tuple-element.65.mine_ref, s16[128,1152]{1,0:T(8,128)(2,1)S(1)} %collective-permute-done.4.other_ref, f32[128,256]{1,0:T(8,128)S(1)} %get-tuple-element.54.sketch_ref, f32[128,128]{1,0:T(8,128)S(1)} %get-tuple-element.70.refs_0_), custom_call_target="tpu_custom_call" | custom-call | flops 2200000000 | tf_op jit(solution)/shard_map/pallas_call | solution.py:460
  73.0 0.6 copy-done.8
  73.6 2.3 %collective-permute-start.10 = (s16[128,1152]{1,0:T(8,128)(2,1)}, s16[128,1152]{1,0:T(8,128)(2,1)}, u32[]{:S(2)}, u32[]{:S(2)}) collective-permute-start(s16[128,1152]{1,0:T(8,128)(2,1)} %get-tuple-element.90.mine_ref), channel_id=1, source_target_pairs={{0,8},{8,0},{16,24},{24,16},{1,9},{9,1},{17,25},{25,17},{2,10},{10... | collective-permute-start | bytes 884744 | tf_op jit(solution)/shard_map/ppermute | solution.py:478
  76.0 1.0 copy-done.5
  77.0 0.7 copy-done.7
  77.7 8.6 %shard_map.93 = (bf16[6,6,128,768]{3,2,1,0:T(8,128)(2,1)}, f32[128,768]{1,0:T(8,128)S(1)}) custom-call(s32[6,6,6]{2,1,0:T(8,128)S(1)} %copy-done.7, bf16[6,6,6,128,128]{4,3,2,1,0:T(8,128)(2,1)} %near_hbm.5, bf16[6,6,128,128]{3,2,1,0:T(8,128)(2,1)} %right_hbm.5, bf16[6,6,128,768]{3,2,1,0:T(8,128)(2,1)} %refs_0_.5, ...), custom_call_target="tpu_custom_call", output_to_operand_aliasing={{0}: (11, {})} | custom-call | flops 1650000000 | tf_op jit(solution)/shard_map/pallas_call | solution.py:134
  86.9 2.5 %collective-permute-start.11 = (f32[4,96,128]{2,1,0:T(8,128)S(1)}, f32[4,96,128]{2,1,0:T(8,128)S(1)}, u32[]{:S(2)}, u32[]{:S(2)}) collective-permute-start(f32[4,96,128]{2,1,0:T(8,128)S(1)} %dynamic-slice_bitcast_fusion), channel_id=1, source_target_pairs={{0,1},{1,0},{2,3},{3,2},{4,5},{5,4},{6,7},{7,6},{8,9},{9,8},{10,11... | collective-permute-start | bytes 589832 | tf_op jit(solution)/shard_map/ppermute | solution.py:478
  89.4 6.9 %shard_map.94 = (s16[128,1152]{1,0:T(8,128)(2,1)S(1)}, f32[128,128]{1,0:T(8,128)S(1)}) custom-call(s16[128,1152]{1,0:T(8,128)(2,1)} %get-tuple-element.90.mine_ref, s16[128,1152]{1,0:T(8,128)(2,1)} %collective-permute-done.10.other_ref, f32[128,256]{1,0:T(8,128)S(1)} %copy-done.11), custom_call_target="tpu_custom_call" | custom-call | flops 2200000000 | tf_op jit(solution)/shard_map/pallas_call | solution.py:460
  96.9 8.1 %collective-permute-done.12.other_ref = s16[128,1152]{1,0:T(8,128)(2,1)S(1)} collective-permute-done((s16[128,1152]{1,0:T(8,128)(2,1)S(1)}, s16[128,1152]{1,0:T(8,128)(2,1)S(1)}, u32[]{:S(2)}, u32[]{:S(2)}) %collective-permute-start.12) | collective-permute-done | bytes 294944 | tf_op jit(solution)/shard_map/ppermute | solution.py:478
  105.0 1.6 %collective-permute-start.13 = (f32[2,96,128]{2,1,0:T(8,128)S(1)}, f32[2,96,128]{2,1,0:T(8,128)S(1)}, u32[]{:S(2)}, u32[]{:S(2)}) collective-permute-start(f32[2,96,128]{2,1,0:T(8,128)S(1)} %dynamic-slice_bitcast_fusion.1), channel_id=1, source_target_pairs={{0,2},{1,3},{2,0},{3,1},{4,6},{5,7},{6,4},{7,5},{8,10},{9,11},{10,... | collective-permute-start | bytes 294920 | tf_op jit(solution)/shard_map/ppermute | solution.py:478
  106.7 5.4 %shard_map.95 = (f32[128,256]{1,0:T(8,128)S(1)}, f32[128,128]{1,0:T(8,128)S(1)}) custom-call(s16[128,1152]{1,0:T(8,128)(2,1)S(1)} %get-tuple-element.92.mine_ref, s16[128,1152]{1,0:T(8,128)(2,1)S(1)} %collective-permute-done.12.other_ref, f32[128,256]{1,0:T(8,128)S(1)} %copy-done.11, f32[128,128]{1,0:T(8,128)S(1)} %get-tuple-element.95.refs_0_), custom_call_target="tpu_custom_call" | custom-call | flops 2200000000 | tf_op jit(solution)/shard_map/pallas_call | solution.py:460
  112.2 1.7 %collective-permute-start.14 = (f32[1,96,128]{2,1,0:T(8,128)S(1)}, f32[1,96,128]{2,1,0:T(8,128)S(1)}, u32[]{:S(2)}, u32[]{:S(2)}) collective-permute-start(f32[1,96,128]{2,1,0:T(8,128)S(1)} %constant_dynamic-slice_fusion), channel_id=1, source_target_pairs={{0,4},{1,5},{2,6},{3,7},{4,0},{5,1},{6,2},{7,3},{8,12},{9,13},{10,... | collective-permute-start | bytes 147464 | tf_op jit(solution)/shard_map/ppermute | solution.py:478
  113.9 3.8 %collective-permute-done.14 = f32[1,96,128]{2,1,0:T(8,128)S(1)} collective-permute-done((f32[1,96,128]{2,1,0:T(8,128)S(1)}, f32[1,96,128]{2,1,0:T(8,128)S(1)}, u32[]{:S(2)}, u32[]{:S(2)}) %collective-permute-start.14) | collective-permute-done | bytes 49184 | tf_op jit(solution)/shard_map/ppermute | solution.py:478
  117.9 1.2 collective-permute-done.15
  119.1 1.0 collective-permute-start.16
  120.2 3.1 %collective-permute-done.16 = f32[96,128]{1,0:T(8,128)S(1)} collective-permute-done((f32[96,128]{1,0:T(8,128)S(1)}, f32[96,128]{1,0:T(8,128)S(1)}, u32[]{:S(2)}, u32[]{:S(2)}) %collective-permute-start.16) | collective-permute-done | bytes 49184 | tf_op jit(solution)/shard_map/ppermute | solution.py:478
  123.3 0.8 fusion.5
  (45 shorter events, 1.8 us)
Async XLA Ops:
  4.2 62.2 %copy-start.10 = (f32[128,256]{1,0:T(8,128)}, f32[128,256]{1,0:T(8,128)S(1)}, u32[]{:S(2)}) copy-start(f32[128,256]{1,0:T(8,128)S(1)} %get-tuple-element.54.sketch_ref) | copy-start | bytes 393220
  4.2 10.8 %collective-permute-start = (s16[128,1152]{1,0:T(8,128)(2,1)S(1)}, s16[128,1152]{1,0:T(8,128)(2,1)S(1)}, u32[]{:S(2)}, u32[]{:S(2)}) collective-permute-start(s16[128,1152]{1,0:T(8,128)(2,1)S(1)} %get-tuple-element.53.mine_ref), channel_id=1, source_target_pairs={{0,1},{1,0},{2,3},{3,2},{4,5},{5,4},{6,7},{7,6},{8,9},{9,8},{10,11... | collective-permute-start | bytes 884744 | tf_op jit(solution)/shard_map/ppermute | solution.py:478
  7.2 16.4 %collective-permute-start.2 = (bf16[6,128,768]{2,1,0:T(8,128)(2,1)S(1)}, bf16[6,128,768]{2,1,0:T(8,128)(2,1)S(1)}, u32[]{:S(2)}, u32[]{:S(2)}) collective-permute-start(bf16[6,128,768]{2,1,0:T(8,128)(2,1)S(1)} %get-tuple-element.59), channel_id=1, source_target_pairs={{0,8},{8,0},{16,24},{24,16},{1,9},{9,1},{17,25},{25,17},{2,10},{10... | collective-permute-start | bytes 3538952 | tf_op jit(solution)/shard_map/ppermute | solution.py:486
  7.2 18.0 %collective-permute-start.3 = (bf16[6,128,768]{2,1,0:T(8,128)(2,1)S(1)}, bf16[6,128,768]{2,1,0:T(8,128)(2,1)S(1)}, u32[]{:S(2)}, u32[]{:S(2)}) collective-permute-start(bf16[6,128,768]{2,1,0:T(8,128)(2,1)S(1)} %get-tuple-element.60), channel_id=1, source_target_pairs={{8,16},{16,8},{9,17},{17,9},{10,18},{18,10},{11,19},{19,11},{12,20... | collective-permute-start | bytes 3538952 | tf_op jit(solution)/shard_map/ppermute | solution.py:486
  7.9 56.1 %collective-permute-start.5 = (bf16[6,128,768]{2,1,0:T(8,128)(2,1)S(1)}, bf16[6,128,768]{2,1,0:T(8,128)(2,1)S(1)}, u32[]{:S(2)}, u32[]{:S(2)}) collective-permute-start(bf16[6,128,768]{2,1,0:T(8,128)(2,1)S(1)} %get-tuple-element.73), channel_id=1, source_target_pairs={{0,1},{1,0},{2,3},{3,2},{4,5},{5,4},{6,7},{7,6},{8,9},{9,8},{10,11... | collective-permute-start | bytes 3538952 | tf_op jit(solution)/shard_map/ppermute | solution.py:486
  15.0 10.2 %copy-start.6 = (s32[6,6,6]{2,1,0:T(8,128)S(1)}, s32[6,6,6]{2,1,0:T(8,128)}, u32[]{:S(2)}) copy-start(s32[6,6,6]{2,1,0:T(8,128)} %nb_ref.2) | copy-start | bytes 2596
  20.8 10.1 %collective-permute-start.1 = (s16[128,1152]{1,0:T(8,128)(2,1)S(1)}, s16[128,1152]{1,0:T(8,128)(2,1)S(1)}, u32[]{:S(2)}, u32[]{:S(2)}) collective-permute-start(s16[128,1152]{1,0:T(8,128)(2,1)S(1)} %get-tuple-element.57.mine_ref), channel_id=1, source_target_pairs={{0,2},{1,3},{2,0},{3,1},{4,6},{5,7},{6,4},{7,5},{8,10},{9,11},{10,... | collective-permute-start | bytes 884744 | tf_op jit(solution)/shard_map/ppermute | solution.py:478
  22.9 41.0 %collective-permute-start.6 = (bf16[2,128,768]{2,1,0:T(8,128)(2,1)S(1)}, bf16[2,128,768]{2,1,0:T(8,128)(2,1)S(1)}, u32[]{:S(2)}, u32[]{:S(2)}) collective-permute-start(bf16[2,128,768]{2,1,0:T(8,128)(2,1)S(1)} %get-tuple-element.74), channel_id=1, source_target_pairs={{1,2},{2,1},{3,4},{4,3},{5,6},{6,5},{9,10},{10,9},{11,12},{12,11},... | collective-permute-start | bytes 1179656 | tf_op jit(solution)/shard_map/ppermute | solution.py:486
  23.6 52.3 %collective-permute-start.9 = (bf16[4,128,768]{2,1,0:T(8,128)(2,1)}, bf16[4,128,768]{2,1,0:T(8,128)(2,1)}, u32[]{:S(2)}, u32[]{:S(2)}) collective-permute-start(bf16[4,128,768]{2,1,0:T(8,128)(2,1)} %get-tuple-element.80), channel_id=1, source_target_pairs={{1,2},{2,1},{3,4},{4,3},{5,6},{6,5},{9,10},{10,9},{11,12},{12,11},... | collective-permute-start | bytes 2359304 | tf_op jit(solution)/shard_map/ppermute | solution.py:486
  30.9 5.9 %copy-start = (f32[128,768]{1,0:T(8,128)}, f32[128,768]{1,0:T(8,128)S(1)}, u32[]{:S(2)}) copy-start(f32[128,768]{1,0:T(8,128)S(1)} %get-tuple-element.83) | copy-start | bytes 1179652
  36.8 27.1 %collective-permute-start.4 = (s16[128,1152]{1,0:T(8,128)(2,1)S(1)}, s16[128,1152]{1,0:T(8,128)(2,1)S(1)}, u32[]{:S(2)}, u32[]{:S(2)}) collective-permute-start(s16[128,1152]{1,0:T(8,128)(2,1)S(1)} %get-tuple-element.65.mine_ref), channel_id=1, source_target_pairs={{0,4},{1,5},{2,6},{3,7},{4,0},{5,1},{6,2},{7,3},{8,12},{9,13},{10,... | collective-permute-start | bytes 884744 | tf_op jit(solution)/shard_map/ppermute | solution.py:478
  52.3 12.7 %copy-start.2 = (f32[128,768]{1,0:T(8,128)}, f32[128,768]{1,0:T(8,128)S(1)}, u32[]{:S(2)}) copy-start(f32[128,768]{1,0:T(8,128)S(1)} %get-tuple-element.84) | copy-start | bytes 1179652
  63.9 1.1 copy-start.4
  65.0 11.0 %collective-permute-start.7 = (bf16[2,128,768]{2,1,0:T(8,128)(2,1)}, bf16[2,128,768]{2,1,0:T(8,128)(2,1)}, u32[]{:S(2)}, u32[]{:S(2)}) collective-permute-start(bf16[2,128,768]{2,1,0:T(8,128)(2,1)} %get-tuple-element.78), channel_id=1, source_target_pairs={{0,8},{8,0},{16,24},{24,16},{1,9},{9,1},{17,25},{25,17},{2,10},{10... | collective-permute-start | bytes 1179656 | tf_op jit(solution)/shard_map/ppermute | solution.py:486
  65.0 11.0 %collective-permute-start.8 = (bf16[2,128,768]{2,1,0:T(8,128)(2,1)}, bf16[2,128,768]{2,1,0:T(8,128)(2,1)}, u32[]{:S(2)}, u32[]{:S(2)}) collective-permute-start(bf16[2,128,768]{2,1,0:T(8,128)(2,1)} %get-tuple-element.79), channel_id=1, source_target_pairs={{8,16},{16,8},{9,17},{17,9},{10,18},{18,10},{11,19},{19,11},{12,20... | collective-permute-start | bytes 1179656 | tf_op jit(solution)/shard_map/ppermute | solution.py:486
  73.0 0.6 copy-start.8
  73.6 12.7 %collective-permute-start.10 = (s16[128,1152]{1,0:T(8,128)(2,1)}, s16[128,1152]{1,0:T(8,128)(2,1)}, u32[]{:S(2)}, u32[]{:S(2)}) collective-permute-start(s16[128,1152]{1,0:T(8,128)(2,1)} %get-tuple-element.90.mine_ref), channel_id=1, source_target_pairs={{0,8},{8,0},{16,24},{24,16},{1,9},{9,1},{17,25},{25,17},{2,10},{10... | collective-permute-start | bytes 884744 | tf_op jit(solution)/shard_map/ppermute | solution.py:478
  76.0 1.0 copy-start.5
  77.0 0.7 copy-start.7
  77.7 8.6 %copy-start.1 = (f32[128,768]{1,0:T(8,128)S(1)}, f32[128,768]{1,0:T(8,128)}, u32[]{:S(2)}) copy-start(f32[128,768]{1,0:T(8,128)} %copy-done) | copy-start | bytes 1179652
  77.7 8.6 %copy-start.3 = (f32[128,768]{1,0:T(8,128)S(1)}, f32[128,768]{1,0:T(8,128)}, u32[]{:S(2)}) copy-start(f32[128,768]{1,0:T(8,128)} %copy-done.2) | copy-start | bytes 1179652
  77.7 8.6 %copy-start.9 = (f32[128,128]{1,0:T(8,128)S(1)}, f32[128,128]{1,0:T(8,128)}, u32[]{:S(2)}) copy-start(f32[128,128]{1,0:T(8,128)} %copy-done.8) | copy-start | bytes 196612
  86.3 3.1 %copy-start.11 = (f32[128,256]{1,0:T(8,128)S(1)}, f32[128,256]{1,0:T(8,128)}, u32[]{:S(2)}) copy-start(f32[128,256]{1,0:T(8,128)} %copy-done.10) | copy-start | bytes 393220
  86.9 10.0 %collective-permute-start.11 = (f32[4,96,128]{2,1,0:T(8,128)S(1)}, f32[4,96,128]{2,1,0:T(8,128)S(1)}, u32[]{:S(2)}, u32[]{:S(2)}) collective-permute-start(f32[4,96,128]{2,1,0:T(8,128)S(1)} %dynamic-slice_bitcast_fusion), channel_id=1, source_target_pairs={{0,1},{1,0},{2,3},{3,2},{4,5},{5,4},{6,7},{7,6},{8,9},{9,8},{10,11... | collective-permute-start | bytes 589832 | tf_op jit(solution)/shard_map/ppermute | solution.py:478
  96.3 8.7 %collective-permute-start.12 = (s16[128,1152]{1,0:T(8,128)(2,1)S(1)}, s16[128,1152]{1,0:T(8,128)(2,1)S(1)}, u32[]{:S(2)}, u32[]{:S(2)}) collective-permute-start(s16[128,1152]{1,0:T(8,128)(2,1)S(1)} %get-tuple-element.92.mine_ref), channel_id=1, source_target_pairs={{0,16},{8,24},{16,0},{24,8},{1,17},{9,25},{17,1},{25,9},{2,18},{10... | collective-permute-start | bytes 884744 | tf_op jit(solution)/shard_map/ppermute | solution.py:478
  105.0 7.1 %collective-permute-start.13 = (f32[2,96,128]{2,1,0:T(8,128)S(1)}, f32[2,96,128]{2,1,0:T(8,128)S(1)}, u32[]{:S(2)}, u32[]{:S(2)}) collective-permute-start(f32[2,96,128]{2,1,0:T(8,128)S(1)} %dynamic-slice_bitcast_fusion.1), channel_id=1, source_target_pairs={{0,2},{1,3},{2,0},{3,1},{4,6},{5,7},{6,4},{7,5},{8,10},{9,11},{10,... | collective-permute-start | bytes 294920 | tf_op jit(solution)/shard_map/ppermute | solution.py:478
  112.2 5.5 %collective-permute-start.14 = (f32[1,96,128]{2,1,0:T(8,128)S(1)}, f32[1,96,128]{2,1,0:T(8,128)S(1)}, u32[]{:S(2)}, u32[]{:S(2)}) collective-permute-start(f32[1,96,128]{2,1,0:T(8,128)S(1)} %constant_dynamic-slice_fusion), channel_id=1, source_target_pairs={{0,4},{1,5},{2,6},{3,7},{4,0},{5,1},{6,2},{7,3},{8,12},{9,13},{10,... | collective-permute-start | bytes 147464 | tf_op jit(solution)/shard_map/ppermute | solution.py:478
  117.8 1.3 %collective-permute-start.15 = (f32[96,128]{1,0:T(8,128)S(1)}, f32[96,128]{1,0:T(8,128)S(1)}, u32[]{:S(2)}, u32[]{:S(2)}) collective-permute-start(f32[96,128]{1,0:T(8,128)S(1)} %fusion.3), channel_id=1, source_target_pairs={{0,8},{8,0},{16,24},{24,16},{1,9},{9,1},{17,25},{25,17},{2,10},{10... | collective-permute-start | bytes 147464 | tf_op jit(solution)/shard_map/ppermute | solution.py:478
  119.1 4.2 %collective-permute-start.16 = (f32[96,128]{1,0:T(8,128)S(1)}, f32[96,128]{1,0:T(8,128)S(1)}, u32[]{:S(2)}, u32[]{:S(2)}) collective-permute-start(f32[96,128]{1,0:T(8,128)S(1)} %add.56), channel_id=1, source_target_pairs={{0,16},{8,24},{16,0},{24,8},{1,17},{9,25},{17,1},{25,9},{2,18},{10... | collective-permute-start | bytes 147464 | tf_op jit(solution)/shard_map/ppermute | solution.py:478

commit v6 on v5

--- a/solution.py
+++ b/solution.py
@@ -187,7 +187,7 @@
     return near_part((density, pu_near, pu_far), plan, (6, gv), near_blocks, far_right, neighbours, prior, 1.5)
 
 
-def near_columns(density, pu_near, pu_far, corner_near, corner_far, beside, ends, mids, near_blocks, far_right, neighbours, prior):
+def near_columns(density, pu_near, pu_far, corner_near, corner_far, across, ends, mids, near_blocks, far_right, neighbours, prior):
     gu, gv = density.shape[:2]
     per_step = 2
     spans = []
@@ -221,7 +221,7 @@
             at = max((row - 1) // per_step, 0)
             here = lambda row=row: row + 1
             spans.append((at, inner(0, row, here)))
-            if not far:
+            if far:
                 spans.append((at, outer(5, row, here)))
             elif row in (0, gu - 1):
                 spans.append((at, outer(6, min(row, 1), here)))
@@ -229,24 +229,24 @@
                 spans.append((at, outer(7, row - 1, here)))
         spans.append((0, inner(1, None, near_row)))
         spans.append((0, inner(2, None, far_row)))
-        spans.append((0, outer(3, far, near_row)))
-        spans.append((0, outer(4, far, far_row)))
+        spans.append((0, outer(3, 1 - far, near_row)))
+        spans.append((0, outer(4, 1 - far, far_row)))
         col = lambda left_side=left_side: (gv - 1) * (1 - left_side())
         parts += [(row, per_step, col, row + 1, per_step, 3 * far + 1) for row in range(per_step)]
     plan = (gu // per_step, spans, parts)
-    sources = (density, pu_near, pu_far, corner_near, corner_far, beside, ends, mids)
+    sources = (density, pu_near, pu_far, corner_near, corner_far, across, ends, mids)
     return near_part(sources, plan, (gu + 2, 6), near_blocks, far_right, neighbours, prior, 1.5)
 
 
-def corners_kernel(beside, ends, to_near, to_far):
+def corners_kernel(across, ends, to_near, to_far):
     low = odd("pu")
-    rows = beside.shape[0]
+    rows = across.shape[0]
     for target, last in ((to_near, 1 - low), (to_far, low)):
-        target[0] = beside[(rows - 1) * last]
+        target[0] = across[(rows - 1) * last]
         target[1] = ends[last]
 
 
-def patch_corners(beside, ends):
+def patch_corners(across, ends):
     whole = pl.BlockSpec(memory_space=pltpu.VMEM)
     return pl.pallas_call(
         corners_kernel,
@@ -255,7 +255,7 @@
         out_shape=[jax.ShapeDtypeStruct(ends.shape, ends.dtype)] * 2,
         cost_estimate=cost(0.7),
         compiler_params=pltpu.CompilerParams(vmem_limit_bytes=merge_vmem),
-    )(beside, ends)
+    )(across, ends)
 
 
 def reciprocal(value):
@@ -360,17 +360,17 @@
 
 
 def first_kernel(counts, order_hbm, value_hbm, sketch_hbm, density, code_ref, sketch_ref, *refs):
-    beside, ends, mids, pu_near, pu_far, order, value, sketch, sems = refs
+    across, ends, mids, pu_near, pu_far, order, value, sketch, sems = refs
     gu, gv = density.shape[:2]
     near_col = (gv - 1) * (1 - odd("pv"))
     far_col = (gv - 1) * odd("pv")
     pairs = [(value_hbm.at[0, 0], value), (order_hbm, order), (sketch_hbm, sketch)]
     inputs = len(pairs)
-    pairs += [(density.at[row, near_col], beside.at[row]) for row in range(gu)]
+    pairs += [(density.at[row, far_col], across.at[row]) for row in range(gu)]
     pairs.append((density.at[(gu - 1) * (1 - odd("pu"))], pu_near))
     pairs.append((density.at[(gu - 1) * odd("pu")], pu_far))
-    pairs += [(density.at[(gu - 1) * row, far_col], ends.at[row]) for row in range(2)]
-    pairs += [(density.at[row + 1, far_col], mids.at[row]) for row in range(gu - 2)]
+    pairs += [(density.at[(gu - 1) * row, near_col], ends.at[row]) for row in range(2)]
+    pairs += [(density.at[row + 1, near_col], mids.at[row]) for row in range(gu - 2)]
     copies = [
         pltpu.make_async_copy(source, target, sems.at[index])
         for index, (source, target) in enumerate(pairs)
@@ -512,11 +512,11 @@
         return keep + from_partner(give, "pv", level)
 
     rows = far_left.shape[2]
-    left, sketch, beside, ends, mids, pu_near, pu_far = first_step(
+    left, sketch, across, ends, mids, pu_near, pu_far = first_step(
         far_left, sketch, density, patch_order, (pu_count, pv_count)
     )
     other = partner(left, 0)
-    beside = swapped(beside, "pv", False)
+    across = swapped(across, "pv", True)
     pu_near = swapped(pu_near, "pu", False)
     pu_far = swapped(pu_far, "pu", True)
 
@@ -530,15 +530,15 @@
         if level in (1, 2, pv_levels):
             links, left = tied(neighbours, left)
         if level == 1:
-            ends, mids, left = tied(ends, mids, left)
-            ends = swapped(ends, "pv", True)
-            mids = swapped(mids, "pv", True)
             corrected, coef = near_rows(density, pu_near, pu_far, near_blocks, far_right, links, corrected)
+            ends, mids, coef = tied(ends, mids, coef)
+            ends = swapped(ends, "pv", False)
+            mids = swapped(mids, "pv", False)
         elif level == 2:
             corrected, coef = near_middle(density, near_blocks, far_right, links, corrected)
         elif level == pv_levels:
-            beside, ends, coefs[-1] = tied(beside, ends, coefs[-1])
-            corner_near, corner_far = patch_corners(beside, ends)
+            across, ends, coefs[-1] = tied(across, ends, coefs[-1])
+            corner_near, corner_far = patch_corners(across, ends)
             corner_near = swapped(corner_near, "pu", False)
             corner_far = swapped(corner_far, "pu", True)
             corrected, coef = near_columns(
@@ -547,7 +547,7 @@
                 pu_far,
                 corner_near,
                 corner_far,
-                beside,
+                across,
                 ends,
                 mids,
                 near_blocks,

time: 124 us -> 133 us (1.073)
  waiting for transfers between devices: 34.8 us -> 48.9 us
  starting transfers between devices: 26.7 us -> 20.9 us
    ppermute x10, waiting for transfers between devices: 34.7 us -> 48.9 us  [from_partner(): return lax.ppermute(value, axis, pairs)]
    ppermute x10, starting transfers between devices: 22.2 us -> 15.9 us  [from_partner(): return lax.ppermute(value, axis, pairs)]
  transfers between devices with their start and end apart: 17 -> 17, of which waited for: 7 -> 6; matrix products, arithmetic and copies ran while one was open for 0% -> 0% of each run, Pallas kernels for 44% -> 41%
where the time goes in v6:
time: 133 us; the launch traced here: 132 us
  Pallas kernels  57.6 us (43%)
  waiting for transfers between devices  48.9 us (37%)
  starting transfers between devices  20.9 us (16%)
  local copies, waits for them, and re-layouts  2.43 us (2%)
  matrix products  1.54 us (1%)
    ppermute x10, waiting for transfers between devices, from_partner(): return lax.ppermute(value, axis, pairs)  48.9 us
    pallas_call x5, Pallas kernels, merge(): pl.pallas_call(functools.partial(merge_kernel, bool(paths), bool(last_row...  30.6 us
    pallas_call x3, Pallas kernels, near_part(): pl.pallas_call(functools.partial(near_kernel, plan, len(sources)), grid_s...  22.4 us
    ppermute x10, starting transfers between devices, from_partner(): return lax.ppermute(value, axis, pairs)  15.9 us
    ppermute x7, starting transfers between devices, swapped(): return lax.ppermute(value, axis, pairs)  5 us
    pallas_call x1, Pallas kernels, first_step(): pl.pallas_call(functools.partial(first_kernel, counts), in_specs=[held] *...  3.52 us
  transfers between devices with their start and end apart: 17, of which 6 were waited for; matrix products, arithmetic and copies ran while one was open for 0% of the time, Pallas kernels for 41%

profile of v6, /device:TPU:0, one launch (start us, length us, event | category | flops | bytes accessed | tf_op | source)
XLA Modules:
  0.0 132.3 jit_solution(7997371459369913877)
XLA Ops:
  0.6 3.5 %shard_map.86 = (s16[128,1152]{1,0:T(8,128)(2,1)S(1)}, f32[128,256]{1,0:T(8,128)S(1)}, bf16[6,128,768]{2,1,0:T(8,128)(2,1)S(1)}, bf16[2,128,768]{2,1,0:T(8,128)(...) custom-call(s32[32]{0:T(128)} %order_hbm.1, ...), custom_call_target="tpu_custom_call" | custom-call | flops 3300000000 | tf_op jit(solution)/shard_map/pallas_call | solution.py:396
  4.2 3.0 %collective-permute-start = (s16[128,1152]{1,0:T(8,128)(2,1)S(1)}, s16[128,1152]{1,0:T(8,128)(2,1)S(1)}, u32[]{:S(2)}, u32[]{:S(2)}) collective-permute-start(s16[128,1152]{1,0:T(8,128)(2,1)S(1)} %get-tuple-element.51.mine_ref), channel_id=1, source_target_pairs={{0,1},{1,0},{2,3},{3,2},{4,5},{5,4},{6,7},{7,6},{8,9},{9,8},{10,11... | collective-permute-start | bytes 884744 | tf_op jit(solution)/shard_map/ppermute | solution.py:478
  7.2 0.7 collective-permute-start.3
  7.9 0.7 collective-permute-start.5
  8.7 30.1 %collective-permute-done.other_ref = s16[128,1152]{1,0:T(8,128)(2,1)S(1)} collective-permute-done((s16[128,1152]{1,0:T(8,128)(2,1)S(1)}, s16[128,1152]{1,0:T(8,128)(2,1)S(1)}, u32[]{:S(2)}, u32[]{:S(2)}) %collective-permute-start) | collective-permute-done | bytes 294944 | tf_op jit(solution)/shard_map/ppermute | solution.py:478
  38.7 5.8 %shard_map.87 = (s16[128,1152]{1,0:T(8,128)(2,1)S(1)}, f32[128,128]{1,0:T(8,128)S(1)}) custom-call(s16[128,1152]{1,0:T(8,128)(2,1)S(1)} %get-tuple-element.51.mine_ref, s16[128,1152]{1,0:T(8,128)(2,1)S(1)} %collective-permute-done.other_ref, f32[128,256]{1,0:T(8,128)S(1)} %get-tuple-element.52.sketch_ref), custom_call_target="tpu_custom_call" | custom-call | flops 9900000256 | tf_op jit(solution)/shard_map/pallas_call | solution.py:460
  44.6 2.6 %collective-permute-start.1 = (s16[128,1152]{1,0:T(8,128)(2,1)S(1)}, s16[128,1152]{1,0:T(8,128)(2,1)S(1)}, u32[]{:S(2)}, u32[]{:S(2)}) collective-permute-start(s16[128,1152]{1,0:T(8,128)(2,1)S(1)} %get-tuple-element.54.mine_ref), channel_id=1, source_target_pairs={{0,2},{1,3},{2,0},{3,1},{4,6},{5,7},{6,4},{7,5},{8,10},{9,11},{10,... | collective-permute-start | bytes 884744 | tf_op jit(solution)/shard_map/ppermute | solution.py:478
  47.2 5.7 %shard_map.88 = (bf16[6,6,128,768]{3,2,1,0:T(8,128)(2,1)}, f32[128,768]{1,0:T(8,128)S(1)}) custom-call(s32[6,6,6]{2,1,0:T(8,128)S(1)} %copy-done.6, bf16[6,6,6,128,128]{4,3,2,1,0:T(8,128)(2,1)} %near_hbm.5, bf16[6,6,128,128]{3,2,1,0:T(8,128)(2,1)} %right_hbm.5, bf16[6,6,128,768]{3,2,1,0:T(8,128)(2,1)} %refs_0_.5, ...), custom_call_target="tpu_custom_call" | custom-call | flops 1650000000 | tf_op jit(solution)/shard_map/pallas_call | solution.py:134
  53.0 2.0 %collective-permute-start.6 = (bf16[2,128,768]{2,1,0:T(8,128)(2,1)S(1)}, bf16[2,128,768]{2,1,0:T(8,128)(2,1)S(1)}, u32[]{:S(2)}, u32[]{:S(2)}) collective-permute-start(bf16[2,128,768]{2,1,0:T(8,128)(2,1)S(1)} %get-tuple-element.74), channel_id=1, source_target_pairs={{0,1},{1,0},{2,3},{3,2},{4,5},{5,4},{6,7},{7,6},{8,9},{9,8},{10,11... | collective-permute-start | bytes 1179656 | tf_op jit(solution)/shard_map/ppermute | solution.py:486
  55.1 5.9 %shard_map.89 = (s16[128,1152]{1,0:T(8,128)(2,1)S(1)}, f32[128,128]{1,0:T(8,128)S(1)}) custom-call(s16[128,1152]{1,0:T(8,128)(2,1)S(1)} %get-tuple-element.54.mine_ref, s16[128,1152]{1,0:T(8,128)(2,1)S(1)} %collective-permute-done.1.other_ref, f32[128,256]{1,0:T(8,128)S(1)} %get-tuple-element.52.sketch_ref, f32[128,128]{1,0:T(8,128)S(1)} %get-tuple-element.63.refs_0_), custom_call_target="tpu_custom_call" | custom-call | flops 1650000000 | tf_op jit(solution)/shard_map/pallas_call | solution.py:460
  60.9 2.7 %collective-permute-start.4 = (s16[128,1152]{1,0:T(8,128)(2,1)S(1)}, s16[128,1152]{1,0:T(8,128)(2,1)S(1)}, u32[]{:S(2)}, u32[]{:S(2)}) collective-permute-start(s16[128,1152]{1,0:T(8,128)(2,1)S(1)} %get-tuple-element.65.mine_ref), channel_id=1, source_target_pairs={{0,4},{1,5},{2,6},{3,7},{4,0},{5,1},{6,2},{7,3},{8,12},{9,13},{10,... | collective-permute-start | bytes 884744 | tf_op jit(solution)/shard_map/ppermute | solution.py:478
  63.6 8.3 %shard_map.90 = (bf16[6,6,128,768]{3,2,1,0:T(8,128)(2,1)}, f32[128,768]{1,0:T(8,128)S(1)}) custom-call(s32[6,6,6]{2,1,0:T(8,128)S(1)} %copy-done.6, bf16[6,6,6,128,128]{4,3,2,1,0:T(8,128)(2,1)} %near_hbm.5, bf16[6,6,128,128]{3,2,1,0:T(8,128)(2,1)} %right_hbm.5, bf16[6,6,128,768]{3,2,1,0:T(8,128)(2,1)} %refs_0_.5, ...), custom_call_target="tpu_custom_call", output_to_operand_aliasing={{0}: (4, {})} | custom-call | flops 1650000000 | tf_op jit(solution)/shard_map/pallas_call | solution.py:134
  71.9 2.9 %collective-permute-done.4.other_ref = s16[128,1152]{1,0:T(8,128)(2,1)S(1)} collective-permute-done((s16[128,1152]{1,0:T(8,128)(2,1)S(1)}, s16[128,1152]{1,0:T(8,128)(2,1)S(1)}, u32[]{:S(2)}, u32[]{:S(2)}) %collective-permute-start.4) | collective-permute-done | bytes 294944 | tf_op jit(solution)/shard_map/ppermute | solution.py:478
  74.9 1.0 shard_map.92
  75.9 1.4 %collective-permute-start.8 = (bf16[2,128,768]{2,1,0:T(8,128)(2,1)}, bf16[2,128,768]{2,1,0:T(8,128)(2,1)}, u32[]{:S(2)}, u32[]{:S(2)}) collective-permute-start(bf16[2,128,768]{2,1,0:T(8,128)(2,1)} %get-tuple-element.79), channel_id=1, source_target_pairs={{8,16},{16,8},{9,17},{17,9},{10,18},{18,10},{11,19},{19,11},{12,20... | collective-permute-start | bytes 1179656 | tf_op jit(solution)/shard_map/ppermute | solution.py:486
  77.4 6.6 %shard_map.91 = (s16[128,1152]{1,0:T(8,128)(2,1)}, f32[128,128]{1,0:T(8,128)S(1)}) custom-call(s16[128,1152]{1,0:T(8,128)(2,1)S(1)} %get-tuple-element.65.mine_ref, s16[128,1152]{1,0:T(8,128)(2,1)S(1)} %collective-permute-done.4.other_ref, f32[128,256]{1,0:T(8,128)S(1)} %get-tuple-element.52.sketch_ref, f32[128,128]{1,0:T(8,128)S(1)} %get-tuple-element.70.refs_0_), custom_call_target="tpu_custom_call" | custom-call | flops 2200000000 | tf_op jit(solution)/shard_map/pallas_call | solution.py:460
  84.0 0.6 copy-done.8
  84.6 2.5 %collective-permute-start.10 = (s16[128,1152]{1,0:T(8,128)(2,1)}, s16[128,1152]{1,0:T(8,128)(2,1)}, u32[]{:S(2)}, u32[]{:S(2)}) collective-permute-start(s16[128,1152]{1,0:T(8,128)(2,1)} %get-tuple-element.90.mine_ref), channel_id=1, source_target_pairs={{0,8},{8,0},{16,24},{24,16},{1,9},{9,1},{17,25},{25,17},{2,10},{10... | collective-permute-start | bytes 884744 | tf_op jit(solution)/shard_map/ppermute | solution.py:478
  87.1 1.0 copy-done.5
  88.1 0.7 copy-done.7
  88.9 8.4 %shard_map.93 = (bf16[6,6,128,768]{3,2,1,0:T(8,128)(2,1)}, f32[128,768]{1,0:T(8,128)S(1)}) custom-call(s32[6,6,6]{2,1,0:T(8,128)S(1)} %copy-done.7, bf16[6,6,6,128,128]{4,3,2,1,0:T(8,128)(2,1)} %near_hbm.5, bf16[6,6,128,128]{3,2,1,0:T(8,128)(2,1)} %right_hbm.5, bf16[6,6,128,768]{3,2,1,0:T(8,128)(2,1)} %refs_0_.5, ...), custom_call_target="tpu_custom_call", output_to_operand_aliasing={{0}: (11, {})} | custom-call | flops 1650000000 | tf_op jit(solution)/shard_map/pallas_call | solution.py:134
  97.3 0.5 fusion
  97.8 1.7 %collective-permute-start.11 = (f32[4,96,128]{2,1,0:T(8,128)S(1)}, f32[4,96,128]{2,1,0:T(8,128)S(1)}, u32[]{:S(2)}, u32[]{:S(2)}) collective-permute-start(f32[4,96,128]{2,1,0:T(8,128)S(1)} %dynamic-slice_bitcast_fusion), channel_id=1, source_target_pairs={{0,1},{1,0},{2,3},{3,2},{4,5},{5,4},{6,7},{7,6},{8,9},{9,8},{10,11... | collective-permute-start | bytes 589832 | tf_op jit(solution)/shard_map/ppermute | solution.py:478
  99.6 6.9 %shard_map.94 = (s16[128,1152]{1,0:T(8,128)(2,1)S(1)}, f32[128,128]{1,0:T(8,128)S(1)}) custom-call(s16[128,1152]{1,0:T(8,128)(2,1)} %get-tuple-element.90.mine_ref, s16[128,1152]{1,0:T(8,128)(2,1)} %collective-permute-done.10.other_ref, f32[128,256]{1,0:T(8,128)S(1)} %copy-done.11), custom_call_target="tpu_custom_call" | custom-call | flops 2200000000 | tf_op jit(solution)/shard_map/pallas_call | solution.py:460
  106.9 8.3 %collective-permute-done.12.other_ref = s16[128,1152]{1,0:T(8,128)(2,1)S(1)} collective-permute-done((s16[128,1152]{1,0:T(8,128)(2,1)S(1)}, s16[128,1152]{1,0:T(8,128)(2,1)S(1)}, u32[]{:S(2)}, u32[]{:S(2)}) %collective-permute-start.12) | collective-permute-done | bytes 294944 | tf_op jit(solution)/shard_map/ppermute | solution.py:478
  115.2 5.4 %shard_map.95 = (f32[128,256]{1,0:T(8,128)S(1)}, f32[128,128]{1,0:T(8,128)S(1)}) custom-call(s16[128,1152]{1,0:T(8,128)(2,1)S(1)} %get-tuple-element.92.mine_ref, s16[128,1152]{1,0:T(8,128)(2,1)S(1)} %collective-permute-done.12.other_ref, f32[128,256]{1,0:T(8,128)S(1)} %copy-done.11, f32[128,128]{1,0:T(8,128)S(1)} %get-tuple-element.95.refs_0_), custom_call_target="tpu_custom_call" | custom-call | flops 2200000000 | tf_op jit(solution)/shard_map/pallas_call | solution.py:460
  120.7 1.8 %collective-permute-start.14 = (f32[1,96,128]{2,1,0:T(8,128)S(1)}, f32[1,96,128]{2,1,0:T(8,128)S(1)}, u32[]{:S(2)}, u32[]{:S(2)}) collective-permute-start(f32[1,96,128]{2,1,0:T(8,128)S(1)} %constant_dynamic-slice_fusion), channel_id=1, source_target_pairs={{0,4},{1,5},{2,6},{3,7},{4,0},{5,1},{6,2},{7,3},{8,12},{9,13},{10,... | collective-permute-start | bytes 147464 | tf_op jit(solution)/shard_map/ppermute | solution.py:478
  122.5 3.3 %collective-permute-done.14 = f32[1,96,128]{2,1,0:T(8,128)S(1)} collective-permute-done((f32[1,96,128]{2,1,0:T(8,128)S(1)}, f32[1,96,128]{2,1,0:T(8,128)S(1)}, u32[]{:S(2)}, u32[]{:S(2)}) %collective-permute-start.14) | collective-permute-done | bytes 49184 | tf_op jit(solution)/shard_map/ppermute | solution.py:478
  126.1 1.2 collective-permute-done.15
  127.3 1.0 collective-permute-start.16
  128.3 3.1 %collective-permute-done.16 = f32[96,128]{1,0:T(8,128)S(1)} collective-permute-done((f32[96,128]{1,0:T(8,128)S(1)}, f32[96,128]{1,0:T(8,128)S(1)}, u32[]{:S(2)}, u32[]{:S(2)}) %collective-permute-start.16) | collective-permute-done | bytes 49184 | tf_op jit(solution)/shard_map/ppermute | solution.py:478
  131.4 0.8 fusion.5
  (45 shorter events, 1.0 us)
Async XLA Ops:
  4.2 73.2 %copy-start.10 = (f32[128,256]{1,0:T(8,128)}, f32[128,256]{1,0:T(8,128)S(1)}, u32[]{:S(2)}) copy-start(f32[128,256]{1,0:T(8,128)S(1)} %get-tuple-element.52.sketch_ref) | copy-start | bytes 393220
  4.2 34.6 %collective-permute-start = (s16[128,1152]{1,0:T(8,128)(2,1)S(1)}, s16[128,1152]{1,0:T(8,128)(2,1)S(1)}, u32[]{:S(2)}, u32[]{:S(2)}) collective-permute-start(s16[128,1152]{1,0:T(8,128)(2,1)S(1)} %get-tuple-element.51.mine_ref), channel_id=1, source_target_pairs={{0,1},{1,0},{2,3},{3,2},{4,5},{5,4},{6,7},{7,6},{8,9},{9,8},{10,11... | collective-permute-start | bytes 884744 | tf_op jit(solution)/shard_map/ppermute | solution.py:478
  7.2 40.0 %collective-permute-start.2 = (bf16[6,128,768]{2,1,0:T(8,128)(2,1)S(1)}, bf16[6,128,768]{2,1,0:T(8,128)(2,1)S(1)}, u32[]{:S(2)}, u32[]{:S(2)}) collective-permute-start(bf16[6,128,768]{2,1,0:T(8,128)(2,1)S(1)} %get-tuple-element.58), channel_id=1, source_target_pairs={{0,8},{8,0},{16,24},{24,16},{1,9},{9,1},{17,25},{25,17},{2,10},{10... | collective-permute-start | bytes 3538952 | tf_op jit(solution)/shard_map/ppermute | solution.py:486
  7.2 40.0 %collective-permute-start.3 = (bf16[6,128,768]{2,1,0:T(8,128)(2,1)S(1)}, bf16[6,128,768]{2,1,0:T(8,128)(2,1)S(1)}, u32[]{:S(2)}, u32[]{:S(2)}) collective-permute-start(bf16[6,128,768]{2,1,0:T(8,128)(2,1)S(1)} %get-tuple-element.59), channel_id=1, source_target_pairs={{8,16},{16,8},{9,17},{17,9},{10,18},{18,10},{11,19},{19,11},{12,20... | collective-permute-start | bytes 3538952 | tf_op jit(solution)/shard_map/ppermute | solution.py:486
  7.9 67.0 %collective-permute-start.5 = (bf16[6,128,768]{2,1,0:T(8,128)(2,1)S(1)}, bf16[6,128,768]{2,1,0:T(8,128)(2,1)S(1)}, u32[]{:S(2)}, u32[]{:S(2)}) collective-permute-start(bf16[6,128,768]{2,1,0:T(8,128)(2,1)S(1)} %get-tuple-element.73), channel_id=1, source_target_pairs={{1,2},{2,1},{3,4},{4,3},{5,6},{6,5},{9,10},{10,9},{11,12},{12,11},... | collective-permute-start | bytes 3538952 | tf_op jit(solution)/shard_map/ppermute | solution.py:486
  38.7 8.5 %copy-start.6 = (s32[6,6,6]{2,1,0:T(8,128)S(1)}, s32[6,6,6]{2,1,0:T(8,128)}, u32[]{:S(2)}) copy-start(s32[6,6,6]{2,1,0:T(8,128)} %nb_ref.2) | copy-start | bytes 2596
  44.6 8.4 %collective-permute-start.1 = (s16[128,1152]{1,0:T(8,128)(2,1)S(1)}, s16[128,1152]{1,0:T(8,128)(2,1)S(1)}, u32[]{:S(2)}, u32[]{:S(2)}) collective-permute-start(s16[128,1152]{1,0:T(8,128)(2,1)S(1)} %get-tuple-element.54.mine_ref), channel_id=1, source_target_pairs={{0,2},{1,3},{2,0},{3,1},{4,6},{5,7},{6,4},{7,5},{8,10},{9,11},{10,... | collective-permute-start | bytes 884744 | tf_op jit(solution)/shard_map/ppermute | solution.py:478
  52.9 8.0 %copy-start = (f32[128,768]{1,0:T(8,128)}, f32[128,768]{1,0:T(8,128)S(1)}, u32[]{:S(2)}) copy-start(f32[128,768]{1,0:T(8,128)S(1)} %get-tuple-element.83) | copy-start | bytes 1179652
  53.0 21.9 %collective-permute-start.6 = (bf16[2,128,768]{2,1,0:T(8,128)(2,1)S(1)}, bf16[2,128,768]{2,1,0:T(8,128)(2,1)S(1)}, u32[]{:S(2)}, u32[]{:S(2)}) collective-permute-start(bf16[2,128,768]{2,1,0:T(8,128)(2,1)S(1)} %get-tuple-element.74), channel_id=1, source_target_pairs={{0,1},{1,0},{2,3},{3,2},{4,5},{5,4},{6,7},{7,6},{8,9},{9,8},{10,11... | collective-permute-start | bytes 1179656 | tf_op jit(solution)/shard_map/ppermute | solution.py:486
  55.0 32.1 %collective-permute-start.9 = (bf16[4,128,768]{2,1,0:T(8,128)(2,1)}, bf16[4,128,768]{2,1,0:T(8,128)(2,1)}, u32[]{:S(2)}, u32[]{:S(2)}) collective-permute-start(bf16[4,128,768]{2,1,0:T(8,128)(2,1)} %get-tuple-element.80), channel_id=1, source_target_pairs={{0,1},{1,0},{2,3},{3,2},{4,5},{5,4},{6,7},{7,6},{8,9},{9,8},{10,11... | collective-permute-start | bytes 2359304 | tf_op jit(solution)/shard_map/ppermute | solution.py:486
  60.9 13.9 %collective-permute-start.4 = (s16[128,1152]{1,0:T(8,128)(2,1)S(1)}, s16[128,1152]{1,0:T(8,128)(2,1)S(1)}, u32[]{:S(2)}, u32[]{:S(2)}) collective-permute-start(s16[128,1152]{1,0:T(8,128)(2,1)S(1)} %get-tuple-element.65.mine_ref), channel_id=1, source_target_pairs={{0,4},{1,5},{2,6},{3,7},{4,0},{5,1},{6,2},{7,3},{8,12},{9,13},{10,... | collective-permute-start | bytes 884744 | tf_op jit(solution)/shard_map/ppermute | solution.py:478
  71.9 4.0 %copy-start.2 = (f32[128,768]{1,0:T(8,128)}, f32[128,768]{1,0:T(8,128)S(1)}, u32[]{:S(2)}) copy-start(f32[128,768]{1,0:T(8,128)S(1)} %get-tuple-element.84) | copy-start | bytes 1179652
  74.9 1.0 copy-start.4
  75.9 11.2 %collective-permute-start.7 = (bf16[2,128,768]{2,1,0:T(8,128)(2,1)}, bf16[2,128,768]{2,1,0:T(8,128)(2,1)}, u32[]{:S(2)}, u32[]{:S(2)}) collective-permute-start(bf16[2,128,768]{2,1,0:T(8,128)(2,1)} %get-tuple-element.78), channel_id=1, source_target_pairs={{0,8},{8,0},{16,24},{24,16},{1,9},{9,1},{17,25},{25,17},{2,10},{10... | collective-permute-start | bytes 1179656 | tf_op jit(solution)/shard_map/ppermute | solution.py:486
  75.9 11.2 %collective-permute-start.8 = (bf16[2,128,768]{2,1,0:T(8,128)(2,1)}, bf16[2,128,768]{2,1,0:T(8,128)(2,1)}, u32[]{:S(2)}, u32[]{:S(2)}) collective-permute-start(bf16[2,128,768]{2,1,0:T(8,128)(2,1)} %get-tuple-element.79), channel_id=1, source_target_pairs={{8,16},{16,8},{9,17},{17,9},{10,18},{18,10},{11,19},{19,11},{12,20... | collective-permute-start | bytes 1179656 | tf_op jit(solution)/shard_map/ppermute | solution.py:486
  84.0 0.6 copy-start.8
  84.6 12.7 %collective-permute-start.10 = (s16[128,1152]{1,0:T(8,128)(2,1)}, s16[128,1152]{1,0:T(8,128)(2,1)}, u32[]{:S(2)}, u32[]{:S(2)}) collective-permute-start(s16[128,1152]{1,0:T(8,128)(2,1)} %get-tuple-element.90.mine_ref), channel_id=1, source_target_pairs={{0,8},{8,0},{16,24},{24,16},{1,9},{9,1},{17,25},{25,17},{2,10},{10... | collective-permute-start | bytes 884744 | tf_op jit(solution)/shard_map/ppermute | solution.py:478
  87.1 1.0 copy-start.5
  88.1 0.7 copy-start.7
  88.9 8.4 %copy-start.1 = (f32[128,768]{1,0:T(8,128)S(1)}, f32[128,768]{1,0:T(8,128)}, u32[]{:S(2)}) copy-start(f32[128,768]{1,0:T(8,128)} %copy-done) | copy-start | bytes 1179652
  88.9 8.4 %copy-start.3 = (f32[128,768]{1,0:T(8,128)S(1)}, f32[128,768]{1,0:T(8,128)}, u32[]{:S(2)}) copy-start(f32[128,768]{1,0:T(8,128)} %copy-done.2) | copy-start | bytes 1179652
  88.9 8.4 %copy-start.9 = (f32[128,128]{1,0:T(8,128)S(1)}, f32[128,128]{1,0:T(8,128)}, u32[]{:S(2)}) copy-start(f32[128,128]{1,0:T(8,128)} %copy-done.8) | copy-start | bytes 196612
  97.3 2.3 %copy-start.11 = (f32[128,256]{1,0:T(8,128)S(1)}, f32[128,256]{1,0:T(8,128)}, u32[]{:S(2)}) copy-start(f32[128,256]{1,0:T(8,128)} %copy-done.10) | copy-start | bytes 393220
  97.8 9.0 %collective-permute-start.11 = (f32[4,96,128]{2,1,0:T(8,128)S(1)}, f32[4,96,128]{2,1,0:T(8,128)S(1)}, u32[]{:S(2)}, u32[]{:S(2)}) collective-permute-start(f32[4,96,128]{2,1,0:T(8,128)S(1)} %dynamic-slice_bitcast_fusion), channel_id=1, source_target_pairs={{0,1},{1,0},{2,3},{3,2},{4,5},{5,4},{6,7},{7,6},{8,9},{9,8},{10,11... | collective-permute-start | bytes 589832 | tf_op jit(solution)/shard_map/ppermute | solution.py:478
  106.4 8.7 %collective-permute-start.12 = (s16[128,1152]{1,0:T(8,128)(2,1)S(1)}, s16[128,1152]{1,0:T(8,128)(2,1)S(1)}, u32[]{:S(2)}, u32[]{:S(2)}) collective-permute-start(s16[128,1152]{1,0:T(8,128)(2,1)S(1)} %get-tuple-element.92.mine_ref), channel_id=1, source_target_pairs={{0,16},{8,24},{16,0},{24,8},{1,17},{9,25},{17,1},{25,9},{2,18},{10... | collective-permute-start | bytes 884744 | tf_op jit(solution)/shard_map/ppermute | solution.py:478
  115.2 5.5 %collective-permute-start.13 = (f32[2,96,128]{2,1,0:T(8,128)S(1)}, f32[2,96,128]{2,1,0:T(8,128)S(1)}, u32[]{:S(2)}, u32[]{:S(2)}) collective-permute-start(f32[2,96,128]{2,1,0:T(8,128)S(1)} %dynamic-slice_bitcast_fusion.1), channel_id=1, source_target_pairs={{0,2},{1,3},{2,0},{3,1},{4,6},{5,7},{6,4},{7,5},{8,10},{9,11},{10,... | collective-permute-start | bytes 294920 | tf_op jit(solution)/shard_map/ppermute | solution.py:478
  120.7 5.1 %collective-permute-start.14 = (f32[1,96,128]{2,1,0:T(8,128)S(1)}, f32[1,96,128]{2,1,0:T(8,128)S(1)}, u32[]{:S(2)}, u32[]{:S(2)}) collective-permute-start(f32[1,96,128]{2,1,0:T(8,128)S(1)} %constant_dynamic-slice_fusion), channel_id=1, source_target_pairs={{0,4},{1,5},{2,6},{3,7},{4,0},{5,1},{6,2},{7,3},{8,12},{9,13},{10,... | collective-permute-start | bytes 147464 | tf_op jit(solution)/shard_map/ppermute | solution.py:478
  126.0 1.3 collective-permute-start.15
  127.3 4.2 %collective-permute-start.16 = (f32[96,128]{1,0:T(8,128)S(1)}, f32[96,128]{1,0:T(8,128)S(1)}, u32[]{:S(2)}, u32[]{:S(2)}) collective-permute-start(f32[96,128]{1,0:T(8,128)S(1)} %add.56), channel_id=1, source_target_pairs={{0,16},{8,24},{16,0},{24,8},{1,17},{9,25},{17,1},{25,9},{2,18},{10... | collective-permute-start | bytes 147464 | tf_op jit(solution)/shard_map/ppermute | solution.py:478

commit v7 on v4

--- a/solution.py
+++ b/solution.py
@@ -9,7 +9,7 @@
 
 high = lax.Precision.HIGH
 empty_slot = 9
-near_vmem = 26 * 1024 * 1024
+near_vmem = 18 * 1024 * 1024
 merge_vmem = 12 * 1024 * 1024
 
 
@@ -174,7 +174,7 @@
     spans = [(max(row - 2, 0), row_span(row, row)) for row in range(gu)]
     parts = [(1, 1, lambda col=col: col, 1, 1, col) for col in range(1, gv - 1)]
     plan = (gu - 2, spans, parts)
-    return near_part((density,), plan, (gu, gv), near_blocks, far_right, neighbours, prior, 8)
+    return near_part((density,), plan, (gu, gv), near_blocks, far_right, neighbours, prior, 0.5)
 
 
 def near_rows(density, pu_near, pu_far, near_blocks, far_right, neighbours, prior):
@@ -184,7 +184,7 @@
     spans.append((0, lambda srcs, ext: (srcs[2], ext.at[5 * odd("pu")])))
     parts = [(0, gu - 1, lambda col=col: col, 1, 3, col) for col in range(1, gv - 1)]
     plan = (2, spans, parts)
-    return near_part((density, pu_near, pu_far), plan, (6, gv), near_blocks, far_right, neighbours, prior, 1.5)
+    return near_part((density, pu_near, pu_far), plan, (6, gv), near_blocks, far_right, neighbours, prior, 0.5)
 
 
 def near_columns(density, pu_near, pu_far, corner_near, corner_far, beside, ends, mids, near_blocks, far_right, neighbours, prior):
@@ -235,7 +235,7 @@
         parts += [(row, per_step, col, row + 1, per_step, 3 * far + 1) for row in range(per_step)]
     plan = (gu // per_step, spans, parts)
     sources = (density, pu_near, pu_far, corner_near, corner_far, beside, ends, mids)
-    return near_part(sources, plan, (gu + 2, 6), near_blocks, far_right, neighbours, prior, 1.5)
+    return near_part(sources, plan, (gu + 2, 6), near_blocks, far_right, neighbours, prior, 0.5)
 
 
 def corners_kernel(beside, ends, to_near, to_far):
@@ -285,41 +285,73 @@
             }
             k_done = k_rows[q]
             e_done = e_rows[q]
-            for k in range(0, tile, 2):
-                a = spread(cols[q, k], k)
-                b = spread(cols[q, k], k + 1)
-                c = spread(cols[q, k + 1], k + 1)
-                det = a * c - b * b
-                inverse = reciprocal(det)
-
-                def solved(one, two):
-                    return (c * one - b * two) * inverse, (a * two - b * one) * inverse
-
-                k_one, k_two = spread(k_rows[q], k), spread(k_rows[q], k + 1)
-                e_one, e_two = spread(e_rows[q], k), spread(e_rows[q], k + 1)
-                k_solved = solved(k_one, k_two)
-                e_solved = solved(e_one, e_two)
+            for k in range(0, tile, 4):
+                pivots = [[spread(cols[q, k + j], k + i) for j in range(i + 1)] for i in range(4)]
+                (a,), (b, c), (d, e, h), (f, g, i, j) = pivots
+                upper = reciprocal(a * c - b * b)
+
+                def halved(one, two):
+                    return (c * one - b * two) * upper, (a * two - b * one) * upper
+
+                t_one, t_two = halved(d, e)
+                u_one, u_two = halved(f, g)
+                s_one = h - (t_one * d + t_two * e)
+                s_mix = i - (t_one * f + t_two * g)
+                s_two = j - (u_one * f + u_two * g)
+                lower_det = s_one * s_two - s_mix * s_mix
+                lower = reciprocal(lower_det)
+
+                def reduced(rows):
+                    y_one, y_two = halved(rows[0], rows[1])
+                    return rows[2] - (d * y_one + e * y_two), rows[3] - (f * y_one + g * y_two), y_one, y_two
+
+                def solved(rows):
+                    q_one, q_two, y_one, y_two = reduced(rows)
+                    x_three = (s_two * q_one - s_mix * q_two) * lower
+                    x_four = (s_one * q_two - s_mix * q_one) * lower
+                    x_one = y_one - (t_one * x_three + u_one * x_four)
+                    x_two = y_two - (t_two * x_three + u_two * x_four)
+                    return x_one, x_two, x_three, x_four
+
+                def finished(rows):
+                    q_one, q_two, _, _ = reduced(rows)
+                    return (
+                        rows[0] * root_one,
+                        (rows[1] - slope_one * rows[0]) * root_two,
+                        q_one * root_three,
+                        (q_two - slope_three * q_one) * root_four,
+                    )
+
+                root_one = lax.rsqrt(a)
+                slope_one = b * root_one * root_one
+                root_two = lax.rsqrt(a * c - b * b) * a * root_one
+                root_three = lax.rsqrt(s_one)
+                slope_three = s_mix * root_three * root_three
+                root_four = lax.rsqrt(lower_det) * s_one * root_three
+                k_four = [spread(k_rows[q], k + n) for n in range(4)]
+                e_four = [spread(e_rows[q], k + n) for n in range(4)]
+                k_solved = solved(k_four)
+                e_solved = solved(e_four)
                 links = {
-                    m: solved(spread(cols[q, k], m), spread(cols[q, k + 1], m)) for m in range(k + 2, tile)
+                    m: solved([spread(cols[q, k + n], m) for n in range(4)]) for m in range(k + 4, tile)
                 }
-                root = lax.rsqrt(a)
-                second = lax.rsqrt(det) * a * root
-                slope = b * root * root
-                k_done = jnp.where(sub == k, k_one * root, k_done)
-                e_done = jnp.where(sub == k, e_one * root, e_done)
-                k_done = jnp.where(sub == k + 1, (k_two - slope * k_one) * second, k_done)
-                e_done = jnp.where(sub == k + 1, (e_two - slope * e_one) * second, e_done)
+                for n, (k_row, e_row) in enumerate(zip(finished(k_four), finished(e_four))):
+                    k_done = jnp.where(sub == k + n, k_row, k_done)
+                    e_done = jnp.where(sub == k + n, e_row, e_done)
+
+                def fallen(value, factors, rows):
+                    return value - ((factors[0] * rows[0] + factors[1] * rows[1]) + (factors[2] * rows[2] + factors[3] * rows[3]))
+
                 for r in range(q, count):
-                    one, two = cols[r, k], cols[r, k + 1]
+                    factors = [cols[r, k + n] for n in range(4)]
                     if r == q:
-                        if k + 2 == tile:
+                        if k + 4 == tile:
                             continue
-                        one = jnp.where(sub > k + 1, one, 0.0)
-                        two = jnp.where(sub > k + 1, two, 0.0)
-                    for m in range(k + 2, tile):
-                        cols[r, m] = cols[r, m] - (one * links[m][0] + two * links[m][1])
-                    k_rows[r] = k_rows[r] - (one * k_solved[0] + two * k_solved[1])
-                    e_rows[r] = e_rows[r] - (one * e_solved[0] + two * e_solved[1])
+                        factors = [jnp.where(sub > k + 3, factor, 0.0) for factor in factors]
+                    for m in range(k + 4, tile):
+                        cols[r, m] = fallen(cols[r, m], factors, links[m])
+                    k_rows[r] = fallen(k_rows[r], factors, k_solved)
+                    e_rows[r] = fallen(e_rows[r], factors, e_solved)
             k_rows[q] = k_done
             e_rows[q] = e_done
         e_now = jnp.concatenate(e_rows, axis=0)
@@ -359,58 +391,72 @@
     return value, tail[:, tail_lanes - 1 :]
 
 
-def first_kernel(counts, order_hbm, value_hbm, sketch_hbm, density, code_ref, sketch_ref, *refs):
-    beside, ends, mids, pu_near, pu_far, order, value, sketch, sems = refs
-    gu, gv = density.shape[:2]
-    near_col = (gv - 1) * (1 - odd("pv"))
-    far_col = (gv - 1) * odd("pv")
-    pairs = [(value_hbm.at[0, 0], value), (order_hbm, order), (sketch_hbm, sketch)]
-    inputs = len(pairs)
-    pairs += [(density.at[row, near_col], beside.at[row]) for row in range(gu)]
-    pairs.append((density.at[(gu - 1) * (1 - odd("pu"))], pu_near))
-    pairs.append((density.at[(gu - 1) * odd("pu")], pu_far))
-    pairs += [(density.at[(gu - 1) * row, far_col], ends.at[row]) for row in range(2)]
-    pairs += [(density.at[row + 1, far_col], mids.at[row]) for row in range(gu - 2)]
+def run_copies(pairs, sems):
     copies = [
         pltpu.make_async_copy(source, target, sems.at[index])
         for index, (source, target) in enumerate(pairs)
     ]
     for copy in copies:
         copy.start()
-    for copy in copies[:inputs]:
+    return copies
+
+
+def leaf_kernel(counts, order_hbm, value_hbm, sketch_hbm, code_ref, sketch_ref, order, value, sketch, sems):
+    pairs = [(value_hbm.at[0, 0], value), (order_hbm, order), (sketch_hbm, sketch)]
+    for copy in run_copies(pairs, sems):
         copy.wait()
     key = order[lax.axis_index("pu") * counts[1] + lax.axis_index("pv")]
     encode(jnp.transpose(value[...]), key.astype(jnp.float32), code_ref)
     sketch_ref[...] = jnp.transpose(sketch[...])
-    for copy in copies[inputs:]:
-        copy.wait()
-
-
-def first_step(value, sketch, density, order, counts):
+
+
+def coded_leaf(value, sketch, order, counts):
     rows, cols = value.shape[2:]
-    gu, gv, size, rhs = density.shape
-    blocks = (gu, 2, gu - 2, gv, gv)
     whole = pl.BlockSpec(memory_space=pltpu.VMEM)
     held = pl.BlockSpec(memory_space=pltpu.HBM)
-    args = [in_hbm(array) for array in (order, value, sketch, density)]
     return pl.pallas_call(
-        functools.partial(first_kernel, counts),
-        in_specs=[held] * len(args),
-        out_specs=[whole] * (2 + len(blocks)),
+        functools.partial(leaf_kernel, counts),
+        in_specs=[held] * 3,
+        out_specs=[whole] * 2,
         out_shape=[
             jax.ShapeDtypeStruct((cols, rows + tail_lanes), jnp.int16),
             jax.ShapeDtypeStruct(sketch.shape[::-1], jnp.float32),
-        ]
-        + [jax.ShapeDtypeStruct((count, size, rhs), density.dtype) for count in blocks],
+        ],
         scratch_shapes=[
             pltpu.SMEM(order.shape, jnp.int32),
             pltpu.VMEM((rows, cols), jnp.float32),
             pltpu.VMEM(sketch.shape, jnp.float32),
-            pltpu.SemaphoreType.DMA((2 * gu + 5,)),
+            pltpu.SemaphoreType.DMA((3,)),
         ],
-        cost_estimate=cost(3),
+        cost_estimate=cost(1.5),
         compiler_params=pltpu.CompilerParams(vmem_limit_bytes=merge_vmem),
-    )(*args)
+    )(in_hbm(order), in_hbm(value), in_hbm(sketch))
+
+
+def edges_kernel(density, beside, across, pu_near, pu_far, sems):
+    gu, gv = density.shape[:2]
+    near_col = (gv - 1) * (1 - odd("pv"))
+    far_col = (gv - 1) * odd("pv")
+    pairs = [(density.at[row, near_col], beside.at[row]) for row in range(gu)]
+    pairs += [(density.at[row, far_col], across.at[at]) for at, row in enumerate([0, gu - 1, *range(1, gu - 1)])]
+    pairs.append((density.at[(gu - 1) * (1 - odd("pu"))], pu_near))
+    pairs.append((density.at[(gu - 1) * odd("pu")], pu_far))
+    for copy in run_copies(pairs, sems):
+        copy.wait()
+
+
+def patch_edges(density):
+    gu, gv, size, rhs = density.shape
+    blocks = (gu, gu, gv, gv)
+    return pl.pallas_call(
+        edges_kernel,
+        in_specs=[pl.BlockSpec(memory_space=pltpu.HBM)],
+        out_specs=[pl.BlockSpec(memory_space=pltpu.VMEM)] * len(blocks),
+        out_shape=[jax.ShapeDtypeStruct((count, size, rhs), density.dtype) for count in blocks],
+        scratch_shapes=[pltpu.SemaphoreType.DMA((2 * gu + 2,))],
+        cost_estimate=cost(2.5),
+        compiler_params=pltpu.CompilerParams(vmem_limit_bytes=merge_vmem),
+    )(in_hbm(density))
 
 
 natural = ((1,), (0,))
@@ -467,7 +513,7 @@
             pltpu.VMEM((rank, rank), jnp.float32),
             pltpu.VMEM((2 * rank, cols - tail_lanes), jnp.float32),
         ],
-        cost_estimate=cost(4 if level < 2 else 2),
+        cost_estimate=cost((9, 1.5)[level] if level < 2 else 0.5),
         compiler_params=pltpu.CompilerParams(vmem_limit_bytes=merge_vmem),
     )(mine, other, sketch, *paths)
 
@@ -483,6 +529,12 @@
     pairs = []
     for low in range(int(far), count - 1, 2):
         pairs += [(low, low + 1), (low + 1, low)]
+    return lax.ppermute(value, axis, pairs)
+
+
+def relayed(value, axis):
+    count = lax.axis_size(axis)
+    pairs = [(at, at + 2) for at in range(1, count - 2, 2)] + [(at, at - 2) for at in range(2, count, 2)]
     return lax.ppermute(value, axis, pairs)
 
 
@@ -512,11 +564,12 @@
         return keep + from_partner(give, "pv", level)
 
     rows = far_left.shape[2]
-    left, sketch, beside, ends, mids, pu_near, pu_far = first_step(
-        far_left, sketch, density, patch_order, (pu_count, pv_count)
-    )
+    left, sketch = coded_leaf(far_left, sketch, patch_order, (pu_count, pv_count))
     other = partner(left, 0)
+    density, left = tied(density, left)
+    beside, across, pu_near, pu_far = patch_edges(density)
     beside = swapped(beside, "pv", False)
+    across = relayed(across, "pv")
     pu_near = swapped(pu_near, "pu", False)
     pu_far = swapped(pu_far, "pu", True)
 
@@ -533,9 +586,9 @@
         if level == 1:
             corrected, coef = near_middle(density, near_blocks, far_right, links, corrected)
         elif level == 2:
-            ends, mids, left = tied(ends, mids, left)
-            ends = swapped(ends, "pv", True)
-            mids = swapped(mids, "pv", True)
+            across, left = tied(across, left)
+            ends = swapped(across[:2], "pv", False)
+            mids = swapped(across[2:], "pv", False)
             corrected, coef = near_rows(density, pu_near, pu_far, near_blocks, far_right, links, corrected)
         elif last:
             corner_near, corner_far = patch_corners(beside, ends)

time: 111 us -> 121 us (1.090)
  waiting for transfers between devices: 19.2 us -> 30.6 us
  starting transfers between devices: 28.4 us -> 22.9 us
  Pallas kernels: 57.8 us -> 60.8 us
    ppermute x10, waiting for transfers between devices: 19.2 us -> 30.6 us  [from_partner(): return lax.ppermute(value, axis, pairs)]
    ppermute x10, starting transfers between devices: 23.3 us -> 13.3 us  [from_partner(): return lax.ppermute(value, axis, pairs)]
    ppermute x7, starting transfers between devices: 5.04 us -> 8.36 us  [swapped(): return lax.ppermute(value, axis, pairs)]
    pallas_call x5, Pallas kernels: 30.6 us -> 32.9 us  [merge(): pl.pallas_call(functools.partial(merge_kernel, bool(paths), bool(last_row...]
    ppermute x0 -> x1, starting transfers between devices: none -> 1.29 us  [relayed(): return lax.ppermute(value, axis, pairs)]
    pallas_call x1 -> x2, Pallas kernels: 3.53 us -> 4.06 us  [the longest x1 2.58 us: patch_edges(): pl.pallas_call(edges_kernel, in_specs=[pl.BlockSpec(memory_space=pltpu.HB...]
  transfers between devices with their start and end apart: 17 -> 18, of which waited for: 6 -> 6; matrix products, arithmetic and copies ran while one was open for 0% -> 1% of each run, Pallas kernels for 49% -> 49%
where the time goes in v7:
time: 121 us; the launch traced here: 120 us
  Pallas kernels  60.8 us (50%)
  waiting for transfers between devices  30.6 us (25%)
  starting transfers between devices  22.9 us (19%)
  local copies, waits for them, and re-layouts  3.6 us (3%)
  matrix products  1.53 us (1%)
    pallas_call x5, Pallas kernels, merge(): pl.pallas_call(functools.partial(merge_kernel, bool(paths), bool(last_row...  32.9 us
    ppermute x10, waiting for transfers between devices, from_partner(): return lax.ppermute(value, axis, pairs)  30.6 us
    pallas_call x3, Pallas kernels, near_part(): pl.pallas_call(functools.partial(near_kernel, plan, len(sources)), grid_s...  22.8 us
    ppermute x10, starting transfers between devices, from_partner(): return lax.ppermute(value, axis, pairs)  13.3 us
    ppermute x7, starting transfers between devices, swapped(): return lax.ppermute(value, axis, pairs)  8.36 us
    pallas_call x1, Pallas kernels, patch_edges(): pl.pallas_call(edges_kernel, in_specs=[pl.BlockSpec(memory_space=pltpu.HB...  2.58 us
    unnamed x28, local copies, waits for them, and re-layouts  2.57 us
  transfers between devices with their start and end apart: 18, of which 6 were waited for; matrix products, arithmetic and copies ran while one was open for 1% of the time, Pallas kernels for 49%

profile of v7, /device:TPU:0, one launch (start us, length us, event | category | flops | bytes accessed | tf_op | source)
XLA Modules:
  0.0 120.5 jit_solution(853105777759208964)
XLA Ops:
  0.6 1.5 %shard_map.86 = (s16[128,1152]{1,0:T(8,128)(2,1)S(1)}, f32[128,256]{1,0:T(8,128)S(1)}) custom-call(s32[32]{0:T(128)} %order_hbm.1, f32[1,1,1024,128]{3,2,1,0:T(8,128)} %value_hbm.1, f32[256,128]{1,0:T(8,128)} %sketch_hbm.1), custom_call_target="tpu_custom_call" | custom-call | flops 1650000000 | tf_op jit(solution)/shard_map/pallas_call | solution.py:417
  2.1 3.0 %collective-permute-start.1 = (s16[128,1152]{1,0:T(8,128)(2,1)S(1)}, s16[128,1152]{1,0:T(8,128)(2,1)S(1)}, u32[]{:S(2)}, u32[]{:S(2)}) collective-permute-start(s16[128,1152]{1,0:T(8,128)(2,1)S(1)} %get-tuple-element.49.mine_ref), channel_id=1, source_target_pairs={{0,1},{1,0},{2,3},{3,2},{4,5},{5,4},{6,7},{7,6},{8,9},{9,8},{10,11... | collective-permute-start | bytes 884744 | tf_op jit(solution)/shard_map/ppermute | solution.py:524
  5.1 2.6 %shard_map.87 = (bf16[6,128,768]{2,1,0:T(8,128)(2,1)S(1)}, bf16[6,128,768]{2,1,0:T(8,128)(2,1)S(1)}, bf16[6,128,768]{2,1,0:T(8,128)(2,1)S(1)}, bf16[6,128,768]{2,1,0:T(8,128)(2,1)S(1)}) custom-call(bf16[6,6,128,768]{3,2,1,0:T(8,128)(2,1)} %refs_0_.2), custom_call_target="tpu_custom_call" | custom-call | flops 2750000128 | tf_op jit(solution)/shard_map/pallas_call | solution.py:451
  7.8 0.7 collective-permute-start.5
  8.5 1.3 %collective-permute-start = (bf16[6,128,768]{2,1,0:T(8,128)(2,1)S(1)}, bf16[6,128,768]{2,1,0:T(8,128)(2,1)S(1)}, u32[]{:S(2)}, u32[]{:S(2)}) collective-permute-start(bf16[6,128,768]{2,1,0:T(8,128)(2,1)S(1)} %get-tuple-element.48), channel_id=1, source_target_pairs={{1,3},{3,5},{5,7},{2,0},{4,2},{6,4},{9,11},{11,13},{13,15},{10,8},... | collective-permute-start | bytes 3538952 | tf_op jit(solution)/shard_map/ppermute | solution.py:538
  9.8 2.9 %collective-permute-start.7 = (bf16[6,128,768]{2,1,0:T(8,128)(2,1)S(1)}, bf16[6,128,768]{2,1,0:T(8,128)(2,1)S(1)}, u32[]{:S(2)}, u32[]{:S(2)}) collective-permute-start(bf16[6,128,768]{2,1,0:T(8,128)(2,1)S(1)} %get-tuple-element.70), channel_id=1, source_target_pairs={{0,1},{1,0},{2,3},{3,2},{4,5},{5,4},{6,7},{7,6},{8,9},{9,8},{10,11... | collective-permute-start | bytes 3538952 | tf_op jit(solution)/shard_map/ppermute | solution.py:532
  12.7 6.3 %shard_map.88 = (s16[128,1152]{1,0:T(8,128)(2,1)S(1)}, f32[128,128]{1,0:T(8,128)S(1)}) custom-call(s16[128,1152]{1,0:T(8,128)(2,1)S(1)} %get-tuple-element.49.mine_ref, s16[128,1152]{1,0:T(8,128)(2,1)S(1)} %collective-permute-done.1.other_ref, f32[128,256]{1,0:T(8,128)S(1)} %get-tuple-element.50.sketch_ref), custom_call_target="tpu_custom_call" | custom-call | flops 9900000256 | tf_op jit(solution)/shard_map/pallas_call | solution.py:506
  19.0 1.6 %collective-permute-start.2 = (s16[128,1152]{1,0:T(8,128)(2,1)S(1)}, s16[128,1152]{1,0:T(8,128)(2,1)S(1)}, u32[]{:S(2)}, u32[]{:S(2)}) collective-permute-start(s16[128,1152]{1,0:T(8,128)(2,1)S(1)} %get-tuple-element.52.mine_ref), channel_id=1, source_target_pairs={{0,2},{1,3},{2,0},{3,1},{4,6},{5,7},{6,4},{7,5},{8,10},{9,11},{10,... | collective-permute-start | bytes 884744 | tf_op jit(solution)/shard_map/ppermute | solution.py:524
  20.6 8.5 %shard_map.89 = (bf16[6,6,128,768]{3,2,1,0:T(8,128)(2,1)}, f32[128,768]{1,0:T(8,128)S(1)}) custom-call(s32[6,6,6]{2,1,0:T(8,128)S(1)} %copy-done.6, bf16[6,6,6,128,128]{4,3,2,1,0:T(8,128)(2,1)} %near_hbm.5, bf16[6,6,128,128]{3,2,1,0:T(8,128)(2,1)} %right_hbm.5, bf16[6,6,128,768]{3,2,1,0:T(8,128)(2,1)} %refs_0_.2), custom_call_target="tpu_custom_call" | custom-call | flops 550000000 | tf_op jit(solution)/shard_map/pallas_call | solution.py:134
  29.1 14.6 %collective-permute-done.2.other_ref = s16[128,1152]{1,0:T(8,128)(2,1)S(1)} collective-permute-done((s16[128,1152]{1,0:T(8,128)(2,1)S(1)}, s16[128,1152]{1,0:T(8,128)(2,1)S(1)}, u32[]{:S(2)}, u32[]{:S(2)}) %collective-permute-start.2) | collective-permute-done | bytes 294944 | tf_op jit(solution)/shard_map/ppermute | solution.py:524
  43.7 6.3 %shard_map.90 = (s16[128,1152]{1,0:T(8,128)(2,1)S(1)}, f32[128,128]{1,0:T(8,128)S(1)}) custom-call(s16[128,1152]{1,0:T(8,128)(2,1)S(1)} %get-tuple-element.52.mine_ref, s16[128,1152]{1,0:T(8,128)(2,1)S(1)} %collective-permute-done.2.other_ref, f32[128,256]{1,0:T(8,128)S(1)} %get-tuple-element.50.sketch_ref, f32[128,128]{1,0:T(8,128)S(1)} %get-tuple-element.56.refs_0_), custom_call_target="tpu_custom_call" | custom-call | flops 1650000000 | tf_op jit(solution)/shard_map/pallas_call | solution.py:506
  50.0 2.7 %collective-permute-start.3 = (s16[128,1152]{1,0:T(8,128)(2,1)S(1)}, s16[128,1152]{1,0:T(8,128)(2,1)S(1)}, u32[]{:S(2)}, u32[]{:S(2)}) collective-permute-start(s16[128,1152]{1,0:T(8,128)(2,1)S(1)} %get-tuple-element.59.mine_ref), channel_id=1, source_target_pairs={{0,4},{1,5},{2,6},{3,7},{4,0},{5,1},{6,2},{7,3},{8,12},{9,13},{10,... | collective-permute-start | bytes 884744 | tf_op jit(solution)/shard_map/ppermute | solution.py:524
  52.8 0.9 slice.7
  53.8 2.0 %collective-permute-start.11 = (bf16[4,128,768]{2,1,0:T(8,128)(2,1)}, bf16[4,128,768]{2,1,0:T(8,128)(2,1)}, u32[]{:S(2)}, u32[]{:S(2)}) collective-permute-start(bf16[4,128,768]{2,1,0:T(8,128)(2,1)} %slice.7), channel_id=1, source_target_pairs={{0,1},{1,0},{2,3},{3,2},{4,5},{5,4},{6,7},{7,6},{8,9},{9,8},{10,11... | collective-permute-start | bytes 2359304 | tf_op jit(solution)/shard_map/ppermute | solution.py:532
  55.8 5.7 %shard_map.91 = (bf16[6,6,128,768]{3,2,1,0:T(8,128)(2,1)}, f32[128,768]{1,0:T(8,128)S(1)}) custom-call(s32[6,6,6]{2,1,0:T(8,128)S(1)} %copy-done.6, bf16[6,6,6,128,128]{4,3,2,1,0:T(8,128)(2,1)} %near_hbm.5, bf16[6,6,128,128]{3,2,1,0:T(8,128)(2,1)} %right_hbm.5, bf16[6,6,128,768]{3,2,1,0:T(8,128)(2,1)} %refs_0_.2, ...), custom_call_target="tpu_custom_call", output_to_operand_aliasing={{0}: (6, {})} | custom-call | flops 550000000 | tf_op jit(solution)/shard_map/pallas_call | solution.py:134
  61.5 4.6 %collective-permute-done.3.other_ref = s16[128,1152]{1,0:T(8,128)(2,1)S(1)} collective-permute-done((s16[128,1152]{1,0:T(8,128)(2,1)S(1)}, s16[128,1152]{1,0:T(8,128)(2,1)S(1)}, u32[]{:S(2)}, u32[]{:S(2)}) %collective-permute-start.3) | collective-permute-done | bytes 294944 | tf_op jit(solution)/shard_map/ppermute | solution.py:524
  66.1 6.3 %shard_map.92 = (s16[128,1152]{1,0:T(8,128)(2,1)S(1)}, f32[128,128]{1,0:T(8,128)S(1)}) custom-call(s16[128,1152]{1,0:T(8,128)(2,1)S(1)} %get-tuple-element.59.mine_ref, s16[128,1152]{1,0:T(8,128)(2,1)S(1)} %collective-permute-done.3.other_ref, f32[128,256]{1,0:T(8,128)S(1)} %get-tuple-element.50.sketch_ref, f32[128,128]{1,0:T(8,128)S(1)} %get-tuple-element.66.refs_0_), custom_call_target="tpu_custom_call" | custom-call | flops 550000000 | tf_op jit(solution)/shard_map/pallas_call | solution.py:506
  72.7 1.0 shard_map.94
  73.7 1.4 %collective-permute-start.10 = (bf16[2,128,768]{2,1,0:T(8,128)(2,1)}, bf16[2,128,768]{2,1,0:T(8,128)(2,1)}, u32[]{:S(2)}, u32[]{:S(2)}) collective-permute-start(bf16[2,128,768]{2,1,0:T(8,128)(2,1)} %get-tuple-element.73), channel_id=1, source_target_pairs={{8,16},{16,8},{9,17},{17,9},{10,18},{18,10},{11,19},{19,11},{12,20... | collective-permute-start | bytes 1179656 | tf_op jit(solution)/shard_map/ppermute | solution.py:532
  75.1 1.2 collective-permute-start.9
  76.3 7.0 %shard_map.93 = (s16[128,1152]{1,0:T(8,128)(2,1)}, f32[128,128]{1,0:T(8,128)S(1)}) custom-call(s16[128,1152]{1,0:T(8,128)(2,1)S(1)} %get-tuple-element.67.mine_ref, s16[128,1152]{1,0:T(8,128)(2,1)S(1)} %collective-permute-done.6.other_ref, f32[128,256]{1,0:T(8,128)S(1)} %get-tuple-element.50.sketch_ref), custom_call_target="tpu_custom_call" | custom-call | flops 550000000 | tf_op jit(solution)/shard_map/pallas_call | solution.py:506
  84.0 1.6 %collective-permute-start.12 = (s16[128,1152]{1,0:T(8,128)(2,1)}, s16[128,1152]{1,0:T(8,128)(2,1)}, u32[]{:S(2)}, u32[]{:S(2)}) collective-permute-start(s16[128,1152]{1,0:T(8,128)(2,1)} %get-tuple-element.83.mine_ref), channel_id=1, source_target_pairs={{0,16},{8,24},{16,0},{24,8},{1,17},{9,25},{17,1},{25,9},{2,18},{10... | collective-permute-start | bytes 884744 | tf_op jit(solution)/shard_map/ppermute | solution.py:524
  85.6 1.0 copy-done.5
  87.4 8.6 %shard_map.95 = (bf16[6,6,128,768]{3,2,1,0:T(8,128)(2,1)}, f32[128,768]{1,0:T(8,128)S(1)}) custom-call(s32[6,6,6]{2,1,0:T(8,128)S(1)} %copy-done.7, bf16[6,6,6,128,128]{4,3,2,1,0:T(8,128)(2,1)} %near_hbm.5, bf16[6,6,128,128]{3,2,1,0:T(8,128)(2,1)} %right_hbm.5, bf16[6,6,128,768]{3,2,1,0:T(8,128)(2,1)} %refs_0_.2, ...), custom_call_target="tpu_custom_call", output_to_operand_aliasing={{0}: (11, {})} | custom-call | flops 550000000 | tf_op jit(solution)/shard_map/pallas_call | solution.py:134
  96.9 7.0 %shard_map.96 = (f32[128,256]{1,0:T(8,128)S(1)}, f32[128,128]{1,0:T(8,128)S(1)}) custom-call(s16[128,1152]{1,0:T(8,128)(2,1)} %get-tuple-element.83.mine_ref, s16[128,1152]{1,0:T(8,128)(2,1)} %collective-permute-done.12.other_ref, f32[128,256]{1,0:T(8,128)S(1)} %copy-done.11, f32[128,128]{1,0:T(8,128)S(1)} %copy-done.13), custom_call_target="tpu_custom_call" | custom-call | flops 550000000 | tf_op jit(solution)/shard_map/pallas_call | solution.py:506
  103.9 1.2 collective-permute-start.14
  105.0 3.8 %collective-permute-done.14 = f32[2,96,128]{2,1,0:T(8,128)S(1)} collective-permute-done((f32[2,96,128]{2,1,0:T(8,128)S(1)}, f32[2,96,128]{2,1,0:T(8,128)S(1)}, u32[]{:S(2)}, u32[]{:S(2)}) %collective-permute-start.14) | collective-permute-done | bytes 98336 | tf_op jit(solution)/shard_map/ppermute | solution.py:524
  108.9 2.5 %collective-permute-start.15 = (f32[1,96,128]{2,1,0:T(8,128)S(1)}, f32[1,96,128]{2,1,0:T(8,128)S(1)}, u32[]{:S(2)}, u32[]{:S(2)}) collective-permute-start(f32[1,96,128]{2,1,0:T(8,128)S(1)} %constant_dynamic-slice_fusion), channel_id=1, source_target_pairs={{0,4},{1,5},{2,6},{3,7},{4,0},{5,1},{6,2},{7,3},{8,12},{9,13},{10,... | collective-permute-start | bytes 147464 | tf_op jit(solution)/shard_map/ppermute | solution.py:524
  111.4 2.6 %collective-permute-done.15 = f32[1,96,128]{2,1,0:T(8,128)S(1)} collective-permute-done((f32[1,96,128]{2,1,0:T(8,128)S(1)}, f32[1,96,128]{2,1,0:T(8,128)S(1)}, u32[]{:S(2)}, u32[]{:S(2)}) %collective-permute-start.15) | collective-permute-done | bytes 49184 | tf_op jit(solution)/shard_map/ppermute | solution.py:524
  114.3 1.2 %collective-permute-done.16 = f32[96,128]{1,0:T(8,128)S(1)} collective-permute-done((f32[96,128]{1,0:T(8,128)S(1)}, f32[96,128]{1,0:T(8,128)S(1)}, u32[]{:S(2)}, u32[]{:S(2)}) %collective-permute-start.16) | collective-permute-done | bytes 49184 | tf_op jit(solution)/shard_map/ppermute | solution.py:524
  115.8 3.8 %collective-permute-done.17 = f32[96,128]{1,0:T(8,128)S(1)} collective-permute-done((f32[96,128]{1,0:T(8,128)S(1)}, f32[96,128]{1,0:T(8,128)S(1)}, u32[]{:S(2)}, u32[]{:S(2)}) %collective-permute-start.17) | collective-permute-done | bytes 49184 | tf_op jit(solution)/shard_map/ppermute | solution.py:524
  119.6 0.8 fusion.5
  (54 shorter events, 3.3 us)
Async XLA Ops:
  2.1 74.2 %copy-start.10 = (f32[128,256]{1,0:T(8,128)}, f32[128,256]{1,0:T(8,128)S(1)}, u32[]{:S(2)}) copy-start(f32[128,256]{1,0:T(8,128)S(1)} %get-tuple-element.50.sketch_ref) | copy-start | bytes 393220
  2.1 10.6 %collective-permute-start.1 = (s16[128,1152]{1,0:T(8,128)(2,1)S(1)}, s16[128,1152]{1,0:T(8,128)(2,1)S(1)}, u32[]{:S(2)}, u32[]{:S(2)}) collective-permute-start(s16[128,1152]{1,0:T(8,128)(2,1)S(1)} %get-tuple-element.49.mine_ref), channel_id=1, source_target_pairs={{0,1},{1,0},{2,3},{3,2},{4,5},{5,4},{6,7},{7,6},{8,9},{9,8},{10,11... | collective-permute-start | bytes 884744 | tf_op jit(solution)/shard_map/ppermute | solution.py:524
  7.7 46.0 %collective-permute-start.4 = (bf16[6,128,768]{2,1,0:T(8,128)(2,1)S(1)}, bf16[6,128,768]{2,1,0:T(8,128)(2,1)S(1)}, u32[]{:S(2)}, u32[]{:S(2)}) collective-permute-start(bf16[6,128,768]{2,1,0:T(8,128)(2,1)S(1)} %get-tuple-element.61), channel_id=1, source_target_pairs={{0,8},{8,0},{16,24},{24,16},{1,9},{9,1},{17,25},{25,17},{2,10},{10... | collective-permute-start | bytes 3538952 | tf_op jit(solution)/shard_map/ppermute | solution.py:532
  7.8 48.0 %collective-permute-start.5 = (bf16[6,128,768]{2,1,0:T(8,128)(2,1)S(1)}, bf16[6,128,768]{2,1,0:T(8,128)(2,1)S(1)}, u32[]{:S(2)}, u32[]{:S(2)}) collective-permute-start(bf16[6,128,768]{2,1,0:T(8,128)(2,1)S(1)} %get-tuple-element.62), channel_id=1, source_target_pairs={{8,16},{16,8},{9,17},{17,9},{10,18},{18,10},{11,19},{19,11},{12,20... | collective-permute-start | bytes 3538952 | tf_op jit(solution)/shard_map/ppermute | solution.py:532
  8.5 44.2 %collective-permute-start = (bf16[6,128,768]{2,1,0:T(8,128)(2,1)S(1)}, bf16[6,128,768]{2,1,0:T(8,128)(2,1)S(1)}, u32[]{:S(2)}, u32[]{:S(2)}) collective-permute-start(bf16[6,128,768]{2,1,0:T(8,128)(2,1)S(1)} %get-tuple-element.48), channel_id=1, source_target_pairs={{1,3},{3,5},{5,7},{2,0},{4,2},{6,4},{9,11},{11,13},{13,15},{10,8},... | collective-permute-start | bytes 3538952 | tf_op jit(solution)/shard_map/ppermute | solution.py:538
  9.8 62.8 %collective-permute-start.7 = (bf16[6,128,768]{2,1,0:T(8,128)(2,1)S(1)}, bf16[6,128,768]{2,1,0:T(8,128)(2,1)S(1)}, u32[]{:S(2)}, u32[]{:S(2)}) collective-permute-start(bf16[6,128,768]{2,1,0:T(8,128)(2,1)S(1)} %get-tuple-element.70), channel_id=1, source_target_pairs={{0,1},{1,0},{2,3},{3,2},{4,5},{5,4},{6,7},{7,6},{8,9},{9,8},{10,11... | collective-permute-start | bytes 3538952 | tf_op jit(solution)/shard_map/ppermute | solution.py:532
  12.7 7.9 %copy-start.6 = (s32[6,6,6]{2,1,0:T(8,128)S(1)}, s32[6,6,6]{2,1,0:T(8,128)}, u32[]{:S(2)}) copy-start(s32[6,6,6]{2,1,0:T(8,128)} %nb_ref.2) | copy-start | bytes 2596
  19.0 24.7 %collective-permute-start.2 = (s16[128,1152]{1,0:T(8,128)(2,1)S(1)}, s16[128,1152]{1,0:T(8,128)(2,1)S(1)}, u32[]{:S(2)}, u32[]{:S(2)}) collective-permute-start(s16[128,1152]{1,0:T(8,128)(2,1)S(1)} %get-tuple-element.52.mine_ref), channel_id=1, source_target_pairs={{0,2},{1,3},{2,0},{3,1},{4,6},{5,7},{6,4},{7,5},{8,10},{9,11},{10,... | collective-permute-start | bytes 884744 | tf_op jit(solution)/shard_map/ppermute | solution.py:524
  29.1 21.0 %copy-start = (f32[128,768]{1,0:T(8,128)}, f32[128,768]{1,0:T(8,128)S(1)}, u32[]{:S(2)}) copy-start(f32[128,768]{1,0:T(8,128)S(1)} %get-tuple-element.76) | copy-start | bytes 1179652
  50.0 16.1 %collective-permute-start.3 = (s16[128,1152]{1,0:T(8,128)(2,1)S(1)}, s16[128,1152]{1,0:T(8,128)(2,1)S(1)}, u32[]{:S(2)}, u32[]{:S(2)}) collective-permute-start(s16[128,1152]{1,0:T(8,128)(2,1)S(1)} %get-tuple-element.59.mine_ref), channel_id=1, source_target_pairs={{0,4},{1,5},{2,6},{3,7},{4,0},{5,1},{6,2},{7,3},{8,12},{9,13},{10,... | collective-permute-start | bytes 884744 | tf_op jit(solution)/shard_map/ppermute | solution.py:524
  52.7 19.9 %collective-permute-start.8 = (bf16[2,128,768]{2,1,0:T(8,128)(2,1)S(1)}, bf16[2,128,768]{2,1,0:T(8,128)(2,1)S(1)}, u32[]{:S(2)}, u32[]{:S(2)}) collective-permute-start(bf16[2,128,768]{2,1,0:T(8,128)(2,1)S(1)} %slice.6), channel_id=1, source_target_pairs={{0,1},{1,0},{2,3},{3,2},{4,5},{5,4},{6,7},{7,6},{8,9},{9,8},{10,11... | collective-permute-start | bytes 1179656 | tf_op jit(solution)/shard_map/ppermute | solution.py:532
  53.8 31.9 %collective-permute-start.11 = (bf16[4,128,768]{2,1,0:T(8,128)(2,1)}, bf16[4,128,768]{2,1,0:T(8,128)(2,1)}, u32[]{:S(2)}, u32[]{:S(2)}) collective-permute-start(bf16[4,128,768]{2,1,0:T(8,128)(2,1)} %slice.7), channel_id=1, source_target_pairs={{0,1},{1,0},{2,3},{3,2},{4,5},{5,4},{6,7},{7,6},{8,9},{9,8},{10,11... | collective-permute-start | bytes 2359304 | tf_op jit(solution)/shard_map/ppermute | solution.py:532
  61.5 12.1 %copy-start.2 = (f32[128,768]{1,0:T(8,128)}, f32[128,768]{1,0:T(8,128)S(1)}, u32[]{:S(2)}) copy-start(f32[128,768]{1,0:T(8,128)S(1)} %get-tuple-element.77) | copy-start | bytes 1179652
  72.4 1.2 %copy-start.8 = (f32[128,128]{1,0:T(8,128)}, f32[128,128]{1,0:T(8,128)S(1)}, u32[]{:S(2)}) copy-start(f32[128,128]{1,0:T(8,128)S(1)} %get-tuple-element.80) | copy-start | bytes 196612
  72.5 3.8 %collective-permute-start.6 = (s16[128,1152]{1,0:T(8,128)(2,1)S(1)}, s16[128,1152]{1,0:T(8,128)(2,1)S(1)}, u32[]{:S(2)}, u32[]{:S(2)}) collective-permute-start(s16[128,1152]{1,0:T(8,128)(2,1)S(1)} %get-tuple-element.67.mine_ref), channel_id=1, source_target_pairs={{0,8},{8,0},{16,24},{24,16},{1,9},{9,1},{17,25},{25,17},{2,10},{10... | collective-permute-start | bytes 884744 | tf_op jit(solution)/shard_map/ppermute | solution.py:524
  72.6 1.0 copy-start.4
  73.7 11.9 %collective-permute-start.10 = (bf16[2,128,768]{2,1,0:T(8,128)(2,1)}, bf16[2,128,768]{2,1,0:T(8,128)(2,1)}, u32[]{:S(2)}, u32[]{:S(2)}) collective-permute-start(bf16[2,128,768]{2,1,0:T(8,128)(2,1)} %get-tuple-element.73), channel_id=1, source_target_pairs={{8,16},{16,8},{9,17},{17,9},{10,18},{18,10},{11,19},{19,11},{12,20... | collective-permute-start | bytes 1179656 | tf_op jit(solution)/shard_map/ppermute | solution.py:532
  75.1 10.5 %collective-permute-start.9 = (bf16[2,128,768]{2,1,0:T(8,128)(2,1)}, bf16[2,128,768]{2,1,0:T(8,128)(2,1)}, u32[]{:S(2)}, u32[]{:S(2)}) collective-permute-start(bf16[2,128,768]{2,1,0:T(8,128)(2,1)} %get-tuple-element.72), channel_id=1, source_target_pairs={{0,8},{8,0},{16,24},{24,16},{1,9},{9,1},{17,25},{25,17},{2,10},{10... | collective-permute-start | bytes 1179656 | tf_op jit(solution)/shard_map/ppermute | solution.py:532
  83.3 0.6 copy-start.12
  84.0 12.0 %collective-permute-start.12 = (s16[128,1152]{1,0:T(8,128)(2,1)}, s16[128,1152]{1,0:T(8,128)(2,1)}, u32[]{:S(2)}, u32[]{:S(2)}) collective-permute-start(s16[128,1152]{1,0:T(8,128)(2,1)} %get-tuple-element.83.mine_ref), channel_id=1, source_target_pairs={{0,16},{8,24},{16,0},{24,8},{1,17},{9,25},{17,1},{25,9},{2,18},{10... | collective-permute-start | bytes 884744 | tf_op jit(solution)/shard_map/ppermute | solution.py:524
  85.6 1.0 copy-start.5
  86.6 0.7 copy-start.7
  87.3 8.6 %copy-start.1 = (f32[128,768]{1,0:T(8,128)S(1)}, f32[128,768]{1,0:T(8,128)}, u32[]{:S(2)}) copy-start(f32[128,768]{1,0:T(8,128)} %copy-done) | copy-start | bytes 1179652
  87.4 8.6 %copy-start.3 = (f32[128,768]{1,0:T(8,128)S(1)}, f32[128,768]{1,0:T(8,128)}, u32[]{:S(2)}) copy-start(f32[128,768]{1,0:T(8,128)} %copy-done.2) | copy-start | bytes 1179652
  87.4 8.6 %copy-start.9 = (f32[128,128]{1,0:T(8,128)S(1)}, f32[128,128]{1,0:T(8,128)}, u32[]{:S(2)}) copy-start(f32[128,128]{1,0:T(8,128)} %copy-done.8) | copy-start | bytes 196612
  95.9 0.9 copy-start.11
  96.0 0.9 copy-start.13
  96.5 7.3 %collective-permute-start.13 = (f32[4,96,128]{2,1,0:T(8,128)S(1)}, f32[4,96,128]{2,1,0:T(8,128)S(1)}, u32[]{:S(2)}, u32[]{:S(2)}) collective-permute-start(f32[4,96,128]{2,1,0:T(8,128)S(1)} %dynamic-slice_bitcast_fusion), channel_id=1, source_target_pairs={{0,1},{1,0},{2,3},{3,2},{4,5},{5,4},{6,7},{7,6},{8,9},{9,8},{10,11... | collective-permute-start | bytes 589832 | tf_op jit(solution)/shard_map/ppermute | solution.py:524
  103.9 5.0 %collective-permute-start.14 = (f32[2,96,128]{2,1,0:T(8,128)S(1)}, f32[2,96,128]{2,1,0:T(8,128)S(1)}, u32[]{:S(2)}, u32[]{:S(2)}) collective-permute-start(f32[2,96,128]{2,1,0:T(8,128)S(1)} %dynamic-slice_bitcast_fusion.1), channel_id=1, source_target_pairs={{0,2},{1,3},{2,0},{3,1},{4,6},{5,7},{6,4},{7,5},{8,10},{9,11},{10,... | collective-permute-start | bytes 294920 | tf_op jit(solution)/shard_map/ppermute | solution.py:524
  108.9 5.1 %collective-permute-start.15 = (f32[1,96,128]{2,1,0:T(8,128)S(1)}, f32[1,96,128]{2,1,0:T(8,128)S(1)}, u32[]{:S(2)}, u32[]{:S(2)}) collective-permute-start(f32[1,96,128]{2,1,0:T(8,128)S(1)} %constant_dynamic-slice_fusion), channel_id=1, source_target_pairs={{0,4},{1,5},{2,6},{3,7},{4,0},{5,1},{6,2},{7,3},{8,12},{9,13},{10,... | collective-permute-start | bytes 147464 | tf_op jit(solution)/shard_map/ppermute | solution.py:524
  114.2 1.3 %collective-permute-start.16 = (f32[96,128]{1,0:T(8,128)S(1)}, f32[96,128]{1,0:T(8,128)S(1)}, u32[]{:S(2)}, u32[]{:S(2)}) collective-permute-start(f32[96,128]{1,0:T(8,128)S(1)} %fusion.3), channel_id=1, source_target_pairs={{0,8},{8,0},{16,24},{24,16},{1,9},{9,1},{17,25},{25,17},{2,10},{10... | collective-permute-start | bytes 147464 | tf_op jit(solution)/shard_map/ppermute | solution.py:524
  115.5 4.2 %collective-permute-start.17 = (f32[96,128]{1,0:T(8,128)S(1)}, f32[96,128]{1,0:T(8,128)S(1)}, u32[]{:S(2)}, u32[]{:S(2)}) collective-permute-start(f32[96,128]{1,0:T(8,128)S(1)} %add.56), channel_id=1, source_target_pairs={{0,16},{8,24},{16,0},{24,8},{1,17},{9,25},{17,1},{25,9},{2,18},{10... | collective-permute-start | bytes 147464 | tf_op jit(solution)/shard_map/ppermute | solution.py:524

commit v8 on v4

--- a/solution.py
+++ b/solution.py
@@ -9,7 +9,7 @@
 
 high = lax.Precision.HIGH
 empty_slot = 9
-near_vmem = 26 * 1024 * 1024
+near_vmem = 18 * 1024 * 1024
 merge_vmem = 12 * 1024 * 1024
 
 
@@ -31,12 +31,13 @@
     return pl.CostEstimate(flops=int(microseconds * 1.1e9), bytes_accessed=0, transcendentals=0)
 
 
-def near_kernel(plan, n_src, nb_ref, near_hbm, right_hbm, *refs):
+def near_kernel(plan, n_src, nb_hbm, near_hbm, right_hbm, *refs):
     steps, spans, parts = plan
     srcs = refs[:n_src]
-    out_ref, coef_ref, ext_ref, near_ref, right_ref, stage_ref, sems, out_sems = refs[-8:]
+    out_ref, coef_ref, nb_ref, ext_ref, near_ref, right_ref, stage_ref, sems, out_sems, nb_sem = refs[-10:]
     step = pl.program_id(0)
     count = len(parts)
+    links = pltpu.make_async_copy(nb_hbm, nb_ref, nb_sem)
 
     def fetch(at_step):
         found = []
@@ -62,9 +63,11 @@
 
     @pl.when(step == 0)
     def _():
+        links.start()
         for at_step in range(steps):
             for copy in fetch(at_step):
                 copy.start()
+        links.wait()
 
     for at_step in range(steps):
 
@@ -124,31 +127,30 @@
     gu, gv, slots, size, _ = near_blocks.shape
     rhs = sources[0].shape[-1]
     rank = far_right.shape[-1]
-    args = [near_blocks, far_right, *sources]
-    args = [in_hbm(value) if value.ndim > 3 else value for value in args]
+    args = [neighbours, near_blocks, far_right, *sources]
+    args = [in_hbm(value) if at < 3 or value.ndim > 3 else value for at, value in enumerate(args)]
     aliases = {}
     if prior is not None:
+        aliases = {len(args): 0}
         args.append(prior)
-        aliases = {len(args): 0}
     held = pl.BlockSpec(memory_space=pltpu.HBM)
     return pl.pallas_call(
         functools.partial(near_kernel, plan, len(sources)),
-        grid_spec=pltpu.PrefetchScalarGridSpec(
-            num_scalar_prefetch=1,
-            grid=(steps,),
-            in_specs=[held, held]
-            + [held if source.ndim == 4 else pl.BlockSpec(memory_space=pl.ANY) for source in sources]
-            + [held] * len(aliases),
-            out_specs=[held, pl.BlockSpec((rank, rhs), lambda i, nb: (0, 0))],
-            scratch_shapes=[
-                pltpu.VMEM((*ext_shape, size, rhs), jnp.bfloat16),
-                pltpu.VMEM((steps, count, slots, size, size), jnp.bfloat16),
-                pltpu.VMEM((steps, count, size, rank), jnp.bfloat16),
-                pltpu.VMEM((2, count, size, rhs), jnp.bfloat16),
-                pltpu.SemaphoreType.DMA((len(spans) + 2 * steps * count,)),
-                pltpu.SemaphoreType.DMA((2, count)),
-            ],
-        ),
+        grid=(steps,),
+        in_specs=[held] * 3
+        + [held if source.ndim == 4 else pl.BlockSpec(memory_space=pl.ANY) for source in sources]
+        + [held] * len(aliases),
+        out_specs=[held, pl.BlockSpec((rank, rhs), lambda i: (0, 0))],
+        scratch_shapes=[
+            pltpu.SMEM(neighbours.shape, jnp.int32),
+            pltpu.VMEM((*ext_shape, size, rhs), jnp.bfloat16),
+            pltpu.VMEM((steps, count, slots, size, size), jnp.bfloat16),
+            pltpu.VMEM((steps, count, size, rank), jnp.bfloat16),
+            pltpu.VMEM((2, count, size, rhs), jnp.bfloat16),
+            pltpu.SemaphoreType.DMA((len(spans) + 2 * steps * count,)),
+            pltpu.SemaphoreType.DMA((2, count)),
+            pltpu.SemaphoreType.DMA,
+        ],
         out_shape=[
             jax.ShapeDtypeStruct((gu, gv, size, rhs), jnp.bfloat16),
             jax.ShapeDtypeStruct((rank, rhs), jnp.float32),
@@ -158,7 +160,7 @@
         compiler_params=pltpu.CompilerParams(
             dimension_semantics=("arbitrary",), vmem_limit_bytes=near_vmem
         ),
-    )(neighbours, *args)
+    )(*args)
 
 
 def odd(axis):
@@ -174,7 +176,7 @@
     spans = [(max(row - 2, 0), row_span(row, row)) for row in range(gu)]
     parts = [(1, 1, lambda col=col: col, 1, 1, col) for col in range(1, gv - 1)]
     plan = (gu - 2, spans, parts)
-    return near_part((density,), plan, (gu, gv), near_blocks, far_right, neighbours, prior, 8)
+    return near_part((density,), plan, (gu, gv), near_blocks, far_right, neighbours, prior, 0.5)
 
 
 def near_rows(density, pu_near, pu_far, near_blocks, far_right, neighbours, prior):
@@ -184,7 +186,7 @@
     spans.append((0, lambda srcs, ext: (srcs[2], ext.at[5 * odd("pu")])))
     parts = [(0, gu - 1, lambda col=col: col, 1, 3, col) for col in range(1, gv - 1)]
     plan = (2, spans, parts)
-    return near_part((density, pu_near, pu_far), plan, (6, gv), near_blocks, far_right, neighbours, prior, 1.5)
+    return near_part((density, pu_near, pu_far), plan, (6, gv), near_blocks, far_right, neighbours, prior, 0.5)
 
 
 def near_columns(density, pu_near, pu_far, corner_near, corner_far, beside, ends, mids, near_blocks, far_right, neighbours, prior):
@@ -235,7 +237,7 @@
         parts += [(row, per_step, col, row + 1, per_step, 3 * far + 1) for row in range(per_step)]
     plan = (gu // per_step, spans, parts)
     sources = (density, pu_near, pu_far, corner_near, corner_far, beside, ends, mids)
-    return near_part(sources, plan, (gu + 2, 6), near_blocks, far_right, neighbours, prior, 1.5)
+    return near_part(sources, plan, (gu + 2, 6), near_blocks, far_right, neighbours, prior, 0.5)
 
 
 def corners_kernel(beside, ends, to_near, to_far):
@@ -359,58 +361,72 @@
     return value, tail[:, tail_lanes - 1 :]
 
 
-def first_kernel(counts, order_hbm, value_hbm, sketch_hbm, density, code_ref, sketch_ref, *refs):
-    beside, ends, mids, pu_near, pu_far, order, value, sketch, sems = refs
-    gu, gv = density.shape[:2]
-    near_col = (gv - 1) * (1 - odd("pv"))
-    far_col = (gv - 1) * odd("pv")
-    pairs = [(value_hbm.at[0, 0], value), (order_hbm, order), (sketch_hbm, sketch)]
-    inputs = len(pairs)
-    pairs += [(density.at[row, near_col], beside.at[row]) for row in range(gu)]
-    pairs.append((density.at[(gu - 1) * (1 - odd("pu"))], pu_near))
-    pairs.append((density.at[(gu - 1) * odd("pu")], pu_far))
-    pairs += [(density.at[(gu - 1) * row, far_col], ends.at[row]) for row in range(2)]
-    pairs += [(density.at[row + 1, far_col], mids.at[row]) for row in range(gu - 2)]
+def run_copies(pairs, sems):
     copies = [
         pltpu.make_async_copy(source, target, sems.at[index])
         for index, (source, target) in enumerate(pairs)
     ]
     for copy in copies:
         copy.start()
-    for copy in copies[:inputs]:
+    return copies
+
+
+def leaf_kernel(counts, order_hbm, value_hbm, sketch_hbm, code_ref, sketch_ref, order, value, sketch, sems):
+    pairs = [(value_hbm.at[0, 0], value), (order_hbm, order), (sketch_hbm, sketch)]
+    for copy in run_copies(pairs, sems):
         copy.wait()
     key = order[lax.axis_index("pu") * counts[1] + lax.axis_index("pv")]
     encode(jnp.transpose(value[...]), key.astype(jnp.float32), code_ref)
     sketch_ref[...] = jnp.transpose(sketch[...])
-    for copy in copies[inputs:]:
-        copy.wait()
-
-
-def first_step(value, sketch, density, order, counts):
+
+
+def coded_leaf(value, sketch, order, counts):
     rows, cols = value.shape[2:]
-    gu, gv, size, rhs = density.shape
-    blocks = (gu, 2, gu - 2, gv, gv)
     whole = pl.BlockSpec(memory_space=pltpu.VMEM)
     held = pl.BlockSpec(memory_space=pltpu.HBM)
-    args = [in_hbm(array) for array in (order, value, sketch, density)]
     return pl.pallas_call(
-        functools.partial(first_kernel, counts),
-        in_specs=[held] * len(args),
-        out_specs=[whole] * (2 + len(blocks)),
+        functools.partial(leaf_kernel, counts),
+        in_specs=[held] * 3,
+        out_specs=[whole] * 2,
         out_shape=[
             jax.ShapeDtypeStruct((cols, rows + tail_lanes), jnp.int16),
             jax.ShapeDtypeStruct(sketch.shape[::-1], jnp.float32),
-        ]
-        + [jax.ShapeDtypeStruct((count, size, rhs), density.dtype) for count in blocks],
+        ],
         scratch_shapes=[
             pltpu.SMEM(order.shape, jnp.int32),
             pltpu.VMEM((rows, cols), jnp.float32),
             pltpu.VMEM(sketch.shape, jnp.float32),
-            pltpu.SemaphoreType.DMA((2 * gu + 5,)),
+            pltpu.SemaphoreType.DMA((3,)),
         ],
-        cost_estimate=cost(3),
+        cost_estimate=cost(1.5),
         compiler_params=pltpu.CompilerParams(vmem_limit_bytes=merge_vmem),
-    )(*args)
+    )(in_hbm(order), in_hbm(value), in_hbm(sketch))
+
+
+def edges_kernel(density, beside, ends, mids, pu_near, pu_far, sems):
+    gu, gv = density.shape[:2]
+    near_col = (gv - 1) * (1 - odd("pv"))
+    far_col = (gv - 1) * odd("pv")
+    pairs = [(density.at[(gu - 1) * (1 - odd("pu"))], pu_near), (density.at[(gu - 1) * odd("pu")], pu_far)]
+    pairs += [(density.at[row, near_col], beside.at[row]) for row in range(gu)]
+    pairs += [(density.at[(gu - 1) * row, far_col], ends.at[row]) for row in range(2)]
+    pairs += [(density.at[row + 1, far_col], mids.at[row]) for row in range(gu - 2)]
+    for copy in run_copies(pairs, sems):
+        copy.wait()
+
+
+def patch_edges(density):
+    gu, gv, size, rhs = density.shape
+    blocks = (gu, 2, gu - 2, gv, gv)
+    return pl.pallas_call(
+        edges_kernel,
+        in_specs=[pl.BlockSpec(memory_space=pltpu.HBM)],
+        out_specs=[pl.BlockSpec(memory_space=pltpu.VMEM)] * len(blocks),
+        out_shape=[jax.ShapeDtypeStruct((count, size, rhs), density.dtype) for count in blocks],
+        scratch_shapes=[pltpu.SemaphoreType.DMA((2 * gu + 2,))],
+        cost_estimate=cost(2.5),
+        compiler_params=pltpu.CompilerParams(vmem_limit_bytes=merge_vmem),
+    )(in_hbm(density))
 
 
 natural = ((1,), (0,))
@@ -467,15 +483,18 @@
             pltpu.VMEM((rank, rank), jnp.float32),
             pltpu.VMEM((2 * rank, cols - tail_lanes), jnp.float32),
         ],
-        cost_estimate=cost(4 if level < 2 else 2),
+        cost_estimate=cost((9, 1.5)[level] if level < 2 else 0.5),
         compiler_params=pltpu.CompilerParams(vmem_limit_bytes=merge_vmem),
     )(mine, other, sketch, *paths)
 
 
-def from_partner(value, axis, distance):
-    mask = 2**distance
+def from_partner(value, axis, mask):
     pairs = [(source, source ^ mask) for source in range(lax.axis_size(axis))]
     return lax.ppermute(value, axis, pairs)
+
+
+def summed(values):
+    return functools.reduce(lambda a, b: a + b, values)
 
 
 def swapped(value, axis, far):
@@ -501,21 +520,21 @@
 
     def partner(value, level):
         if level < pv_levels:
-            return from_partner(value, "pv", level)
-        return from_partner(value, "pu", level - pv_levels)
-
-    def scattered(share, level):
-        bit = (pv_index >> level) & 1
+            return from_partner(value, "pv", 1 << level)
+        return from_partner(value, "pu", 1 << level - pv_levels)
+
+    def halved(share):
+        bit = pv_index & 1
         pairs = share.reshape(share.shape[0] // 2, 2, *share.shape[1:])
         keep = lax.dynamic_index_in_dim(pairs, bit, 1, keepdims=False)
         give = lax.dynamic_index_in_dim(pairs, 1 - bit, 1, keepdims=False)
-        return keep + from_partner(give, "pv", level)
+        return keep + from_partner(give, "pv", 1)
 
     rows = far_left.shape[2]
-    left, sketch, beside, ends, mids, pu_near, pu_far = first_step(
-        far_left, sketch, density, patch_order, (pu_count, pv_count)
-    )
+    left, sketch = coded_leaf(far_left, sketch, patch_order, (pu_count, pv_count))
     other = partner(left, 0)
+    density, left = tied(density, left)
+    beside, ends, mids, pu_near, pu_far = patch_edges(density)
     beside = swapped(beside, "pv", False)
     pu_near = swapped(pu_near, "pu", False)
     pu_far = swapped(pu_far, "pu", True)
@@ -531,12 +550,12 @@
         if level in (1, 2) or last:
             links, left = tied(neighbours, left)
         if level == 1:
-            corrected, coef = near_middle(density, near_blocks, far_right, links, corrected)
+            corrected, coef = near_rows(density, pu_near, pu_far, near_blocks, far_right, links, corrected)
         elif level == 2:
             ends, mids, left = tied(ends, mids, left)
             ends = swapped(ends, "pv", True)
             mids = swapped(mids, "pv", True)
-            corrected, coef = near_rows(density, pu_near, pu_far, near_blocks, far_right, links, corrected)
+            corrected, coef = near_middle(density, near_blocks, far_right, links, corrected)
         elif last:
             corner_near, corner_far = patch_corners(beside, ends)
             corner_near = swapped(corner_near, "pu", False)
@@ -559,11 +578,11 @@
             other, coef = tied(other, coef)
             coefs.append(coef)
         if last:
-            coef = functools.reduce(lambda a, b: a + b, coefs)
+            coef = summed(coefs)
             share = lax.dot_general(coef, pv_path, (((0,), (1,)), ((), ())), precision=high)
             share = share.reshape(pv_count, rhs // pv_count, -1)
             share, other = tied(share, other)
-            share = scattered(share, 0)
+            share = halved(share)
         path = pv_path if level < pv_levels else pu_path
         last_rows = rows // pu_count if last else 0
         left, path = merge(level, left, other, sketch, path, last_rows)
@@ -573,11 +592,14 @@
             pu_path = path
 
     share, left = tied(share, left)
-    for level in range(1, pv_levels):
-        share = scattered(share, level)
-    root_coef = lax.dot_general(share[0], pu_path, (((1,), (1,)), ((), ())), precision=high)
-    for level in range(pu_levels):
-        root_coef = root_coef + from_partner(root_coef, "pu", level)
+    far_index = pv_index // 2
+    mine = lax.dynamic_index_in_dim(share, far_index, 0, keepdims=False)
+    parts = [mine]
+    for by in range(1, pv_count // 2):
+        give = lax.dynamic_index_in_dim(share, far_index ^ by, 0, keepdims=False)
+        parts.append(from_partner(give, "pv", 2 * by))
+    root_coef = lax.dot_general(summed(parts), pu_path, (((1,), (1,)), ((), ())), precision=high)
+    root_coef = summed([root_coef] + [from_partner(root_coef, "pu", by) for by in range(1, pu_count)])
     far_field = lax.dot_general(left, root_coef, (((0,), (1,)), ((), ())), precision=high)
     return (corrected, far_field)
 

time: 111 us -> 108 us (0.973)
  waiting for transfers between devices: 19.2 us -> 16.5 us
  starting transfers between devices: 28.4 us -> 30.5 us
  Pallas kernels: 57.8 us -> 56.2 us
    ppermute x10 -> x12, waiting for transfers between devices: 19.2 us -> 16.5 us  [from_partner(): return lax.ppermute(value, axis, pairs)]
    ppermute x10 -> x12, starting transfers between devices: 23.3 us -> 25.9 us  [from_partner(): return lax.ppermute(value, axis, pairs)]
    pallas_call x4 -> x5, Pallas kernels: 26.2 us -> 24.6 us  [the longest x3 19.8 us: near_part(): pl.pallas_call(functools.partial(near_kernel, plan, len(sources)), grid=(...]
    unnamed x28 -> x24, local copies, waits for them, and re-layouts: 2.4 us -> 1.66 us
  transfers between devices with their start and end apart: 17 -> 19, of which waited for: 6 -> 7; matrix products, arithmetic and copies ran while one was open for 0% -> 0% of each run, Pallas kernels for 49% -> 51%
where the time goes in v8:
time: 108 us; the launch traced here: 107 us
  Pallas kernels  56.2 us (52%)
  starting transfers between devices  30.5 us (28%)
  waiting for transfers between devices  16.5 us (15%)
  local copies, waits for them, and re-layouts  1.7 us (2%)
  matrix products  1.53 us (1%)
    pallas_call x5, Pallas kernels, merge(): pl.pallas_call(functools.partial(merge_kernel, bool(paths), bool(last_row...  30.6 us
    ppermute x12, starting transfers between devices, from_partner(): return lax.ppermute(value, axis, pairs)  25.9 us
    pallas_call x3, Pallas kernels, near_part(): pl.pallas_call(functools.partial(near_kernel, plan, len(sources)), grid=(...  19.8 us
    ppermute x12, waiting for transfers between devices, from_partner(): return lax.ppermute(value, axis, pairs)  16.5 us
    ppermute x7, starting transfers between devices, swapped(): return lax.ppermute(value, axis, pairs)  4.64 us
    pallas_call x1, Pallas kernels, patch_edges(): pl.pallas_call(edges_kernel, in_specs=[pl.BlockSpec(memory_space=pltpu.HB...  3.32 us
  transfers between devices with their start and end apart: 19, of which 7 were waited for; matrix products, arithmetic and copies ran while one was open for 0% of the time, Pallas kernels for 51%

profile of v8, /device:TPU:0, one launch (start us, length us, event | category | flops | bytes accessed | tf_op | source)
XLA Modules:
  0.0 107.4 jit_solution(13131994790107055366)
XLA Ops:
  0.6 1.5 %shard_map.86 = (s16[128,1152]{1,0:T(8,128)(2,1)S(1)}, f32[128,256]{1,0:T(8,128)S(1)}) custom-call(s32[32]{0:T(128)} %order_hbm.1, f32[1,1,1024,128]{3,2,1,0:T(8,128)} %value_hbm.1, f32[256,128]{1,0:T(8,128)} %sketch_hbm.1), custom_call_target="tpu_custom_call" | custom-call | flops 1650000000 | tf_op jit(solution)/shard_map/pallas_call | solution.py:387
  2.1 3.0 %collective-permute-start = (s16[128,1152]{1,0:T(8,128)(2,1)S(1)}, s16[128,1152]{1,0:T(8,128)(2,1)S(1)}, u32[]{:S(2)}, u32[]{:S(2)}) collective-permute-start(s16[128,1152]{1,0:T(8,128)(2,1)S(1)} %get-tuple-element.52.mine_ref), channel_id=1, source_target_pairs={{0,1},{1,0},{2,3},{3,2},{4,5},{5,4},{6,7},{7,6},{8,9},{9,8},{10,11... | collective-permute-start | bytes 884744 | tf_op jit(solution)/shard_map/ppermute | solution.py:493
  5.1 3.3 %shard_map.87 = (bf16[6,128,768]{2,1,0:T(8,128)(2,1)S(1)}, bf16[2,128,768]{2,1,0:T(8,128)(2,1)S(1)}, bf16[4,128,768]{2,1,0:T(8,128)(2,1)}, bf16[6,128,768]{2,1,0:T(8,128)(2,1)S(1)}, bf16[6,128,768]{2,1,0:T(8,128)(2,1)S(1)}) custom-call(bf16[6,6,128,768]{3,2,1,0:T(8,128)(2,1)} %refs_0_.2), custom_call_target="tpu_custom_call" | custom-call | flops 2750000128 | tf_op jit(solution)/shard_map/pallas_call | solution.py:421
  8.5 0.7 collective-permute-start.3
  9.4 2.8 %collective-permute-done.other_ref = s16[128,1152]{1,0:T(8,128)(2,1)S(1)} collective-permute-done((s16[128,1152]{1,0:T(8,128)(2,1)S(1)}, s16[128,1152]{1,0:T(8,128)(2,1)S(1)}, u32[]{:S(2)}, u32[]{:S(2)}) %collective-permute-start) | collective-permute-done | bytes 294944 | tf_op jit(solution)/shard_map/ppermute | solution.py:493
  12.1 5.8 %shard_map.88 = (s16[128,1152]{1,0:T(8,128)(2,1)S(1)}, f32[128,128]{1,0:T(8,128)S(1)}) custom-call(s16[128,1152]{1,0:T(8,128)(2,1)S(1)} %get-tuple-element.52.mine_ref, s16[128,1152]{1,0:T(8,128)(2,1)S(1)} %collective-permute-done.other_ref, f32[128,256]{1,0:T(8,128)S(1)} %get-tuple-element.53.sketch_ref), custom_call_target="tpu_custom_call" | custom-call | flops 9900000256 | tf_op jit(solution)/shard_map/pallas_call | solution.py:476
  18.0 1.9 %collective-permute-start.1 = (s16[128,1152]{1,0:T(8,128)(2,1)S(1)}, s16[128,1152]{1,0:T(8,128)(2,1)S(1)}, u32[]{:S(2)}, u32[]{:S(2)}) collective-permute-start(s16[128,1152]{1,0:T(8,128)(2,1)S(1)} %get-tuple-element.55.mine_ref), channel_id=1, source_target_pairs={{0,2},{1,3},{2,0},{3,1},{4,6},{5,7},{6,4},{7,5},{8,10},{9,11},{10,... | collective-permute-start | bytes 884744 | tf_op jit(solution)/shard_map/ppermute | solution.py:493
  19.9 4.8 %shard_map.89 = (bf16[6,6,128,768]{3,2,1,0:T(8,128)(2,1)}, f32[128,768]{1,0:T(8,128)S(1)}) custom-call(s32[6,6,6]{2,1,0:T(8,128)} %nb_hbm.2, bf16[6,6,6,128,128]{4,3,2,1,0:T(8,128)(2,1)} %near_hbm.5, bf16[6,6,128,128]{3,2,1,0:T(8,128)(2,1)} %right_hbm.5, bf16[6,6,128,768]{3,2,1,0:T(8,128)(2,1)} %refs_0_.2, ...), custom_call_target="tpu_custom_call" | custom-call | flops 550000000 | tf_op jit(solution)/shard_map/pallas_call | solution.py:137
  24.7 2.5 %collective-permute-done.1.other_ref = s16[128,1152]{1,0:T(8,128)(2,1)S(1)} collective-permute-done((s16[128,1152]{1,0:T(8,128)(2,1)S(1)}, s16[128,1152]{1,0:T(8,128)(2,1)S(1)}, u32[]{:S(2)}, u32[]{:S(2)}) %collective-permute-start.1) | collective-permute-done | bytes 294944 | tf_op jit(solution)/shard_map/ppermute | solution.py:493
  27.2 5.9 %shard_map.90 = (s16[128,1152]{1,0:T(8,128)(2,1)S(1)}, f32[128,128]{1,0:T(8,128)S(1)}) custom-call(s16[128,1152]{1,0:T(8,128)(2,1)S(1)} %get-tuple-element.55.mine_ref, s16[128,1152]{1,0:T(8,128)(2,1)S(1)} %collective-permute-done.1.other_ref, f32[128,256]{1,0:T(8,128)S(1)} %get-tuple-element.53.sketch_ref, f32[128,128]{1,0:T(8,128)S(1)} %get-tuple-element.61.refs_0_), custom_call_target="tpu_custom_call" | custom-call | flops 1650000000 | tf_op jit(solution)/shard_map/pallas_call | solution.py:476
  33.1 2.7 %collective-permute-start.4 = (s16[128,1152]{1,0:T(8,128)(2,1)S(1)}, s16[128,1152]{1,0:T(8,128)(2,1)S(1)}, u32[]{:S(2)}, u32[]{:S(2)}) collective-permute-start(s16[128,1152]{1,0:T(8,128)(2,1)S(1)} %get-tuple-element.64.mine_ref), channel_id=1, source_target_pairs={{0,4},{1,5},{2,6},{3,7},{4,0},{5,1},{6,2},{7,3},{8,12},{9,13},{10,... | collective-permute-start | bytes 884744 | tf_op jit(solution)/shard_map/ppermute | solution.py:493
  36.4 1.6 %collective-permute-start.10 = (bf16[4,128,768]{2,1,0:T(8,128)(2,1)}, bf16[4,128,768]{2,1,0:T(8,128)(2,1)}, u32[]{:S(2)}, u32[]{:S(2)}) collective-permute-start(bf16[4,128,768]{2,1,0:T(8,128)(2,1)} %get-tuple-element.77), channel_id=1, source_target_pairs={{1,2},{2,1},{3,4},{4,3},{5,6},{6,5},{9,10},{10,9},{11,12},{12,11},... | collective-permute-start | bytes 2359304 | tf_op jit(solution)/shard_map/ppermute | solution.py:505
  38.0 7.4 %shard_map.91 = (bf16[6,6,128,768]{3,2,1,0:T(8,128)(2,1)}, f32[128,768]{1,0:T(8,128)S(1)}) custom-call(s32[6,6,6]{2,1,0:T(8,128)} %nb_hbm.2, bf16[6,6,6,128,128]{4,3,2,1,0:T(8,128)(2,1)} %near_hbm.5, bf16[6,6,128,128]{3,2,1,0:T(8,128)(2,1)} %right_hbm.5, bf16[6,6,128,768]{3,2,1,0:T(8,128)(2,1)} %refs_0_.2, ...), custom_call_target="tpu_custom_call", output_to_operand_aliasing={{0}: (4, {})} | custom-call | flops 550000000 | tf_op jit(solution)/shard_map/pallas_call | solution.py:137
  45.4 3.7 %collective-permute-done.4.other_ref = s16[128,1152]{1,0:T(8,128)(2,1)S(1)} collective-permute-done((s16[128,1152]{1,0:T(8,128)(2,1)S(1)}, s16[128,1152]{1,0:T(8,128)(2,1)S(1)}, u32[]{:S(2)}, u32[]{:S(2)}) %collective-permute-start.4) | collective-permute-done | bytes 294944 | tf_op jit(solution)/shard_map/ppermute | solution.py:493
  49.1 5.9 %shard_map.92 = (s16[128,1152]{1,0:T(8,128)(2,1)S(1)}, f32[128,128]{1,0:T(8,128)S(1)}) custom-call(s16[128,1152]{1,0:T(8,128)(2,1)S(1)} %get-tuple-element.64.mine_ref, s16[128,1152]{1,0:T(8,128)(2,1)S(1)} %collective-permute-done.4.other_ref, f32[128,256]{1,0:T(8,128)S(1)} %get-tuple-element.53.sketch_ref, f32[128,128]{1,0:T(8,128)S(1)} %get-tuple-element.69.refs_0_), custom_call_target="tpu_custom_call" | custom-call | flops 550000000 | tf_op jit(solution)/shard_map/pallas_call | solution.py:476
  55.0 2.2 %collective-permute-start.5 = (s16[128,1152]{1,0:T(8,128)(2,1)S(1)}, s16[128,1152]{1,0:T(8,128)(2,1)S(1)}, u32[]{:S(2)}, u32[]{:S(2)}) collective-permute-start(s16[128,1152]{1,0:T(8,128)(2,1)S(1)} %get-tuple-element.70.mine_ref), channel_id=1, source_target_pairs={{0,8},{8,0},{16,24},{24,16},{1,9},{9,1},{17,25},{25,17},{2,10},{10... | collective-permute-start | bytes 884744 | tf_op jit(solution)/shard_map/ppermute | solution.py:493
  57.2 1.0 shard_map.94
  58.3 1.4 %collective-permute-start.9 = (bf16[2,128,768]{2,1,0:T(8,128)(2,1)}, bf16[2,128,768]{2,1,0:T(8,128)(2,1)}, u32[]{:S(2)}, u32[]{:S(2)}) collective-permute-start(bf16[2,128,768]{2,1,0:T(8,128)(2,1)} %get-tuple-element.76), channel_id=1, source_target_pairs={{8,16},{16,8},{9,17},{17,9},{10,18},{18,10},{11,19},{19,11},{12,20... | collective-permute-start | bytes 1179656 | tf_op jit(solution)/shard_map/ppermute | solution.py:505
  59.8 6.6 %shard_map.93 = (s16[128,1152]{1,0:T(8,128)(2,1)}, f32[128,128]{1,0:T(8,128)S(1)}) custom-call(s16[128,1152]{1,0:T(8,128)(2,1)S(1)} %get-tuple-element.70.mine_ref, s16[128,1152]{1,0:T(8,128)(2,1)S(1)} %collective-permute-done.5.other_ref, f32[128,256]{1,0:T(8,128)S(1)} %get-tuple-element.53.sketch_ref), custom_call_target="tpu_custom_call" | custom-call | flops 550000000 | tf_op jit(solution)/shard_map/pallas_call | solution.py:476
  67.0 2.6 %collective-permute-start.11 = (s16[128,1152]{1,0:T(8,128)(2,1)}, s16[128,1152]{1,0:T(8,128)(2,1)}, u32[]{:S(2)}, u32[]{:S(2)}) collective-permute-start(s16[128,1152]{1,0:T(8,128)(2,1)} %get-tuple-element.87.mine_ref), channel_id=1, source_target_pairs={{0,16},{8,24},{16,0},{24,8},{1,17},{9,25},{17,1},{25,9},{2,18},{10... | collective-permute-start | bytes 884744 | tf_op jit(solution)/shard_map/ppermute | solution.py:493
  69.6 1.0 copy-done.5
  70.6 7.6 %shard_map.95 = (bf16[6,6,128,768]{3,2,1,0:T(8,128)(2,1)}, f32[128,768]{1,0:T(8,128)S(1)}) custom-call(s32[6,6,6]{2,1,0:T(8,128)} %nb_hbm.2, bf16[6,6,6,128,128]{4,3,2,1,0:T(8,128)(2,1)} %near_hbm.5, bf16[6,6,128,128]{3,2,1,0:T(8,128)(2,1)} %right_hbm.5, bf16[6,6,128,768]{3,2,1,0:T(8,128)(2,1)} %refs_0_.2, ...), custom_call_target="tpu_custom_call", output_to_operand_aliasing={{0}: (11, {})} | custom-call | flops 550000000 | tf_op jit(solution)/shard_map/pallas_call | solution.py:137
  78.8 3.3 %collective-permute-start.12 = (f32[4,96,128]{2,1,0:T(8,128)S(1)}, f32[4,96,128]{2,1,0:T(8,128)S(1)}, u32[]{:S(2)}, u32[]{:S(2)}) collective-permute-start(f32[4,96,128]{2,1,0:T(8,128)S(1)} %dynamic-slice_bitcast_fusion), channel_id=1, source_target_pairs={{0,1},{1,0},{2,3},{3,2},{4,5},{5,4},{6,7},{7,6},{8,9},{9,8},{10,11... | collective-permute-start | bytes 589832 | tf_op jit(solution)/shard_map/ppermute | solution.py:493
  82.1 6.5 %shard_map.96 = (f32[128,256]{1,0:T(8,128)S(1)}, f32[128,128]{1,0:T(8,128)S(1)}) custom-call(s16[128,1152]{1,0:T(8,128)(2,1)} %get-tuple-element.87.mine_ref, s16[128,1152]{1,0:T(8,128)(2,1)} %collective-permute-done.11.other_ref, f32[128,256]{1,0:T(8,128)S(1)} %copy-done.9, f32[128,128]{1,0:T(8,128)S(1)} %copy-done.11), custom_call_target="tpu_custom_call" | custom-call | flops 550000000 | tf_op jit(solution)/shard_map/pallas_call | solution.py:476
  88.6 5.1 %collective-permute-start.13 = (f32[96,128]{1,0:T(8,128)S(1)}, f32[96,128]{1,0:T(8,128)S(1)}, u32[]{:S(2)}, u32[]{:S(2)}) collective-permute-start(f32[96,128]{1,0:T(8,128)S(1)} %get-tuple-element.94), channel_id=1, source_target_pairs={{0,2},{1,3},{2,0},{3,1},{4,6},{5,7},{6,4},{7,5},{8,10},{9,11},{10,... | collective-permute-start | bytes 147464 | tf_op jit(solution)/shard_map/ppermute | solution.py:493
  93.7 1.8 %collective-permute-start.14 = (f32[96,128]{1,0:T(8,128)S(1)}, f32[96,128]{1,0:T(8,128)S(1)}, u32[]{:S(2)}, u32[]{:S(2)}) collective-permute-start(f32[96,128]{1,0:T(8,128)S(1)} %get-tuple-element.96), channel_id=1, source_target_pairs={{0,4},{1,5},{2,6},{3,7},{4,0},{5,1},{6,2},{7,3},{8,12},{9,13},{10,... | collective-permute-start | bytes 147464 | tf_op jit(solution)/shard_map/ppermute | solution.py:493
  95.6 1.4 %collective-permute-start.15 = (f32[96,128]{1,0:T(8,128)S(1)}, f32[96,128]{1,0:T(8,128)S(1)}, u32[]{:S(2)}, u32[]{:S(2)}) collective-permute-start(f32[96,128]{1,0:T(8,128)S(1)} %get-tuple-element.95), channel_id=1, source_target_pairs={{0,6},{1,7},{2,4},{3,5},{4,2},{5,3},{6,0},{7,1},{8,14},{9,15},{10,... | collective-permute-start | bytes 147464 | tf_op jit(solution)/shard_map/ppermute | solution.py:493
  96.9 3.3 %collective-permute-done.14 = f32[96,128]{1,0:T(8,128)S(1)} collective-permute-done((f32[96,128]{1,0:T(8,128)S(1)}, f32[96,128]{1,0:T(8,128)S(1)}, u32[]{:S(2)}, u32[]{:S(2)}) %collective-permute-start.14) | collective-permute-done | bytes 49184 | tf_op jit(solution)/shard_map/ppermute | solution.py:493
  100.2 1.3 %collective-permute-done.15 = f32[96,128]{1,0:T(8,128)S(1)} collective-permute-done((f32[96,128]{1,0:T(8,128)S(1)}, f32[96,128]{1,0:T(8,128)S(1)}, u32[]{:S(2)}, u32[]{:S(2)}) %collective-permute-start.15) | collective-permute-done | bytes 49184 | tf_op jit(solution)/shard_map/ppermute | solution.py:493
  101.9 1.8 %collective-permute-start.18 = (f32[96,128]{1,0:T(8,128)S(1)}, f32[96,128]{1,0:T(8,128)S(1)}, u32[]{:S(2)}, u32[]{:S(2)}) collective-permute-start(f32[96,128]{1,0:T(8,128)S(1)} %fusion.5), channel_id=1, source_target_pairs={{0,24},{8,16},{16,8},{24,0},{1,25},{9,17},{17,9},{25,1},{2,26},{10... | collective-permute-start | bytes 147464 | tf_op jit(solution)/shard_map/ppermute | solution.py:493
  103.7 2.7 %collective-permute-done.17 = f32[96,128]{1,0:T(8,128)S(1)} collective-permute-done((f32[96,128]{1,0:T(8,128)S(1)}, f32[96,128]{1,0:T(8,128)S(1)}, u32[]{:S(2)}, u32[]{:S(2)}) %collective-permute-start.17) | collective-permute-done | bytes 49184 | tf_op jit(solution)/shard_map/ppermute | solution.py:493
  106.6 0.8 fusion.7
  (47 shorter events, 2.7 us)
Async XLA Ops:
  2.1 57.6 %copy-start.8 = (f32[128,256]{1,0:T(8,128)}, f32[128,256]{1,0:T(8,128)S(1)}, u32[]{:S(2)}) copy-start(f32[128,256]{1,0:T(8,128)S(1)} %get-tuple-element.53.sketch_ref) | copy-start | bytes 393220
  2.1 10.0 %collective-permute-start = (s16[128,1152]{1,0:T(8,128)(2,1)S(1)}, s16[128,1152]{1,0:T(8,128)(2,1)S(1)}, u32[]{:S(2)}, u32[]{:S(2)}) collective-permute-start(s16[128,1152]{1,0:T(8,128)(2,1)S(1)} %get-tuple-element.52.mine_ref), channel_id=1, source_target_pairs={{0,1},{1,0},{2,3},{3,2},{4,5},{5,4},{6,7},{7,6},{8,9},{9,8},{10,11... | collective-permute-start | bytes 884744 | tf_op jit(solution)/shard_map/ppermute | solution.py:493
  8.5 11.4 %collective-permute-start.2 = (bf16[6,128,768]{2,1,0:T(8,128)(2,1)S(1)}, bf16[6,128,768]{2,1,0:T(8,128)(2,1)S(1)}, u32[]{:S(2)}, u32[]{:S(2)}) collective-permute-start(bf16[6,128,768]{2,1,0:T(8,128)(2,1)S(1)} %get-tuple-element.57), channel_id=1, source_target_pairs={{0,8},{8,0},{16,24},{24,16},{1,9},{9,1},{17,25},{25,17},{2,10},{10... | collective-permute-start | bytes 3538952 | tf_op jit(solution)/shard_map/ppermute | solution.py:505
  8.5 11.3 %collective-permute-start.3 = (bf16[6,128,768]{2,1,0:T(8,128)(2,1)S(1)}, bf16[6,128,768]{2,1,0:T(8,128)(2,1)S(1)}, u32[]{:S(2)}, u32[]{:S(2)}) collective-permute-start(bf16[6,128,768]{2,1,0:T(8,128)(2,1)S(1)} %get-tuple-element.58), channel_id=1, source_target_pairs={{8,16},{16,8},{9,17},{17,9},{10,18},{18,10},{11,19},{19,11},{12,20... | collective-permute-start | bytes 3538952 | tf_op jit(solution)/shard_map/ppermute | solution.py:505
  9.3 47.9 %collective-permute-start.6 = (bf16[6,128,768]{2,1,0:T(8,128)(2,1)S(1)}, bf16[6,128,768]{2,1,0:T(8,128)(2,1)S(1)}, u32[]{:S(2)}, u32[]{:S(2)}) collective-permute-start(bf16[6,128,768]{2,1,0:T(8,128)(2,1)S(1)} %get-tuple-element.73), channel_id=1, source_target_pairs={{0,1},{1,0},{2,3},{3,2},{4,5},{5,4},{6,7},{7,6},{8,9},{9,8},{10,11... | collective-permute-start | bytes 3538952 | tf_op jit(solution)/shard_map/ppermute | solution.py:505
  18.0 9.2 %collective-permute-start.1 = (s16[128,1152]{1,0:T(8,128)(2,1)S(1)}, s16[128,1152]{1,0:T(8,128)(2,1)S(1)}, u32[]{:S(2)}, u32[]{:S(2)}) collective-permute-start(s16[128,1152]{1,0:T(8,128)(2,1)S(1)} %get-tuple-element.55.mine_ref), channel_id=1, source_target_pairs={{0,2},{1,3},{2,0},{3,1},{4,6},{5,7},{6,4},{7,5},{8,10},{9,11},{10,... | collective-permute-start | bytes 884744 | tf_op jit(solution)/shard_map/ppermute | solution.py:493
  24.7 8.4 %copy-start = (f32[128,768]{1,0:T(8,128)}, f32[128,768]{1,0:T(8,128)S(1)}, u32[]{:S(2)}) copy-start(f32[128,768]{1,0:T(8,128)S(1)} %get-tuple-element.80) | copy-start | bytes 1179652
  33.1 16.0 %collective-permute-start.4 = (s16[128,1152]{1,0:T(8,128)(2,1)S(1)}, s16[128,1152]{1,0:T(8,128)(2,1)S(1)}, u32[]{:S(2)}, u32[]{:S(2)}) collective-permute-start(s16[128,1152]{1,0:T(8,128)(2,1)S(1)} %get-tuple-element.64.mine_ref), channel_id=1, source_target_pairs={{0,4},{1,5},{2,6},{3,7},{4,0},{5,1},{6,2},{7,3},{8,12},{9,13},{10,... | collective-permute-start | bytes 884744 | tf_op jit(solution)/shard_map/ppermute | solution.py:493
  35.8 21.5 %collective-permute-start.7 = (bf16[2,128,768]{2,1,0:T(8,128)(2,1)S(1)}, bf16[2,128,768]{2,1,0:T(8,128)(2,1)S(1)}, u32[]{:S(2)}, u32[]{:S(2)}) collective-permute-start(bf16[2,128,768]{2,1,0:T(8,128)(2,1)S(1)} %get-tuple-element.74), channel_id=1, source_target_pairs={{1,2},{2,1},{3,4},{4,3},{5,6},{6,5},{9,10},{10,9},{11,12},{12,11},... | collective-permute-start | bytes 1179656 | tf_op jit(solution)/shard_map/ppermute | solution.py:505
  36.4 33.1 %collective-permute-start.10 = (bf16[4,128,768]{2,1,0:T(8,128)(2,1)}, bf16[4,128,768]{2,1,0:T(8,128)(2,1)}, u32[]{:S(2)}, u32[]{:S(2)}) collective-permute-start(bf16[4,128,768]{2,1,0:T(8,128)(2,1)} %get-tuple-element.77), channel_id=1, source_target_pairs={{1,2},{2,1},{3,4},{4,3},{5,6},{6,5},{9,10},{10,9},{11,12},{12,11},... | collective-permute-start | bytes 2359304 | tf_op jit(solution)/shard_map/ppermute | solution.py:505
  45.4 12.9 %copy-start.2 = (f32[128,768]{1,0:T(8,128)}, f32[128,768]{1,0:T(8,128)S(1)}, u32[]{:S(2)}) copy-start(f32[128,768]{1,0:T(8,128)S(1)} %get-tuple-element.81) | copy-start | bytes 1179652
  55.0 3.3 %copy-start.6 = (f32[128,128]{1,0:T(8,128)}, f32[128,128]{1,0:T(8,128)S(1)}, u32[]{:S(2)}) copy-start(f32[128,128]{1,0:T(8,128)S(1)} %get-tuple-element.84) | copy-start | bytes 196612
  55.0 4.8 %collective-permute-start.5 = (s16[128,1152]{1,0:T(8,128)(2,1)S(1)}, s16[128,1152]{1,0:T(8,128)(2,1)S(1)}, u32[]{:S(2)}, u32[]{:S(2)}) collective-permute-start(s16[128,1152]{1,0:T(8,128)(2,1)S(1)} %get-tuple-element.70.mine_ref), channel_id=1, source_target_pairs={{0,8},{8,0},{16,24},{24,16},{1,9},{9,1},{17,25},{25,17},{2,10},{10... | collective-permute-start | bytes 884744 | tf_op jit(solution)/shard_map/ppermute | solution.py:493
  57.2 1.0 copy-start.4
  58.3 11.3 %collective-permute-start.8 = (bf16[2,128,768]{2,1,0:T(8,128)(2,1)}, bf16[2,128,768]{2,1,0:T(8,128)(2,1)}, u32[]{:S(2)}, u32[]{:S(2)}) collective-permute-start(bf16[2,128,768]{2,1,0:T(8,128)(2,1)} %get-tuple-element.75), channel_id=1, source_target_pairs={{0,8},{8,0},{16,24},{24,16},{1,9},{9,1},{17,25},{25,17},{2,10},{10... | collective-permute-start | bytes 1179656 | tf_op jit(solution)/shard_map/ppermute | solution.py:505
  58.3 11.2 %collective-permute-start.9 = (bf16[2,128,768]{2,1,0:T(8,128)(2,1)}, bf16[2,128,768]{2,1,0:T(8,128)(2,1)}, u32[]{:S(2)}, u32[]{:S(2)}) collective-permute-start(bf16[2,128,768]{2,1,0:T(8,128)(2,1)} %get-tuple-element.76), channel_id=1, source_target_pairs={{8,16},{16,8},{9,17},{17,9},{10,18},{18,10},{11,19},{19,11},{12,20... | collective-permute-start | bytes 1179656 | tf_op jit(solution)/shard_map/ppermute | solution.py:505
  66.3 0.6 copy-start.10
  67.0 11.3 %collective-permute-start.11 = (s16[128,1152]{1,0:T(8,128)(2,1)}, s16[128,1152]{1,0:T(8,128)(2,1)}, u32[]{:S(2)}, u32[]{:S(2)}) collective-permute-start(s16[128,1152]{1,0:T(8,128)(2,1)} %get-tuple-element.87.mine_ref), channel_id=1, source_target_pairs={{0,16},{8,24},{16,0},{24,8},{1,17},{9,25},{17,1},{25,9},{2,18},{10... | collective-permute-start | bytes 884744 | tf_op jit(solution)/shard_map/ppermute | solution.py:493
  69.6 1.0 copy-start.5
  70.6 7.7 %copy-start.1 = (f32[128,768]{1,0:T(8,128)S(1)}, f32[128,768]{1,0:T(8,128)}, u32[]{:S(2)}) copy-start(f32[128,768]{1,0:T(8,128)} %copy-done) | copy-start | bytes 1179652
  70.6 7.7 %copy-start.3 = (f32[128,768]{1,0:T(8,128)S(1)}, f32[128,768]{1,0:T(8,128)}, u32[]{:S(2)}) copy-start(f32[128,768]{1,0:T(8,128)} %copy-done.2) | copy-start | bytes 1179652
  70.6 7.7 %copy-start.7 = (f32[128,128]{1,0:T(8,128)S(1)}, f32[128,128]{1,0:T(8,128)}, u32[]{:S(2)}) copy-start(f32[128,128]{1,0:T(8,128)} %copy-done.6) | copy-start | bytes 196612
  78.2 3.9 %copy-start.9 = (f32[128,256]{1,0:T(8,128)S(1)}, f32[128,256]{1,0:T(8,128)}, u32[]{:S(2)}) copy-start(f32[128,256]{1,0:T(8,128)} %copy-done.8) | copy-start | bytes 393220
  78.2 3.8 %copy-start.11 = (f32[128,128]{1,0:T(8,128)S(1)}, f32[128,128]{1,0:T(8,128)}, u32[]{:S(2)}) copy-start(f32[128,128]{1,0:T(8,128)} %copy-done.10) | copy-start | bytes 196612
  78.8 9.7 %collective-permute-start.12 = (f32[4,96,128]{2,1,0:T(8,128)S(1)}, f32[4,96,128]{2,1,0:T(8,128)S(1)}, u32[]{:S(2)}, u32[]{:S(2)}) collective-permute-start(f32[4,96,128]{2,1,0:T(8,128)S(1)} %dynamic-slice_bitcast_fusion), channel_id=1, source_target_pairs={{0,1},{1,0},{2,3},{3,2},{4,5},{5,4},{6,7},{7,6},{8,9},{9,8},{10,11... | collective-permute-start | bytes 589832 | tf_op jit(solution)/shard_map/ppermute | solution.py:493
  88.6 8.3 %collective-permute-start.13 = (f32[96,128]{1,0:T(8,128)S(1)}, f32[96,128]{1,0:T(8,128)S(1)}, u32[]{:S(2)}, u32[]{:S(2)}) collective-permute-start(f32[96,128]{1,0:T(8,128)S(1)} %get-tuple-element.94), channel_id=1, source_target_pairs={{0,2},{1,3},{2,0},{3,1},{4,6},{5,7},{6,4},{7,5},{8,10},{9,11},{10,... | collective-permute-start | bytes 147464 | tf_op jit(solution)/shard_map/ppermute | solution.py:493
  93.7 6.5 %collective-permute-start.14 = (f32[96,128]{1,0:T(8,128)S(1)}, f32[96,128]{1,0:T(8,128)S(1)}, u32[]{:S(2)}, u32[]{:S(2)}) collective-permute-start(f32[96,128]{1,0:T(8,128)S(1)} %get-tuple-element.96), channel_id=1, source_target_pairs={{0,4},{1,5},{2,6},{3,7},{4,0},{5,1},{6,2},{7,3},{8,12},{9,13},{10,... | collective-permute-start | bytes 147464 | tf_op jit(solution)/shard_map/ppermute | solution.py:493
  95.6 6.0 %collective-permute-start.15 = (f32[96,128]{1,0:T(8,128)S(1)}, f32[96,128]{1,0:T(8,128)S(1)}, u32[]{:S(2)}, u32[]{:S(2)}) collective-permute-start(f32[96,128]{1,0:T(8,128)S(1)} %get-tuple-element.95), channel_id=1, source_target_pairs={{0,6},{1,7},{2,4},{3,5},{4,2},{5,3},{6,0},{7,1},{8,14},{9,15},{10,... | collective-permute-start | bytes 147464 | tf_op jit(solution)/shard_map/ppermute | solution.py:493
  101.8 1.9 %collective-permute-start.16 = (f32[96,128]{1,0:T(8,128)S(1)}, f32[96,128]{1,0:T(8,128)S(1)}, u32[]{:S(2)}, u32[]{:S(2)}) collective-permute-start(f32[96,128]{1,0:T(8,128)S(1)} %fusion.5), channel_id=1, source_target_pairs={{0,8},{8,0},{16,24},{24,16},{1,9},{9,1},{17,25},{25,17},{2,10},{10... | collective-permute-start | bytes 147464 | tf_op jit(solution)/shard_map/ppermute | solution.py:493
  101.8 4.6 %collective-permute-start.17 = (f32[96,128]{1,0:T(8,128)S(1)}, f32[96,128]{1,0:T(8,128)S(1)}, u32[]{:S(2)}, u32[]{:S(2)}) collective-permute-start(f32[96,128]{1,0:T(8,128)S(1)} %fusion.5), channel_id=1, source_target_pairs={{0,16},{8,24},{16,0},{24,8},{1,17},{9,25},{17,1},{25,9},{2,18},{10... | collective-permute-start | bytes 147464 | tf_op jit(solution)/shard_map/ppermute | solution.py:493
  101.9 4.7 %collective-permute-start.18 = (f32[96,128]{1,0:T(8,128)S(1)}, f32[96,128]{1,0:T(8,128)S(1)}, u32[]{:S(2)}, u32[]{:S(2)}) collective-permute-start(f32[96,128]{1,0:T(8,128)S(1)} %fusion.5), channel_id=1, source_target_pairs={{0,24},{8,16},{16,8},{24,0},{1,25},{9,17},{17,9},{25,1},{2,26},{10... | collective-permute-start | bytes 147464 | tf_op jit(solution)/shard_map/ppermute | solution.py:493

commit v9 on v8

--- a/solution.py
+++ b/solution.py
@@ -9,8 +9,8 @@
 
 high = lax.Precision.HIGH
 empty_slot = 9
-near_vmem = 18 * 1024 * 1024
-merge_vmem = 12 * 1024 * 1024
+near_vmem = 17 * 1024 * 1024
+merge_vmem = 8 * 1024 * 1024
 
 
 def dot_t(a, b, dims, precision=None):
@@ -407,7 +407,8 @@
     gu, gv = density.shape[:2]
     near_col = (gv - 1) * (1 - odd("pv"))
     far_col = (gv - 1) * odd("pv")
-    pairs = [(density.at[(gu - 1) * (1 - odd("pu"))], pu_near), (density.at[(gu - 1) * odd("pu")], pu_far)]
+    pairs = [(density.at[(gu - 1) * odd("pu"), col], pu_far.at[col]) for col in range(gv)]
+    pairs += [(density.at[(gu - 1) * (1 - odd("pu")), col], pu_near.at[col]) for col in range(gv)]
     pairs += [(density.at[row, near_col], beside.at[row]) for row in range(gu)]
     pairs += [(density.at[(gu - 1) * row, far_col], ends.at[row]) for row in range(2)]
     pairs += [(density.at[row + 1, far_col], mids.at[row]) for row in range(gu - 2)]
@@ -423,7 +424,7 @@
         in_specs=[pl.BlockSpec(memory_space=pltpu.HBM)],
         out_specs=[pl.BlockSpec(memory_space=pltpu.VMEM)] * len(blocks),
         out_shape=[jax.ShapeDtypeStruct((count, size, rhs), density.dtype) for count in blocks],
-        scratch_shapes=[pltpu.SemaphoreType.DMA((2 * gu + 2,))],
+        scratch_shapes=[pltpu.SemaphoreType.DMA((2 * gu + 2 * gv,))],
         cost_estimate=cost(2.5),
         compiler_params=pltpu.CompilerParams(vmem_limit_bytes=merge_vmem),
     )(in_hbm(density))
@@ -551,10 +552,12 @@
             links, left = tied(neighbours, left)
         if level == 1:
             corrected, coef = near_rows(density, pu_near, pu_far, near_blocks, far_right, links, corrected)
+            ends, coef = tied(ends, coef)
+            ends = swapped(ends, "pv", True)
         elif level == 2:
-            ends, mids, left = tied(ends, mids, left)
-            ends = swapped(ends, "pv", True)
+            mids, left = tied(mids, left)
             mids = swapped(mids, "pv", True)
+            ends, other = tied(ends, other)
             corrected, coef = near_middle(density, near_blocks, far_right, links, corrected)
         elif last:
             corner_near, corner_far = patch_corners(beside, ends)
@@ -581,8 +584,12 @@
             coef = summed(coefs)
             share = lax.dot_general(coef, pv_path, (((0,), (1,)), ((), ())), precision=high)
             share = share.reshape(pv_count, rhs // pv_count, -1)
-            share, other = tied(share, other)
-            share = halved(share)
+            share, other = tied(halved(share), other)
+            here = pv_index // 2
+            parts = [lax.dynamic_index_in_dim(share, here, 0, keepdims=False)]
+            for by in range(1, pv_count // 2):
+                give = lax.dynamic_index_in_dim(share, here ^ by, 0, keepdims=False)
+                parts.append(from_partner(give, "pv", 2 * by))
         path = pv_path if level < pv_levels else pu_path
         last_rows = rows // pu_count if last else 0
         left, path = merge(level, left, other, sketch, path, last_rows)
@@ -591,13 +598,6 @@
         else:
             pu_path = path
 
-    share, left = tied(share, left)
-    far_index = pv_index // 2
-    mine = lax.dynamic_index_in_dim(share, far_index, 0, keepdims=False)
-    parts = [mine]
-    for by in range(1, pv_count // 2):
-        give = lax.dynamic_index_in_dim(share, far_index ^ by, 0, keepdims=False)
-        parts.append(from_partner(give, "pv", 2 * by))
     root_coef = lax.dot_general(summed(parts), pu_path, (((1,), (1,)), ((), ())), precision=high)
     root_coef = summed([root_coef] + [from_partner(root_coef, "pu", by) for by in range(1, pu_count)])
     far_field = lax.dot_general(left, root_coef, (((0,), (1,)), ((), ())), precision=high)

time: 108 us -> 111 us (1.028)
  waiting for transfers between devices: 16.5 us -> 21.2 us
  starting transfers between devices: 30.5 us -> 28.5 us
    ppermute x12, waiting for transfers between devices: 16.5 us -> 21.2 us  [from_partner(): return lax.ppermute(value, axis, pairs)]
    ppermute x12, starting transfers between devices: 25.9 us -> 23.9 us  [from_partner(): return lax.ppermute(value, axis, pairs)]
  transfers between devices with their start and end apart: 19 -> 19, of which waited for: 7 -> 6; matrix products, arithmetic and copies ran while one was open for 0% -> 0% of each run, Pallas kernels for 51% -> 50%
where the time goes in v9:
time: 111 us; the launch traced here: 110 us
  Pallas kernels  56.3 us (51%)
  starting transfers between devices  28.5 us (26%)
  waiting for transfers between devices  21.2 us (19%)
  local copies, waits for them, and re-layouts  1.7 us (2%)
  matrix products  1.54 us (1%)
    pallas_call x5, Pallas kernels, merge(): pl.pallas_call(functools.partial(merge_kernel, bool(paths), bool(last_row...  30.6 us
    ppermute x12, starting transfers between devices, from_partner(): return lax.ppermute(value, axis, pairs)  23.9 us
    ppermute x12, waiting for transfers between devices, from_partner(): return lax.ppermute(value, axis, pairs)  21.2 us
    pallas_call x3, Pallas kernels, near_part(): pl.pallas_call(functools.partial(near_kernel, plan, len(sources)), grid=(...  19.8 us
    ppermute x7, starting transfers between devices, swapped(): return lax.ppermute(value, axis, pairs)  4.64 us
    pallas_call x1, Pallas kernels, patch_edges(): pl.pallas_call(edges_kernel, in_specs=[pl.BlockSpec(memory_space=pltpu.HB...  3.52 us
  transfers between devices with their start and end apart: 19, of which 6 were waited for; matrix products, arithmetic and copies ran while one was open for 0% of the time, Pallas kernels for 50%

profile of v9, /device:TPU:0, one launch (start us, length us, event | category | flops | bytes accessed | tf_op | source)
XLA Modules:
  0.0 110.3 jit_solution(9202101933591585227)
XLA Ops:
  0.6 1.5 %shard_map.86 = (s16[128,1152]{1,0:T(8,128)(2,1)S(1)}, f32[128,256]{1,0:T(8,128)S(1)}) custom-call(s32[32]{0:T(128)} %order_hbm.1, f32[1,1,1024,128]{3,2,1,0:T(8,128)} %value_hbm.1, f32[256,128]{1,0:T(8,128)} %sketch_hbm.1), custom_call_target="tpu_custom_call" | custom-call | flops 1650000000 | tf_op jit(solution)/shard_map/pallas_call | solution.py:387
  2.1 3.0 %collective-permute-start = (s16[128,1152]{1,0:T(8,128)(2,1)S(1)}, s16[128,1152]{1,0:T(8,128)(2,1)S(1)}, u32[]{:S(2)}, u32[]{:S(2)}) collective-permute-start(s16[128,1152]{1,0:T(8,128)(2,1)S(1)} %get-tuple-element.52.mine_ref), channel_id=1, source_target_pairs={{0,1},{1,0},{2,3},{3,2},{4,5},{5,4},{6,7},{7,6},{8,9},{9,8},{10,11... | collective-permute-start | bytes 884744 | tf_op jit(solution)/shard_map/ppermute | solution.py:494
  5.1 3.5 %shard_map.87 = (bf16[6,128,768]{2,1,0:T(8,128)(2,1)S(1)}, bf16[2,128,768]{2,1,0:T(8,128)(2,1)S(1)}, bf16[4,128,768]{2,1,0:T(8,128)(2,1)}, bf16[6,128,768]{2,1,0:T(8,128)(2,1)S(1)}, bf16[6,128,768]{2,1,0:T(8,128)(2,1)S(1)}) custom-call(bf16[6,6,128,768]{3,2,1,0:T(8,128)(2,1)} %refs_0_.2), custom_call_target="tpu_custom_call" | custom-call | flops 2750000128 | tf_op jit(solution)/shard_map/pallas_call | solution.py:422
  8.7 0.7 collective-permute-start.3
  9.6 2.6 %collective-permute-done.other_ref = s16[128,1152]{1,0:T(8,128)(2,1)S(1)} collective-permute-done((s16[128,1152]{1,0:T(8,128)(2,1)S(1)}, s16[128,1152]{1,0:T(8,128)(2,1)S(1)}, u32[]{:S(2)}, u32[]{:S(2)}) %collective-permute-start) | collective-permute-done | bytes 294944 | tf_op jit(solution)/shard_map/ppermute | solution.py:494
  12.1 5.8 %shard_map.88 = (s16[128,1152]{1,0:T(8,128)(2,1)S(1)}, f32[128,128]{1,0:T(8,128)S(1)}) custom-call(s16[128,1152]{1,0:T(8,128)(2,1)S(1)} %get-tuple-element.52.mine_ref, s16[128,1152]{1,0:T(8,128)(2,1)S(1)} %collective-permute-done.other_ref, f32[128,256]{1,0:T(8,128)S(1)} %get-tuple-element.53.sketch_ref), custom_call_target="tpu_custom_call" | custom-call | flops 9900000256 | tf_op jit(solution)/shard_map/pallas_call | solution.py:477
  18.0 1.9 %collective-permute-start.1 = (s16[128,1152]{1,0:T(8,128)(2,1)S(1)}, s16[128,1152]{1,0:T(8,128)(2,1)S(1)}, u32[]{:S(2)}, u32[]{:S(2)}) collective-permute-start(s16[128,1152]{1,0:T(8,128)(2,1)S(1)} %get-tuple-element.55.mine_ref), channel_id=1, source_target_pairs={{0,2},{1,3},{2,0},{3,1},{4,6},{5,7},{6,4},{7,5},{8,10},{9,11},{10,... | collective-permute-start | bytes 884744 | tf_op jit(solution)/shard_map/ppermute | solution.py:494
  19.9 4.8 %shard_map.89 = (bf16[6,6,128,768]{3,2,1,0:T(8,128)(2,1)}, f32[128,768]{1,0:T(8,128)S(1)}) custom-call(s32[6,6,6]{2,1,0:T(8,128)} %nb_hbm.2, bf16[6,6,6,128,128]{4,3,2,1,0:T(8,128)(2,1)} %near_hbm.5, bf16[6,6,128,128]{3,2,1,0:T(8,128)(2,1)} %right_hbm.5, bf16[6,6,128,768]{3,2,1,0:T(8,128)(2,1)} %refs_0_.2, ...), custom_call_target="tpu_custom_call" | custom-call | flops 550000000 | tf_op jit(solution)/shard_map/pallas_call | solution.py:137
  24.7 2.7 %collective-permute-done.1.other_ref = s16[128,1152]{1,0:T(8,128)(2,1)S(1)} collective-permute-done((s16[128,1152]{1,0:T(8,128)(2,1)S(1)}, s16[128,1152]{1,0:T(8,128)(2,1)S(1)}, u32[]{:S(2)}, u32[]{:S(2)}) %collective-permute-start.1) | collective-permute-done | bytes 294944 | tf_op jit(solution)/shard_map/ppermute | solution.py:494
  27.4 0.7 collective-permute-start.4
  28.1 5.9 %shard_map.90 = (s16[128,1152]{1,0:T(8,128)(2,1)S(1)}, f32[128,128]{1,0:T(8,128)S(1)}) custom-call(s16[128,1152]{1,0:T(8,128)(2,1)S(1)} %get-tuple-element.55.mine_ref, s16[128,1152]{1,0:T(8,128)(2,1)S(1)} %collective-permute-done.1.other_ref, f32[128,256]{1,0:T(8,128)S(1)} %get-tuple-element.53.sketch_ref, f32[128,128]{1,0:T(8,128)S(1)} %get-tuple-element.63.refs_0_), custom_call_target="tpu_custom_call" | custom-call | flops 1650000000 | tf_op jit(solution)/shard_map/pallas_call | solution.py:477
  34.0 5.3 %collective-permute-start.5 = (s16[128,1152]{1,0:T(8,128)(2,1)S(1)}, s16[128,1152]{1,0:T(8,128)(2,1)S(1)}, u32[]{:S(2)}, u32[]{:S(2)}) collective-permute-start(s16[128,1152]{1,0:T(8,128)(2,1)S(1)} %get-tuple-element.66.mine_ref), channel_id=1, source_target_pairs={{0,4},{1,5},{2,6},{3,7},{4,0},{5,1},{6,2},{7,3},{8,12},{9,13},{10,... | collective-permute-start | bytes 884744 | tf_op jit(solution)/shard_map/ppermute | solution.py:494
  39.2 1.6 %collective-permute-start.10 = (bf16[4,128,768]{2,1,0:T(8,128)(2,1)}, bf16[4,128,768]{2,1,0:T(8,128)(2,1)}, u32[]{:S(2)}, u32[]{:S(2)}) collective-permute-start(bf16[4,128,768]{2,1,0:T(8,128)(2,1)} %get-tuple-element.81), channel_id=1, source_target_pairs={{1,2},{2,1},{3,4},{4,3},{5,6},{6,5},{9,10},{10,9},{11,12},{12,11},... | collective-permute-start | bytes 2359304 | tf_op jit(solution)/shard_map/ppermute | solution.py:506
  40.8 7.3 %shard_map.91 = (bf16[6,6,128,768]{3,2,1,0:T(8,128)(2,1)}, f32[128,768]{1,0:T(8,128)S(1)}) custom-call(s32[6,6,6]{2,1,0:T(8,128)} %nb_hbm.2, bf16[6,6,6,128,128]{4,3,2,1,0:T(8,128)(2,1)} %near_hbm.5, bf16[6,6,128,128]{3,2,1,0:T(8,128)(2,1)} %right_hbm.5, bf16[6,6,128,768]{3,2,1,0:T(8,128)(2,1)} %refs_0_.2, ...), custom_call_target="tpu_custom_call", output_to_operand_aliasing={{0}: (4, {})} | custom-call | flops 550000000 | tf_op jit(solution)/shard_map/pallas_call | solution.py:137
  48.2 5.4 %collective-permute-done.5.other_ref = s16[128,1152]{1,0:T(8,128)(2,1)S(1)} collective-permute-done((s16[128,1152]{1,0:T(8,128)(2,1)S(1)}, s16[128,1152]{1,0:T(8,128)(2,1)S(1)}, u32[]{:S(2)}, u32[]{:S(2)}) %collective-permute-start.5) | collective-permute-done | bytes 294944 | tf_op jit(solution)/shard_map/ppermute | solution.py:494
  53.6 5.9 %shard_map.92 = (s16[128,1152]{1,0:T(8,128)(2,1)S(1)}, f32[128,128]{1,0:T(8,128)S(1)}) custom-call(s16[128,1152]{1,0:T(8,128)(2,1)S(1)} %get-tuple-element.66.mine_ref, s16[128,1152]{1,0:T(8,128)(2,1)S(1)} %collective-permute-done.5.other_ref, f32[128,256]{1,0:T(8,128)S(1)} %get-tuple-element.53.sketch_ref, f32[128,128]{1,0:T(8,128)S(1)} %get-tuple-element.73.refs_0_), custom_call_target="tpu_custom_call" | custom-call | flops 550000000 | tf_op jit(solution)/shard_map/pallas_call | solution.py:477
  59.5 4.6 %collective-permute-start.6 = (s16[128,1152]{1,0:T(8,128)(2,1)S(1)}, s16[128,1152]{1,0:T(8,128)(2,1)S(1)}, u32[]{:S(2)}, u32[]{:S(2)}) collective-permute-start(s16[128,1152]{1,0:T(8,128)(2,1)S(1)} %get-tuple-element.74.mine_ref), channel_id=1, source_target_pairs={{0,8},{8,0},{16,24},{24,16},{1,9},{9,1},{17,25},{25,17},{2,10},{10... | collective-permute-start | bytes 884744 | tf_op jit(solution)/shard_map/ppermute | solution.py:494
  64.1 0.9 shard_map.94
  65.2 1.4 %collective-permute-start.9 = (bf16[2,128,768]{2,1,0:T(8,128)(2,1)}, bf16[2,128,768]{2,1,0:T(8,128)(2,1)}, u32[]{:S(2)}, u32[]{:S(2)}) collective-permute-start(bf16[2,128,768]{2,1,0:T(8,128)(2,1)} %get-tuple-element.80), channel_id=1, source_target_pairs={{8,16},{16,8},{9,17},{17,9},{10,18},{18,10},{11,19},{19,11},{12,20... | collective-permute-start | bytes 1179656 | tf_op jit(solution)/shard_map/ppermute | solution.py:506
  66.6 6.6 %shard_map.93 = (s16[128,1152]{1,0:T(8,128)(2,1)}, f32[128,128]{1,0:T(8,128)S(1)}) custom-call(s16[128,1152]{1,0:T(8,128)(2,1)S(1)} %get-tuple-element.74.mine_ref, s16[128,1152]{1,0:T(8,128)(2,1)S(1)} %collective-permute-done.6.other_ref, f32[128,256]{1,0:T(8,128)S(1)} %get-tuple-element.53.sketch_ref), custom_call_target="tpu_custom_call" | custom-call | flops 550000000 | tf_op jit(solution)/shard_map/pallas_call | solution.py:477
  73.2 0.6 copy-done.10
  73.8 2.6 %collective-permute-start.11 = (s16[128,1152]{1,0:T(8,128)(2,1)}, s16[128,1152]{1,0:T(8,128)(2,1)}, u32[]{:S(2)}, u32[]{:S(2)}) collective-permute-start(s16[128,1152]{1,0:T(8,128)(2,1)} %get-tuple-element.84.mine_ref), channel_id=1, source_target_pairs={{0,16},{8,24},{16,0},{24,8},{1,17},{9,25},{17,1},{25,9},{2,18},{10... | collective-permute-start | bytes 884744 | tf_op jit(solution)/shard_map/ppermute | solution.py:494
  76.4 1.0 copy-done.5
  77.4 7.6 %shard_map.95 = (bf16[6,6,128,768]{3,2,1,0:T(8,128)(2,1)}, f32[128,768]{1,0:T(8,128)S(1)}) custom-call(s32[6,6,6]{2,1,0:T(8,128)} %nb_hbm.2, bf16[6,6,6,128,128]{4,3,2,1,0:T(8,128)(2,1)} %near_hbm.5, bf16[6,6,128,128]{3,2,1,0:T(8,128)(2,1)} %right_hbm.5, bf16[6,6,128,768]{3,2,1,0:T(8,128)(2,1)} %refs_0_.2, ...), custom_call_target="tpu_custom_call", output_to_operand_aliasing={{0}: (11, {})} | custom-call | flops 550000000 | tf_op jit(solution)/shard_map/pallas_call | solution.py:137
  85.8 6.9 %collective-permute-done.12 = f32[4,96,128]{2,1,0:T(8,128)S(1)} collective-permute-done((f32[4,96,128]{2,1,0:T(8,128)S(1)}, f32[4,96,128]{2,1,0:T(8,128)S(1)}, u32[]{:S(2)}, u32[]{:S(2)}) %collective-permute-start.12) | collective-permute-done | bytes 196640 | tf_op jit(solution)/shard_map/ppermute | solution.py:494
  92.8 3.2 %collective-permute-start.14 = (f32[96,128]{1,0:T(8,128)S(1)}, f32[96,128]{1,0:T(8,128)S(1)}, u32[]{:S(2)}, u32[]{:S(2)}) collective-permute-start(f32[96,128]{1,0:T(8,128)S(1)} %get-tuple-element.98), channel_id=1, source_target_pairs={{0,4},{1,5},{2,6},{3,7},{4,0},{5,1},{6,2},{7,3},{8,12},{9,13},{10,... | collective-permute-start | bytes 147464 | tf_op jit(solution)/shard_map/ppermute | solution.py:494
  96.0 1.1 %collective-permute-start.15 = (f32[96,128]{1,0:T(8,128)S(1)}, f32[96,128]{1,0:T(8,128)S(1)}, u32[]{:S(2)}, u32[]{:S(2)}) collective-permute-start(f32[96,128]{1,0:T(8,128)S(1)} %get-tuple-element.97), channel_id=1, source_target_pairs={{0,6},{1,7},{2,4},{3,5},{4,2},{5,3},{6,0},{7,1},{8,14},{9,15},{10,... | collective-permute-start | bytes 147464 | tf_op jit(solution)/shard_map/ppermute | solution.py:494
  97.2 6.5 %shard_map.96 = (f32[128,256]{1,0:T(8,128)S(1)}, f32[128,128]{1,0:T(8,128)S(1)}) custom-call(s16[128,1152]{1,0:T(8,128)(2,1)} %get-tuple-element.84.mine_ref, s16[128,1152]{1,0:T(8,128)(2,1)} %collective-permute-done.11.other_ref, f32[128,256]{1,0:T(8,128)S(1)} %copy-done.9, f32[128,128]{1,0:T(8,128)S(1)} %copy-done.11), custom_call_target="tpu_custom_call" | custom-call | flops 550000000 | tf_op jit(solution)/shard_map/pallas_call | solution.py:477
  104.0 1.8 %collective-permute-start.17 = (f32[96,128]{1,0:T(8,128)S(1)}, f32[96,128]{1,0:T(8,128)S(1)}, u32[]{:S(2)}, u32[]{:S(2)}) collective-permute-start(f32[96,128]{1,0:T(8,128)S(1)} %fusion.5), channel_id=1, source_target_pairs={{0,16},{8,24},{16,0},{24,8},{1,17},{9,25},{17,1},{25,9},{2,18},{10... | collective-permute-start | bytes 147464 | tf_op jit(solution)/shard_map/ppermute | solution.py:494
  105.8 2.3 %collective-permute-done.17 = f32[96,128]{1,0:T(8,128)S(1)} collective-permute-done((f32[96,128]{1,0:T(8,128)S(1)}, f32[96,128]{1,0:T(8,128)S(1)}, u32[]{:S(2)}, u32[]{:S(2)}) %collective-permute-start.17) | collective-permute-done | bytes 49184 | tf_op jit(solution)/shard_map/ppermute | solution.py:494
  108.1 1.3 %collective-permute-done.18 = f32[96,128]{1,0:T(8,128)S(1)} collective-permute-done((f32[96,128]{1,0:T(8,128)S(1)}, f32[96,128]{1,0:T(8,128)S(1)}, u32[]{:S(2)}, u32[]{:S(2)}) %collective-permute-start.18) | collective-permute-done | bytes 49184 | tf_op jit(solution)/shard_map/ppermute | solution.py:494
  109.5 0.8 fusion.7
  (47 shorter events, 1.4 us)
Async XLA Ops:
  2.1 64.5 %copy-start.8 = (f32[128,256]{1,0:T(8,128)}, f32[128,256]{1,0:T(8,128)S(1)}, u32[]{:S(2)}) copy-start(f32[128,256]{1,0:T(8,128)S(1)} %get-tuple-element.53.sketch_ref) | copy-start | bytes 393220
  2.1 10.0 %collective-permute-start = (s16[128,1152]{1,0:T(8,128)(2,1)S(1)}, s16[128,1152]{1,0:T(8,128)(2,1)S(1)}, u32[]{:S(2)}, u32[]{:S(2)}) collective-permute-start(s16[128,1152]{1,0:T(8,128)(2,1)S(1)} %get-tuple-element.52.mine_ref), channel_id=1, source_target_pairs={{0,1},{1,0},{2,3},{3,2},{4,5},{5,4},{6,7},{7,6},{8,9},{9,8},{10,11... | collective-permute-start | bytes 884744 | tf_op jit(solution)/shard_map/ppermute | solution.py:494
  8.7 11.2 %collective-permute-start.2 = (bf16[6,128,768]{2,1,0:T(8,128)(2,1)S(1)}, bf16[6,128,768]{2,1,0:T(8,128)(2,1)S(1)}, u32[]{:S(2)}, u32[]{:S(2)}) collective-permute-start(bf16[6,128,768]{2,1,0:T(8,128)(2,1)S(1)} %get-tuple-element.58), channel_id=1, source_target_pairs={{0,8},{8,0},{16,24},{24,16},{1,9},{9,1},{17,25},{25,17},{2,10},{10... | collective-permute-start | bytes 3538952 | tf_op jit(solution)/shard_map/ppermute | solution.py:506
  8.7 11.1 %collective-permute-start.3 = (bf16[6,128,768]{2,1,0:T(8,128)(2,1)S(1)}, bf16[6,128,768]{2,1,0:T(8,128)(2,1)S(1)}, u32[]{:S(2)}, u32[]{:S(2)}) collective-permute-start(bf16[6,128,768]{2,1,0:T(8,128)(2,1)S(1)} %get-tuple-element.59), channel_id=1, source_target_pairs={{8,16},{16,8},{9,17},{17,9},{10,18},{18,10},{11,19},{19,11},{12,20... | collective-permute-start | bytes 3538952 | tf_op jit(solution)/shard_map/ppermute | solution.py:506
  9.5 54.7 %collective-permute-start.7 = (bf16[6,128,768]{2,1,0:T(8,128)(2,1)S(1)}, bf16[6,128,768]{2,1,0:T(8,128)(2,1)S(1)}, u32[]{:S(2)}, u32[]{:S(2)}) collective-permute-start(bf16[6,128,768]{2,1,0:T(8,128)(2,1)S(1)} %get-tuple-element.77), channel_id=1, source_target_pairs={{0,1},{1,0},{2,3},{3,2},{4,5},{5,4},{6,7},{7,6},{8,9},{9,8},{10,11... | collective-permute-start | bytes 3538952 | tf_op jit(solution)/shard_map/ppermute | solution.py:506
  18.0 9.5 %collective-permute-start.1 = (s16[128,1152]{1,0:T(8,128)(2,1)S(1)}, s16[128,1152]{1,0:T(8,128)(2,1)S(1)}, u32[]{:S(2)}, u32[]{:S(2)}) collective-permute-start(s16[128,1152]{1,0:T(8,128)(2,1)S(1)} %get-tuple-element.55.mine_ref), channel_id=1, source_target_pairs={{0,2},{1,3},{2,0},{3,1},{4,6},{5,7},{6,4},{7,5},{8,10},{9,11},{10,... | collective-permute-start | bytes 884744 | tf_op jit(solution)/shard_map/ppermute | solution.py:494
  24.7 9.3 %copy-start = (f32[128,768]{1,0:T(8,128)}, f32[128,768]{1,0:T(8,128)S(1)}, u32[]{:S(2)}) copy-start(f32[128,768]{1,0:T(8,128)S(1)} %get-tuple-element.85) | copy-start | bytes 1179652
  27.4 26.2 %collective-permute-start.4 = (bf16[2,128,768]{2,1,0:T(8,128)(2,1)S(1)}, bf16[2,128,768]{2,1,0:T(8,128)(2,1)S(1)}, u32[]{:S(2)}, u32[]{:S(2)}) collective-permute-start(bf16[2,128,768]{2,1,0:T(8,128)(2,1)S(1)} %get-tuple-element.67), channel_id=1, source_target_pairs={{1,2},{2,1},{3,4},{4,3},{5,6},{6,5},{9,10},{10,9},{11,12},{12,11},... | collective-permute-start | bytes 1179656 | tf_op jit(solution)/shard_map/ppermute | solution.py:506
  34.0 19.6 %collective-permute-start.5 = (s16[128,1152]{1,0:T(8,128)(2,1)S(1)}, s16[128,1152]{1,0:T(8,128)(2,1)S(1)}, u32[]{:S(2)}, u32[]{:S(2)}) collective-permute-start(s16[128,1152]{1,0:T(8,128)(2,1)S(1)} %get-tuple-element.66.mine_ref), channel_id=1, source_target_pairs={{0,4},{1,5},{2,6},{3,7},{4,0},{5,1},{6,2},{7,3},{8,12},{9,13},{10,... | collective-permute-start | bytes 884744 | tf_op jit(solution)/shard_map/ppermute | solution.py:494
  39.2 37.2 %collective-permute-start.10 = (bf16[4,128,768]{2,1,0:T(8,128)(2,1)}, bf16[4,128,768]{2,1,0:T(8,128)(2,1)}, u32[]{:S(2)}, u32[]{:S(2)}) collective-permute-start(bf16[4,128,768]{2,1,0:T(8,128)(2,1)} %get-tuple-element.81), channel_id=1, source_target_pairs={{1,2},{2,1},{3,4},{4,3},{5,6},{6,5},{9,10},{10,9},{11,12},{12,11},... | collective-permute-start | bytes 2359304 | tf_op jit(solution)/shard_map/ppermute | solution.py:506
  48.2 16.9 %copy-start.2 = (f32[128,768]{1,0:T(8,128)}, f32[128,768]{1,0:T(8,128)S(1)}, u32[]{:S(2)}) copy-start(f32[128,768]{1,0:T(8,128)S(1)} %get-tuple-element.86) | copy-start | bytes 1179652
  53.6 11.5 %copy-start.4 = (bf16[2,128,768]{2,1,0:T(8,128)(2,1)}, bf16[2,128,768]{2,1,0:T(8,128)(2,1)S(1)}, u32[]{:S(2)}) copy-start(bf16[2,128,768]{2,1,0:T(8,128)(2,1)S(1)} %collective-permute-done.4.ends.refs_6_) | copy-start | bytes 1179652
  59.5 5.6 %copy-start.6 = (f32[128,128]{1,0:T(8,128)}, f32[128,128]{1,0:T(8,128)S(1)}, u32[]{:S(2)}) copy-start(f32[128,128]{1,0:T(8,128)S(1)} %get-tuple-element.89) | copy-start | bytes 196612
  59.5 7.1 %collective-permute-start.6 = (s16[128,1152]{1,0:T(8,128)(2,1)S(1)}, s16[128,1152]{1,0:T(8,128)(2,1)S(1)}, u32[]{:S(2)}, u32[]{:S(2)}) collective-permute-start(s16[128,1152]{1,0:T(8,128)(2,1)S(1)} %get-tuple-element.74.mine_ref), channel_id=1, source_target_pairs={{0,8},{8,0},{16,24},{24,16},{1,9},{9,1},{17,25},{25,17},{2,10},{10... | collective-permute-start | bytes 884744 | tf_op jit(solution)/shard_map/ppermute | solution.py:494
  65.1 11.3 %collective-permute-start.8 = (bf16[2,128,768]{2,1,0:T(8,128)(2,1)}, bf16[2,128,768]{2,1,0:T(8,128)(2,1)}, u32[]{:S(2)}, u32[]{:S(2)}) collective-permute-start(bf16[2,128,768]{2,1,0:T(8,128)(2,1)} %get-tuple-element.79), channel_id=1, source_target_pairs={{0,8},{8,0},{16,24},{24,16},{1,9},{9,1},{17,25},{25,17},{2,10},{10... | collective-permute-start | bytes 1179656 | tf_op jit(solution)/shard_map/ppermute | solution.py:506
  65.2 11.2 %collective-permute-start.9 = (bf16[2,128,768]{2,1,0:T(8,128)(2,1)}, bf16[2,128,768]{2,1,0:T(8,128)(2,1)}, u32[]{:S(2)}, u32[]{:S(2)}) collective-permute-start(bf16[2,128,768]{2,1,0:T(8,128)(2,1)} %get-tuple-element.80), channel_id=1, source_target_pairs={{8,16},{16,8},{9,17},{17,9},{10,18},{18,10},{11,19},{19,11},{12,20... | collective-permute-start | bytes 1179656 | tf_op jit(solution)/shard_map/ppermute | solution.py:506
  73.2 0.6 copy-start.10
  73.8 11.3 %collective-permute-start.11 = (s16[128,1152]{1,0:T(8,128)(2,1)}, s16[128,1152]{1,0:T(8,128)(2,1)}, u32[]{:S(2)}, u32[]{:S(2)}) collective-permute-start(s16[128,1152]{1,0:T(8,128)(2,1)} %get-tuple-element.84.mine_ref), channel_id=1, source_target_pairs={{0,16},{8,24},{16,0},{24,8},{1,17},{9,25},{17,1},{25,9},{2,18},{10... | collective-permute-start | bytes 884744 | tf_op jit(solution)/shard_map/ppermute | solution.py:494
  76.4 1.0 copy-start.5
  77.4 7.7 %copy-start.1 = (f32[128,768]{1,0:T(8,128)S(1)}, f32[128,768]{1,0:T(8,128)}, u32[]{:S(2)}) copy-start(f32[128,768]{1,0:T(8,128)} %copy-done) | copy-start | bytes 1179652
  77.4 7.7 %copy-start.3 = (f32[128,768]{1,0:T(8,128)S(1)}, f32[128,768]{1,0:T(8,128)}, u32[]{:S(2)}) copy-start(f32[128,768]{1,0:T(8,128)} %copy-done.2) | copy-start | bytes 1179652
  77.4 7.7 %copy-start.7 = (f32[128,128]{1,0:T(8,128)S(1)}, f32[128,128]{1,0:T(8,128)}, u32[]{:S(2)}) copy-start(f32[128,128]{1,0:T(8,128)} %copy-done.6) | copy-start | bytes 196612
  85.1 12.0 %copy-start.9 = (f32[128,256]{1,0:T(8,128)S(1)}, f32[128,256]{1,0:T(8,128)}, u32[]{:S(2)}) copy-start(f32[128,256]{1,0:T(8,128)} %copy-done.8) | copy-start | bytes 393220
  85.1 12.0 %copy-start.11 = (f32[128,128]{1,0:T(8,128)S(1)}, f32[128,128]{1,0:T(8,128)}, u32[]{:S(2)}) copy-start(f32[128,128]{1,0:T(8,128)} %copy-done.10) | copy-start | bytes 196612
  85.7 7.0 %collective-permute-start.12 = (f32[4,96,128]{2,1,0:T(8,128)S(1)}, f32[4,96,128]{2,1,0:T(8,128)S(1)}, u32[]{:S(2)}, u32[]{:S(2)}) collective-permute-start(f32[4,96,128]{2,1,0:T(8,128)S(1)} %dynamic-slice_bitcast_fusion), channel_id=1, source_target_pairs={{0,1},{1,0},{2,3},{3,2},{4,5},{5,4},{6,7},{7,6},{8,9},{9,8},{10,11... | collective-permute-start | bytes 589832 | tf_op jit(solution)/shard_map/ppermute | solution.py:494
  92.7 10.9 %collective-permute-start.13 = (f32[96,128]{1,0:T(8,128)S(1)}, f32[96,128]{1,0:T(8,128)S(1)}, u32[]{:S(2)}, u32[]{:S(2)}) collective-permute-start(f32[96,128]{1,0:T(8,128)S(1)} %get-tuple-element.96), channel_id=1, source_target_pairs={{0,2},{1,3},{2,0},{3,1},{4,6},{5,7},{6,4},{7,5},{8,10},{9,11},{10,... | collective-permute-start | bytes 147464 | tf_op jit(solution)/shard_map/ppermute | solution.py:494
  92.8 10.9 %collective-permute-start.14 = (f32[96,128]{1,0:T(8,128)S(1)}, f32[96,128]{1,0:T(8,128)S(1)}, u32[]{:S(2)}, u32[]{:S(2)}) collective-permute-start(f32[96,128]{1,0:T(8,128)S(1)} %get-tuple-element.98), channel_id=1, source_target_pairs={{0,4},{1,5},{2,6},{3,7},{4,0},{5,1},{6,2},{7,3},{8,12},{9,13},{10,... | collective-permute-start | bytes 147464 | tf_op jit(solution)/shard_map/ppermute | solution.py:494
  96.0 7.6 %collective-permute-start.15 = (f32[96,128]{1,0:T(8,128)S(1)}, f32[96,128]{1,0:T(8,128)S(1)}, u32[]{:S(2)}, u32[]{:S(2)}) collective-permute-start(f32[96,128]{1,0:T(8,128)S(1)} %get-tuple-element.97), channel_id=1, source_target_pairs={{0,6},{1,7},{2,4},{3,5},{4,2},{5,3},{6,0},{7,1},{8,14},{9,15},{10,... | collective-permute-start | bytes 147464 | tf_op jit(solution)/shard_map/ppermute | solution.py:494
  103.9 2.0 %collective-permute-start.16 = (f32[96,128]{1,0:T(8,128)S(1)}, f32[96,128]{1,0:T(8,128)S(1)}, u32[]{:S(2)}, u32[]{:S(2)}) collective-permute-start(f32[96,128]{1,0:T(8,128)S(1)} %fusion.5), channel_id=1, source_target_pairs={{0,8},{8,0},{16,24},{24,16},{1,9},{9,1},{17,25},{25,17},{2,10},{10... | collective-permute-start | bytes 147464 | tf_op jit(solution)/shard_map/ppermute | solution.py:494
  104.0 4.2 %collective-permute-start.17 = (f32[96,128]{1,0:T(8,128)S(1)}, f32[96,128]{1,0:T(8,128)S(1)}, u32[]{:S(2)}, u32[]{:S(2)}) collective-permute-start(f32[96,128]{1,0:T(8,128)S(1)} %fusion.5), channel_id=1, source_target_pairs={{0,16},{8,24},{16,0},{24,8},{1,17},{9,25},{17,1},{25,9},{2,18},{10... | collective-permute-start | bytes 147464 | tf_op jit(solution)/shard_map/ppermute | solution.py:494
  105.8 3.7 %collective-permute-start.18 = (f32[96,128]{1,0:T(8,128)S(1)}, f32[96,128]{1,0:T(8,128)S(1)}, u32[]{:S(2)}, u32[]{:S(2)}) collective-permute-start(f32[96,128]{1,0:T(8,128)S(1)} %fusion.5), channel_id=1, source_target_pairs={{0,24},{8,16},{16,8},{24,0},{1,25},{9,17},{17,9},{25,1},{2,26},{10... | collective-permute-start | bytes 147464 | tf_op jit(solution)/shard_map/ppermute | solution.py:494

commit v10 on v8

--- a/solution.py
+++ b/solution.py
@@ -9,8 +9,8 @@
 
 high = lax.Precision.HIGH
 empty_slot = 9
-near_vmem = 18 * 1024 * 1024
-merge_vmem = 12 * 1024 * 1024
+near_vmem = 17 * 1024 * 1024
+merge_vmem = 8 * 1024 * 1024
 
 
 def dot_t(a, b, dims, precision=None):
@@ -189,11 +189,10 @@
     return near_part((density, pu_near, pu_far), plan, (6, gv), near_blocks, far_right, neighbours, prior, 0.5)
 
 
-def near_columns(density, pu_near, pu_far, corner_near, corner_far, beside, ends, mids, near_blocks, far_right, neighbours, prior):
+def near_column(far, density, pu_near, pu_far, corner_near, corner_far, halo, near_blocks, far_right, neighbours, prior):
     gu, gv = density.shape[:2]
-    per_step = 2
+    per_step = 3
     spans = []
-    parts = []
 
     def near_row():
         return (gu + 1) * (1 - odd("pu"))
@@ -201,60 +200,69 @@
     def far_row():
         return (gu + 1) * odd("pu")
 
-    for far in (0, 1):
-
-        def left_side(far=far):
-            return 1 - odd("pv") if far else odd("pv")
-
-        def inner(source, at, ext_row, far=far, left_side=left_side):
-            def views(srcs, ext):
-                view = srcs[source]
-                if at is not None:
-                    view = view.at[at]
-                from_cols = pl.ds((gv - 2) * (1 - left_side()), 2)
-                return view.at[from_cols], ext.at[ext_row(), pl.ds(3 * far + left_side(), 2)]
-
-            return views
-
-        def outer(source, at, ext_row, far=far, left_side=left_side):
-            return lambda srcs, ext: (srcs[source].at[at], ext.at[ext_row(), 3 * far + 2 * (1 - left_side())])
-
-        for row in range(gu):
-            at = max((row - 1) // per_step, 0)
-            here = lambda row=row: row + 1
-            spans.append((at, inner(0, row, here)))
-            if not far:
-                spans.append((at, outer(5, row, here)))
-            elif row in (0, gu - 1):
-                spans.append((at, outer(6, min(row, 1), here)))
-            else:
-                spans.append((at, outer(7, row - 1, here)))
-        spans.append((0, inner(1, None, near_row)))
-        spans.append((0, inner(2, None, far_row)))
-        spans.append((0, outer(3, far, near_row)))
-        spans.append((0, outer(4, far, far_row)))
-        col = lambda left_side=left_side: (gv - 1) * (1 - left_side())
-        parts += [(row, per_step, col, row + 1, per_step, 3 * far + 1) for row in range(per_step)]
+    def left_side():
+        return 1 - odd("pv") if far else odd("pv")
+
+    def inner(source, at, ext_row):
+        def views(srcs, ext):
+            view = srcs[source]
+            if at is not None:
+                view = view.at[at]
+            return view.at[pl.ds((gv - 2) * (1 - left_side()), 2)], ext.at[ext_row(), pl.ds(left_side(), 2)]
+
+        return views
+
+    def outer(source, at, ext_row):
+        return lambda srcs, ext: (srcs[source].at[at], ext.at[ext_row(), 2 * (1 - left_side())])
+
+    for row in range(gu):
+        at = max((row - 1) // per_step, 0)
+        here = lambda row=row: row + 1
+        spans.append((at, inner(0, row, here)))
+        if len(halo) == 1:
+            spans.append((at, outer(5, row, here)))
+        elif row in (0, gu - 1):
+            spans.append((at, outer(5, min(row, 1), here)))
+        else:
+            spans.append((at, outer(6, row - 1, here)))
+    spans.append((0, inner(1, None, near_row)))
+    spans.append((0, inner(2, None, far_row)))
+    spans.append((0, outer(3, far, near_row)))
+    spans.append((0, outer(4, far, far_row)))
+    col = lambda: (gv - 1) * (1 - left_side())
+    parts = [(row, per_step, col, row + 1, per_step, 1) for row in range(per_step)]
     plan = (gu // per_step, spans, parts)
-    sources = (density, pu_near, pu_far, corner_near, corner_far, beside, ends, mids)
-    return near_part(sources, plan, (gu + 2, 6), near_blocks, far_right, neighbours, prior, 0.5)
-
-
-def corners_kernel(beside, ends, to_near, to_far):
+    sources = (density, pu_near, pu_far, corner_near, corner_far, *halo)
+    return near_part(sources, plan, (gu + 2, 3), near_blocks, far_right, neighbours, prior, 0.5)
+
+
+def run_copies(pairs, sems):
+    copies = [
+        pltpu.make_async_copy(source, target, sems.at[index])
+        for index, (source, target) in enumerate(pairs)
+    ]
+    for copy in copies:
+        copy.start()
+    return copies
+
+
+def corners_kernel(beside, ends, to_near, to_far, sems):
     low = odd("pu")
     rows = beside.shape[0]
+    pairs = []
     for target, last in ((to_near, 1 - low), (to_far, low)):
-        target[0] = beside[(rows - 1) * last]
-        target[1] = ends[last]
+        pairs += [(beside.at[(rows - 1) * last], target.at[0]), (ends.at[last], target.at[1])]
+    for copy in run_copies(pairs, sems):
+        copy.wait()
 
 
 def patch_corners(beside, ends):
-    whole = pl.BlockSpec(memory_space=pltpu.VMEM)
     return pl.pallas_call(
         corners_kernel,
-        in_specs=[whole, whole],
-        out_specs=[whole, whole],
+        in_specs=[pl.BlockSpec(memory_space=pl.ANY)] * 2,
+        out_specs=[pl.BlockSpec(memory_space=pltpu.VMEM)] * 2,
         out_shape=[jax.ShapeDtypeStruct(ends.shape, ends.dtype)] * 2,
+        scratch_shapes=[pltpu.SemaphoreType.DMA((4,))],
         cost_estimate=cost(0.7),
         compiler_params=pltpu.CompilerParams(vmem_limit_bytes=merge_vmem),
     )(beside, ends)
@@ -361,16 +369,6 @@
     return value, tail[:, tail_lanes - 1 :]
 
 
-def run_copies(pairs, sems):
-    copies = [
-        pltpu.make_async_copy(source, target, sems.at[index])
-        for index, (source, target) in enumerate(pairs)
-    ]
-    for copy in copies:
-        copy.start()
-    return copies
-
-
 def leaf_kernel(counts, order_hbm, value_hbm, sketch_hbm, code_ref, sketch_ref, order, value, sketch, sems):
     pairs = [(value_hbm.at[0, 0], value), (order_hbm, order), (sketch_hbm, sketch)]
     for copy in run_copies(pairs, sems):
@@ -407,7 +405,8 @@
     gu, gv = density.shape[:2]
     near_col = (gv - 1) * (1 - odd("pv"))
     far_col = (gv - 1) * odd("pv")
-    pairs = [(density.at[(gu - 1) * (1 - odd("pu"))], pu_near), (density.at[(gu - 1) * odd("pu")], pu_far)]
+    pairs = [(density.at[(gu - 1) * odd("pu"), col], pu_far.at[col]) for col in range(gv)]
+    pairs += [(density.at[(gu - 1) * (1 - odd("pu")), col], pu_near.at[col]) for col in range(gv)]
     pairs += [(density.at[row, near_col], beside.at[row]) for row in range(gu)]
     pairs += [(density.at[(gu - 1) * row, far_col], ends.at[row]) for row in range(2)]
     pairs += [(density.at[row + 1, far_col], mids.at[row]) for row in range(gu - 2)]
@@ -423,7 +422,7 @@
         in_specs=[pl.BlockSpec(memory_space=pltpu.HBM)],
         out_specs=[pl.BlockSpec(memory_space=pltpu.VMEM)] * len(blocks),
         out_shape=[jax.ShapeDtypeStruct((count, size, rhs), density.dtype) for count in blocks],
-        scratch_shapes=[pltpu.SemaphoreType.DMA((2 * gu + 2,))],
+        scratch_shapes=[pltpu.SemaphoreType.DMA((2 * gu + 2 * gv,))],
         cost_estimate=cost(2.5),
         compiler_params=pltpu.CompilerParams(vmem_limit_bytes=merge_vmem),
     )(in_hbm(density))
@@ -550,30 +549,20 @@
         if level in (1, 2) or last:
             links, left = tied(neighbours, left)
         if level == 1:
-            corrected, coef = near_rows(density, pu_near, pu_far, near_blocks, far_right, links, corrected)
+            corrected, coef = near_middle(density, near_blocks, far_right, links, corrected)
         elif level == 2:
             ends, mids, left = tied(ends, mids, left)
             ends = swapped(ends, "pv", True)
             mids = swapped(mids, "pv", True)
-            corrected, coef = near_middle(density, near_blocks, far_right, links, corrected)
+            corrected, coef = near_rows(density, pu_near, pu_far, near_blocks, far_right, links, corrected)
         elif last:
             corner_near, corner_far = patch_corners(beside, ends)
             corner_near = swapped(corner_near, "pu", False)
             corner_far = swapped(corner_far, "pu", True)
-            corrected, coef = near_columns(
-                density,
-                pu_near,
-                pu_far,
-                corner_near,
-                corner_far,
-                beside,
-                ends,
-                mids,
-                near_blocks,
-                far_right,
-                links,
-                corrected,
-            )
+            halo = (density, pu_near, pu_far, corner_near, corner_far)
+            corrected, coef = near_column(0, *halo, (beside,), near_blocks, far_right, links, corrected)
+            coefs.append(coef)
+            corrected, coef = near_column(1, *halo, (ends, mids), near_blocks, far_right, links, corrected)
         if coef is not None:
             other, coef = tied(other, coef)
             coefs.append(coef)

time: 108 us -> 105 us (0.972)
  starting transfers between devices: 30.5 us -> 23.1 us
  Pallas kernels: 56.2 us -> 60.7 us
    ppermute x12, starting transfers between devices: 25.9 us -> 18.8 us  [from_partner(): return lax.ppermute(value, axis, pairs)]
    pallas_call x3 -> x4, Pallas kernels: 19.8 us -> 23.2 us  [near_part(): pl.pallas_call(functools.partial(near_kernel, plan, len(sources)), grid=(...]
  transfers between devices with their start and end apart: 19 -> 19, of which waited for: 7 -> 8; matrix products, arithmetic and copies ran while one was open for 0% -> 0% of each run, Pallas kernels for 51% -> 57%
where the time goes in v10:
time: 105 us
  Pallas kernels  60.7 us (58%)
  starting transfers between devices  23.1 us (22%)
  waiting for transfers between devices  16.3 us (16%)
  local copies, waits for them, and re-layouts  1.99 us (2%)
  matrix products  1.53 us (1%)
    pallas_call x5, Pallas kernels, merge(): pl.pallas_call(functools.partial(merge_kernel, bool(paths), bool(last_row...  30.6 us
    pallas_call x4, Pallas kernels, near_part(): pl.pallas_call(functools.partial(near_kernel, plan, len(sources)), grid=(...  23.2 us
    ppermute x12, starting transfers between devices, from_partner(): return lax.ppermute(value, axis, pairs)  18.8 us
    ppermute x12, waiting for transfers between devices, from_partner(): return lax.ppermute(value, axis, pairs)  16.3 us
    ppermute x7, starting transfers between devices, swapped(): return lax.ppermute(value, axis, pairs)  4.34 us
    pallas_call x1, Pallas kernels, patch_edges(): pl.pallas_call(edges_kernel, in_specs=[pl.BlockSpec(memory_space=pltpu.HB...  3.49 us
  transfers between devices with their start and end apart: 19, of which 8 were waited for; matrix products, arithmetic and copies ran while one was open for 0% of the time, Pallas kernels for 57%

profile of v10, /device:TPU:0, one launch (start us, length us, event | category | flops | bytes accessed | tf_op | source)
XLA Modules:
  0.0 104.7 jit_solution(14357893733908582542)
XLA Ops:
  0.6 1.5 %shard_map.86 = (s16[128,1152]{1,0:T(8,128)(2,1)S(1)}, f32[128,256]{1,0:T(8,128)S(1)}) custom-call(s32[32]{0:T(128)} %order_hbm.1, f32[1,1,1024,128]{3,2,1,0:T(8,128)} %value_hbm.1, f32[256,128]{1,0:T(8,128)} %sketch_hbm.1), custom_call_target="tpu_custom_call" | custom-call | flops 1650000000 | tf_op jit(solution)/shard_map/pallas_call | solution.py:385
  2.1 3.0 %collective-permute-start = (s16[128,1152]{1,0:T(8,128)(2,1)S(1)}, s16[128,1152]{1,0:T(8,128)(2,1)S(1)}, u32[]{:S(2)}, u32[]{:S(2)}) collective-permute-start(s16[128,1152]{1,0:T(8,128)(2,1)S(1)} %get-tuple-element.54.mine_ref), channel_id=1, source_target_pairs={{0,1},{1,0},{2,3},{3,2},{4,5},{5,4},{6,7},{7,6},{8,9},{9,8},{10,11... | collective-permute-start | bytes 884744 | tf_op jit(solution)/shard_map/ppermute | solution.py:492
  5.1 3.5 %shard_map.87 = (bf16[6,128,768]{2,1,0:T(8,128)(2,1)S(1)}, bf16[2,128,768]{2,1,0:T(8,128)(2,1)S(1)}, bf16[4,128,768]{2,1,0:T(8,128)(2,1)}, bf16[6,128,768]{2,1,0:T(8,128)(2,1)S(1)}, bf16[6,128,768]{2,1,0:T(8,128)(2,1)S(1)}) custom-call(bf16[6,6,128,768]{3,2,1,0:T(8,128)(2,1)} %refs_0_.3), custom_call_target="tpu_custom_call" | custom-call | flops 2750000128 | tf_op jit(solution)/shard_map/pallas_call | solution.py:420
  8.7 0.7 collective-permute-start.4
  9.5 2.6 %collective-permute-done.other_ref = s16[128,1152]{1,0:T(8,128)(2,1)S(1)} collective-permute-done((s16[128,1152]{1,0:T(8,128)(2,1)S(1)}, s16[128,1152]{1,0:T(8,128)(2,1)S(1)}, u32[]{:S(2)}, u32[]{:S(2)}) %collective-permute-start) | collective-permute-done | bytes 294944 | tf_op jit(solution)/shard_map/ppermute | solution.py:492
  12.1 5.8 %shard_map.88 = (s16[128,1152]{1,0:T(8,128)(2,1)S(1)}, f32[128,128]{1,0:T(8,128)S(1)}) custom-call(s16[128,1152]{1,0:T(8,128)(2,1)S(1)} %get-tuple-element.54.mine_ref, s16[128,1152]{1,0:T(8,128)(2,1)S(1)} %collective-permute-done.other_ref, f32[128,256]{1,0:T(8,128)S(1)} %get-tuple-element.55.sketch_ref), custom_call_target="tpu_custom_call" | custom-call | flops 9900000256 | tf_op jit(solution)/shard_map/pallas_call | solution.py:475
  18.0 1.9 %collective-permute-start.1 = (s16[128,1152]{1,0:T(8,128)(2,1)S(1)}, s16[128,1152]{1,0:T(8,128)(2,1)S(1)}, u32[]{:S(2)}, u32[]{:S(2)}) collective-permute-start(s16[128,1152]{1,0:T(8,128)(2,1)S(1)} %get-tuple-element.57.mine_ref), channel_id=1, source_target_pairs={{0,2},{1,3},{2,0},{3,1},{4,6},{5,7},{6,4},{7,5},{8,10},{9,11},{10,... | collective-permute-start | bytes 884744 | tf_op jit(solution)/shard_map/ppermute | solution.py:492
  19.9 7.4 %shard_map.89 = (bf16[6,6,128,768]{3,2,1,0:T(8,128)(2,1)}, f32[128,768]{1,0:T(8,128)S(1)}) custom-call(s32[6,6,6]{2,1,0:T(8,128)} %nb_hbm.3, bf16[6,6,6,128,128]{4,3,2,1,0:T(8,128)(2,1)} %near_hbm.7, bf16[6,6,128,128]{3,2,1,0:T(8,128)(2,1)} %right_hbm.7, bf16[6,6,128,768]{3,2,1,0:T(8,128)(2,1)} %refs_0_.3), custom_call_target="tpu_custom_call" | custom-call | flops 550000000 | tf_op jit(solution)/shard_map/pallas_call | solution.py:137
  27.4 5.9 %shard_map.90 = (s16[128,1152]{1,0:T(8,128)(2,1)S(1)}, f32[128,128]{1,0:T(8,128)S(1)}) custom-call(s16[128,1152]{1,0:T(8,128)(2,1)S(1)} %get-tuple-element.57.mine_ref, s16[128,1152]{1,0:T(8,128)(2,1)S(1)} %collective-permute-done.1.other_ref, f32[128,256]{1,0:T(8,128)S(1)} %get-tuple-element.55.sketch_ref, f32[128,128]{1,0:T(8,128)S(1)} %get-tuple-element.61.refs_0_), custom_call_target="tpu_custom_call" | custom-call | flops 1650000000 | tf_op jit(solution)/shard_map/pallas_call | solution.py:475
  33.3 2.7 %collective-permute-start.2 = (s16[128,1152]{1,0:T(8,128)(2,1)S(1)}, s16[128,1152]{1,0:T(8,128)(2,1)S(1)}, u32[]{:S(2)}, u32[]{:S(2)}) collective-permute-start(s16[128,1152]{1,0:T(8,128)(2,1)S(1)} %get-tuple-element.64.mine_ref), channel_id=1, source_target_pairs={{0,4},{1,5},{2,6},{3,7},{4,0},{5,1},{6,2},{7,3},{8,12},{9,13},{10,... | collective-permute-start | bytes 884744 | tf_op jit(solution)/shard_map/ppermute | solution.py:492
  35.9 0.7 collective-permute-start.7
  36.6 1.6 %collective-permute-start.10 = (bf16[4,128,768]{2,1,0:T(8,128)(2,1)}, bf16[4,128,768]{2,1,0:T(8,128)(2,1)}, u32[]{:S(2)}, u32[]{:S(2)}) collective-permute-start(bf16[4,128,768]{2,1,0:T(8,128)(2,1)} %get-tuple-element.79), channel_id=1, source_target_pairs={{1,2},{2,1},{3,4},{4,3},{5,6},{6,5},{9,10},{10,9},{11,12},{12,11},... | collective-permute-start | bytes 2359304 | tf_op jit(solution)/shard_map/ppermute | solution.py:504
  38.2 4.8 %shard_map.91 = (bf16[6,6,128,768]{3,2,1,0:T(8,128)(2,1)}, f32[128,768]{1,0:T(8,128)S(1)}) custom-call(s32[6,6,6]{2,1,0:T(8,128)} %nb_hbm.3, bf16[6,6,6,128,128]{4,3,2,1,0:T(8,128)(2,1)} %near_hbm.7, bf16[6,6,128,128]{3,2,1,0:T(8,128)(2,1)} %right_hbm.7, bf16[6,6,128,768]{3,2,1,0:T(8,128)(2,1)} %refs_0_.3, ...), custom_call_target="tpu_custom_call", output_to_operand_aliasing={{0}: (6, {})} | custom-call | flops 550000000 | tf_op jit(solution)/shard_map/pallas_call | solution.py:137
  43.0 7.0 %collective-permute-done.2.other_ref = s16[128,1152]{1,0:T(8,128)(2,1)S(1)} collective-permute-done((s16[128,1152]{1,0:T(8,128)(2,1)S(1)}, s16[128,1152]{1,0:T(8,128)(2,1)S(1)}, u32[]{:S(2)}, u32[]{:S(2)}) %collective-permute-start.2) | collective-permute-done | bytes 294944 | tf_op jit(solution)/shard_map/ppermute | solution.py:492
  50.0 5.9 %shard_map.92 = (s16[128,1152]{1,0:T(8,128)(2,1)S(1)}, f32[128,128]{1,0:T(8,128)S(1)}) custom-call(s16[128,1152]{1,0:T(8,128)(2,1)S(1)} %get-tuple-element.64.mine_ref, s16[128,1152]{1,0:T(8,128)(2,1)S(1)} %collective-permute-done.2.other_ref, f32[128,256]{1,0:T(8,128)S(1)} %get-tuple-element.55.sketch_ref, f32[128,128]{1,0:T(8,128)S(1)} %get-tuple-element.71.refs_0_), custom_call_target="tpu_custom_call" | custom-call | flops 550000000 | tf_op jit(solution)/shard_map/pallas_call | solution.py:475
  56.0 1.9 %shard_map.94 = (bf16[2,128,768]{2,1,0:T(8,128)(2,1)}, bf16[2,128,768]{2,1,0:T(8,128)(2,1)}) custom-call(bf16[6,128,768]{2,1,0:T(8,128)(2,1)S(1)} %collective-permute-done.6.beside.refs_5_, bf16[2,128,768]{2,1,0:T(8,128)(2,1)S(1)} %collective-permute-done.7.ends.refs_5_), custom_call_target="tpu_custom_call" | custom-call | flops 770000000 | tf_op jit(solution)/shard_map/pallas_call | solution.py:260
  59.3 6.6 %shard_map.93 = (s16[128,1152]{1,0:T(8,128)(2,1)}, f32[128,128]{1,0:T(8,128)S(1)}) custom-call(s16[128,1152]{1,0:T(8,128)(2,1)S(1)} %get-tuple-element.72.mine_ref, s16[128,1152]{1,0:T(8,128)(2,1)S(1)} %collective-permute-done.5.other_ref, f32[128,256]{1,0:T(8,128)S(1)} %get-tuple-element.55.sketch_ref), custom_call_target="tpu_custom_call" | custom-call | flops 550000000 | tf_op jit(solution)/shard_map/pallas_call | solution.py:475
  66.4 2.9 %collective-permute-start.11 = (s16[128,1152]{1,0:T(8,128)(2,1)}, s16[128,1152]{1,0:T(8,128)(2,1)}, u32[]{:S(2)}, u32[]{:S(2)}) collective-permute-start(s16[128,1152]{1,0:T(8,128)(2,1)} %get-tuple-element.91.mine_ref), channel_id=1, source_target_pairs={{0,16},{8,24},{16,0},{24,8},{1,17},{9,25},{17,1},{25,9},{2,18},{10... | collective-permute-start | bytes 884744 | tf_op jit(solution)/shard_map/ppermute | solution.py:492
  69.3 1.3 %copy-done.1 = bf16[6,128,768]{2,1,0:T(8,128)(2,1)S(1)} copy-done((bf16[6,128,768]{2,1,0:T(8,128)(2,1)S(1)}, bf16[6,128,768]{2,1,0:T(8,128)(2,1)}, u32[]{:S(2)}) %copy-start.1) | copy-done | bytes 1179672
  70.6 5.9 %shard_map.95 = (bf16[6,6,128,768]{3,2,1,0:T(8,128)(2,1)}, f32[128,768]{1,0:T(8,128)S(1)}) custom-call(s32[6,6,6]{2,1,0:T(8,128)} %nb_hbm.3, bf16[6,6,6,128,128]{4,3,2,1,0:T(8,128)(2,1)} %near_hbm.7, bf16[6,6,128,128]{3,2,1,0:T(8,128)(2,1)} %right_hbm.7, bf16[6,6,128,768]{3,2,1,0:T(8,128)(2,1)} %refs_0_.3, ...), custom_call_target="tpu_custom_call", output_to_operand_aliasing={{0}: (9, {})} | custom-call | flops 550000000 | tf_op jit(solution)/shard_map/pallas_call | solution.py:137
  76.6 5.1 %shard_map.96 = (bf16[6,6,128,768]{3,2,1,0:T(8,128)(2,1)}, f32[128,768]{1,0:T(8,128)S(1)}) custom-call(s32[6,6,6]{2,1,0:T(8,128)} %nb_hbm.3, bf16[6,6,6,128,128]{4,3,2,1,0:T(8,128)(2,1)} %near_hbm.7, bf16[6,6,128,128]{3,2,1,0:T(8,128)(2,1)} %right_hbm.7, bf16[6,6,128,768]{3,2,1,0:T(8,128)(2,1)} %refs_0_.3, ...), custom_call_target="tpu_custom_call", output_to_operand_aliasing={{0}: (10, {})} | custom-call | flops 550000000 | tf_op jit(solution)/shard_map/pallas_call | solution.py:137
  82.3 1.8 %collective-permute-start.12 = (f32[4,96,128]{2,1,0:T(8,128)S(1)}, f32[4,96,128]{2,1,0:T(8,128)S(1)}, u32[]{:S(2)}, u32[]{:S(2)}) collective-permute-start(f32[4,96,128]{2,1,0:T(8,128)S(1)} %dynamic-slice_bitcast_fusion), channel_id=1, source_target_pairs={{0,1},{1,0},{2,3},{3,2},{4,5},{5,4},{6,7},{7,6},{8,9},{9,8},{10,11... | collective-permute-start | bytes 589832 | tf_op jit(solution)/shard_map/ppermute | solution.py:492
  84.1 6.5 %shard_map.97 = (f32[128,256]{1,0:T(8,128)S(1)}, f32[128,128]{1,0:T(8,128)S(1)}) custom-call(s16[128,1152]{1,0:T(8,128)(2,1)} %get-tuple-element.91.mine_ref, s16[128,1152]{1,0:T(8,128)(2,1)} %collective-permute-done.11.other_ref, f32[128,256]{1,0:T(8,128)S(1)} %copy-done.9, f32[128,128]{1,0:T(8,128)S(1)} %copy-done.11), custom_call_target="tpu_custom_call" | custom-call | flops 550000000 | tf_op jit(solution)/shard_map/pallas_call | solution.py:475
  90.6 2.8 %collective-permute-start.15 = (f32[96,128]{1,0:T(8,128)S(1)}, f32[96,128]{1,0:T(8,128)S(1)}, u32[]{:S(2)}, u32[]{:S(2)}) collective-permute-start(f32[96,128]{1,0:T(8,128)S(1)} %get-tuple-element.99), channel_id=1, source_target_pairs={{0,6},{1,7},{2,4},{3,5},{4,2},{5,3},{6,0},{7,1},{8,14},{9,15},{10,... | collective-permute-start | bytes 147464 | tf_op jit(solution)/shard_map/ppermute | solution.py:492
  93.4 1.5 %collective-permute-start.14 = (f32[96,128]{1,0:T(8,128)S(1)}, f32[96,128]{1,0:T(8,128)S(1)}, u32[]{:S(2)}, u32[]{:S(2)}) collective-permute-start(f32[96,128]{1,0:T(8,128)S(1)} %get-tuple-element.100), channel_id=1, source_target_pairs={{0,4},{1,5},{2,6},{3,7},{4,0},{5,1},{6,2},{7,3},{8,12},{9,13},{10,... | collective-permute-start | bytes 147464 | tf_op jit(solution)/shard_map/ppermute | solution.py:492
  95.2 1.5 %collective-permute-done.15 = f32[96,128]{1,0:T(8,128)S(1)} collective-permute-done((f32[96,128]{1,0:T(8,128)S(1)}, f32[96,128]{1,0:T(8,128)S(1)}, u32[]{:S(2)}, u32[]{:S(2)}) %collective-permute-start.15) | collective-permute-done | bytes 49184 | tf_op jit(solution)/shard_map/ppermute | solution.py:492
  96.7 1.7 %collective-permute-done.14 = f32[96,128]{1,0:T(8,128)S(1)} collective-permute-done((f32[96,128]{1,0:T(8,128)S(1)}, f32[96,128]{1,0:T(8,128)S(1)}, u32[]{:S(2)}, u32[]{:S(2)}) %collective-permute-start.14) | collective-permute-done | bytes 49184 | tf_op jit(solution)/shard_map/ppermute | solution.py:492
  99.3 0.8 collective-permute-start.17
  100.0 1.1 %collective-permute-start.16 = (f32[96,128]{1,0:T(8,128)S(1)}, f32[96,128]{1,0:T(8,128)S(1)}, u32[]{:S(2)}, u32[]{:S(2)}) collective-permute-start(f32[96,128]{1,0:T(8,128)S(1)} %fusion.6), channel_id=1, source_target_pairs={{0,8},{8,0},{16,24},{24,16},{1,9},{9,1},{17,25},{25,17},{2,10},{10... | collective-permute-start | bytes 147464 | tf_op jit(solution)/shard_map/ppermute | solution.py:492
  101.1 1.7 %collective-permute-done.18 = f32[96,128]{1,0:T(8,128)S(1)} collective-permute-done((f32[96,128]{1,0:T(8,128)S(1)}, f32[96,128]{1,0:T(8,128)S(1)}, u32[]{:S(2)}, u32[]{:S(2)}) %collective-permute-start.18) | collective-permute-done | bytes 49184 | tf_op jit(solution)/shard_map/ppermute | solution.py:492
  102.8 1.1 %collective-permute-done.17 = f32[96,128]{1,0:T(8,128)S(1)} collective-permute-done((f32[96,128]{1,0:T(8,128)S(1)}, f32[96,128]{1,0:T(8,128)S(1)}, u32[]{:S(2)}, u32[]{:S(2)}) %collective-permute-start.17) | collective-permute-done | bytes 49184 | tf_op jit(solution)/shard_map/ppermute | solution.py:492
  103.8 0.8 fusion.8
  (48 shorter events, 4.1 us)
Async XLA Ops:
  2.1 57.1 %copy-start.8 = (f32[128,256]{1,0:T(8,128)}, f32[128,256]{1,0:T(8,128)S(1)}, u32[]{:S(2)}) copy-start(f32[128,256]{1,0:T(8,128)S(1)} %get-tuple-element.55.sketch_ref) | copy-start | bytes 393220
  2.1 10.0 %collective-permute-start = (s16[128,1152]{1,0:T(8,128)(2,1)S(1)}, s16[128,1152]{1,0:T(8,128)(2,1)S(1)}, u32[]{:S(2)}, u32[]{:S(2)}) collective-permute-start(s16[128,1152]{1,0:T(8,128)(2,1)S(1)} %get-tuple-element.54.mine_ref), channel_id=1, source_target_pairs={{0,1},{1,0},{2,3},{3,2},{4,5},{5,4},{6,7},{7,6},{8,9},{9,8},{10,11... | collective-permute-start | bytes 884744 | tf_op jit(solution)/shard_map/ppermute | solution.py:492
  8.6 28.0 %collective-permute-start.3 = (bf16[6,128,768]{2,1,0:T(8,128)(2,1)S(1)}, bf16[6,128,768]{2,1,0:T(8,128)(2,1)S(1)}, u32[]{:S(2)}, u32[]{:S(2)}) collective-permute-start(bf16[6,128,768]{2,1,0:T(8,128)(2,1)S(1)} %get-tuple-element.66), channel_id=1, source_target_pairs={{0,8},{8,0},{16,24},{24,16},{1,9},{9,1},{17,25},{25,17},{2,10},{10... | collective-permute-start | bytes 3538952 | tf_op jit(solution)/shard_map/ppermute | solution.py:504
  8.7 29.5 %collective-permute-start.4 = (bf16[6,128,768]{2,1,0:T(8,128)(2,1)S(1)}, bf16[6,128,768]{2,1,0:T(8,128)(2,1)S(1)}, u32[]{:S(2)}, u32[]{:S(2)}) collective-permute-start(bf16[6,128,768]{2,1,0:T(8,128)(2,1)S(1)} %get-tuple-element.67), channel_id=1, source_target_pairs={{8,16},{16,8},{9,17},{17,9},{10,18},{18,10},{11,19},{19,11},{12,20... | collective-permute-start | bytes 3538952 | tf_op jit(solution)/shard_map/ppermute | solution.py:504
  9.4 46.6 %collective-permute-start.6 = (bf16[6,128,768]{2,1,0:T(8,128)(2,1)S(1)}, bf16[6,128,768]{2,1,0:T(8,128)(2,1)S(1)}, u32[]{:S(2)}, u32[]{:S(2)}) collective-permute-start(bf16[6,128,768]{2,1,0:T(8,128)(2,1)S(1)} %get-tuple-element.75), channel_id=1, source_target_pairs={{0,1},{1,0},{2,3},{3,2},{4,5},{5,4},{6,7},{7,6},{8,9},{9,8},{10,11... | collective-permute-start | bytes 3538952 | tf_op jit(solution)/shard_map/ppermute | solution.py:504
  18.0 9.4 %collective-permute-start.1 = (s16[128,1152]{1,0:T(8,128)(2,1)S(1)}, s16[128,1152]{1,0:T(8,128)(2,1)S(1)}, u32[]{:S(2)}, u32[]{:S(2)}) collective-permute-start(s16[128,1152]{1,0:T(8,128)(2,1)S(1)} %get-tuple-element.57.mine_ref), channel_id=1, source_target_pairs={{0,2},{1,3},{2,0},{3,1},{4,6},{5,7},{6,4},{7,5},{8,10},{9,11},{10,... | collective-permute-start | bytes 884744 | tf_op jit(solution)/shard_map/ppermute | solution.py:492
  33.3 16.7 %collective-permute-start.2 = (s16[128,1152]{1,0:T(8,128)(2,1)S(1)}, s16[128,1152]{1,0:T(8,128)(2,1)S(1)}, u32[]{:S(2)}, u32[]{:S(2)}) collective-permute-start(s16[128,1152]{1,0:T(8,128)(2,1)S(1)} %get-tuple-element.64.mine_ref), channel_id=1, source_target_pairs={{0,4},{1,5},{2,6},{3,7},{4,0},{5,1},{6,2},{7,3},{8,12},{9,13},{10,... | collective-permute-start | bytes 884744 | tf_op jit(solution)/shard_map/ppermute | solution.py:492
  35.9 20.1 %collective-permute-start.7 = (bf16[2,128,768]{2,1,0:T(8,128)(2,1)S(1)}, bf16[2,128,768]{2,1,0:T(8,128)(2,1)S(1)}, u32[]{:S(2)}, u32[]{:S(2)}) collective-permute-start(bf16[2,128,768]{2,1,0:T(8,128)(2,1)S(1)} %get-tuple-element.76), channel_id=1, source_target_pairs={{1,2},{2,1},{3,4},{4,3},{5,6},{6,5},{9,10},{10,9},{11,12},{12,11},... | collective-permute-start | bytes 1179656 | tf_op jit(solution)/shard_map/ppermute | solution.py:504
  36.6 39.9 %collective-permute-start.10 = (bf16[4,128,768]{2,1,0:T(8,128)(2,1)}, bf16[4,128,768]{2,1,0:T(8,128)(2,1)}, u32[]{:S(2)}, u32[]{:S(2)}) collective-permute-start(bf16[4,128,768]{2,1,0:T(8,128)(2,1)} %get-tuple-element.79), channel_id=1, source_target_pairs={{1,2},{2,1},{3,4},{4,3},{5,6},{6,5},{9,10},{10,9},{11,12},{12,11},... | collective-permute-start | bytes 2359304 | tf_op jit(solution)/shard_map/ppermute | solution.py:504
  43.0 15.0 %copy-start.2 = (f32[128,768]{1,0:T(8,128)}, f32[128,768]{1,0:T(8,128)S(1)}, u32[]{:S(2)}) copy-start(f32[128,768]{1,0:T(8,128)S(1)} %get-tuple-element.84) | copy-start | bytes 1179652
  55.9 2.1 %copy-start.6 = (f32[128,128]{1,0:T(8,128)}, f32[128,128]{1,0:T(8,128)S(1)}, u32[]{:S(2)}) copy-start(f32[128,128]{1,0:T(8,128)S(1)} %get-tuple-element.88) | copy-start | bytes 196612
  55.9 3.3 %collective-permute-start.5 = (s16[128,1152]{1,0:T(8,128)(2,1)S(1)}, s16[128,1152]{1,0:T(8,128)(2,1)S(1)}, u32[]{:S(2)}, u32[]{:S(2)}) collective-permute-start(s16[128,1152]{1,0:T(8,128)(2,1)S(1)} %get-tuple-element.72.mine_ref), channel_id=1, source_target_pairs={{0,8},{8,0},{16,24},{24,16},{1,9},{9,1},{17,25},{25,17},{2,10},{10... | collective-permute-start | bytes 884744 | tf_op jit(solution)/shard_map/ppermute | solution.py:492
  56.0 2.0 %copy-start.4 = (bf16[2,128,768]{2,1,0:T(8,128)(2,1)}, bf16[2,128,768]{2,1,0:T(8,128)(2,1)S(1)}, u32[]{:S(2)}) copy-start(bf16[2,128,768]{2,1,0:T(8,128)(2,1)S(1)} %collective-permute-done.7.ends.refs_5_) | copy-start | bytes 1179652
  56.0 2.0 %copy-start = (bf16[6,128,768]{2,1,0:T(8,128)(2,1)}, bf16[6,128,768]{2,1,0:T(8,128)(2,1)S(1)}, u32[]{:S(2)}) copy-start(bf16[6,128,768]{2,1,0:T(8,128)(2,1)S(1)} %collective-permute-done.6.beside.refs_5_) | copy-start | bytes 3538948
  58.0 11.3 %collective-permute-start.8 = (bf16[2,128,768]{2,1,0:T(8,128)(2,1)}, bf16[2,128,768]{2,1,0:T(8,128)(2,1)S(1)}, u32[]{:S(2)}, u32[]{:S(2)}) collective-permute-start(bf16[2,128,768]{2,1,0:T(8,128)(2,1)} %get-tuple-element.77), channel_id=1, source_target_pairs={{0,8},{8,0},{16,24},{24,16},{1,9},{9,1},{17,25},{25,17},{2,10},{10... | collective-permute-start | bytes 1179656 | tf_op jit(solution)/shard_map/ppermute | solution.py:504
  58.6 10.8 %collective-permute-start.9 = (bf16[2,128,768]{2,1,0:T(8,128)(2,1)}, bf16[2,128,768]{2,1,0:T(8,128)(2,1)S(1)}, u32[]{:S(2)}, u32[]{:S(2)}) collective-permute-start(bf16[2,128,768]{2,1,0:T(8,128)(2,1)} %get-tuple-element.78), channel_id=1, source_target_pairs={{8,16},{16,8},{9,17},{17,9},{10,18},{18,10},{11,19},{19,11},{12,20... | collective-permute-start | bytes 1179656 | tf_op jit(solution)/shard_map/ppermute | solution.py:504
  65.8 0.6 copy-start.10
  66.4 15.3 %collective-permute-start.11 = (s16[128,1152]{1,0:T(8,128)(2,1)}, s16[128,1152]{1,0:T(8,128)(2,1)}, u32[]{:S(2)}, u32[]{:S(2)}) collective-permute-start(s16[128,1152]{1,0:T(8,128)(2,1)} %get-tuple-element.91.mine_ref), channel_id=1, source_target_pairs={{0,16},{8,24},{16,0},{24,8},{1,17},{9,25},{17,1},{25,9},{2,18},{10... | collective-permute-start | bytes 884744 | tf_op jit(solution)/shard_map/ppermute | solution.py:492
  69.3 1.3 %copy-start.1 = (bf16[6,128,768]{2,1,0:T(8,128)(2,1)S(1)}, bf16[6,128,768]{2,1,0:T(8,128)(2,1)}, u32[]{:S(2)}) copy-start(bf16[6,128,768]{2,1,0:T(8,128)(2,1)} %copy-done) | copy-start | bytes 3538948
  70.6 5.9 %copy-start.5 = (bf16[2,128,768]{2,1,0:T(8,128)(2,1)S(1)}, bf16[2,128,768]{2,1,0:T(8,128)(2,1)}, u32[]{:S(2)}) copy-start(bf16[2,128,768]{2,1,0:T(8,128)(2,1)} %copy-done.4) | copy-start | bytes 1179652
  76.6 5.2 %copy-start.3 = (f32[128,768]{1,0:T(8,128)S(1)}, f32[128,768]{1,0:T(8,128)}, u32[]{:S(2)}) copy-start(f32[128,768]{1,0:T(8,128)} %copy-done.2) | copy-start | bytes 1179652
  76.6 5.2 %copy-start.7 = (f32[128,128]{1,0:T(8,128)S(1)}, f32[128,128]{1,0:T(8,128)}, u32[]{:S(2)}) copy-start(f32[128,128]{1,0:T(8,128)} %copy-done.6) | copy-start | bytes 196612
  81.7 2.3 %copy-start.9 = (f32[128,256]{1,0:T(8,128)S(1)}, f32[128,256]{1,0:T(8,128)}, u32[]{:S(2)}) copy-start(f32[128,256]{1,0:T(8,128)} %copy-done.8) | copy-start | bytes 393220
  81.8 2.3 %copy-start.11 = (f32[128,128]{1,0:T(8,128)S(1)}, f32[128,128]{1,0:T(8,128)}, u32[]{:S(2)}) copy-start(f32[128,128]{1,0:T(8,128)} %copy-done.10) | copy-start | bytes 196612
  82.3 8.3 %collective-permute-start.12 = (f32[4,96,128]{2,1,0:T(8,128)S(1)}, f32[4,96,128]{2,1,0:T(8,128)S(1)}, u32[]{:S(2)}, u32[]{:S(2)}) collective-permute-start(f32[4,96,128]{2,1,0:T(8,128)S(1)} %dynamic-slice_bitcast_fusion), channel_id=1, source_target_pairs={{0,1},{1,0},{2,3},{3,2},{4,5},{5,4},{6,7},{7,6},{8,9},{9,8},{10,11... | collective-permute-start | bytes 589832 | tf_op jit(solution)/shard_map/ppermute | solution.py:492
  90.6 6.1 %collective-permute-start.15 = (f32[96,128]{1,0:T(8,128)S(1)}, f32[96,128]{1,0:T(8,128)S(1)}, u32[]{:S(2)}, u32[]{:S(2)}) collective-permute-start(f32[96,128]{1,0:T(8,128)S(1)} %get-tuple-element.99), channel_id=1, source_target_pairs={{0,6},{1,7},{2,4},{3,5},{4,2},{5,3},{6,0},{7,1},{8,14},{9,15},{10,... | collective-permute-start | bytes 147464 | tf_op jit(solution)/shard_map/ppermute | solution.py:492
  93.4 5.0 %collective-permute-start.14 = (f32[96,128]{1,0:T(8,128)S(1)}, f32[96,128]{1,0:T(8,128)S(1)}, u32[]{:S(2)}, u32[]{:S(2)}) collective-permute-start(f32[96,128]{1,0:T(8,128)S(1)} %get-tuple-element.100), channel_id=1, source_target_pairs={{0,4},{1,5},{2,6},{3,7},{4,0},{5,1},{6,2},{7,3},{8,12},{9,13},{10,... | collective-permute-start | bytes 147464 | tf_op jit(solution)/shard_map/ppermute | solution.py:492
  94.9 4.1 %collective-permute-start.13 = (f32[96,128]{1,0:T(8,128)S(1)}, f32[96,128]{1,0:T(8,128)S(1)}, u32[]{:S(2)}, u32[]{:S(2)}) collective-permute-start(f32[96,128]{1,0:T(8,128)S(1)} %get-tuple-element.98), channel_id=1, source_target_pairs={{0,2},{1,3},{2,0},{3,1},{4,6},{5,7},{6,4},{7,5},{8,10},{9,11},{10,... | collective-permute-start | bytes 147464 | tf_op jit(solution)/shard_map/ppermute | solution.py:492
  99.2 3.6 %collective-permute-start.18 = (f32[96,128]{1,0:T(8,128)S(1)}, f32[96,128]{1,0:T(8,128)S(1)}, u32[]{:S(2)}, u32[]{:S(2)}) collective-permute-start(f32[96,128]{1,0:T(8,128)S(1)} %fusion.6), channel_id=1, source_target_pairs={{0,24},{8,16},{16,8},{24,0},{1,25},{9,17},{17,9},{25,1},{2,26},{10... | collective-permute-start | bytes 147464 | tf_op jit(solution)/shard_map/ppermute | solution.py:492
  99.3 4.6 %collective-permute-start.17 = (f32[96,128]{1,0:T(8,128)S(1)}, f32[96,128]{1,0:T(8,128)S(1)}, u32[]{:S(2)}, u32[]{:S(2)}) collective-permute-start(f32[96,128]{1,0:T(8,128)S(1)} %fusion.6), channel_id=1, source_target_pairs={{0,16},{8,24},{16,0},{24,8},{1,17},{9,25},{17,1},{25,9},{2,18},{10... | collective-permute-start | bytes 147464 | tf_op jit(solution)/shard_map/ppermute | solution.py:492
  100.0 3.8 %collective-permute-start.16 = (f32[96,128]{1,0:T(8,128)S(1)}, f32[96,128]{1,0:T(8,128)S(1)}, u32[]{:S(2)}, u32[]{:S(2)}) collective-permute-start(f32[96,128]{1,0:T(8,128)S(1)} %fusion.6), channel_id=1, source_target_pairs={{0,8},{8,0},{16,24},{24,16},{1,9},{9,1},{17,25},{25,17},{2,10},{10... | collective-permute-start | bytes 147464 | tf_op jit(solution)/shard_map/ppermute | solution.py:492

commit v11 on v10

--- a/solution.py
+++ b/solution.py
@@ -9,7 +9,7 @@
 
 high = lax.Precision.HIGH
 empty_slot = 9
-near_vmem = 17 * 1024 * 1024
+spare_vmem = 2 * 1024 * 1024
 merge_vmem = 8 * 1024 * 1024
 
 
@@ -134,6 +134,8 @@
         aliases = {len(args): 0}
         args.append(prior)
     held = pl.BlockSpec(memory_space=pltpu.HBM)
+    blocks = ext_shape[0] * ext_shape[1] + 2 * count + 2
+    scratch = 2 * size * (blocks * rhs + steps * count * (slots * size + rank)) + 8 * rank * rhs
     return pl.pallas_call(
         functools.partial(near_kernel, plan, len(sources)),
         grid=(steps,),
@@ -158,7 +160,7 @@
         input_output_aliases=aliases,
         cost_estimate=cost(time),
         compiler_params=pltpu.CompilerParams(
-            dimension_semantics=("arbitrary",), vmem_limit_bytes=near_vmem
+            dimension_semantics=("arbitrary",), vmem_limit_bytes=scratch + spare_vmem
         ),
     )(*args)
 
@@ -221,14 +223,14 @@
         spans.append((at, inner(0, row, here)))
         if len(halo) == 1:
             spans.append((at, outer(5, row, here)))
-        elif row in (0, gu - 1):
-            spans.append((at, outer(5, min(row, 1), here)))
         else:
-            spans.append((at, outer(6, row - 1, here)))
+            order = far_order(gu).index(row)
+            sent = halo[0].shape[0]
+            spans.append((at, outer(5, order, here) if order < sent else outer(6, order - sent, here)))
     spans.append((0, inner(1, None, near_row)))
     spans.append((0, inner(2, None, far_row)))
-    spans.append((0, outer(3, far, near_row)))
-    spans.append((0, outer(4, far, far_row)))
+    spans.append((0, outer(3, 0, near_row)))
+    spans.append((0, outer(4, 0, far_row)))
     col = lambda: (gv - 1) * (1 - left_side())
     parts = [(row, per_step, col, row + 1, per_step, 1) for row in range(per_step)]
     plan = (gu // per_step, spans, parts)
@@ -246,26 +248,23 @@
     return copies
 
 
-def corners_kernel(beside, ends, to_near, to_far, sems):
+def corners_kernel(last, column, to_near, to_far):
     low = odd("pu")
-    rows = beside.shape[0]
-    pairs = []
-    for target, last in ((to_near, 1 - low), (to_far, low)):
-        pairs += [(beside.at[(rows - 1) * last], target.at[0]), (ends.at[last], target.at[1])]
-    for copy in run_copies(pairs, sems):
-        copy.wait()
-
-
-def patch_corners(beside, ends):
-    return pl.pallas_call(
-        corners_kernel,
-        in_specs=[pl.BlockSpec(memory_space=pl.ANY)] * 2,
-        out_specs=[pl.BlockSpec(memory_space=pltpu.VMEM)] * 2,
-        out_shape=[jax.ShapeDtypeStruct(ends.shape, ends.dtype)] * 2,
-        scratch_shapes=[pltpu.SemaphoreType.DMA((4,))],
-        cost_estimate=cost(0.7),
+    to_near[0] = column[last * (1 - low)]
+    to_far[0] = column[last * low]
+
+
+def swapped_corners(column, last):
+    whole = pl.BlockSpec(memory_space=pltpu.VMEM)
+    to_near, to_far = pl.pallas_call(
+        functools.partial(corners_kernel, last),
+        in_specs=[whole],
+        out_specs=[whole, whole],
+        out_shape=[jax.ShapeDtypeStruct((1, *column.shape[1:]), column.dtype)] * 2,
+        cost_estimate=cost(0.5),
         compiler_params=pltpu.CompilerParams(vmem_limit_bytes=merge_vmem),
-    )(beside, ends)
+    )(column)
+    return swapped(to_near, "pu", False), swapped(to_far, "pu", True)
 
 
 def reciprocal(value):
@@ -369,6 +368,16 @@
     return value, tail[:, tail_lanes - 1 :]
 
 
+def run_copies(pairs, sems):
+    copies = [
+        pltpu.make_async_copy(source, target, sems.at[index])
+        for index, (source, target) in enumerate(pairs)
+    ]
+    for copy in copies:
+        copy.start()
+    return copies
+
+
 def leaf_kernel(counts, order_hbm, value_hbm, sketch_hbm, code_ref, sketch_ref, order, value, sketch, sems):
     pairs = [(value_hbm.at[0, 0], value), (order_hbm, order), (sketch_hbm, sketch)]
     for copy in run_copies(pairs, sems):
@@ -401,28 +410,33 @@
     )(in_hbm(order), in_hbm(value), in_hbm(sketch))
 
 
+def far_order(gu):
+    return [0, gu - 1, *range(1, gu - 1)]
+
+
 def edges_kernel(density, beside, ends, mids, pu_near, pu_far, sems):
     gu, gv = density.shape[:2]
     near_col = (gv - 1) * (1 - odd("pv"))
     far_col = (gv - 1) * odd("pv")
-    pairs = [(density.at[(gu - 1) * odd("pu"), col], pu_far.at[col]) for col in range(gv)]
-    pairs += [(density.at[(gu - 1) * (1 - odd("pu")), col], pu_near.at[col]) for col in range(gv)]
-    pairs += [(density.at[row, near_col], beside.at[row]) for row in range(gu)]
-    pairs += [(density.at[(gu - 1) * row, far_col], ends.at[row]) for row in range(2)]
-    pairs += [(density.at[row + 1, far_col], mids.at[row]) for row in range(gu - 2)]
+    pairs = [(density.at[row, near_col], beside.at[row]) for row in range(gu)]
+    for at, row in enumerate(far_order(gu)):
+        target = ends.at[at] if at < ends.shape[0] else mids.at[at - ends.shape[0]]
+        pairs.append((density.at[row, far_col], target))
+    pairs.append((density.at[(gu - 1) * (1 - odd("pu"))], pu_near))
+    pairs.append((density.at[(gu - 1) * odd("pu")], pu_far))
     for copy in run_copies(pairs, sems):
         copy.wait()
 
 
 def patch_edges(density):
     gu, gv, size, rhs = density.shape
-    blocks = (gu, 2, gu - 2, gv, gv)
+    blocks = (gu, 3, gu - 3, gv, gv)
     return pl.pallas_call(
         edges_kernel,
         in_specs=[pl.BlockSpec(memory_space=pltpu.HBM)],
         out_specs=[pl.BlockSpec(memory_space=pltpu.VMEM)] * len(blocks),
         out_shape=[jax.ShapeDtypeStruct((count, size, rhs), density.dtype) for count in blocks],
-        scratch_shapes=[pltpu.SemaphoreType.DMA((2 * gu + 2 * gv,))],
+        scratch_shapes=[pltpu.SemaphoreType.DMA((2 * gu + 2,))],
         cost_estimate=cost(2.5),
         compiler_params=pltpu.CompilerParams(vmem_limit_bytes=merge_vmem),
     )(in_hbm(density))
@@ -555,14 +569,19 @@
             ends = swapped(ends, "pv", True)
             mids = swapped(mids, "pv", True)
             corrected, coef = near_rows(density, pu_near, pu_far, near_blocks, far_right, links, corrected)
+            beside, coef = tied(beside, coef)
+            near_corners = swapped_corners(beside, density.shape[0] - 1)
         elif last:
-            corner_near, corner_far = patch_corners(beside, ends)
-            corner_near = swapped(corner_near, "pu", False)
-            corner_far = swapped(corner_far, "pu", True)
-            halo = (density, pu_near, pu_far, corner_near, corner_far)
-            corrected, coef = near_column(0, *halo, (beside,), near_blocks, far_right, links, corrected)
+            ends, left = tied(ends, left)
+            far_corners = swapped_corners(ends, 1)
+            halo = (density, pu_near, pu_far)
+            corrected, coef = near_column(
+                0, *halo, *near_corners, (beside,), near_blocks, far_right, links, corrected
+            )
             coefs.append(coef)
-            corrected, coef = near_column(1, *halo, (ends, mids), near_blocks, far_right, links, corrected)
+            corrected, coef = near_column(
+                1, *halo, *far_corners, (ends, mids), near_blocks, far_right, links, corrected
+            )
         if coef is not None:
             other, coef = tied(other, coef)
             coefs.append(coef)

time: 105 us -> 110 us (1.048)
  waiting for transfers between devices: 16.3 us -> 19.5 us
  starting transfers between devices: 23.1 us -> 25.6 us
    ppermute x12, waiting for transfers between devices: 16.3 us -> 19.5 us  [from_partner(): return lax.ppermute(value, axis, pairs)]
    ppermute x7 -> x9, starting transfers between devices: 4.34 us -> 6.42 us  [swapped(): return lax.ppermute(value, axis, pairs)]
    unnamed x24 -> x28, local copies, waits for them, and re-layouts: 1.94 us -> 2.47 us
  transfers between devices with their start and end apart: 19 -> 21, of which waited for: 8 -> 7; matrix products, arithmetic and copies ran while one was open for 0% -> 0% of each run, Pallas kernels for 57% -> 53%
where the time goes in v11:
time: 110 us
  Pallas kernels  59.7 us (54%)
  starting transfers between devices  25.6 us (23%)
  waiting for transfers between devices  19.5 us (18%)
  local copies, waits for them, and re-layouts  2.51 us (2%)
  matrix products  1.56 us (1%)
    pallas_call x5, Pallas kernels, merge(): pl.pallas_call(functools.partial(merge_kernel, bool(paths), bool(last_row...  30.6 us
    pallas_call x4, Pallas kernels, near_part(): pl.pallas_call(functools.partial(near_kernel, plan, len(sources)), grid=(...  22.8 us
    ppermute x12, waiting for transfers between devices, from_partner(): return lax.ppermute(value, axis, pairs)  19.5 us
    ppermute x12, starting transfers between devices, from_partner(): return lax.ppermute(value, axis, pairs)  19.2 us
    ppermute x9, starting transfers between devices, swapped(): return lax.ppermute(value, axis, pairs)  6.42 us
    pallas_call x1, Pallas kernels, patch_edges(): pl.pallas_call(edges_kernel, in_specs=[pl.BlockSpec(memory_space=pltpu.HB...  3.4 us
    unnamed x28, local copies, waits for them, and re-layouts  2.47 us
  transfers between devices with their start and end apart: 21, of which 7 were waited for; matrix products, arithmetic and copies ran while one was open for 0% of the time, Pallas kernels for 53%

profile of v11, /device:TPU:0, one launch (start us, length us, event | category | flops | bytes accessed | tf_op | source)
XLA Modules:
  0.0 110.0 jit_solution(164510640332357061)
XLA Ops:
  0.6 1.5 %shard_map.86 = (s16[128,1152]{1,0:T(8,128)(2,1)S(1)}, f32[128,256]{1,0:T(8,128)S(1)}) custom-call(s32[32]{0:T(128)} %order_hbm.1, f32[1,1,1024,128]{3,2,1,0:T(8,128)} %value_hbm.1, f32[256,128]{1,0:T(8,128)} %sketch_hbm.1), custom_call_target="tpu_custom_call" | custom-call | flops 1650000000 | tf_op jit(solution)/shard_map/pallas_call | solution.py:394
  2.1 3.0 %collective-permute-start = (s16[128,1152]{1,0:T(8,128)(2,1)S(1)}, s16[128,1152]{1,0:T(8,128)(2,1)S(1)}, u32[]{:S(2)}, u32[]{:S(2)}) collective-permute-start(s16[128,1152]{1,0:T(8,128)(2,1)S(1)} %get-tuple-element.60.mine_ref), channel_id=1, source_target_pairs={{0,1},{1,0},{2,3},{3,2},{4,5},{5,4},{6,7},{7,6},{8,9},{9,8},{10,11... | collective-permute-start | bytes 884744 | tf_op jit(solution)/shard_map/ppermute | solution.py:506
  5.1 3.4 %shard_map.87 = (bf16[6,128,768]{2,1,0:T(8,128)(2,1)S(1)}, bf16[3,128,768]{2,1,0:T(8,128)(2,1)S(1)}, bf16[3,128,768]{2,1,0:T(8,128)(2,1)}, bf16[6,128,768]{2,1,0:T(8,128)(2,1)S(1)}, bf16[6,128,768]{2,1,0:T(8,128)(2,1)S(1)}) custom-call(bf16[6,6,128,768]{3,2,1,0:T(8,128)(2,1)} %refs_0_.3), custom_call_target="tpu_custom_call" | custom-call | flops 2750000128 | tf_op jit(solution)/shard_map/pallas_call | solution.py:434
  9.5 2.7 %collective-permute-done.other_ref = s16[128,1152]{1,0:T(8,128)(2,1)S(1)} collective-permute-done((s16[128,1152]{1,0:T(8,128)(2,1)S(1)}, s16[128,1152]{1,0:T(8,128)(2,1)S(1)}, u32[]{:S(2)}, u32[]{:S(2)}) %collective-permute-start) | collective-permute-done | bytes 294944 | tf_op jit(solution)/shard_map/ppermute | solution.py:506
  12.1 5.8 %shard_map.88 = (s16[128,1152]{1,0:T(8,128)(2,1)S(1)}, f32[128,128]{1,0:T(8,128)S(1)}) custom-call(s16[128,1152]{1,0:T(8,128)(2,1)S(1)} %get-tuple-element.60.mine_ref, s16[128,1152]{1,0:T(8,128)(2,1)S(1)} %collective-permute-done.other_ref, f32[128,256]{1,0:T(8,128)S(1)} %get-tuple-element.61.sketch_ref), custom_call_target="tpu_custom_call" | custom-call | flops 9900000256 | tf_op jit(solution)/shard_map/pallas_call | solution.py:489
  18.0 1.9 %collective-permute-start.1 = (s16[128,1152]{1,0:T(8,128)(2,1)S(1)}, s16[128,1152]{1,0:T(8,128)(2,1)S(1)}, u32[]{:S(2)}, u32[]{:S(2)}) collective-permute-start(s16[128,1152]{1,0:T(8,128)(2,1)S(1)} %get-tuple-element.63.mine_ref), channel_id=1, source_target_pairs={{0,2},{1,3},{2,0},{3,1},{4,6},{5,7},{6,4},{7,5},{8,10},{9,11},{10,... | collective-permute-start | bytes 884744 | tf_op jit(solution)/shard_map/ppermute | solution.py:506
  19.9 7.4 %shard_map.89 = (bf16[6,6,128,768]{3,2,1,0:T(8,128)(2,1)}, f32[128,768]{1,0:T(8,128)S(1)}) custom-call(s32[6,6,6]{2,1,0:T(8,128)} %nb_hbm.3, bf16[6,6,6,128,128]{4,3,2,1,0:T(8,128)(2,1)} %near_hbm.7, bf16[6,6,128,128]{3,2,1,0:T(8,128)(2,1)} %right_hbm.7, bf16[6,6,128,768]{3,2,1,0:T(8,128)(2,1)} %refs_0_.3), custom_call_target="tpu_custom_call" | custom-call | flops 550000000 | tf_op jit(solution)/shard_map/pallas_call | solution.py:139
  27.3 5.9 %shard_map.90 = (s16[128,1152]{1,0:T(8,128)(2,1)S(1)}, f32[128,128]{1,0:T(8,128)S(1)}) custom-call(s16[128,1152]{1,0:T(8,128)(2,1)S(1)} %get-tuple-element.63.mine_ref, s16[128,1152]{1,0:T(8,128)(2,1)S(1)} %collective-permute-done.1.other_ref, f32[128,256]{1,0:T(8,128)S(1)} %get-tuple-element.61.sketch_ref, f32[128,128]{1,0:T(8,128)S(1)} %get-tuple-element.67.refs_0_), custom_call_target="tpu_custom_call" | custom-call | flops 1650000000 | tf_op jit(solution)/shard_map/pallas_call | solution.py:489
  33.2 2.7 %collective-permute-start.2 = (s16[128,1152]{1,0:T(8,128)(2,1)S(1)}, s16[128,1152]{1,0:T(8,128)(2,1)S(1)}, u32[]{:S(2)}, u32[]{:S(2)}) collective-permute-start(s16[128,1152]{1,0:T(8,128)(2,1)S(1)} %get-tuple-element.70.mine_ref), channel_id=1, source_target_pairs={{0,4},{1,5},{2,6},{3,7},{4,0},{5,1},{6,2},{7,3},{8,12},{9,13},{10,... | collective-permute-start | bytes 884744 | tf_op jit(solution)/shard_map/ppermute | solution.py:506
  35.8 0.9 collective-permute-start.7
  36.7 4.8 %shard_map.91 = (bf16[6,6,128,768]{3,2,1,0:T(8,128)(2,1)}, f32[128,768]{1,0:T(8,128)S(1)}) custom-call(s32[6,6,6]{2,1,0:T(8,128)} %nb_hbm.3, bf16[6,6,6,128,128]{4,3,2,1,0:T(8,128)(2,1)} %near_hbm.7, bf16[6,6,128,128]{3,2,1,0:T(8,128)(2,1)} %right_hbm.7, bf16[6,6,128,768]{3,2,1,0:T(8,128)(2,1)} %refs_0_.3, ...), custom_call_target="tpu_custom_call", output_to_operand_aliasing={{0}: (6, {})} | custom-call | flops 550000000 | tf_op jit(solution)/shard_map/pallas_call | solution.py:139
  41.6 8.2 %collective-permute-done.2.other_ref = s16[128,1152]{1,0:T(8,128)(2,1)S(1)} collective-permute-done((s16[128,1152]{1,0:T(8,128)(2,1)S(1)}, s16[128,1152]{1,0:T(8,128)(2,1)S(1)}, u32[]{:S(2)}, u32[]{:S(2)}) %collective-permute-start.2) | collective-permute-done | bytes 294944 | tf_op jit(solution)/shard_map/ppermute | solution.py:506
  49.8 5.9 %shard_map.92 = (s16[128,1152]{1,0:T(8,128)(2,1)S(1)}, f32[128,128]{1,0:T(8,128)S(1)}) custom-call(s16[128,1152]{1,0:T(8,128)(2,1)S(1)} %get-tuple-element.70.mine_ref, s16[128,1152]{1,0:T(8,128)(2,1)S(1)} %collective-permute-done.2.other_ref, f32[128,256]{1,0:T(8,128)S(1)} %get-tuple-element.61.sketch_ref, f32[128,128]{1,0:T(8,128)S(1)} %get-tuple-element.79.refs_0_), custom_call_target="tpu_custom_call" | custom-call | flops 550000000 | tf_op jit(solution)/shard_map/pallas_call | solution.py:489
  55.8 1.5 %collective-permute-start.10 = (bf16[3,128,768]{2,1,0:T(8,128)(2,1)}, bf16[3,128,768]{2,1,0:T(8,128)(2,1)}, u32[]{:S(2)}, u32[]{:S(2)}) collective-permute-start(bf16[3,128,768]{2,1,0:T(8,128)(2,1)} %get-tuple-element.88), channel_id=1, source_target_pairs={{1,2},{2,1},{3,4},{4,3},{5,6},{6,5},{9,10},{10,9},{11,12},{12,11},... | collective-permute-start | bytes 1769480 | tf_op jit(solution)/shard_map/ppermute | solution.py:518
  58.5 1.3 %collective-permute-start.12 = (bf16[1,128,768]{2,1,0:T(8,128)(2,1)}, bf16[1,128,768]{2,1,0:T(8,128)(2,1)}, u32[]{:S(2)}, u32[]{:S(2)}) collective-permute-start(bf16[1,128,768]{2,1,0:T(8,128)(2,1)} %get-tuple-element.91), channel_id=1, source_target_pairs={{8,16},{16,8},{9,17},{17,9},{10,18},{18,10},{11,19},{19,11},{12,20... | collective-permute-start | bytes 589832 | tf_op jit(solution)/shard_map/ppermute | solution.py:518
  59.8 6.5 %shard_map.93 = (s16[128,1152]{1,0:T(8,128)(2,1)}, f32[128,128]{1,0:T(8,128)S(1)}) custom-call(s16[128,1152]{1,0:T(8,128)(2,1)S(1)} %get-tuple-element.80.mine_ref, s16[128,1152]{1,0:T(8,128)(2,1)S(1)} %collective-permute-done.6.other_ref, f32[128,256]{1,0:T(8,128)S(1)} %get-tuple-element.61.sketch_ref), custom_call_target="tpu_custom_call" | custom-call | flops 550000000 | tf_op jit(solution)/shard_map/pallas_call | solution.py:489
  66.4 2.2 %collective-permute-start.13 = (s16[128,1152]{1,0:T(8,128)(2,1)}, s16[128,1152]{1,0:T(8,128)(2,1)}, u32[]{:S(2)}, u32[]{:S(2)}) collective-permute-start(s16[128,1152]{1,0:T(8,128)(2,1)} %get-tuple-element.103.mine_ref), channel_id=1, source_target_pairs={{0,16},{8,24},{16,0},{24,8},{1,17},{9,25},{17,1},{25,9},{2,18},{10... | collective-permute-start | bytes 884744 | tf_op jit(solution)/shard_map/ppermute | solution.py:506
  70.9 1.3 %collective-permute-start.9 = (bf16[1,128,768]{2,1,0:T(8,128)(2,1)}, bf16[1,128,768]{2,1,0:T(8,128)(2,1)}, u32[]{:S(2)}, u32[]{:S(2)}) collective-permute-start(bf16[1,128,768]{2,1,0:T(8,128)(2,1)} %get-tuple-element.87), channel_id=1, source_target_pairs={{8,16},{16,8},{9,17},{17,9},{10,18},{18,10},{11,19},{19,11},{12,20... | collective-permute-start | bytes 589832 | tf_op jit(solution)/shard_map/ppermute | solution.py:518
  72.2 0.9 copy-done.7
  73.2 5.7 %shard_map.96 = (bf16[6,6,128,768]{3,2,1,0:T(8,128)(2,1)}, f32[128,768]{1,0:T(8,128)S(1)}) custom-call(s32[6,6,6]{2,1,0:T(8,128)} %nb_hbm.3, bf16[6,6,6,128,128]{4,3,2,1,0:T(8,128)(2,1)} %near_hbm.7, bf16[6,6,128,128]{3,2,1,0:T(8,128)(2,1)} %right_hbm.7, bf16[6,6,128,768]{3,2,1,0:T(8,128)(2,1)} %refs_0_.3, ...), custom_call_target="tpu_custom_call", output_to_operand_aliasing={{0}: (9, {})} | custom-call | flops 550000000 | tf_op jit(solution)/shard_map/pallas_call | solution.py:139
  78.9 4.9 %shard_map.97 = (bf16[6,6,128,768]{3,2,1,0:T(8,128)(2,1)}, f32[128,768]{1,0:T(8,128)S(1)}) custom-call(s32[6,6,6]{2,1,0:T(8,128)} %nb_hbm.3, bf16[6,6,6,128,128]{4,3,2,1,0:T(8,128)(2,1)} %near_hbm.7, bf16[6,6,128,128]{3,2,1,0:T(8,128)(2,1)} %right_hbm.7, bf16[6,6,128,768]{3,2,1,0:T(8,128)(2,1)} %refs_0_.3, ...), custom_call_target="tpu_custom_call", output_to_operand_aliasing={{0}: (10, {})} | custom-call | flops 550000000 | tf_op jit(solution)/shard_map/pallas_call | solution.py:139
  84.5 1.6 %collective-permute-start.14 = (f32[4,96,128]{2,1,0:T(8,128)S(1)}, f32[4,96,128]{2,1,0:T(8,128)S(1)}, u32[]{:S(2)}, u32[]{:S(2)}) collective-permute-start(f32[4,96,128]{2,1,0:T(8,128)S(1)} %dynamic-slice_bitcast_fusion), channel_id=1, source_target_pairs={{0,1},{1,0},{2,3},{3,2},{4,5},{5,4},{6,7},{7,6},{8,9},{9,8},{10,11... | collective-permute-start | bytes 589832 | tf_op jit(solution)/shard_map/ppermute | solution.py:506
  86.1 6.5 %shard_map.98 = (f32[128,256]{1,0:T(8,128)S(1)}, f32[128,128]{1,0:T(8,128)S(1)}) custom-call(s16[128,1152]{1,0:T(8,128)(2,1)} %get-tuple-element.103.mine_ref, s16[128,1152]{1,0:T(8,128)(2,1)} %collective-permute-done.13.other_ref, f32[128,256]{1,0:T(8,128)S(1)} %copy-done.11, f32[128,128]{1,0:T(8,128)S(1)} %copy-done.13), custom_call_target="tpu_custom_call" | custom-call | flops 550000000 | tf_op jit(solution)/shard_map/pallas_call | solution.py:489
  92.6 2.2 %collective-permute-start.15 = (f32[96,128]{1,0:T(8,128)S(1)}, f32[96,128]{1,0:T(8,128)S(1)}, u32[]{:S(2)}, u32[]{:S(2)}) collective-permute-start(f32[96,128]{1,0:T(8,128)S(1)} %get-tuple-element.110), channel_id=1, source_target_pairs={{0,2},{1,3},{2,0},{3,1},{4,6},{5,7},{6,4},{7,5},{8,10},{9,11},{10,... | collective-permute-start | bytes 147464 | tf_op jit(solution)/shard_map/ppermute | solution.py:506
  94.8 1.4 %collective-permute-start.16 = (f32[96,128]{1,0:T(8,128)S(1)}, f32[96,128]{1,0:T(8,128)S(1)}, u32[]{:S(2)}, u32[]{:S(2)}) collective-permute-start(f32[96,128]{1,0:T(8,128)S(1)} %get-tuple-element.112), channel_id=1, source_target_pairs={{0,4},{1,5},{2,6},{3,7},{4,0},{5,1},{6,2},{7,3},{8,12},{9,13},{10,... | collective-permute-start | bytes 147464 | tf_op jit(solution)/shard_map/ppermute | solution.py:506
  96.3 1.3 %collective-permute-start.17 = (f32[96,128]{1,0:T(8,128)S(1)}, f32[96,128]{1,0:T(8,128)S(1)}, u32[]{:S(2)}, u32[]{:S(2)}) collective-permute-start(f32[96,128]{1,0:T(8,128)S(1)} %get-tuple-element.111), channel_id=1, source_target_pairs={{0,6},{1,7},{2,4},{3,5},{4,2},{5,3},{6,0},{7,1},{8,14},{9,15},{10,... | collective-permute-start | bytes 147464 | tf_op jit(solution)/shard_map/ppermute | solution.py:506
  97.5 2.3 %collective-permute-done.16 = f32[96,128]{1,0:T(8,128)S(1)} collective-permute-done((f32[96,128]{1,0:T(8,128)S(1)}, f32[96,128]{1,0:T(8,128)S(1)}, u32[]{:S(2)}, u32[]{:S(2)}) %collective-permute-start.16) | collective-permute-done | bytes 49184 | tf_op jit(solution)/shard_map/ppermute | solution.py:506
  99.8 2.6 %collective-permute-done.17 = f32[96,128]{1,0:T(8,128)S(1)} collective-permute-done((f32[96,128]{1,0:T(8,128)S(1)}, f32[96,128]{1,0:T(8,128)S(1)}, u32[]{:S(2)}, u32[]{:S(2)}) %collective-permute-start.17) | collective-permute-done | bytes 49184 | tf_op jit(solution)/shard_map/ppermute | solution.py:506
  102.7 2.7 %collective-permute-start.19 = (f32[96,128]{1,0:T(8,128)S(1)}, f32[96,128]{1,0:T(8,128)S(1)}, u32[]{:S(2)}, u32[]{:S(2)}) collective-permute-start(f32[96,128]{1,0:T(8,128)S(1)} %fusion.6), channel_id=1, source_target_pairs={{0,16},{8,24},{16,0},{24,8},{1,17},{9,25},{17,1},{25,9},{2,18},{10... | collective-permute-start | bytes 147464 | tf_op jit(solution)/shard_map/ppermute | solution.py:506
  105.5 2.3 %collective-permute-done.19 = f32[96,128]{1,0:T(8,128)S(1)} collective-permute-done((f32[96,128]{1,0:T(8,128)S(1)}, f32[96,128]{1,0:T(8,128)S(1)}, u32[]{:S(2)}, u32[]{:S(2)}) %collective-permute-start.19) | collective-permute-done | bytes 49184 | tf_op jit(solution)/shard_map/ppermute | solution.py:506
  107.8 1.4 %collective-permute-done.20 = f32[96,128]{1,0:T(8,128)S(1)} collective-permute-done((f32[96,128]{1,0:T(8,128)S(1)}, f32[96,128]{1,0:T(8,128)S(1)}, u32[]{:S(2)}, u32[]{:S(2)}) %collective-permute-start.20) | collective-permute-done | bytes 49184 | tf_op jit(solution)/shard_map/ppermute | solution.py:506
  109.1 0.8 fusion.8
  (57 shorter events, 5.5 us)
Async XLA Ops:
  2.1 57.7 %copy-start.10 = (f32[128,256]{1,0:T(8,128)}, f32[128,256]{1,0:T(8,128)S(1)}, u32[]{:S(2)}) copy-start(f32[128,256]{1,0:T(8,128)S(1)} %get-tuple-element.61.sketch_ref) | copy-start | bytes 393220
  2.1 10.0 %collective-permute-start = (s16[128,1152]{1,0:T(8,128)(2,1)S(1)}, s16[128,1152]{1,0:T(8,128)(2,1)S(1)}, u32[]{:S(2)}, u32[]{:S(2)}) collective-permute-start(s16[128,1152]{1,0:T(8,128)(2,1)S(1)} %get-tuple-element.60.mine_ref), channel_id=1, source_target_pairs={{0,1},{1,0},{2,3},{3,2},{4,5},{5,4},{6,7},{7,6},{8,9},{9,8},{10,11... | collective-permute-start | bytes 884744 | tf_op jit(solution)/shard_map/ppermute | solution.py:506
  8.5 28.2 %collective-permute-start.4 = (bf16[6,128,768]{2,1,0:T(8,128)(2,1)S(1)}, bf16[6,128,768]{2,1,0:T(8,128)(2,1)S(1)}, u32[]{:S(2)}, u32[]{:S(2)}) collective-permute-start(bf16[6,128,768]{2,1,0:T(8,128)(2,1)S(1)} %get-tuple-element.73), channel_id=1, source_target_pairs={{0,8},{8,0},{16,24},{24,16},{1,9},{9,1},{17,25},{25,17},{2,10},{10... | collective-permute-start | bytes 3538952 | tf_op jit(solution)/shard_map/ppermute | solution.py:518
  8.6 28.1 %collective-permute-start.5 = (bf16[6,128,768]{2,1,0:T(8,128)(2,1)S(1)}, bf16[6,128,768]{2,1,0:T(8,128)(2,1)S(1)}, u32[]{:S(2)}, u32[]{:S(2)}) collective-permute-start(bf16[6,128,768]{2,1,0:T(8,128)(2,1)S(1)} %get-tuple-element.74), channel_id=1, source_target_pairs={{8,16},{16,8},{9,17},{17,9},{10,18},{18,10},{11,19},{19,11},{12,20... | collective-permute-start | bytes 3538952 | tf_op jit(solution)/shard_map/ppermute | solution.py:518
  9.4 32.2 %collective-permute-start.3 = (bf16[6,128,768]{2,1,0:T(8,128)(2,1)S(1)}, bf16[6,128,768]{2,1,0:T(8,128)(2,1)S(1)}, u32[]{:S(2)}, u32[]{:S(2)}) collective-permute-start(bf16[6,128,768]{2,1,0:T(8,128)(2,1)S(1)} %get-tuple-element.71), channel_id=1, source_target_pairs={{0,1},{1,0},{2,3},{3,2},{4,5},{5,4},{6,7},{7,6},{8,9},{9,8},{10,11... | collective-permute-start | bytes 3538952 | tf_op jit(solution)/shard_map/ppermute | solution.py:518
  18.0 9.3 %collective-permute-start.1 = (s16[128,1152]{1,0:T(8,128)(2,1)S(1)}, s16[128,1152]{1,0:T(8,128)(2,1)S(1)}, u32[]{:S(2)}, u32[]{:S(2)}) collective-permute-start(s16[128,1152]{1,0:T(8,128)(2,1)S(1)} %get-tuple-element.63.mine_ref), channel_id=1, source_target_pairs={{0,2},{1,3},{2,0},{3,1},{4,6},{5,7},{6,4},{7,5},{8,10},{9,11},{10,... | collective-permute-start | bytes 884744 | tf_op jit(solution)/shard_map/ppermute | solution.py:506
  27.2 6.0 %copy-start.2 = (f32[128,768]{1,0:T(8,128)}, f32[128,768]{1,0:T(8,128)S(1)}, u32[]{:S(2)}) copy-start(f32[128,768]{1,0:T(8,128)S(1)} %get-tuple-element.95) | copy-start | bytes 1179652
  33.2 16.6 %collective-permute-start.2 = (s16[128,1152]{1,0:T(8,128)(2,1)S(1)}, s16[128,1152]{1,0:T(8,128)(2,1)S(1)}, u32[]{:S(2)}, u32[]{:S(2)}) collective-permute-start(s16[128,1152]{1,0:T(8,128)(2,1)S(1)} %get-tuple-element.70.mine_ref), channel_id=1, source_target_pairs={{0,4},{1,5},{2,6},{3,7},{4,0},{5,1},{6,2},{7,3},{8,12},{9,13},{10,... | collective-permute-start | bytes 884744 | tf_op jit(solution)/shard_map/ppermute | solution.py:506
  35.8 32.8 %collective-permute-start.7 = (bf16[3,128,768]{2,1,0:T(8,128)(2,1)S(1)}, bf16[3,128,768]{2,1,0:T(8,128)(2,1)S(1)}, u32[]{:S(2)}, u32[]{:S(2)}) collective-permute-start(bf16[3,128,768]{2,1,0:T(8,128)(2,1)S(1)} %get-tuple-element.83), channel_id=1, source_target_pairs={{1,2},{2,1},{3,4},{4,3},{5,6},{6,5},{9,10},{10,9},{11,12},{12,11},... | collective-permute-start | bytes 1769480 | tf_op jit(solution)/shard_map/ppermute | solution.py:518
  41.6 16.4 %copy-start.4 = (f32[128,768]{1,0:T(8,128)}, f32[128,768]{1,0:T(8,128)S(1)}, u32[]{:S(2)}) copy-start(f32[128,768]{1,0:T(8,128)S(1)} %get-tuple-element.96) | copy-start | bytes 1179652
  55.7 2.3 %copy-start.8 = (f32[128,128]{1,0:T(8,128)}, f32[128,128]{1,0:T(8,128)S(1)}, u32[]{:S(2)}) copy-start(f32[128,128]{1,0:T(8,128)S(1)} %get-tuple-element.100) | copy-start | bytes 196612
  55.7 4.1 %collective-permute-start.6 = (s16[128,1152]{1,0:T(8,128)(2,1)S(1)}, s16[128,1152]{1,0:T(8,128)(2,1)S(1)}, u32[]{:S(2)}, u32[]{:S(2)}) collective-permute-start(s16[128,1152]{1,0:T(8,128)(2,1)S(1)} %get-tuple-element.80.mine_ref), channel_id=1, source_target_pairs={{0,8},{8,0},{16,24},{24,16},{1,9},{9,1},{17,25},{25,17},{2,10},{10... | collective-permute-start | bytes 884744 | tf_op jit(solution)/shard_map/ppermute | solution.py:506
  55.8 23.1 %collective-permute-start.10 = (bf16[3,128,768]{2,1,0:T(8,128)(2,1)}, bf16[3,128,768]{2,1,0:T(8,128)(2,1)}, u32[]{:S(2)}, u32[]{:S(2)}) collective-permute-start(bf16[3,128,768]{2,1,0:T(8,128)(2,1)} %get-tuple-element.88), channel_id=1, source_target_pairs={{1,2},{2,1},{3,4},{4,3},{5,6},{6,5},{9,10},{10,9},{11,12},{12,11},... | collective-permute-start | bytes 1769480 | tf_op jit(solution)/shard_map/ppermute | solution.py:518
  58.0 12.2 %collective-permute-start.11 = (bf16[1,128,768]{2,1,0:T(8,128)(2,1)S(1)}, bf16[1,128,768]{2,1,0:T(8,128)(2,1)S(1)}, u32[]{:S(2)}, u32[]{:S(2)}) collective-permute-start(bf16[1,128,768]{2,1,0:T(8,128)(2,1)S(1)} %get-tuple-element.90), channel_id=1, source_target_pairs={{0,8},{8,0},{16,24},{24,16},{1,9},{9,1},{17,25},{25,17},{2,10},{10... | collective-permute-start | bytes 589832 | tf_op jit(solution)/shard_map/ppermute | solution.py:518
  58.5 13.8 %collective-permute-start.12 = (bf16[1,128,768]{2,1,0:T(8,128)(2,1)}, bf16[1,128,768]{2,1,0:T(8,128)(2,1)}, u32[]{:S(2)}, u32[]{:S(2)}) collective-permute-start(bf16[1,128,768]{2,1,0:T(8,128)(2,1)} %get-tuple-element.91), channel_id=1, source_target_pairs={{8,16},{16,8},{9,17},{17,9},{10,18},{18,10},{11,19},{19,11},{12,20... | collective-permute-start | bytes 589832 | tf_op jit(solution)/shard_map/ppermute | solution.py:518
  66.4 3.8 %copy-start.12 = (f32[128,128]{1,0:T(8,128)}, f32[128,128]{1,0:T(8,128)S(1)}, u32[]{:S(2)}) copy-start(f32[128,128]{1,0:T(8,128)S(1)} %get-tuple-element.105.refs_0_) | copy-start | bytes 196612
  66.4 17.5 %collective-permute-start.13 = (s16[128,1152]{1,0:T(8,128)(2,1)}, s16[128,1152]{1,0:T(8,128)(2,1)}, u32[]{:S(2)}, u32[]{:S(2)}) collective-permute-start(s16[128,1152]{1,0:T(8,128)(2,1)} %get-tuple-element.103.mine_ref), channel_id=1, source_target_pairs={{0,16},{8,24},{16,0},{24,8},{1,17},{9,25},{17,1},{25,9},{2,18},{10... | collective-permute-start | bytes 884744 | tf_op jit(solution)/shard_map/ppermute | solution.py:506
  70.2 8.7 %collective-permute-start.8 = (bf16[1,128,768]{2,1,0:T(8,128)(2,1)}, bf16[1,128,768]{2,1,0:T(8,128)(2,1)}, u32[]{:S(2)}, u32[]{:S(2)}) collective-permute-start(bf16[1,128,768]{2,1,0:T(8,128)(2,1)} %get-tuple-element.86), channel_id=1, source_target_pairs={{0,8},{8,0},{16,24},{24,16},{1,9},{9,1},{17,25},{25,17},{2,10},{10... | collective-permute-start | bytes 589832 | tf_op jit(solution)/shard_map/ppermute | solution.py:518
  70.9 8.0 %collective-permute-start.9 = (bf16[1,128,768]{2,1,0:T(8,128)(2,1)}, bf16[1,128,768]{2,1,0:T(8,128)(2,1)}, u32[]{:S(2)}, u32[]{:S(2)}) collective-permute-start(bf16[1,128,768]{2,1,0:T(8,128)(2,1)} %get-tuple-element.87), channel_id=1, source_target_pairs={{8,16},{16,8},{9,17},{17,9},{10,18},{18,10},{11,19},{19,11},{12,20... | collective-permute-start | bytes 589832 | tf_op jit(solution)/shard_map/ppermute | solution.py:518
  73.2 5.7 %copy-start.1 = (bf16[3,128,768]{2,1,0:T(8,128)(2,1)S(1)}, bf16[3,128,768]{2,1,0:T(8,128)(2,1)}, u32[]{:S(2)}) copy-start(bf16[3,128,768]{2,1,0:T(8,128)(2,1)} %copy-done) | copy-start | bytes 1769476
  78.9 5.0 %copy-start.3 = (f32[128,768]{1,0:T(8,128)S(1)}, f32[128,768]{1,0:T(8,128)}, u32[]{:S(2)}) copy-start(f32[128,768]{1,0:T(8,128)} %copy-done.2) | copy-start | bytes 1179652
  78.9 5.0 %copy-start.5 = (f32[128,768]{1,0:T(8,128)S(1)}, f32[128,768]{1,0:T(8,128)}, u32[]{:S(2)}) copy-start(f32[128,768]{1,0:T(8,128)} %copy-done.4) | copy-start | bytes 1179652
  78.9 5.0 %copy-start.9 = (f32[128,128]{1,0:T(8,128)S(1)}, f32[128,128]{1,0:T(8,128)}, u32[]{:S(2)}) copy-start(f32[128,128]{1,0:T(8,128)} %copy-done.8) | copy-start | bytes 196612
  83.9 2.2 %copy-start.11 = (f32[128,256]{1,0:T(8,128)S(1)}, f32[128,256]{1,0:T(8,128)}, u32[]{:S(2)}) copy-start(f32[128,256]{1,0:T(8,128)} %copy-done.10) | copy-start | bytes 393220
  83.9 2.2 %copy-start.13 = (f32[128,128]{1,0:T(8,128)S(1)}, f32[128,128]{1,0:T(8,128)}, u32[]{:S(2)}) copy-start(f32[128,128]{1,0:T(8,128)} %copy-done.12) | copy-start | bytes 196612
  84.5 8.1 %collective-permute-start.14 = (f32[4,96,128]{2,1,0:T(8,128)S(1)}, f32[4,96,128]{2,1,0:T(8,128)S(1)}, u32[]{:S(2)}, u32[]{:S(2)}) collective-permute-start(f32[4,96,128]{2,1,0:T(8,128)S(1)} %dynamic-slice_bitcast_fusion), channel_id=1, source_target_pairs={{0,1},{1,0},{2,3},{3,2},{4,5},{5,4},{6,7},{7,6},{8,9},{9,8},{10,11... | collective-permute-start | bytes 589832 | tf_op jit(solution)/shard_map/ppermute | solution.py:506
  92.6 4.9 %collective-permute-start.15 = (f32[96,128]{1,0:T(8,128)S(1)}, f32[96,128]{1,0:T(8,128)S(1)}, u32[]{:S(2)}, u32[]{:S(2)}) collective-permute-start(f32[96,128]{1,0:T(8,128)S(1)} %get-tuple-element.110), channel_id=1, source_target_pairs={{0,2},{1,3},{2,0},{3,1},{4,6},{5,7},{6,4},{7,5},{8,10},{9,11},{10,... | collective-permute-start | bytes 147464 | tf_op jit(solution)/shard_map/ppermute | solution.py:506
  94.8 5.0 %collective-permute-start.16 = (f32[96,128]{1,0:T(8,128)S(1)}, f32[96,128]{1,0:T(8,128)S(1)}, u32[]{:S(2)}, u32[]{:S(2)}) collective-permute-start(f32[96,128]{1,0:T(8,128)S(1)} %get-tuple-element.112), channel_id=1, source_target_pairs={{0,4},{1,5},{2,6},{3,7},{4,0},{5,1},{6,2},{7,3},{8,12},{9,13},{10,... | collective-permute-start | bytes 147464 | tf_op jit(solution)/shard_map/ppermute | solution.py:506
  96.3 6.2 %collective-permute-start.17 = (f32[96,128]{1,0:T(8,128)S(1)}, f32[96,128]{1,0:T(8,128)S(1)}, u32[]{:S(2)}, u32[]{:S(2)}) collective-permute-start(f32[96,128]{1,0:T(8,128)S(1)} %get-tuple-element.111), channel_id=1, source_target_pairs={{0,6},{1,7},{2,4},{3,5},{4,2},{5,3},{6,0},{7,1},{8,14},{9,15},{10,... | collective-permute-start | bytes 147464 | tf_op jit(solution)/shard_map/ppermute | solution.py:506
  102.6 2.9 %collective-permute-start.18 = (f32[96,128]{1,0:T(8,128)S(1)}, f32[96,128]{1,0:T(8,128)S(1)}, u32[]{:S(2)}, u32[]{:S(2)}) collective-permute-start(f32[96,128]{1,0:T(8,128)S(1)} %fusion.6), channel_id=1, source_target_pairs={{0,8},{8,0},{16,24},{24,16},{1,9},{9,1},{17,25},{25,17},{2,10},{10... | collective-permute-start | bytes 147464 | tf_op jit(solution)/shard_map/ppermute | solution.py:506
  102.7 5.1 %collective-permute-start.19 = (f32[96,128]{1,0:T(8,128)S(1)}, f32[96,128]{1,0:T(8,128)S(1)}, u32[]{:S(2)}, u32[]{:S(2)}) collective-permute-start(f32[96,128]{1,0:T(8,128)S(1)} %fusion.6), channel_id=1, source_target_pairs={{0,16},{8,24},{16,0},{24,8},{1,17},{9,25},{17,1},{25,9},{2,18},{10... | collective-permute-start | bytes 147464 | tf_op jit(solution)/shard_map/ppermute | solution.py:506
  105.4 3.7 %collective-permute-start.20 = (f32[96,128]{1,0:T(8,128)S(1)}, f32[96,128]{1,0:T(8,128)S(1)}, u32[]{:S(2)}, u32[]{:S(2)}) collective-permute-start(f32[96,128]{1,0:T(8,128)S(1)} %fusion.6), channel_id=1, source_target_pairs={{0,24},{8,16},{16,8},{24,0},{1,25},{9,17},{17,9},{25,1},{2,26},{10... | collective-permute-start | bytes 147464 | tf_op jit(solution)/shard_map/ppermute | solution.py:506
  (3 other events, 2.4 us)

commit v12 on v8

--- a/solution.py
+++ b/solution.py
@@ -9,8 +9,8 @@
 
 high = lax.Precision.HIGH
 empty_slot = 9
-near_vmem = 18 * 1024 * 1024
-merge_vmem = 12 * 1024 * 1024
+near_vmem = 17 * 1024 * 1024
+merge_vmem = 8 * 1024 * 1024
 
 
 def dot_t(a, b, dims, precision=None):
@@ -240,6 +240,16 @@
     return near_part(sources, plan, (gu + 2, 6), near_blocks, far_right, neighbours, prior, 0.5)
 
 
+def run_copies(pairs, sems):
+    copies = [
+        pltpu.make_async_copy(source, target, sems.at[index])
+        for index, (source, target) in enumerate(pairs)
+    ]
+    for copy in copies:
+        copy.start()
+    return copies
+
+
 def corners_kernel(beside, ends, to_near, to_far):
     low = odd("pu")
     rows = beside.shape[0]
@@ -333,12 +343,11 @@
             e_hi = e_now.astype(jnp.bfloat16)
             e_lo = (e_now - e_hi.astype(jnp.float32)).astype(jnp.bfloat16)
             lhs = jnp.concatenate([k_hi, k_hi, k_lo], axis=0)
-            k_rhs = jnp.concatenate([k_hi, k_lo, k_hi], axis=0)
-            e_rhs = jnp.concatenate([e_hi, e_lo, e_hi], axis=0)
-            k_fall = dot_t(lhs, k_rhs, ((0,), (0,)))
-            e_fall = dot_t(lhs, e_rhs, ((0,), (0,)))
-            w_k[base + step :, :] -= k_fall[base + step :, :]
-            w_e[base + step :, :] -= e_fall[base + step :, :]
+            hi = jnp.concatenate([k_hi, e_hi], axis=1)
+            lo = jnp.concatenate([k_lo, e_lo], axis=1)
+            fall = dot_t(lhs, jnp.concatenate([hi, lo, hi], axis=0), ((0,), (0,)))
+            w_k[base + step :, :] -= fall[base + step :, :size]
+            w_e[base + step :, :] -= fall[base + step :, size:]
 
 
 tail_lanes = 128
@@ -359,16 +368,6 @@
     tail = ref[:, cols:].astype(jnp.int32).astype(jnp.float32)
     value = ref[:, :cols].astype(jnp.int32).astype(jnp.float32) * jnp.exp2(-tail[:, :1])
     return value, tail[:, tail_lanes - 1 :]
-
-
-def run_copies(pairs, sems):
-    copies = [
-        pltpu.make_async_copy(source, target, sems.at[index])
-        for index, (source, target) in enumerate(pairs)
-    ]
-    for copy in copies:
-        copy.start()
-    return copies
 
 
 def leaf_kernel(counts, order_hbm, value_hbm, sketch_hbm, code_ref, sketch_ref, order, value, sketch, sems):
@@ -407,7 +406,8 @@
     gu, gv = density.shape[:2]
     near_col = (gv - 1) * (1 - odd("pv"))
     far_col = (gv - 1) * odd("pv")
-    pairs = [(density.at[(gu - 1) * (1 - odd("pu"))], pu_near), (density.at[(gu - 1) * odd("pu")], pu_far)]
+    pairs = [(density.at[(gu - 1) * odd("pu"), col], pu_far.at[col]) for col in range(gv)]
+    pairs += [(density.at[(gu - 1) * (1 - odd("pu")), col], pu_near.at[col]) for col in range(gv)]
     pairs += [(density.at[row, near_col], beside.at[row]) for row in range(gu)]
     pairs += [(density.at[(gu - 1) * row, far_col], ends.at[row]) for row in range(2)]
     pairs += [(density.at[row + 1, far_col], mids.at[row]) for row in range(gu - 2)]
@@ -423,7 +423,7 @@
         in_specs=[pl.BlockSpec(memory_space=pltpu.HBM)],
         out_specs=[pl.BlockSpec(memory_space=pltpu.VMEM)] * len(blocks),
         out_shape=[jax.ShapeDtypeStruct((count, size, rhs), density.dtype) for count in blocks],
-        scratch_shapes=[pltpu.SemaphoreType.DMA((2 * gu + 2,))],
+        scratch_shapes=[pltpu.SemaphoreType.DMA((2 * gu + 2 * gv,))],
         cost_estimate=cost(2.5),
         compiler_params=pltpu.CompilerParams(vmem_limit_bytes=merge_vmem),
     )(in_hbm(density))
@@ -550,12 +550,12 @@
         if level in (1, 2) or last:
             links, left = tied(neighbours, left)
         if level == 1:
-            corrected, coef = near_rows(density, pu_near, pu_far, near_blocks, far_right, links, corrected)
+            corrected, coef = near_middle(density, near_blocks, far_right, links, corrected)
         elif level == 2:
             ends, mids, left = tied(ends, mids, left)
             ends = swapped(ends, "pv", True)
             mids = swapped(mids, "pv", True)
-            corrected, coef = near_middle(density, near_blocks, far_right, links, corrected)
+            corrected, coef = near_rows(density, pu_near, pu_far, near_blocks, far_right, links, corrected)
         elif last:
             corner_near, corner_far = patch_corners(beside, ends)
             corner_near = swapped(corner_near, "pu", False)

time: 108 us -> 106 us (0.981)
  starting transfers between devices: 30.5 us -> 28.1 us
    ppermute x12, starting transfers between devices: 25.9 us -> 23 us  [from_partner(): return lax.ppermute(value, axis, pairs)]
  transfers between devices with their start and end apart: 19 -> 19, of which waited for: 7 -> 7; matrix products, arithmetic and copies ran while one was open for 0% -> 0% of each run, Pallas kernels for 51% -> 52%
where the time goes in v12:
time: 106 us
  Pallas kernels  56.5 us (53%)
  starting transfers between devices  28.1 us (27%)
  waiting for transfers between devices  17.3 us (16%)
  local copies, waits for them, and re-layouts  1.7 us (2%)
  matrix products  1.53 us (1%)
    pallas_call x5, Pallas kernels, merge(): pl.pallas_call(functools.partial(merge_kernel, bool(paths), bool(last_row...  30.7 us
    ppermute x12, starting transfers between devices, from_partner(): return lax.ppermute(value, axis, pairs)  23 us
    pallas_call x3, Pallas kernels, near_part(): pl.pallas_call(functools.partial(near_kernel, plan, len(sources)), grid=(...  19.8 us
    ppermute x12, waiting for transfers between devices, from_partner(): return lax.ppermute(value, axis, pairs)  17.3 us
    ppermute x7, starting transfers between devices, swapped(): return lax.ppermute(value, axis, pairs)  5.12 us
    pallas_call x1, Pallas kernels, patch_edges(): pl.pallas_call(edges_kernel, in_specs=[pl.BlockSpec(memory_space=pltpu.HB...  3.5 us
  transfers between devices with their start and end apart: 19, of which 7 were waited for; matrix products, arithmetic and copies ran while one was open for 0% of the time, Pallas kernels for 52%

profile of v12, /device:TPU:0, one launch (start us, length us, event | category | flops | bytes accessed | tf_op | source)
XLA Modules:
  0.0 106.1 jit_solution(10389123057670580080)
XLA Ops:
  0.6 1.5 %shard_map.86 = (s16[128,1152]{1,0:T(8,128)(2,1)S(1)}, f32[128,256]{1,0:T(8,128)S(1)}) custom-call(s32[32]{0:T(128)} %order_hbm.1, f32[1,1,1024,128]{3,2,1,0:T(8,128)} %value_hbm.1, f32[256,128]{1,0:T(8,128)} %sketch_hbm.1), custom_call_target="tpu_custom_call" | custom-call | flops 1650000000 | tf_op jit(solution)/shard_map/pallas_call | solution.py:386
  2.1 3.0 %collective-permute-start = (s16[128,1152]{1,0:T(8,128)(2,1)S(1)}, s16[128,1152]{1,0:T(8,128)(2,1)S(1)}, u32[]{:S(2)}, u32[]{:S(2)}) collective-permute-start(s16[128,1152]{1,0:T(8,128)(2,1)S(1)} %get-tuple-element.52.mine_ref), channel_id=1, source_target_pairs={{0,1},{1,0},{2,3},{3,2},{4,5},{5,4},{6,7},{7,6},{8,9},{9,8},{10,11... | collective-permute-start | bytes 884744 | tf_op jit(solution)/shard_map/ppermute | solution.py:493
  5.1 3.5 %shard_map.87 = (bf16[6,128,768]{2,1,0:T(8,128)(2,1)S(1)}, bf16[2,128,768]{2,1,0:T(8,128)(2,1)S(1)}, bf16[4,128,768]{2,1,0:T(8,128)(2,1)}, bf16[6,128,768]{2,1,0:T(8,128)(2,1)S(1)}, bf16[6,128,768]{2,1,0:T(8,128)(2,1)S(1)}) custom-call(bf16[6,6,128,768]{3,2,1,0:T(8,128)(2,1)} %refs_0_.2), custom_call_target="tpu_custom_call" | custom-call | flops 2750000128 | tf_op jit(solution)/shard_map/pallas_call | solution.py:421
  8.7 0.7 collective-permute-start.4
  9.6 2.6 %collective-permute-done.other_ref = s16[128,1152]{1,0:T(8,128)(2,1)S(1)} collective-permute-done((s16[128,1152]{1,0:T(8,128)(2,1)S(1)}, s16[128,1152]{1,0:T(8,128)(2,1)S(1)}, u32[]{:S(2)}, u32[]{:S(2)}) %collective-permute-start) | collective-permute-done | bytes 294944 | tf_op jit(solution)/shard_map/ppermute | solution.py:493
  12.1 5.8 %shard_map.88 = (s16[128,1152]{1,0:T(8,128)(2,1)S(1)}, f32[128,128]{1,0:T(8,128)S(1)}) custom-call(s16[128,1152]{1,0:T(8,128)(2,1)S(1)} %get-tuple-element.52.mine_ref, s16[128,1152]{1,0:T(8,128)(2,1)S(1)} %collective-permute-done.other_ref, f32[128,256]{1,0:T(8,128)S(1)} %get-tuple-element.53.sketch_ref), custom_call_target="tpu_custom_call" | custom-call | flops 9900000256 | tf_op jit(solution)/shard_map/pallas_call | solution.py:476
  18.0 1.9 %collective-permute-start.1 = (s16[128,1152]{1,0:T(8,128)(2,1)S(1)}, s16[128,1152]{1,0:T(8,128)(2,1)S(1)}, u32[]{:S(2)}, u32[]{:S(2)}) collective-permute-start(s16[128,1152]{1,0:T(8,128)(2,1)S(1)} %get-tuple-element.55.mine_ref), channel_id=1, source_target_pairs={{0,2},{1,3},{2,0},{3,1},{4,6},{5,7},{6,4},{7,5},{8,10},{9,11},{10,... | collective-permute-start | bytes 884744 | tf_op jit(solution)/shard_map/ppermute | solution.py:493
  19.9 7.3 %shard_map.89 = (bf16[6,6,128,768]{3,2,1,0:T(8,128)(2,1)}, f32[128,768]{1,0:T(8,128)S(1)}) custom-call(s32[6,6,6]{2,1,0:T(8,128)} %nb_hbm.2, bf16[6,6,6,128,128]{4,3,2,1,0:T(8,128)(2,1)} %near_hbm.5, bf16[6,6,128,128]{3,2,1,0:T(8,128)(2,1)} %right_hbm.5, bf16[6,6,128,768]{3,2,1,0:T(8,128)(2,1)} %refs_0_.2), custom_call_target="tpu_custom_call" | custom-call | flops 550000000 | tf_op jit(solution)/shard_map/pallas_call | solution.py:137
  27.4 5.9 %shard_map.90 = (s16[128,1152]{1,0:T(8,128)(2,1)S(1)}, f32[128,128]{1,0:T(8,128)S(1)}) custom-call(s16[128,1152]{1,0:T(8,128)(2,1)S(1)} %get-tuple-element.55.mine_ref, s16[128,1152]{1,0:T(8,128)(2,1)S(1)} %collective-permute-done.1.other_ref, f32[128,256]{1,0:T(8,128)S(1)} %get-tuple-element.53.sketch_ref, f32[128,128]{1,0:T(8,128)S(1)} %get-tuple-element.59.refs_0_), custom_call_target="tpu_custom_call" | custom-call | flops 1650000000 | tf_op jit(solution)/shard_map/pallas_call | solution.py:476
  33.3 2.7 %collective-permute-start.2 = (s16[128,1152]{1,0:T(8,128)(2,1)S(1)}, s16[128,1152]{1,0:T(8,128)(2,1)S(1)}, u32[]{:S(2)}, u32[]{:S(2)}) collective-permute-start(s16[128,1152]{1,0:T(8,128)(2,1)S(1)} %get-tuple-element.62.mine_ref), channel_id=1, source_target_pairs={{0,4},{1,5},{2,6},{3,7},{4,0},{5,1},{6,2},{7,3},{8,12},{9,13},{10,... | collective-permute-start | bytes 884744 | tf_op jit(solution)/shard_map/ppermute | solution.py:493
  36.0 0.7 collective-permute-start.7
  36.7 1.6 %collective-permute-start.10 = (bf16[4,128,768]{2,1,0:T(8,128)(2,1)}, bf16[4,128,768]{2,1,0:T(8,128)(2,1)}, u32[]{:S(2)}, u32[]{:S(2)}) collective-permute-start(bf16[4,128,768]{2,1,0:T(8,128)(2,1)} %get-tuple-element.77), channel_id=1, source_target_pairs={{1,2},{2,1},{3,4},{4,3},{5,6},{6,5},{9,10},{10,9},{11,12},{12,11},... | collective-permute-start | bytes 2359304 | tf_op jit(solution)/shard_map/ppermute | solution.py:505
  38.3 4.8 %shard_map.91 = (bf16[6,6,128,768]{3,2,1,0:T(8,128)(2,1)}, f32[128,768]{1,0:T(8,128)S(1)}) custom-call(s32[6,6,6]{2,1,0:T(8,128)} %nb_hbm.2, bf16[6,6,6,128,128]{4,3,2,1,0:T(8,128)(2,1)} %near_hbm.5, bf16[6,6,128,128]{3,2,1,0:T(8,128)(2,1)} %right_hbm.5, bf16[6,6,128,768]{3,2,1,0:T(8,128)(2,1)} %refs_0_.2, ...), custom_call_target="tpu_custom_call", output_to_operand_aliasing={{0}: (6, {})} | custom-call | flops 550000000 | tf_op jit(solution)/shard_map/pallas_call | solution.py:137
  43.1 7.0 %collective-permute-done.2.other_ref = s16[128,1152]{1,0:T(8,128)(2,1)S(1)} collective-permute-done((s16[128,1152]{1,0:T(8,128)(2,1)S(1)}, s16[128,1152]{1,0:T(8,128)(2,1)S(1)}, u32[]{:S(2)}, u32[]{:S(2)}) %collective-permute-start.2) | collective-permute-done | bytes 294944 | tf_op jit(solution)/shard_map/ppermute | solution.py:493
  50.1 5.9 %shard_map.92 = (s16[128,1152]{1,0:T(8,128)(2,1)S(1)}, f32[128,128]{1,0:T(8,128)S(1)}) custom-call(s16[128,1152]{1,0:T(8,128)(2,1)S(1)} %get-tuple-element.62.mine_ref, s16[128,1152]{1,0:T(8,128)(2,1)S(1)} %collective-permute-done.2.other_ref, f32[128,256]{1,0:T(8,128)S(1)} %get-tuple-element.53.sketch_ref, f32[128,128]{1,0:T(8,128)S(1)} %get-tuple-element.69.refs_0_), custom_call_target="tpu_custom_call" | custom-call | flops 550000000 | tf_op jit(solution)/shard_map/pallas_call | solution.py:476
  56.1 1.0 shard_map.94
  57.7 1.4 %collective-permute-start.9 = (bf16[2,128,768]{2,1,0:T(8,128)(2,1)}, bf16[2,128,768]{2,1,0:T(8,128)(2,1)}, u32[]{:S(2)}, u32[]{:S(2)}) collective-permute-start(bf16[2,128,768]{2,1,0:T(8,128)(2,1)} %get-tuple-element.76), channel_id=1, source_target_pairs={{8,16},{16,8},{9,17},{17,9},{10,18},{18,10},{11,19},{19,11},{12,20... | collective-permute-start | bytes 1179656 | tf_op jit(solution)/shard_map/ppermute | solution.py:505
  59.1 6.6 %shard_map.93 = (s16[128,1152]{1,0:T(8,128)(2,1)}, f32[128,128]{1,0:T(8,128)S(1)}) custom-call(s16[128,1152]{1,0:T(8,128)(2,1)S(1)} %get-tuple-element.70.mine_ref, s16[128,1152]{1,0:T(8,128)(2,1)S(1)} %collective-permute-done.5.other_ref, f32[128,256]{1,0:T(8,128)S(1)} %get-tuple-element.53.sketch_ref), custom_call_target="tpu_custom_call" | custom-call | flops 550000000 | tf_op jit(solution)/shard_map/pallas_call | solution.py:476
  65.7 0.6 copy-done.10
  66.3 2.2 %collective-permute-start.11 = (s16[128,1152]{1,0:T(8,128)(2,1)}, s16[128,1152]{1,0:T(8,128)(2,1)}, u32[]{:S(2)}, u32[]{:S(2)}) collective-permute-start(s16[128,1152]{1,0:T(8,128)(2,1)} %get-tuple-element.87.mine_ref), channel_id=1, source_target_pairs={{0,16},{8,24},{16,0},{24,8},{1,17},{9,25},{17,1},{25,9},{2,18},{10... | collective-permute-start | bytes 884744 | tf_op jit(solution)/shard_map/ppermute | solution.py:493
  68.5 1.0 copy-done.5
  69.5 7.7 %shard_map.95 = (bf16[6,6,128,768]{3,2,1,0:T(8,128)(2,1)}, f32[128,768]{1,0:T(8,128)S(1)}) custom-call(s32[6,6,6]{2,1,0:T(8,128)} %nb_hbm.2, bf16[6,6,6,128,128]{4,3,2,1,0:T(8,128)(2,1)} %near_hbm.5, bf16[6,6,128,128]{3,2,1,0:T(8,128)(2,1)} %right_hbm.5, bf16[6,6,128,768]{3,2,1,0:T(8,128)(2,1)} %refs_0_.2, ...), custom_call_target="tpu_custom_call", output_to_operand_aliasing={{0}: (11, {})} | custom-call | flops 550000000 | tf_op jit(solution)/shard_map/pallas_call | solution.py:137
  77.8 4.9 %collective-permute-start.12 = (f32[4,96,128]{2,1,0:T(8,128)S(1)}, f32[4,96,128]{2,1,0:T(8,128)S(1)}, u32[]{:S(2)}, u32[]{:S(2)}) collective-permute-start(f32[4,96,128]{2,1,0:T(8,128)S(1)} %dynamic-slice_bitcast_fusion), channel_id=1, source_target_pairs={{0,1},{1,0},{2,3},{3,2},{4,5},{5,4},{6,7},{7,6},{8,9},{9,8},{10,11... | collective-permute-start | bytes 589832 | tf_op jit(solution)/shard_map/ppermute | solution.py:493
  82.7 6.5 %shard_map.96 = (f32[128,256]{1,0:T(8,128)S(1)}, f32[128,128]{1,0:T(8,128)S(1)}) custom-call(s16[128,1152]{1,0:T(8,128)(2,1)} %get-tuple-element.87.mine_ref, s16[128,1152]{1,0:T(8,128)(2,1)} %collective-permute-done.11.other_ref, f32[128,256]{1,0:T(8,128)S(1)} %copy-done.9, f32[128,128]{1,0:T(8,128)S(1)} %copy-done.11), custom_call_target="tpu_custom_call" | custom-call | flops 550000000 | tf_op jit(solution)/shard_map/pallas_call | solution.py:476
  89.2 3.5 %collective-permute-start.13 = (f32[96,128]{1,0:T(8,128)S(1)}, f32[96,128]{1,0:T(8,128)S(1)}, u32[]{:S(2)}, u32[]{:S(2)}) collective-permute-start(f32[96,128]{1,0:T(8,128)S(1)} %get-tuple-element.94), channel_id=1, source_target_pairs={{0,2},{1,3},{2,0},{3,1},{4,6},{5,7},{6,4},{7,5},{8,10},{9,11},{10,... | collective-permute-start | bytes 147464 | tf_op jit(solution)/shard_map/ppermute | solution.py:493
  92.7 1.5 %collective-permute-start.14 = (f32[96,128]{1,0:T(8,128)S(1)}, f32[96,128]{1,0:T(8,128)S(1)}, u32[]{:S(2)}, u32[]{:S(2)}) collective-permute-start(f32[96,128]{1,0:T(8,128)S(1)} %get-tuple-element.96), channel_id=1, source_target_pairs={{0,4},{1,5},{2,6},{3,7},{4,0},{5,1},{6,2},{7,3},{8,12},{9,13},{10,... | collective-permute-start | bytes 147464 | tf_op jit(solution)/shard_map/ppermute | solution.py:493
  94.3 1.4 %collective-permute-start.15 = (f32[96,128]{1,0:T(8,128)S(1)}, f32[96,128]{1,0:T(8,128)S(1)}, u32[]{:S(2)}, u32[]{:S(2)}) collective-permute-start(f32[96,128]{1,0:T(8,128)S(1)} %get-tuple-element.95), channel_id=1, source_target_pairs={{0,6},{1,7},{2,4},{3,5},{4,2},{5,3},{6,0},{7,1},{8,14},{9,15},{10,... | collective-permute-start | bytes 147464 | tf_op jit(solution)/shard_map/ppermute | solution.py:493
  95.7 3.5 %collective-permute-done.14 = f32[96,128]{1,0:T(8,128)S(1)} collective-permute-done((f32[96,128]{1,0:T(8,128)S(1)}, f32[96,128]{1,0:T(8,128)S(1)}, u32[]{:S(2)}, u32[]{:S(2)}) %collective-permute-start.14) | collective-permute-done | bytes 49184 | tf_op jit(solution)/shard_map/ppermute | solution.py:493
  99.1 1.1 %collective-permute-done.15 = f32[96,128]{1,0:T(8,128)S(1)} collective-permute-done((f32[96,128]{1,0:T(8,128)S(1)}, f32[96,128]{1,0:T(8,128)S(1)}, u32[]{:S(2)}, u32[]{:S(2)}) %collective-permute-start.15) | collective-permute-done | bytes 49184 | tf_op jit(solution)/shard_map/ppermute | solution.py:493
  100.6 1.8 %collective-permute-start.18 = (f32[96,128]{1,0:T(8,128)S(1)}, f32[96,128]{1,0:T(8,128)S(1)}, u32[]{:S(2)}, u32[]{:S(2)}) collective-permute-start(f32[96,128]{1,0:T(8,128)S(1)} %fusion.5), channel_id=1, source_target_pairs={{0,24},{8,16},{16,8},{24,0},{1,25},{9,17},{17,9},{25,1},{2,26},{10... | collective-permute-start | bytes 147464 | tf_op jit(solution)/shard_map/ppermute | solution.py:493
  102.4 2.7 %collective-permute-done.17 = f32[96,128]{1,0:T(8,128)S(1)} collective-permute-done((f32[96,128]{1,0:T(8,128)S(1)}, f32[96,128]{1,0:T(8,128)S(1)}, u32[]{:S(2)}, u32[]{:S(2)}) %collective-permute-start.17) | collective-permute-done | bytes 49184 | tf_op jit(solution)/shard_map/ppermute | solution.py:493
  105.3 0.8 fusion.7
  (47 shorter events, 2.1 us)
Async XLA Ops:
  2.1 57.0 %copy-start.8 = (f32[128,256]{1,0:T(8,128)}, f32[128,256]{1,0:T(8,128)S(1)}, u32[]{:S(2)}) copy-start(f32[128,256]{1,0:T(8,128)S(1)} %get-tuple-element.53.sketch_ref) | copy-start | bytes 393220
  2.1 10.0 %collective-permute-start = (s16[128,1152]{1,0:T(8,128)(2,1)S(1)}, s16[128,1152]{1,0:T(8,128)(2,1)S(1)}, u32[]{:S(2)}, u32[]{:S(2)}) collective-permute-start(s16[128,1152]{1,0:T(8,128)(2,1)S(1)} %get-tuple-element.52.mine_ref), channel_id=1, source_target_pairs={{0,1},{1,0},{2,3},{3,2},{4,5},{5,4},{6,7},{7,6},{8,9},{9,8},{10,11... | collective-permute-start | bytes 884744 | tf_op jit(solution)/shard_map/ppermute | solution.py:493
  8.6 28.0 %collective-permute-start.3 = (bf16[6,128,768]{2,1,0:T(8,128)(2,1)S(1)}, bf16[6,128,768]{2,1,0:T(8,128)(2,1)S(1)}, u32[]{:S(2)}, u32[]{:S(2)}) collective-permute-start(bf16[6,128,768]{2,1,0:T(8,128)(2,1)S(1)} %get-tuple-element.64), channel_id=1, source_target_pairs={{0,8},{8,0},{16,24},{24,16},{1,9},{9,1},{17,25},{25,17},{2,10},{10... | collective-permute-start | bytes 3538952 | tf_op jit(solution)/shard_map/ppermute | solution.py:505
  8.7 29.5 %collective-permute-start.4 = (bf16[6,128,768]{2,1,0:T(8,128)(2,1)S(1)}, bf16[6,128,768]{2,1,0:T(8,128)(2,1)S(1)}, u32[]{:S(2)}, u32[]{:S(2)}) collective-permute-start(bf16[6,128,768]{2,1,0:T(8,128)(2,1)S(1)} %get-tuple-element.65), channel_id=1, source_target_pairs={{8,16},{16,8},{9,17},{17,9},{10,18},{18,10},{11,19},{19,11},{12,20... | collective-permute-start | bytes 3538952 | tf_op jit(solution)/shard_map/ppermute | solution.py:505
  9.5 46.6 %collective-permute-start.6 = (bf16[6,128,768]{2,1,0:T(8,128)(2,1)S(1)}, bf16[6,128,768]{2,1,0:T(8,128)(2,1)S(1)}, u32[]{:S(2)}, u32[]{:S(2)}) collective-permute-start(bf16[6,128,768]{2,1,0:T(8,128)(2,1)S(1)} %get-tuple-element.73), channel_id=1, source_target_pairs={{0,1},{1,0},{2,3},{3,2},{4,5},{5,4},{6,7},{7,6},{8,9},{9,8},{10,11... | collective-permute-start | bytes 3538952 | tf_op jit(solution)/shard_map/ppermute | solution.py:505
  18.0 9.4 %collective-permute-start.1 = (s16[128,1152]{1,0:T(8,128)(2,1)S(1)}, s16[128,1152]{1,0:T(8,128)(2,1)S(1)}, u32[]{:S(2)}, u32[]{:S(2)}) collective-permute-start(s16[128,1152]{1,0:T(8,128)(2,1)S(1)} %get-tuple-element.55.mine_ref), channel_id=1, source_target_pairs={{0,2},{1,3},{2,0},{3,1},{4,6},{5,7},{6,4},{7,5},{8,10},{9,11},{10,... | collective-permute-start | bytes 884744 | tf_op jit(solution)/shard_map/ppermute | solution.py:493
  27.2 6.1 %copy-start = (f32[128,768]{1,0:T(8,128)}, f32[128,768]{1,0:T(8,128)S(1)}, u32[]{:S(2)}) copy-start(f32[128,768]{1,0:T(8,128)S(1)} %get-tuple-element.80) | copy-start | bytes 1179652
  33.3 16.8 %collective-permute-start.2 = (s16[128,1152]{1,0:T(8,128)(2,1)S(1)}, s16[128,1152]{1,0:T(8,128)(2,1)S(1)}, u32[]{:S(2)}, u32[]{:S(2)}) collective-permute-start(s16[128,1152]{1,0:T(8,128)(2,1)S(1)} %get-tuple-element.62.mine_ref), channel_id=1, source_target_pairs={{0,4},{1,5},{2,6},{3,7},{4,0},{5,1},{6,2},{7,3},{8,12},{9,13},{10,... | collective-permute-start | bytes 884744 | tf_op jit(solution)/shard_map/ppermute | solution.py:493
  36.0 20.1 %collective-permute-start.7 = (bf16[2,128,768]{2,1,0:T(8,128)(2,1)S(1)}, bf16[2,128,768]{2,1,0:T(8,128)(2,1)S(1)}, u32[]{:S(2)}, u32[]{:S(2)}) collective-permute-start(bf16[2,128,768]{2,1,0:T(8,128)(2,1)S(1)} %get-tuple-element.74), channel_id=1, source_target_pairs={{1,2},{2,1},{3,4},{4,3},{5,6},{6,5},{9,10},{10,9},{11,12},{12,11},... | collective-permute-start | bytes 1179656 | tf_op jit(solution)/shard_map/ppermute | solution.py:505
  36.7 31.8 %collective-permute-start.10 = (bf16[4,128,768]{2,1,0:T(8,128)(2,1)}, bf16[4,128,768]{2,1,0:T(8,128)(2,1)}, u32[]{:S(2)}, u32[]{:S(2)}) collective-permute-start(bf16[4,128,768]{2,1,0:T(8,128)(2,1)} %get-tuple-element.77), channel_id=1, source_target_pairs={{1,2},{2,1},{3,4},{4,3},{5,6},{6,5},{9,10},{10,9},{11,12},{12,11},... | collective-permute-start | bytes 2359304 | tf_op jit(solution)/shard_map/ppermute | solution.py:505
  43.1 14.0 %copy-start.2 = (f32[128,768]{1,0:T(8,128)}, f32[128,768]{1,0:T(8,128)S(1)}, u32[]{:S(2)}) copy-start(f32[128,768]{1,0:T(8,128)S(1)} %get-tuple-element.81) | copy-start | bytes 1179652
  56.0 1.1 %copy-start.6 = (f32[128,128]{1,0:T(8,128)}, f32[128,128]{1,0:T(8,128)S(1)}, u32[]{:S(2)}) copy-start(f32[128,128]{1,0:T(8,128)S(1)} %get-tuple-element.84) | copy-start | bytes 196612
  56.0 3.1 %collective-permute-start.5 = (s16[128,1152]{1,0:T(8,128)(2,1)S(1)}, s16[128,1152]{1,0:T(8,128)(2,1)S(1)}, u32[]{:S(2)}, u32[]{:S(2)}) collective-permute-start(s16[128,1152]{1,0:T(8,128)(2,1)S(1)} %get-tuple-element.70.mine_ref), channel_id=1, source_target_pairs={{0,8},{8,0},{16,24},{24,16},{1,9},{9,1},{17,25},{25,17},{2,10},{10... | collective-permute-start | bytes 884744 | tf_op jit(solution)/shard_map/ppermute | solution.py:493
  56.1 1.0 copy-start.4
  57.1 11.4 %collective-permute-start.8 = (bf16[2,128,768]{2,1,0:T(8,128)(2,1)}, bf16[2,128,768]{2,1,0:T(8,128)(2,1)}, u32[]{:S(2)}, u32[]{:S(2)}) collective-permute-start(bf16[2,128,768]{2,1,0:T(8,128)(2,1)} %get-tuple-element.75), channel_id=1, source_target_pairs={{0,8},{8,0},{16,24},{24,16},{1,9},{9,1},{17,25},{25,17},{2,10},{10... | collective-permute-start | bytes 1179656 | tf_op jit(solution)/shard_map/ppermute | solution.py:505
  57.7 10.8 %collective-permute-start.9 = (bf16[2,128,768]{2,1,0:T(8,128)(2,1)}, bf16[2,128,768]{2,1,0:T(8,128)(2,1)}, u32[]{:S(2)}, u32[]{:S(2)}) collective-permute-start(bf16[2,128,768]{2,1,0:T(8,128)(2,1)} %get-tuple-element.76), channel_id=1, source_target_pairs={{8,16},{16,8},{9,17},{17,9},{10,18},{18,10},{11,19},{19,11},{12,20... | collective-permute-start | bytes 1179656 | tf_op jit(solution)/shard_map/ppermute | solution.py:505
  65.7 0.6 copy-start.10
  66.3 10.9 %collective-permute-start.11 = (s16[128,1152]{1,0:T(8,128)(2,1)}, s16[128,1152]{1,0:T(8,128)(2,1)}, u32[]{:S(2)}, u32[]{:S(2)}) collective-permute-start(s16[128,1152]{1,0:T(8,128)(2,1)} %get-tuple-element.87.mine_ref), channel_id=1, source_target_pairs={{0,16},{8,24},{16,0},{24,8},{1,17},{9,25},{17,1},{25,9},{2,18},{10... | collective-permute-start | bytes 884744 | tf_op jit(solution)/shard_map/ppermute | solution.py:493
  68.5 1.0 copy-start.5
  69.5 7.7 %copy-start.1 = (f32[128,768]{1,0:T(8,128)S(1)}, f32[128,768]{1,0:T(8,128)}, u32[]{:S(2)}) copy-start(f32[128,768]{1,0:T(8,128)} %copy-done) | copy-start | bytes 1179652
  69.5 7.7 %copy-start.3 = (f32[128,768]{1,0:T(8,128)S(1)}, f32[128,768]{1,0:T(8,128)}, u32[]{:S(2)}) copy-start(f32[128,768]{1,0:T(8,128)} %copy-done.2) | copy-start | bytes 1179652
  69.5 7.7 %copy-start.7 = (f32[128,128]{1,0:T(8,128)S(1)}, f32[128,128]{1,0:T(8,128)}, u32[]{:S(2)}) copy-start(f32[128,128]{1,0:T(8,128)} %copy-done.6) | copy-start | bytes 196612
  77.2 5.5 %copy-start.9 = (f32[128,256]{1,0:T(8,128)S(1)}, f32[128,256]{1,0:T(8,128)}, u32[]{:S(2)}) copy-start(f32[128,256]{1,0:T(8,128)} %copy-done.8) | copy-start | bytes 393220
  77.2 5.5 %copy-start.11 = (f32[128,128]{1,0:T(8,128)S(1)}, f32[128,128]{1,0:T(8,128)}, u32[]{:S(2)}) copy-start(f32[128,128]{1,0:T(8,128)} %copy-done.10) | copy-start | bytes 196612
  77.8 11.4 %collective-permute-start.12 = (f32[4,96,128]{2,1,0:T(8,128)S(1)}, f32[4,96,128]{2,1,0:T(8,128)S(1)}, u32[]{:S(2)}, u32[]{:S(2)}) collective-permute-start(f32[4,96,128]{2,1,0:T(8,128)S(1)} %dynamic-slice_bitcast_fusion), channel_id=1, source_target_pairs={{0,1},{1,0},{2,3},{3,2},{4,5},{5,4},{6,7},{7,6},{8,9},{9,8},{10,11... | collective-permute-start | bytes 589832 | tf_op jit(solution)/shard_map/ppermute | solution.py:493
  89.2 6.4 %collective-permute-start.13 = (f32[96,128]{1,0:T(8,128)S(1)}, f32[96,128]{1,0:T(8,128)S(1)}, u32[]{:S(2)}, u32[]{:S(2)}) collective-permute-start(f32[96,128]{1,0:T(8,128)S(1)} %get-tuple-element.94), channel_id=1, source_target_pairs={{0,2},{1,3},{2,0},{3,1},{4,6},{5,7},{6,4},{7,5},{8,10},{9,11},{10,... | collective-permute-start | bytes 147464 | tf_op jit(solution)/shard_map/ppermute | solution.py:493
  92.7 6.4 %collective-permute-start.14 = (f32[96,128]{1,0:T(8,128)S(1)}, f32[96,128]{1,0:T(8,128)S(1)}, u32[]{:S(2)}, u32[]{:S(2)}) collective-permute-start(f32[96,128]{1,0:T(8,128)S(1)} %get-tuple-element.96), channel_id=1, source_target_pairs={{0,4},{1,5},{2,6},{3,7},{4,0},{5,1},{6,2},{7,3},{8,12},{9,13},{10,... | collective-permute-start | bytes 147464 | tf_op jit(solution)/shard_map/ppermute | solution.py:493
  94.3 6.0 %collective-permute-start.15 = (f32[96,128]{1,0:T(8,128)S(1)}, f32[96,128]{1,0:T(8,128)S(1)}, u32[]{:S(2)}, u32[]{:S(2)}) collective-permute-start(f32[96,128]{1,0:T(8,128)S(1)} %get-tuple-element.95), channel_id=1, source_target_pairs={{0,6},{1,7},{2,4},{3,5},{4,2},{5,3},{6,0},{7,1},{8,14},{9,15},{10,... | collective-permute-start | bytes 147464 | tf_op jit(solution)/shard_map/ppermute | solution.py:493
  100.5 1.9 %collective-permute-start.16 = (f32[96,128]{1,0:T(8,128)S(1)}, f32[96,128]{1,0:T(8,128)S(1)}, u32[]{:S(2)}, u32[]{:S(2)}) collective-permute-start(f32[96,128]{1,0:T(8,128)S(1)} %fusion.5), channel_id=1, source_target_pairs={{0,8},{8,0},{16,24},{24,16},{1,9},{9,1},{17,25},{25,17},{2,10},{10... | collective-permute-start | bytes 147464 | tf_op jit(solution)/shard_map/ppermute | solution.py:493
  100.6 4.6 %collective-permute-start.17 = (f32[96,128]{1,0:T(8,128)S(1)}, f32[96,128]{1,0:T(8,128)S(1)}, u32[]{:S(2)}, u32[]{:S(2)}) collective-permute-start(f32[96,128]{1,0:T(8,128)S(1)} %fusion.5), channel_id=1, source_target_pairs={{0,16},{8,24},{16,0},{24,8},{1,17},{9,25},{17,1},{25,9},{2,18},{10... | collective-permute-start | bytes 147464 | tf_op jit(solution)/shard_map/ppermute | solution.py:493
  100.6 4.7 %collective-permute-start.18 = (f32[96,128]{1,0:T(8,128)S(1)}, f32[96,128]{1,0:T(8,128)S(1)}, u32[]{:S(2)}, u32[]{:S(2)}) collective-permute-start(f32[96,128]{1,0:T(8,128)S(1)} %fusion.5), channel_id=1, source_target_pairs={{0,24},{8,16},{16,8},{24,0},{1,25},{9,17},{17,9},{25,1},{2,26},{10... | collective-permute-start | bytes 147464 | tf_op jit(solution)/shard_map/ppermute | solution.py:493

commit v13 on v10

--- a/solution.py
+++ b/solution.py
@@ -246,23 +246,21 @@
     return copies
 
 
-def corners_kernel(beside, ends, to_near, to_far, sems):
+def corners_kernel(beside, ends, to_near, to_far):
     low = odd("pu")
     rows = beside.shape[0]
-    pairs = []
     for target, last in ((to_near, 1 - low), (to_far, low)):
-        pairs += [(beside.at[(rows - 1) * last], target.at[0]), (ends.at[last], target.at[1])]
-    for copy in run_copies(pairs, sems):
-        copy.wait()
+        target[0] = beside[(rows - 1) * last]
+        target[1] = ends[last]
 
 
 def patch_corners(beside, ends):
+    whole = pl.BlockSpec(memory_space=pltpu.VMEM)
     return pl.pallas_call(
         corners_kernel,
-        in_specs=[pl.BlockSpec(memory_space=pl.ANY)] * 2,
-        out_specs=[pl.BlockSpec(memory_space=pltpu.VMEM)] * 2,
+        in_specs=[whole, whole],
+        out_specs=[whole, whole],
         out_shape=[jax.ShapeDtypeStruct(ends.shape, ends.dtype)] * 2,
-        scratch_shapes=[pltpu.SemaphoreType.DMA((4,))],
         cost_estimate=cost(0.7),
         compiler_params=pltpu.CompilerParams(vmem_limit_bytes=merge_vmem),
     )(beside, ends)
@@ -511,7 +509,6 @@
 def per_device(density, near_blocks, neighbours, far_right, far_left, sketch, patch_order):
     pu_count = lax.axis_size("pu")
     pv_count = lax.axis_size("pv")
-    pv_index = lax.axis_index("pv")
     rhs = density.shape[3]
     pv_levels = pv_count.bit_length() - 1
     pu_levels = pu_count.bit_length() - 1
@@ -521,13 +518,6 @@
         if level < pv_levels:
             return from_partner(value, "pv", 1 << level)
         return from_partner(value, "pu", 1 << level - pv_levels)
-
-    def halved(share):
-        bit = pv_index & 1
-        pairs = share.reshape(share.shape[0] // 2, 2, *share.shape[1:])
-        keep = lax.dynamic_index_in_dim(pairs, bit, 1, keepdims=False)
-        give = lax.dynamic_index_in_dim(pairs, 1 - bit, 1, keepdims=False)
-        return keep + from_partner(give, "pv", 1)
 
     rows = far_left.shape[2]
     left, sketch = coded_leaf(far_left, sketch, patch_order, (pu_count, pv_count))
@@ -571,7 +561,7 @@
             share = lax.dot_general(coef, pv_path, (((0,), (1,)), ((), ())), precision=high)
             share = share.reshape(pv_count, rhs // pv_count, -1)
             share, other = tied(share, other)
-            share = halved(share)
+            share = lax.psum_scatter(share, "pv", scatter_dimension=0)
         path = pv_path if level < pv_levels else pu_path
         last_rows = rows // pu_count if last else 0
         left, path = merge(level, left, other, sketch, path, last_rows)
@@ -580,14 +570,7 @@
         else:
             pu_path = path
 
-    share, left = tied(share, left)
-    far_index = pv_index // 2
-    mine = lax.dynamic_index_in_dim(share, far_index, 0, keepdims=False)
-    parts = [mine]
-    for by in range(1, pv_count // 2):
-        give = lax.dynamic_index_in_dim(share, far_index ^ by, 0, keepdims=False)
-        parts.append(from_partner(give, "pv", 2 * by))
-    root_coef = lax.dot_general(summed(parts), pu_path, (((1,), (1,)), ((), ())), precision=high)
+    root_coef = lax.dot_general(share, pu_path, (((1,), (1,)), ((), ())), precision=high)
     root_coef = summed([root_coef] + [from_partner(root_coef, "pu", by) for by in range(1, pu_count)])
     far_field = lax.dot_general(left, root_coef, (((0,), (1,)), ((), ())), precision=high)
     return (corrected, far_field)

time: 105 us -> 162 us (1.54)
  waiting for transfers between devices: 16.3 us -> 71.2 us
  between operations: 1.01 us -> 14.3 us
  starting transfers between devices: 23.1 us -> 15.9 us
  Pallas kernels: 60.7 us -> 57.1 us
  local copies, waits for them, and re-layouts: 1.99 us -> 0 us
    reduce_scatter x0 -> x1, waiting for transfers between devices: none -> 58.2 us  [per_device(): share = lax.psum_scatter(share, 'pv', scatter_dimension=0)]
    ppermute x12 -> x8, starting transfers between devices: 18.8 us -> 12.2 us  [from_partner(): return lax.ppermute(value, axis, pairs)]
    ppermute x12 -> x8, waiting for transfers between devices: 16.3 us -> 13 us  [from_partner(): return lax.ppermute(value, axis, pairs)]
    unnamed x24 -> x0, local copies, waits for them, and re-layouts: 1.94 us -> none
    pallas_call x1, Pallas kernels: 1.95 us -> 0.07 us  [patch_corners(): pl.pallas_call(corners_kernel, in_specs=[whole, whole], out_specs=[whole,...]
    pallas_call x5, Pallas kernels: 30.6 us -> 28.8 us  [merge(): pl.pallas_call(functools.partial(merge_kernel, bool(paths), bool(last_row...]
  transfers between devices with their start and end apart: 19 -> 16, of which waited for: 8 -> 6; matrix products, arithmetic and copies ran while one was open for 0% -> 0% of each run, Pallas kernels for 57% -> 34%
where the time goes in v13:
time: 162 us
  waiting for transfers between devices  71.2 us (44%)
  Pallas kernels  57.1 us (35%)
  starting transfers between devices  15.9 us (10%)
  between operations  14.3 us (9%)
  matrix products  3.08 us (2%)
    reduce_scatter x1, waiting for transfers between devices, per_device(): share = lax.psum_scatter(share, 'pv', scatter_dimension=0)  58.2 us
    pallas_call x5, Pallas kernels, merge(): pl.pallas_call(functools.partial(merge_kernel, bool(paths), bool(last_row...  28.8 us
    pallas_call x4, Pallas kernels, near_part(): pl.pallas_call(functools.partial(near_kernel, plan, len(sources)), grid=(...  24.1 us
    ppermute x8, waiting for transfers between devices, from_partner(): return lax.ppermute(value, axis, pairs)  13 us
    ppermute x8, starting transfers between devices, from_partner(): return lax.ppermute(value, axis, pairs)  12.2 us
    ppermute x7, starting transfers between devices, swapped(): return lax.ppermute(value, axis, pairs)  3.65 us
  transfers between devices with their start and end apart: 16, of which 6 were waited for; matrix products, arithmetic and copies ran while one was open for 0% of the time, Pallas kernels for 34%

profile of v13, /device:TPU:0, one launch (start us, length us, event | category | flops | bytes accessed | tf_op | source)
XLA Modules:
  0.0 161.6 jit_solution(16096141003869280255)
XLA Ops:
  7.2 1.5 shard_map.86
  8.7 3.0 %collective-permute-start = (s16[128,1152]{1,0:T(8,128)(2,1)S(1)}, s16[128,1152]{1,0:T(8,128)(2,1)S(1)}, u32[]{:S(2)}, u32[]{:S(2)}) collective-permute-start(s16[128,1152]{1,0:T(8,128)(2,1)S(1)} %get-tuple-element.52.mine_ref), channel_id=1, source_target_pairs={{0,1},{1,0},{2,3},{3,2},{4,5},{5,4},{6,7},{7,6},{8,9},{9,8},{10,11... | collective-permute-start | bytes 884744 | tf_op jit(solution)/shard_map/ppermute | solution.py:490
  11.7 2.6 %shard_map.87 = (bf16[6,128,768]{2,1,0:T(8,128)(2,1)S(1)}, bf16[2,128,768]{2,1,0:T(8,128)(2,1)S(1)}, bf16[4,128,768]{2,1,0:T(8,128)(2,1)S(1)}, bf16[6,128,768]{2,1,0:T(8,128)(2,1)S(1)}, bf16[6,128,768]{2,1,0:T(8,128)(2,1)S(1)}) custom-call(bf16[6,6,128,768]{3,2,1,0:T(8,128)(2,1)} %refs_0_.3), custom_call_target="tpu_custom_call" | custom-call | flops 2750000128 | tf_op jit(solution)/shard_map/pallas_call | solution.py:418
  14.4 0.7 collective-permute-start.4
  15.2 3.5 %collective-permute-done.other_ref = s16[128,1152]{1,0:T(8,128)(2,1)S(1)} collective-permute-done((s16[128,1152]{1,0:T(8,128)(2,1)S(1)}, s16[128,1152]{1,0:T(8,128)(2,1)S(1)}, u32[]{:S(2)}, u32[]{:S(2)}) %collective-permute-start) | collective-permute-done | bytes 294944 | tf_op jit(solution)/shard_map/ppermute | solution.py:490
  18.7 5.8 %shard_map.88 = (s16[128,1152]{1,0:T(8,128)(2,1)S(1)}, f32[128,128]{1,0:T(8,128)S(1)}) custom-call(s16[128,1152]{1,0:T(8,128)(2,1)S(1)} %get-tuple-element.52.mine_ref, s16[128,1152]{1,0:T(8,128)(2,1)S(1)} %collective-permute-done.other_ref, f32[128,256]{1,0:T(8,128)S(1)} %get-tuple-element.53.sketch_ref), custom_call_target="tpu_custom_call" | custom-call | flops 9900000256 | tf_op jit(solution)/shard_map/pallas_call | solution.py:473
  24.5 1.9 %collective-permute-start.1 = (s16[128,1152]{1,0:T(8,128)(2,1)S(1)}, s16[128,1152]{1,0:T(8,128)(2,1)S(1)}, u32[]{:S(2)}, u32[]{:S(2)}) collective-permute-start(s16[128,1152]{1,0:T(8,128)(2,1)S(1)} %get-tuple-element.55.mine_ref), channel_id=1, source_target_pairs={{0,2},{1,3},{2,0},{3,1},{4,6},{5,7},{6,4},{7,5},{8,10},{9,11},{10,... | collective-permute-start | bytes 884744 | tf_op jit(solution)/shard_map/ppermute | solution.py:490
  26.4 7.4 %shard_map.89 = (bf16[6,6,128,768]{3,2,1,0:T(8,128)(2,1)}, f32[128,768]{1,0:T(8,128)S(1)}) custom-call(s32[6,6,6]{2,1,0:T(8,128)} %nb_hbm.3, bf16[6,6,6,128,128]{4,3,2,1,0:T(8,128)(2,1)} %near_hbm.7, bf16[6,6,128,128]{3,2,1,0:T(8,128)(2,1)} %right_hbm.7, bf16[6,6,128,768]{3,2,1,0:T(8,128)(2,1)} %refs_0_.3), custom_call_target="tpu_custom_call" | custom-call | flops 550000000 | tf_op jit(solution)/shard_map/pallas_call | solution.py:137
  33.8 5.9 %shard_map.90 = (s16[128,1152]{1,0:T(8,128)(2,1)S(1)}, f32[128,128]{1,0:T(8,128)S(1)}) custom-call(s16[128,1152]{1,0:T(8,128)(2,1)S(1)} %get-tuple-element.55.mine_ref, s16[128,1152]{1,0:T(8,128)(2,1)S(1)} %collective-permute-done.1.other_ref, f32[128,256]{1,0:T(8,128)S(1)} %get-tuple-element.53.sketch_ref, f32[128,128]{1,0:T(8,128)S(1)} %get-tuple-element.59.refs_0_), custom_call_target="tpu_custom_call" | custom-call | flops 1650000000 | tf_op jit(solution)/shard_map/pallas_call | solution.py:473
  39.7 2.6 %collective-permute-start.2 = (s16[128,1152]{1,0:T(8,128)(2,1)S(1)}, s16[128,1152]{1,0:T(8,128)(2,1)S(1)}, u32[]{:S(2)}, u32[]{:S(2)}) collective-permute-start(s16[128,1152]{1,0:T(8,128)(2,1)S(1)} %get-tuple-element.62.mine_ref), channel_id=1, source_target_pairs={{0,4},{1,5},{2,6},{3,7},{4,0},{5,1},{6,2},{7,3},{8,12},{9,13},{10,... | collective-permute-start | bytes 884744 | tf_op jit(solution)/shard_map/ppermute | solution.py:490
  42.3 0.7 collective-permute-start.7
  43.0 0.9 collective-permute-start.10
  43.9 4.8 %shard_map.91 = (bf16[6,6,128,768]{3,2,1,0:T(8,128)(2,1)}, f32[128,768]{1,0:T(8,128)S(1)}) custom-call(s32[6,6,6]{2,1,0:T(8,128)} %nb_hbm.3, bf16[6,6,6,128,128]{4,3,2,1,0:T(8,128)(2,1)} %near_hbm.7, bf16[6,6,128,128]{3,2,1,0:T(8,128)(2,1)} %right_hbm.7, bf16[6,6,128,768]{3,2,1,0:T(8,128)(2,1)} %refs_0_.3, ...), custom_call_target="tpu_custom_call", output_to_operand_aliasing={{0}: (6, {})} | custom-call | flops 550000000 | tf_op jit(solution)/shard_map/pallas_call | solution.py:137
  48.8 6.2 %collective-permute-done.2.other_ref = s16[128,1152]{1,0:T(8,128)(2,1)S(1)} collective-permute-done((s16[128,1152]{1,0:T(8,128)(2,1)S(1)}, s16[128,1152]{1,0:T(8,128)(2,1)S(1)}, u32[]{:S(2)}, u32[]{:S(2)}) %collective-permute-start.2) | collective-permute-done | bytes 294944 | tf_op jit(solution)/shard_map/ppermute | solution.py:490
  54.9 5.9 %shard_map.92 = (s16[128,1152]{1,0:T(8,128)(2,1)S(1)}, f32[128,128]{1,0:T(8,128)S(1)}) custom-call(s16[128,1152]{1,0:T(8,128)(2,1)S(1)} %get-tuple-element.62.mine_ref, s16[128,1152]{1,0:T(8,128)(2,1)S(1)} %collective-permute-done.2.other_ref, f32[128,256]{1,0:T(8,128)S(1)} %get-tuple-element.53.sketch_ref, f32[128,128]{1,0:T(8,128)S(1)} %get-tuple-element.69.refs_0_), custom_call_target="tpu_custom_call" | custom-call | flops 550000000 | tf_op jit(solution)/shard_map/pallas_call | solution.py:473
  60.8 0.1 collective-permute-start.5
  61.0 0.5 collective-permute-start.8
  61.5 0.7 collective-permute-start.9
  62.2 0.3 collective-permute-done.5.other_ref
  62.5 5.8 %shard_map.93 = (s16[128,1152]{1,0:T(8,128)(2,1)S(1)}, f32[128,128]{1,0:T(8,128)S(1)}) custom-call(s16[128,1152]{1,0:T(8,128)(2,1)S(1)} %get-tuple-element.70.mine_ref, s16[128,1152]{1,0:T(8,128)(2,1)S(1)} %collective-permute-done.5.other_ref, f32[128,256]{1,0:T(8,128)S(1)} %get-tuple-element.53.sketch_ref), custom_call_target="tpu_custom_call" | custom-call | flops 550000000 | tf_op jit(solution)/shard_map/pallas_call | solution.py:473
  68.3 2.7 %collective-permute-start.11 = (s16[128,1152]{1,0:T(8,128)(2,1)S(1)}, s16[128,1152]{1,0:T(8,128)(2,1)S(1)}, u32[]{:S(2)}, u32[]{:S(2)}) collective-permute-start(s16[128,1152]{1,0:T(8,128)(2,1)S(1)} %get-tuple-element.81.mine_ref), channel_id=1, source_target_pairs={{0,16},{8,24},{16,0},{24,8},{1,17},{9,25},{17,1},{25,9},{2,18},{10... | collective-permute-start | bytes 884744 | tf_op jit(solution)/shard_map/ppermute | solution.py:490
  71.0 5.9 %shard_map.95 = (bf16[6,6,128,768]{3,2,1,0:T(8,128)(2,1)}, f32[128,768]{1,0:T(8,128)S(1)}) custom-call(s32[6,6,6]{2,1,0:T(8,128)} %nb_hbm.3, bf16[6,6,6,128,128]{4,3,2,1,0:T(8,128)(2,1)} %near_hbm.7, bf16[6,6,128,128]{3,2,1,0:T(8,128)(2,1)} %right_hbm.7, bf16[6,6,128,768]{3,2,1,0:T(8,128)(2,1)} %refs_0_.3, ...), custom_call_target="tpu_custom_call", output_to_operand_aliasing={{0}: (9, {})} | custom-call | flops 550000000 | tf_op jit(solution)/shard_map/pallas_call | solution.py:137
  77.0 6.0 %shard_map.96 = (bf16[6,6,128,768]{3,2,1,0:T(8,128)(2,1)}, f32[128,768]{1,0:T(8,128)S(1)}) custom-call(s32[6,6,6]{2,1,0:T(8,128)} %nb_hbm.3, bf16[6,6,6,128,128]{4,3,2,1,0:T(8,128)(2,1)} %near_hbm.7, bf16[6,6,128,128]{3,2,1,0:T(8,128)(2,1)} %right_hbm.7, bf16[6,6,128,768]{3,2,1,0:T(8,128)(2,1)} %refs_0_.3, ...), custom_call_target="tpu_custom_call", output_to_operand_aliasing={{0}: (10, {})} | custom-call | flops 550000000 | tf_op jit(solution)/shard_map/pallas_call | solution.py:137
  83.0 1.2 fusion
  84.3 5.4 %shard_map.97 = (f32[128,256]{1,0:T(8,128)S(1)}, f32[128,128]{1,0:T(8,128)S(1)}) custom-call(s16[128,1152]{1,0:T(8,128)(2,1)S(1)} %get-tuple-element.81.mine_ref, s16[128,1152]{1,0:T(8,128)(2,1)S(1)} %collective-permute-done.11.other_ref, f32[128,256]{1,0:T(8,128)S(1)} %get-tuple-element.53.sketch_ref, f32[128,128]{1,0:T(8,128)S(1)} %get-tuple-element.90.refs_0_), custom_call_target="tpu_custom_call" | custom-call | flops 550000000 | tf_op jit(solution)/shard_map/pallas_call | solution.py:473
  89.7 58.2 %reduce-scatter.2.cloned.1.call-done = f32[1,96,128]{2,1,0:T(8,128)} async-done(((f32[8,96,128]{2,1,0:T(8,128)}), f32[1,96,128]{2,1,0:T(8,128)}) %reduce-scatter.2.cloned.1.call-update) | async-done | bytes 49168 | tf_op jit(solution)/shard_map/reduce_scatter | solution.py:564
  147.9 1.0 fusion.4
  148.9 1.5 collective-permute-start.13
  150.5 0.3 collective-permute-start.12
  150.8 2.2 %collective-permute-done.14 = f32[96,128]{1,0:T(8,128)S(1)} collective-permute-done((f32[96,128]{1,0:T(8,128)S(1)}, f32[96,128]{1,0:T(8,128)S(1)}, u32[]{:S(2)}, u32[]{:S(2)}) %collective-permute-start.14) | collective-permute-done | bytes 49184 | tf_op jit(solution)/shard_map/ppermute | solution.py:490
  153.0 0.9 collective-permute-done.13
  153.9 0.8 fusion.6
  (16 shorter events, 0.4 us)
Async XLA Ops:
  7.2 140.7 %reduce-scatter.2.cloned.1.call-start = ((), (), s32[]{:S(2)}) async-start(), calls=%async_computation.1 | async-start | bytes 442368 | tf_op jit(solution)/shard_map/reduce_scatter | solution.py:564
  8.7 10.0 %collective-permute-start = (s16[128,1152]{1,0:T(8,128)(2,1)S(1)}, s16[128,1152]{1,0:T(8,128)(2,1)S(1)}, u32[]{:S(2)}, u32[]{:S(2)}) collective-permute-start(s16[128,1152]{1,0:T(8,128)(2,1)S(1)} %get-tuple-element.52.mine_ref), channel_id=1, source_target_pairs={{0,1},{1,0},{2,3},{3,2},{4,5},{5,4},{6,7},{7,6},{8,9},{9,8},{10,11... | collective-permute-start | bytes 884744 | tf_op jit(solution)/shard_map/ppermute | solution.py:490
  14.3 28.7 %collective-permute-start.3 = (bf16[6,128,768]{2,1,0:T(8,128)(2,1)S(1)}, bf16[6,128,768]{2,1,0:T(8,128)(2,1)S(1)}, u32[]{:S(2)}, u32[]{:S(2)}) collective-permute-start(bf16[6,128,768]{2,1,0:T(8,128)(2,1)S(1)} %get-tuple-element.64), channel_id=1, source_target_pairs={{0,8},{8,0},{16,24},{24,16},{1,9},{9,1},{17,25},{25,17},{2,10},{10... | collective-permute-start | bytes 3538952 | tf_op jit(solution)/shard_map/ppermute | solution.py:502
  14.4 29.5 %collective-permute-start.4 = (bf16[6,128,768]{2,1,0:T(8,128)(2,1)S(1)}, bf16[6,128,768]{2,1,0:T(8,128)(2,1)S(1)}, u32[]{:S(2)}, u32[]{:S(2)}) collective-permute-start(bf16[6,128,768]{2,1,0:T(8,128)(2,1)S(1)} %get-tuple-element.65), channel_id=1, source_target_pairs={{8,16},{16,8},{9,17},{17,9},{10,18},{18,10},{11,19},{19,11},{12,20... | collective-permute-start | bytes 3538952 | tf_op jit(solution)/shard_map/ppermute | solution.py:502
  15.2 45.7 %collective-permute-start.6 = (bf16[6,128,768]{2,1,0:T(8,128)(2,1)S(1)}, bf16[6,128,768]{2,1,0:T(8,128)(2,1)S(1)}, u32[]{:S(2)}, u32[]{:S(2)}) collective-permute-start(bf16[6,128,768]{2,1,0:T(8,128)(2,1)S(1)} %get-tuple-element.73), channel_id=1, source_target_pairs={{0,1},{1,0},{2,3},{3,2},{4,5},{5,4},{6,7},{7,6},{8,9},{9,8},{10,11... | collective-permute-start | bytes 3538952 | tf_op jit(solution)/shard_map/ppermute | solution.py:502
  24.5 9.3 %collective-permute-start.1 = (s16[128,1152]{1,0:T(8,128)(2,1)S(1)}, s16[128,1152]{1,0:T(8,128)(2,1)S(1)}, u32[]{:S(2)}, u32[]{:S(2)}) collective-permute-start(s16[128,1152]{1,0:T(8,128)(2,1)S(1)} %get-tuple-element.55.mine_ref), channel_id=1, source_target_pairs={{0,2},{1,3},{2,0},{3,1},{4,6},{5,7},{6,4},{7,5},{8,10},{9,11},{10,... | collective-permute-start | bytes 884744 | tf_op jit(solution)/shard_map/ppermute | solution.py:490
  39.7 15.3 %collective-permute-start.2 = (s16[128,1152]{1,0:T(8,128)(2,1)S(1)}, s16[128,1152]{1,0:T(8,128)(2,1)S(1)}, u32[]{:S(2)}, u32[]{:S(2)}) collective-permute-start(s16[128,1152]{1,0:T(8,128)(2,1)S(1)} %get-tuple-element.62.mine_ref), channel_id=1, source_target_pairs={{0,4},{1,5},{2,6},{3,7},{4,0},{5,1},{6,2},{7,3},{8,12},{9,13},{10,... | collective-permute-start | bytes 884744 | tf_op jit(solution)/shard_map/ppermute | solution.py:490
  42.3 18.6 %collective-permute-start.7 = (bf16[2,128,768]{2,1,0:T(8,128)(2,1)S(1)}, bf16[2,128,768]{2,1,0:T(8,128)(2,1)S(1)}, u32[]{:S(2)}, u32[]{:S(2)}) collective-permute-start(bf16[2,128,768]{2,1,0:T(8,128)(2,1)S(1)} %get-tuple-element.74), channel_id=1, source_target_pairs={{1,2},{2,1},{3,4},{4,3},{5,6},{6,5},{9,10},{10,9},{11,12},{12,11},... | collective-permute-start | bytes 1179656 | tf_op jit(solution)/shard_map/ppermute | solution.py:502
  43.0 34.0 %collective-permute-start.10 = (bf16[4,128,768]{2,1,0:T(8,128)(2,1)S(1)}, bf16[4,128,768]{2,1,0:T(8,128)(2,1)S(1)}, u32[]{:S(2)}, u32[]{:S(2)}) collective-permute-start(bf16[4,128,768]{2,1,0:T(8,128)(2,1)S(1)} %get-tuple-element.77), channel_id=1, source_target_pairs={{1,2},{2,1},{3,4},{4,3},{5,6},{6,5},{9,10},{10,9},{11,12},{12,11},... | collective-permute-start | bytes 2359304 | tf_op jit(solution)/shard_map/ppermute | solution.py:502
  60.8 1.6 %collective-permute-start.5 = (s16[128,1152]{1,0:T(8,128)(2,1)S(1)}, s16[128,1152]{1,0:T(8,128)(2,1)S(1)}, u32[]{:S(2)}, u32[]{:S(2)}) collective-permute-start(s16[128,1152]{1,0:T(8,128)(2,1)S(1)} %get-tuple-element.70.mine_ref), channel_id=1, source_target_pairs={{0,8},{8,0},{16,24},{24,16},{1,9},{9,1},{17,25},{25,17},{2,10},{10... | collective-permute-start | bytes 884744 | tf_op jit(solution)/shard_map/ppermute | solution.py:490
  61.0 10.0 %collective-permute-start.8 = (bf16[2,128,768]{2,1,0:T(8,128)(2,1)S(1)}, bf16[2,128,768]{2,1,0:T(8,128)(2,1)S(1)}, u32[]{:S(2)}, u32[]{:S(2)}) collective-permute-start(bf16[2,128,768]{2,1,0:T(8,128)(2,1)S(1)} %get-tuple-element.75), channel_id=1, source_target_pairs={{0,8},{8,0},{16,24},{24,16},{1,9},{9,1},{17,25},{25,17},{2,10},{10... | collective-permute-start | bytes 1179656 | tf_op jit(solution)/shard_map/ppermute | solution.py:502
  61.5 9.5 %collective-permute-start.9 = (bf16[2,128,768]{2,1,0:T(8,128)(2,1)S(1)}, bf16[2,128,768]{2,1,0:T(8,128)(2,1)S(1)}, u32[]{:S(2)}, u32[]{:S(2)}) collective-permute-start(bf16[2,128,768]{2,1,0:T(8,128)(2,1)S(1)} %get-tuple-element.76), channel_id=1, source_target_pairs={{8,16},{16,8},{9,17},{17,9},{10,18},{18,10},{11,19},{19,11},{12,20... | collective-permute-start | bytes 1179656 | tf_op jit(solution)/shard_map/ppermute | solution.py:502
  68.3 14.7 %collective-permute-start.11 = (s16[128,1152]{1,0:T(8,128)(2,1)S(1)}, s16[128,1152]{1,0:T(8,128)(2,1)S(1)}, u32[]{:S(2)}, u32[]{:S(2)}) collective-permute-start(s16[128,1152]{1,0:T(8,128)(2,1)S(1)} %get-tuple-element.81.mine_ref), channel_id=1, source_target_pairs={{0,16},{8,24},{16,0},{24,8},{1,17},{9,25},{17,1},{25,9},{2,18},{10... | collective-permute-start | bytes 884744 | tf_op jit(solution)/shard_map/ppermute | solution.py:490
  148.9 4.1 %collective-permute-start.14 = (f32[96,128]{1,0:T(8,128)S(1)}, f32[96,128]{1,0:T(8,128)S(1)}, u32[]{:S(2)}, u32[]{:S(2)}) collective-permute-start(f32[96,128]{1,0:T(8,128)S(1)} %fusion.4), channel_id=1, source_target_pairs={{0,24},{8,16},{16,8},{24,0},{1,25},{9,17},{17,9},{25,1},{2,26},{10... | collective-permute-start | bytes 147464 | tf_op jit(solution)/shard_map/ppermute | solution.py:490
  148.9 4.9 %collective-permute-start.13 = (f32[96,128]{1,0:T(8,128)S(1)}, f32[96,128]{1,0:T(8,128)S(1)}, u32[]{:S(2)}, u32[]{:S(2)}) collective-permute-start(f32[96,128]{1,0:T(8,128)S(1)} %fusion.4), channel_id=1, source_target_pairs={{0,16},{8,24},{16,0},{24,8},{1,17},{9,25},{17,1},{25,9},{2,18},{10... | collective-permute-start | bytes 147464 | tf_op jit(solution)/shard_map/ppermute | solution.py:490
  150.5 3.4 %collective-permute-start.12 = (f32[96,128]{1,0:T(8,128)S(1)}, f32[96,128]{1,0:T(8,128)S(1)}, u32[]{:S(2)}, u32[]{:S(2)}) collective-permute-start(f32[96,128]{1,0:T(8,128)S(1)} %fusion.4), channel_id=1, source_target_pairs={{0,8},{8,0},{16,24},{24,16},{1,9},{9,1},{17,25},{25,17},{2,10},{10... | collective-permute-start | bytes 147464 | tf_op jit(solution)/shard_map/ppermute | solution.py:490
Sparse Core Ops, SparseCore 0:
  84.4 63.4 reduce-scatter.1
